TPU v7x, 32 devices: a whole 2x2x4 slice. The times are simulated.
32 devices in a mesh: macro: 8 (over y, x, core), grid: 4 (over z).
Axes of the slice: x: 2, y: 2, z: 4, core: 2. Of those that a mesh axis runs over, the one named last changes fastest.
Arguments:
- orbitals: float32 [8, 2, 16, 32, 1024], P('macro', None, None, 'grid'), may hold values from -45 to 45
- local_potential: float32 [32, 1024], P('grid'), may hold values from -8 to 2
- atom_sites: int32 [8, 3], replicated, may hold values from 0 to 31, as said below
- host_point: int32 [8], P('macro'), may hold values from 0 to 511, as said below
- fields: float32 [2, 512], P(None, 'macro'), may hold values from -4 to 4
Outputs:
- orbitals_out: float32 [8, 2, 16, 32, 1024], P('macro', None, None, 'grid')
- fields_out: float32 [2, 512], P(None, 'macro')
Inputs may be any that keep to these rules, and one draw needn't show every extreme that they name: `host_point`: distinct macroscopic points; for every index g of macro the points g * 64 to (g + 1) * 64 - 1 hold exactly one of them. `atom_sites`: two atoms may share a position.
All inputs are finite; a program needn't handle non-finite values.
Results may differ from a plain program's by a relative error of at most 0.0003.
Values sent between devices are 32-bit elements; how exact they have to be, the bound alone decides.
No kernel may reach another device: no remote copies, remote signals or barrier semaphores. Data moves between devices by JAX's collectives and lax.ppermute only.
A program may use at most 128 MiB of HBM per device.

v0:
```python
import jax
import jax.numpy as jnp
from jax import lax
from jax.sharding import PartitionSpec as P

G = 32
NORB = 16
ORDER = 4
STEPS = 2


second_weights = (-205.0 / 72.0, 8.0 / 5.0, -1.0 / 5.0, 8.0 / 315.0, -1.0 / 560.0)
first_weights = (4.0 / 5.0, -1.0 / 5.0, 4.0 / 105.0, -1.0 / 280.0)
spacing = 0.3206
time_step = 0.02
courant_square = 0.81
source_weight = 0.1
radial_strength = 0.3
polar_strength = -0.2
projector_width = 2.5
highest = lax.Precision.HIGHEST


def along_last(field, offset, width):
    position = lax.broadcasted_iota(jnp.int32, (field.shape[-1],), 0) % width
    direct = jnp.roll(field, -offset, axis=-1)
    if offset > 0:
        wrapped = jnp.roll(field, width - offset, axis=-1)
        inside = position + offset < width
    else:
        wrapped = jnp.roll(field, -offset - width, axis=-1)
        inside = position + offset >= 0
    return jnp.where(inside, direct, wrapped)


def first_derivative(along_first):
    total = first_weights[0] * (along_first(1) - along_first(-1))
    for reach in range(2, 5):
        total = total + first_weights[reach - 1] * (along_first(reach) - along_first(-reach))
    return total / spacing


def laplacian(field, along_first, width):
    total = 3.0 * second_weights[0] * field
    for reach in range(1, 5):
        beside_all = along_first(reach) + along_first(-reach)
        beside_all = (
            beside_all
            + jnp.roll(field, -reach * width, axis=-1)
            + jnp.roll(field, reach * width, axis=-1)
        )
        beside_all = beside_all + along_last(field, reach, width) + along_last(field, -reach, width)
        total = total + second_weights[reach] * beside_all
    return total / (spacing * spacing)


def hamiltonian(field, along_first, potential, vector_value, project, width):
    derivative = first_derivative(along_first)
    drift = jnp.stack([vector_value * derivative[1], -vector_value * derivative[0]])
    local = (0.5 * vector_value * vector_value + potential) * field
    return -0.5 * laplacian(field, along_first, width) + drift + local + project(field)


def propagate(field, neighbours, potential, vector_value, project, width, order_count):
    total = field
    term = field
    for order in range(1, order_count + 1):
        image = hamiltonian(term, neighbours(term), potential, vector_value, project, width)
        term = time_step / order * jnp.stack([image[1], -image[0]])
        total = total + term
    return total


def projector_tables(atom_sites, width):
    positions = lax.broadcasted_iota(jnp.int32, (1, width), 1)
    tables = []
    for axis_number in range(3):
        offset = (
            jnp.mod(positions - atom_sites[:, axis_number : axis_number + 1] + width // 2, width)
            - width // 2
        )
        distance = offset.astype(jnp.float32)
        bell = jnp.exp(-0.5 * distance * distance / (projector_width * projector_width))
        rows = [bell, bell, bell, bell]
        rows[axis_number + 1] = distance / projector_width * bell
        tables.append(jnp.stack(rows, axis=1).reshape(-1, width))
    count = tables[1].shape[0]
    cross = (tables[1][:, :, None] * tables[2][:, None, :]).reshape(count, width * width)
    pattern = jnp.array(
        [radial_strength, polar_strength, polar_strength, polar_strength], jnp.float32
    )
    strengths = jnp.tile(pattern, atom_sites.shape[0])
    return (tables[0], cross, strengths)


def nonlocal_part(field, first_table, cross_table, strengths, finish):
    inner = jnp.einsum("coxr,pr->coxp", field, cross_table, precision=highest)
    projection = finish(jnp.einsum("coxp,px->cop", inner, first_table, precision=highest))
    spread = jnp.einsum("cop,px->coxp", projection * strengths, first_table, precision=highest)
    return jnp.einsum("coxp,pr->coxr", spread, cross_table, precision=highest)


def per_device(orbitals, local_potential, atom_sites, host_point, fields):
    field = orbitals[0]
    first_full, cross_table, strengths = projector_tables(atom_sites, G)
    field = lax.all_to_all(field, "grid", split_axis=1, concat_axis=2, tiled=True)
    potential = lax.all_gather(local_potential, "grid", axis=0, tiled=True)

    def neighbours(term):
        return lambda reach: jnp.roll(term, -reach, axis=2)

    def finish(projection):
        return projection

    def project(term):
        return nonlocal_part(term, first_full, cross_table, strengths, finish)

    owned = fields.shape[1]
    previous = fields[0]
    present = fields[1]
    host = host_point[0]
    offset_start = lax.axis_index("macro") * owned
    for step in range(STEPS):
        seen = lax.all_gather(present, "macro", axis=0, tiled=True)
        positions = lax.broadcasted_iota(jnp.int32, seen.shape, 0)
        vector_value = jnp.sum(jnp.where(positions == host, seen, 0.0))
        field = propagate(field, neighbours, potential, vector_value, project, G, ORDER)
        derivative = first_derivative(neighbours(field))
        flow = jnp.sum(field[0] * derivative[1] - field[1] * derivative[0])
        density = jnp.sum(field * field)
        flow, density = lax.psum((flow, density), "grid")
        current = (flow + vector_value * density) / (G**3 * NORB)
        source = lax.psum_scatter(
            jnp.where(positions == host, current, 0.0), "macro", scatter_dimension=0, tiled=True
        )
        rim = lax.dynamic_slice_in_dim(jnp.pad(seen, 1), offset_start, owned + 2)
        following = (
            2.0 * present
            - previous
            + courant_square * (rim[2:] - 2.0 * present + rim[:-2])
            - source_weight * source
        )
        previous, present = (present, following)
    field = lax.all_to_all(field, "grid", split_axis=2, concat_axis=1, tiled=True)
    return (field[None], jnp.stack([previous, present]))


def solution(mesh):
    in_specs = (
        P("macro", None, None, "grid", None),
        P("grid", None),
        P(),
        P("macro"),
        P(None, "macro"),
    )
    out_specs = (P("macro", None, None, "grid", None), P(None, "macro"))
    return jax.shard_map(
        per_device, mesh=mesh, in_specs=in_specs, out_specs=out_specs, check_vma=False
    )
```

profile of v0, /device:TPU:17, one launch (start us, length us, event | category | flops | bytes accessed | tf_op | source)
XLA Modules:
  0.0 576.3 jit_solution(16013890159284555611)
XLA Ops:
  0.6 2.3 copy.82
  2.9 4.6 all-to-all-start
  11.0 12.4 %all-reduce.2 = f32[512]{0:T(512)S(1)} all-reduce(f32[512]{0:T(512)S(1)} %bitcast_dynamic-update-slice_fusion), channel_id=2, replica_groups=mesh['macro'=8,'grid'=4] {'macro'}, use_global_device_ids=true, to_apply=%add.2 | all-reduce | flops 512 | bytes 4096 | tf_op jit(solution)/shard_map/all_gather | solution.py:124
  28.8 8.7 %all_gather.10 = f32[32,1024]{1,0:T(8,128)S(1)} all-gather(f32[8,1024]{1,0:T(8,128)S(1)} %copy-done.144), channel_id=1, replica_groups=mesh['macro'=8,'grid'=4] {'grid'}, dimensions={0}, use_global_device_ids=true | all-gather | bytes 163840 | tf_op jit(solution)/shard_map/all_gather | solution.py:107
  79.8 2.5 convolution_bitcast_fusion.7
  82.2 4.2 fusion.261
  89.2 4.4 add_multiply_fusion.7
  96.4 12.1 %convolution_add_fusion.7 = f32[2,4,32,1024]{3,2,1,0:T(8,128)S(1)} fusion(f32[2,4,32,32]{3,2,1,0:T(8,128)} %get-tuple-element.587, f32[2,4,32,992]{3,2,1,0:T(8,128)} %get-tuple-element.589, f32[2,4,32,992]{3,2,1,0:T(8,128)} %get-tuple-element.588, f32[2,4,32,32]{3,2,1,0:T(8,128)} %get-tuple-element.586, f32[2,4,32,1]{3,2,1,0:T(8,128)} %get-tuple-element.583, ...), kind=kOutput, calls=%fused_computation.7 | convolution fusion | flops 120332288 | bytes 36975616 | tf_op jit(solution)/shard_map/coxp,pr->coxr/dot_general | solution.py:100
  145.9 12.4 %convolution_add_fusion.6 = f32[2,4,32,1024]{3,2,1,0:T(8,128)S(1)} fusion(f32[2,4,32,32]{3,2,1,0:T(8,128)} %get-tuple-element.521, f32[2,4,32,992]{3,2,1,0:T(8,128)} %get-tuple-element.523, f32[2,4,32,992]{3,2,1,0:T(8,128)} %get-tuple-element.522, f32[2,4,32,32]{3,2,1,0:T(8,128)} %get-tuple-element.520, f32[2,4,32,1]{3,2,1,0:T(8,128)} %get-tuple-element.517, ...), kind=kOutput, calls=%fused_computation.6 | convolution fusion | flops 120594432 | bytes 36975616 | tf_op jit(solution)/shard_map/coxp,pr->coxr/dot_general | solution.py:100
  195.3 12.5 %convolution_add_fusion.5 = f32[2,4,32,1024]{3,2,1,0:T(8,128)S(1)} fusion(f32[2,4,32,32]{3,2,1,0:T(8,128)} %get-tuple-element.455, f32[2,4,32,992]{3,2,1,0:T(8,128)} %get-tuple-element.457, f32[2,4,32,992]{3,2,1,0:T(8,128)} %get-tuple-element.456, f32[2,4,32,32]{3,2,1,0:T(8,128)} %get-tuple-element.454, f32[2,4,32,1]{3,2,1,0:T(8,128)} %get-tuple-element.451, ...), kind=kOutput, calls=%fused_computation.5 | convolution fusion | flops 120594432 | bytes 36975616 | tf_op jit(solution)/shard_map/coxp,pr->coxr/dot_general | solution.py:100
  244.4 13.7 %convolution_add_fusion.4 = f32[2,4,32,1024]{3,2,1,0:T(8,128)} fusion(f32[2,4,32,32]{3,2,1,0:T(8,128)} %get-tuple-element.389, f32[2,4,32,992]{3,2,1,0:T(8,128)} %get-tuple-element.391, f32[2,4,32,992]{3,2,1,0:T(8,128)} %get-tuple-element.390, f32[2,4,32,32]{3,2,1,0:T(8,128)} %get-tuple-element.388, f32[2,4,32,1]{3,2,1,0:T(8,128)} %get-tuple-element.385, ...), kind=kOutput, calls=%fused_computation.4 | convolution fusion | flops 120594432 | bytes 36975616 | tf_op jit(solution)/shard_map/coxp,pr->coxr/dot_general | solution.py:100
  297.0 9.6 %all-reduce.7 = (f32[]{:T(128)}, f32[]{:T(128)}) all-reduce(f32[]{:T(128)} %fusion.228, f32[]{:T(128)} %get-tuple-element.10), channel_id=1, replica_groups=mesh['macro'=8,'grid'=4] {'grid'}, use_global_device_ids=true, to_apply=%region_2.3 | all-reduce | flops 2 | bytes 16 | tf_op jit(solution)/shard_map/psum | solution.py:131
  308.5 18.1 %all-reduce.4 = f32[512]{0:T(512)S(1)} all-reduce(f32[512]{0:T(512)S(1)} %fusion.298), channel_id=3, replica_groups=mesh['macro'=8,'grid'=4] {'macro'}, use_global_device_ids=true, to_apply=%region_5.6.clone | all-reduce | flops 512 | bytes 4096
  327.9 11.8 %all-reduce.3 = f32[512]{0:T(512)S(1)} all-reduce(f32[512]{0:T(512)S(1)} %get-tuple-element.8), channel_id=1, replica_groups=mesh['macro'=8,'grid'=4] {'macro'}, use_global_device_ids=true, to_apply=%add.3 | all-reduce | flops 512 | bytes 4096
  348.7 13.7 %convolution_add_fusion.3 = f32[2,4,32,1024]{3,2,1,0:T(8,128)S(1)} fusion(f32[2,4,32,32]{3,2,1,0:T(8,128)} %get-tuple-element.323, f32[2,4,32,992]{3,2,1,0:T(8,128)} %get-tuple-element.325, f32[2,4,32,992]{3,2,1,0:T(8,128)} %get-tuple-element.324, f32[2,4,32,32]{3,2,1,0:T(8,128)} %get-tuple-element.322, f32[2,4,32,1]{3,2,1,0:T(8,128)} %get-tuple-element.319, ...), kind=kOutput, calls=%fused_computation.3 | convolution fusion | flops 120332288 | bytes 36975616 | tf_op jit(solution)/shard_map/coxp,pr->coxr/dot_general | solution.py:100
  399.8 12.2 %convolution_add_fusion.2 = f32[2,4,32,1024]{3,2,1,0:T(8,128)S(1)} fusion(f32[2,4,32,32]{3,2,1,0:T(8,128)} %get-tuple-element.241, f32[2,4,32,992]{3,2,1,0:T(8,128)} %get-tuple-element.243, f32[2,4,32,992]{3,2,1,0:T(8,128)} %get-tuple-element.242, f32[2,4,32,32]{3,2,1,0:T(8,128)} %get-tuple-element.240, f32[2,4,32,1]{3,2,1,0:T(8,128)} %get-tuple-element.237, ...), kind=kOutput, calls=%fused_computation.2 | convolution fusion | flops 120594432 | bytes 36975616 | tf_op jit(solution)/shard_map/coxp,pr->coxr/dot_general | solution.py:100
  448.9 12.7 %convolution_add_fusion.1 = f32[2,4,32,1024]{3,2,1,0:T(8,128)S(1)} fusion(f32[2,4,32,32]{3,2,1,0:T(8,128)} %get-tuple-element.175, f32[2,4,32,992]{3,2,1,0:T(8,128)} %get-tuple-element.177, f32[2,4,32,992]{3,2,1,0:T(8,128)} %get-tuple-element.176, f32[2,4,32,32]{3,2,1,0:T(8,128)} %get-tuple-element.174, f32[2,4,32,1]{3,2,1,0:T(8,128)} %get-tuple-element.171, ...), kind=kOutput, calls=%fused_computation.1 | convolution fusion | flops 120594432 | bytes 36975616 | tf_op jit(solution)/shard_map/coxp,pr->coxr/dot_general | solution.py:100
  498.5 13.6 %convolution_add_fusion = f32[2,4,32,1024]{3,2,1,0:T(8,128)} fusion(f32[2,4,32,32]{3,2,1,0:T(8,128)} %get-tuple-element.109, f32[2,4,32,992]{3,2,1,0:T(8,128)} %get-tuple-element.111, f32[2,4,32,992]{3,2,1,0:T(8,128)} %get-tuple-element.110, f32[2,4,32,32]{3,2,1,0:T(8,128)} %get-tuple-element.108, f32[2,4,32,1]{3,2,1,0:T(8,128)} %get-tuple-element.105, ...), kind=kOutput, calls=%fused_computation | convolution fusion | flops 120594432 | bytes 36975616 | tf_op jit(solution)/shard_map/coxp,pr->coxr/dot_general | solution.py:100
  512.1 2.5 slice_bitcast_fusion.3
  514.6 2.7 fusion.203
  525.1 6.5 %all-to-all-start.1 = ((f32[2,4,32,1024]{3,1,0,2:T(4,128)}), f32[2,4,32,1024]{3,1,0,2:T(4,128)S(1)}, u32[]{:S(2)}, u32[]{:S(2)}) async-start(f32[2,4,32,1024]{3,1,0,2:T(4,128)} %copy.26), calls=%async_computation.1 | async-start | bytes 2097152 | tf_op jit(solution)/shard_map/all_to_all | solution.py:144
  533.9 3.0 fusion.208
  539.1 18.4 %all-reduce.6 = (f32[]{:T(128)}, f32[]{:T(128)}) all-reduce(f32[]{:T(128)} %fusion.226, f32[]{:T(128)} %fusion.217), channel_id=1, replica_groups=mesh['macro'=8,'grid'=4] {'grid'}, use_global_device_ids=true, to_apply=%region_8.9 | all-reduce | flops 2 | bytes 16 | tf_op jit(solution)/shard_map/psum | solution.py:131
  559.4 13.7 %all-reduce.5 = f32[512]{0:T(512)S(1)} all-reduce(f32[512]{0:T(512)S(1)} %fusion.297), channel_id=4, replica_groups=mesh['macro'=8,'grid'=4] {'macro'}, use_global_device_ids=true, to_apply=%region_11.12.clone | all-reduce | flops 512 | bytes 4096
  (665 shorter events, 335.4 us)
Async XLA Ops:
  2.9 38.8 %all-to-all-start = ((f32[2,16,8,1024]{3,2,0,1:T(8,128)}), f32[2,16,8,1024]{3,2,0,1:T(8,128)S(1)}, u32[]{:S(2)}, u32[]{:S(2)}) async-start(f32[2,16,8,1024]{3,2,0,1:T(8,128)} %bitcast.204), calls=%async_computation | async-start | bytes 2097152 | tf_op jit(solution)/shard_map/all_to_all | solution.py:106
  109.8 149.8 %copy-start = (f32[1,4,32,1024]{3,2,1,0:T(8,128)}, f32[1,4,32,1024]{3,2,1,0:T(8,128)S(1)}, u32[]{:S(2)}) copy-start(f32[1,4,32,1024]{3,2,1,0:T(8,128)S(1)} %get-tuple-element.248) | copy-start | bytes 1572868
  109.8 149.8 %copy-start.2 = (f32[1,4,32,1024]{3,2,1,0:T(8,128)}, f32[1,4,32,1024]{3,2,1,0:T(8,128)S(1)}, u32[]{:S(2)}) copy-start(f32[1,4,32,1024]{3,2,1,0:T(8,128)S(1)} %get-tuple-element.249) | copy-start | bytes 1572868
  110.9 31.0 %copy-start.129 = (f32[2,4,1,1024]{3,2,1,0:T(1,128)}, f32[2,4,1,1024]{3,2,1,0:T(1,128)S(1)}, u32[]{:S(2)}) copy-start(f32[2,4,1,1024]{3,2,1,0:T(1,128)S(1)} %get-tuple-element.474) | copy-start | bytes 98308
  159.6 100.0 %copy-start.4 = (f32[1,4,32,1024]{3,2,1,0:T(8,128)}, f32[1,4,32,1024]{3,2,1,0:T(8,128)S(1)}, u32[]{:S(2)}) copy-start(f32[1,4,32,1024]{3,2,1,0:T(8,128)S(1)} %get-tuple-element.252) | copy-start | bytes 1572868
  159.6 100.0 %copy-start.6 = (f32[1,4,32,1024]{3,2,1,0:T(8,128)}, f32[1,4,32,1024]{3,2,1,0:T(8,128)S(1)}, u32[]{:S(2)}) copy-start(f32[1,4,32,1024]{3,2,1,0:T(8,128)S(1)} %get-tuple-element.253) | copy-start | bytes 1572868
  160.8 31.4 %copy-start.125 = (f32[2,4,1,1024]{3,2,1,0:T(1,128)}, f32[2,4,1,1024]{3,2,1,0:T(1,128)S(1)}, u32[]{:S(2)}) copy-start(f32[2,4,1,1024]{3,2,1,0:T(1,128)S(1)} %get-tuple-element.408) | copy-start | bytes 98308
  160.8 31.4 %copy-start.126 = (f32[2,4,1,1024]{3,2,1,0:T(1,128)}, f32[2,4,1,1024]{3,2,1,0:T(1,128)S(1)}, u32[]{:S(2)}) copy-start(f32[2,4,1,1024]{3,2,1,0:T(1,128)S(1)} %get-tuple-element.409) | copy-start | bytes 98308
  160.8 31.4 %copy-start.96 = (f32[2,4,2,1024]{3,2,1,0:T(2,128)}, f32[2,4,2,1024]{3,2,1,0:T(2,128)S(1)}, u32[]{:S(2)}) copy-start(f32[2,4,2,1024]{3,2,1,0:T(2,128)S(1)} %get-tuple-element.405) | copy-start | bytes 196612
  209.1 50.6 %copy-start.8 = (f32[1,4,32,1024]{3,2,1,0:T(8,128)}, f32[1,4,32,1024]{3,2,1,0:T(8,128)S(1)}, u32[]{:S(2)}) copy-start(f32[1,4,32,1024]{3,2,1,0:T(8,128)S(1)} %get-tuple-element.256) | copy-start | bytes 1572868
  209.1 50.6 %copy-start.10 = (f32[1,4,32,1024]{3,2,1,0:T(8,128)}, f32[1,4,32,1024]{3,2,1,0:T(8,128)S(1)}, u32[]{:S(2)}) copy-start(f32[1,4,32,1024]{3,2,1,0:T(8,128)S(1)} %get-tuple-element.257) | copy-start | bytes 1572868
  210.2 31.1 %copy-start.123 = (f32[2,4,1,1024]{3,2,1,0:T(1,128)}, f32[2,4,1,1024]{3,2,1,0:T(1,128)S(1)}, u32[]{:S(2)}) copy-start(f32[2,4,1,1024]{3,2,1,0:T(1,128)S(1)} %get-tuple-element.342) | copy-start | bytes 98308
  210.2 31.1 %copy-start.124 = (f32[2,4,1,1024]{3,2,1,0:T(1,128)}, f32[2,4,1,1024]{3,2,1,0:T(1,128)S(1)}, u32[]{:S(2)}) copy-start(f32[2,4,1,1024]{3,2,1,0:T(1,128)S(1)} %get-tuple-element.343) | copy-start | bytes 98308
  294.9 31.7 %copy-start.149 = (f32[66]{0:T(128)S(1)}, f32[66]{0:T(128)}, u32[]{:S(2)}) copy-start(f32[66]{0:T(128)} %pad_dynamic-slice_fusion.1) | copy-start | bytes 796
  364.9 31.2 %copy-start.131 = (f32[2,4,1,1024]{3,2,1,0:T(1,128)}, f32[2,4,1,1024]{3,2,1,0:T(1,128)S(1)}, u32[]{:S(2)}) copy-start(f32[2,4,1,1024]{3,2,1,0:T(1,128)S(1)} %get-tuple-element.194) | copy-start | bytes 98308
  364.9 31.2 %copy-start.132 = (f32[2,4,1,1024]{3,2,1,0:T(1,128)}, f32[2,4,1,1024]{3,2,1,0:T(1,128)S(1)}, u32[]{:S(2)}) copy-start(f32[2,4,1,1024]{3,2,1,0:T(1,128)S(1)} %get-tuple-element.195) | copy-start | bytes 98308
  365.0 31.1 %copy-start.99 = (f32[2,4,2,1024]{3,2,1,0:T(2,128)}, f32[2,4,2,1024]{3,2,1,0:T(2,128)S(1)}, u32[]{:S(2)}) copy-start(f32[2,4,2,1024]{3,2,1,0:T(2,128)S(1)} %get-tuple-element.191) | copy-start | bytes 196612
  414.5 31.3 %copy-start.127 = (f32[2,4,1,1024]{3,2,1,0:T(1,128)}, f32[2,4,1,1024]{3,2,1,0:T(1,128)S(1)}, u32[]{:S(2)}) copy-start(f32[2,4,1,1024]{3,2,1,0:T(1,128)S(1)} %get-tuple-element.128) | copy-start | bytes 98308
  414.5 31.3 %copy-start.128 = (f32[2,4,1,1024]{3,2,1,0:T(1,128)}, f32[2,4,1,1024]{3,2,1,0:T(1,128)S(1)}, u32[]{:S(2)}) copy-start(f32[2,4,1,1024]{3,2,1,0:T(1,128)S(1)} %get-tuple-element.129) | copy-start | bytes 98308
  414.6 31.3 %copy-start.97 = (f32[2,4,2,1024]{3,2,1,0:T(2,128)}, f32[2,4,2,1024]{3,2,1,0:T(2,128)S(1)}, u32[]{:S(2)}) copy-start(f32[2,4,2,1024]{3,2,1,0:T(2,128)S(1)} %get-tuple-element.125) | copy-start | bytes 196612
  464.0 31.5 %copy-start.120 = (f32[2,4,1,1024]{3,2,1,0:T(1,128)}, f32[2,4,1,1024]{3,2,1,0:T(1,128)S(1)}, u32[]{:S(2)}) copy-start(f32[2,4,1,1024]{3,2,1,0:T(1,128)S(1)} %get-tuple-element.62) | copy-start | bytes 98308
  464.0 31.5 %copy-start.121 = (f32[2,4,1,1024]{3,2,1,0:T(1,128)}, f32[2,4,1,1024]{3,2,1,0:T(1,128)S(1)}, u32[]{:S(2)}) copy-start(f32[2,4,1,1024]{3,2,1,0:T(1,128)S(1)} %get-tuple-element.63) | copy-start | bytes 98308
  464.1 31.4 %copy-start.93 = (f32[2,4,2,1024]{3,2,1,0:T(2,128)}, f32[2,4,2,1024]{3,2,1,0:T(2,128)S(1)}, u32[]{:S(2)}) copy-start(f32[2,4,2,1024]{3,2,1,0:T(2,128)S(1)} %get-tuple-element.59) | copy-start | bytes 196612
  525.1 49.5 %all-to-all-start.1 = ((f32[2,4,32,1024]{3,1,0,2:T(4,128)}), f32[2,4,32,1024]{3,1,0,2:T(4,128)S(1)}, u32[]{:S(2)}, u32[]{:S(2)}) async-start(f32[2,4,32,1024]{3,1,0,2:T(4,128)} %copy.26), calls=%async_computation.1 | async-start | bytes 2097152 | tf_op jit(solution)/shard_map/all_to_all | solution.py:144
  (134 other events, 1076.0 us)
where the time goes:
time: 586 us; the launch traced here: 576 us
  local copies, waits for them, and re-layouts  278 us (47%)
  matrix products  118 us (20%)
  blocking collectives  92.6 us (16%)
  other arithmetic  64.3 us (11%)
  between operations  12.7 us (2%)
  starting transfers between devices  11.2 us (2%)
    dot_general x8, matrix products, nonlocal_part(): return jnp.einsum('coxp,pr->coxr', spread, cross_table, precision=highest)  103 us
    slice x64, local copies, waits for them, and re-layouts, along_last(): direct = jnp.roll(field, -offset, axis=-1)  78.5 us
    slice x64, local copies, waits for them, and re-layouts, along_last(): wrapped = jnp.roll(field, -offset - width, axis=-1)  78.5 us
    slice x64, local copies, waits for them, and re-layouts, laplacian(): jnp.roll(field, reach * width, axis=-1)  76.4 us
    unnamed x3, blocking collectives  43.6 us
    psum x2, blocking collectives, per_device(): flow, density = lax.psum((flow, density), 'grid')  28 us
    slice x72, local copies, waits for them, and re-layouts, neighbours(): return lambda reach: jnp.roll(term, -reach, axis=2)  22.2 us
    div x9, other arithmetic, first_derivative(): return total / spacing  16.5 us
  transfers between devices with their start and end apart: 2, of which 0 were waited for; matrix products, arithmetic and copies ran while one was open for 2% of the time, Pallas kernels for 0%

commit v1 on v0

v1 whole, which is shorter than its diff:
```python
import functools

import jax
import jax.numpy as jnp
import numpy as np
from jax import lax
from jax.experimental import pallas as pl
from jax.experimental.pallas import tpu as pltpu
from jax.sharding import PartitionSpec as P

ORDER = 4
STEPS = 2
spacing = 0.3206
time_step = 0.02
courant_square = 0.81
source_weight = 0.1
radial_strength = 0.3
polar_strength = -0.2
projector_width = 2.5

SECOND = (-14350.0, 8064.0, -1008.0, 128.0, -9.0)
FIRST = (672.0, -168.0, 32.0, -3.0)
KINETIC = 1.0 / (2.0 * 5040.0 * spacing * spacing)
SLOPE = 1.0 / (840.0 * spacing)

LANES = 128
ROWS = 8
LIMIT = 24 * 1024 * 1024


def stencil_weights(width):
    group = LANES // width
    total = np.zeros((LANES, 3 * LANES), np.float32)
    for y_in in range(group):
        for z_in in range(width):
            for y_out in range(group):
                for part, step in enumerate((0, group, -group)):
                    reach = abs(step + y_in - y_out)
                    if 1 <= reach <= 4:
                        total[y_in * width + z_in, part * LANES + y_out * width + z_in] += SECOND[reach]
            for reach in range(1, 5):
                for z_out in ((z_in + reach) % width, (z_in - reach) % width):
                    total[y_in * width + z_in, y_in * width + z_out] += SECOND[reach]
    return jnp.asarray(np.concatenate([total, total], axis=0), jnp.bfloat16)


def periodic(distance, width):
    return ((distance + width // 2) & (width - 1)) - width // 2


def bell_of(offset):
    distance = offset.astype(jnp.float32)
    bell = jnp.exp(-0.5 * distance * distance / (projector_width * projector_width))
    return bell, distance / projector_width * bell


def tables_kernel(atoms, planes, site_ref, grid_ref, stencil_ref, yz_ref, zy_ref, xbell_ref, xslope_ref, y_ref):
    width = xbell_ref.shape[0]
    kinds = 2 * atoms
    group = LANES // width

    def site_of(column, axis_number):
        atom = (column % kinds) // 2
        position = jnp.zeros(column.shape, jnp.int32)
        for number in range(atoms):
            position = jnp.where(atom == number, site_ref[number, axis_number], position)
        return position

    def factor(coordinate, column):
        bell, slope = bell_of(periodic(coordinate - site_of(column, 2), width))
        value = jnp.where(column % 2 == 0, bell, slope)
        high = value.astype(jnp.bfloat16).astype(jnp.float32)
        return jnp.where(column % LANES < LANES // 2, high, value - high)

    def groups_agree(point, column):
        return (point % LANES) // width == (column // kinds) % group

    shape = (2 * LANES, LANES)
    first = lax.broadcasted_iota(jnp.int32, shape, 0)
    last = lax.broadcasted_iota(jnp.int32, shape, 1)
    yz_ref[:, : 3 * LANES] = stencil_ref[...]
    inward = jnp.where(groups_agree(first, last), factor(first % width, last), 0.0)
    yz_ref[:, 3 * LANES :] = inward.astype(jnp.bfloat16)
    outward = jnp.where(groups_agree(last, first), factor(last % width, first), 0.0)
    zy_ref[...] = outward.astype(jnp.bfloat16)

    shape = (width, ROWS, LANES)
    plane = lax.broadcasted_iota(jnp.int32, shape, 0) + grid_ref[0] * planes
    column = lax.broadcasted_iota(jnp.int32, shape, 2)
    bell, slope = bell_of(periodic(plane - site_of(column, 0), width))
    xbell_ref[...] = bell
    xslope_ref[...] = slope

    shape = (ROWS, LANES)
    column = lax.broadcasted_iota(jnp.int32, shape, 1)
    row = lax.broadcasted_iota(jnp.int32, shape, 0) * group + (column // kinds) % group
    bell, slope = bell_of(periodic(row - site_of(column, 1), width))
    scale = -1.0 / KINETIC
    even = column % 2 == 0
    y_ref[0] = bell
    y_ref[1] = slope
    y_ref[2] = bell * jnp.where(even, scale * radial_strength, scale * polar_strength)
    y_ref[3] = bell * jnp.where(even, scale * polar_strength, 0.0)
    y_ref[4] = slope * jnp.where(even, scale * polar_strength, 0.0)


def vector_kernel(blocks, host_ref, *refs):
    out_ref = refs[blocks]
    owned = refs[0].shape[1]
    host = host_ref[0]
    here = host_ref[1]
    sums = [jnp.zeros((1, owned), jnp.float32) for _ in range(4)]
    for number in range(blocks):
        start = lax.rem(here + number, blocks) * owned
        position = lax.broadcasted_iota(jnp.int32, (1, owned), 1) + start
        previous = refs[number][0:1, :]
        present = refs[number][1:2, :]
        for index, (value, place) in enumerate(
            ((present, host), (previous, host), (present, host - 1), (present, host + 1))
        ):
            sums[index] = sums[index] + jnp.where(position == place, value, 0.0)
    present, previous, left, right = [jnp.sum(value) for value in sums]
    out_ref[0] = present
    out_ref[1] = 2.0 * present - previous + courant_square * (right - 2.0 * present + left)


def pack_kernel(parts, share, grid_ref, source_ref, *refs):
    outs, sems = refs[:-1], refs[-1]
    copies = []
    for part in range(parts):
        owner = lax.rem(grid_ref[0] + part, parts)
        for orbital in range(share):
            number = part * share + orbital
            copies.append(
                pltpu.make_async_copy(
                    source_ref.at[:, owner * share + orbital], outs[number], sems.at[number]
                )
            )
    for copy in copies:
        copy.start()
    for copy in copies:
        copy.wait()


def unpack_kernel(parts, share, grid_ref, *refs):
    pieces, out_ref, sems = refs[: parts * share], refs[parts * share], refs[parts * share + 1]
    copies = []
    for part in range(parts):
        owner = lax.rem(grid_ref[0] + parts - part, parts)
        for orbital in range(share):
            number = part * share + orbital
            copies.append(
                pltpu.make_async_copy(
                    pieces[number], out_ref.at[:, owner * share + orbital], sems.at[number]
                )
            )
    for copy in copies:
        copy.start()
    for copy in copies:
        copy.wait()


def roll_rows(value, shift):
    return pltpu.roll(value, shift % ROWS, 1)


def total_of_groups(value, kinds):
    for shift in (4, 2, 1):
        value = value + pltpu.roll(value, shift, 0)
    shift = LANES // 2
    while shift >= kinds:
        value = value + pltpu.roll(value, shift, 1)
        shift //= 2
    return value


def fold(values):
    while len(values) > 1:
        half = len(values) // 2
        values = [values[number] + values[number + half] for number in range(half)]
    return values[0]


def propagate_in_kernel(
    vector_value, field_ref, total_ref, potential_ref, tables, scratch, width, kinds
):
    yz_ref, zy_ref, xbell_ref, xslope_ref, y_ref = tables
    split_ref, product_ref, partial_ref, drift_ref, spread_ref, diagonal_ref = scratch
    diagonal_ref[...] = (3.0 * SECOND[0] - 0.5 * vector_value * vector_value / KINETIC) - potential_ref[
        ...
    ] * (1.0 / KINETIC)
    block = ROWS
    slab = block * ROWS

    def split(part, start, planes):
        rows = planes.reshape(slab, LANES)
        high = rows.astype(jnp.bfloat16)
        low = (rows - high.astype(jnp.float32)).astype(jnp.bfloat16)
        where = pl.ds((part * width + start) * ROWS, slab)
        return where, high, low

    for part in range(2):
        for start in range(0, width, block):
            planes = field_ref[part, start : start + block]
            where, high, low = split(part, start, planes)
            split_ref[where, :LANES] = high
            split_ref[where, LANES:] = low

    def one_order(order, carry):
        inverse = jnp.where(order == 1, 1.0, jnp.where(order == 2, 0.5, jnp.where(order == 3, 1.0 / 3.0, 0.25)))
        step_scale = inverse * time_step
        kinetic = step_scale * KINETIC
        drift = step_scale * SLOPE * vector_value
        slopes = [drift * weight for weight in FIRST]
        product_ref[...] = jnp.dot(split_ref[...], yz_ref[...], preferred_element_type=jnp.float32)
        bells = [jnp.zeros((ROWS, LANES), jnp.float32)] * 2
        inclines = [jnp.zeros((ROWS, LANES), jnp.float32)] * 2
        for start in range(0, width, block):
            for part in range(2):
                rows = pl.ds((part * width + start) * ROWS, slab)
                near = {
                    plane: field_ref[part, plane % width] for plane in range(start - 4, start + block + 4)
                }
                for index in range(block):
                    plane = start + index
                    line = pl.ds((part * width + plane) * ROWS, ROWS)
                    total = product_ref[line, :LANES]
                    total = total + pltpu.roll(product_ref[line, LANES : 2 * LANES], ROWS - 1, 0)
                    total = total + pltpu.roll(product_ref[line, 2 * LANES : 3 * LANES], 1, 0)
                    inner = product_ref[line, 3 * LANES :]
                    bells[part] = bells[part] + inner * xbell_ref[plane]
                    inclines[part] = inclines[part] + inner * xslope_ref[plane]
                    total = total + diagonal_ref[plane] * near[plane]
                    moved = None
                    for reach in range(1, 5):
                        ahead, behind = near[plane + reach], near[plane - reach]
                        total = total + SECOND[reach] * (ahead + behind)
                        term = slopes[reach - 1] * (ahead - behind)
                        moved = term if moved is None else moved + term
                    partial_ref[part, plane] = total
                    drift_ref[part, plane] = moved
        outers = []
        for part in range(2):
            first = total_of_groups(bells[part] * y_ref[0], kinds)
            second = total_of_groups(inclines[part] * y_ref[0], kinds)
            third = total_of_groups(bells[part] * y_ref[1], kinds)
            outers.append((first * y_ref[2] + third * y_ref[4], second * y_ref[3]))
        for part in range(2):
            for start in range(0, width, block):
                spread = (
                    xbell_ref[start : start + block] * outers[part][0][None]
                    + xslope_ref[start : start + block] * outers[part][1][None]
                )
                where, high, low = split(part, start, spread)
                spread_ref[where, :LANES] = high
                spread_ref[where, LANES:] = low
        product_ref[:, :LANES] = jnp.dot(spread_ref[...], zy_ref[...], preferred_element_type=jnp.float32)
        for start in range(0, width, block):
            images = []
            for part in range(2):
                rows = pl.ds((part * width + start) * ROWS, slab)
                images.append(
                    partial_ref[part, start : start + block]
                    + product_ref[rows, :LANES].reshape(block, ROWS, LANES)
                )
            new = (
                -kinetic * images[1] - drift_ref[0, start : start + block],
                kinetic * images[0] - drift_ref[1, start : start + block],
            )
            for part in range(2):
                field_ref[part, start : start + block] = new[part]
                total_ref[part, start : start + block] += new[part]
                where, high, low = split(part, start, new[part])
                split_ref[where, :LANES] = high
                split_ref[where, LANES:] = low
        return carry

    lax.fori_loop(1, ORDER + 1, one_order, 0)


def sums_in_kernel(total_ref, width):
    flow = jnp.zeros((ROWS, LANES), jnp.float32)
    density = jnp.zeros((ROWS, LANES), jnp.float32)
    for plane in range(width):
        real = total_ref[0, plane]
        imaginary = total_ref[1, plane]
        moved = None
        for reach in range(1, 5):
            ahead = total_ref[1, (plane + reach) % width]
            behind = total_ref[1, (plane - reach) % width]
            term = FIRST[reach - 1] * (ahead - behind)
            moved = term if moved is None else moved + term
        flow = flow + real * moved
        density = density + (real * real + imaginary * imaginary)
    return (2.0 * SLOPE) * flow, density


def first_kernel(parts, kinds, scalar_ref, *refs):
    pieces, refs = refs[:parts], refs[parts:]
    potential_ref, *tables, sums_ref, total_ref, out_ref, field_ref = refs[:10]
    scratch = refs[10:]
    width = total_ref.shape[1]
    planes = width // parts
    for part in range(2):
        for number in range(parts):
            for index in range(planes):
                plane = pieces[number][part, pl.ds(index, ROWS, stride=planes), :]
                field_ref[part, number * planes + index] = plane
                total_ref[part, number * planes + index] = plane
    propagate_in_kernel(scalar_ref[0], field_ref, total_ref, potential_ref, tables, scratch, width, kinds)
    flow, density = sums_in_kernel(total_ref, width)
    out_ref[0] = sums_ref[0] + flow
    out_ref[1] = sums_ref[1] + density


def second_kernel(parts, kinds, points, scalar_ref, *refs):
    seen, refs = refs[:parts], refs[parts:]
    psi_ref, potential_ref, *tables, sums_ref = refs[:8]
    refs = refs[8:]
    pieces, refs = refs[:parts], refs[parts:]
    out_ref, vector_ref, field_ref, total_ref = refs[:4]
    scratch = refs[4:]
    width = total_ref.shape[1]
    planes = width // parts
    flow = jnp.sum(fold([ref[0] for ref in seen]))
    density = jnp.sum(fold([ref[1] for ref in seen]))
    current = (flow + scalar_ref[0] * density) * (1.0 / points)
    vector_value = scalar_ref[1] - source_weight * current
    vector_ref[0] = vector_value
    field_ref[...] = psi_ref[...]
    total_ref[...] = psi_ref[...]
    propagate_in_kernel(vector_value, field_ref, total_ref, potential_ref, tables, scratch, width, kinds)
    flow, density = sums_in_kernel(total_ref, width)
    out_ref[0] = sums_ref[0] + flow
    out_ref[1] = sums_ref[1] + density
    for part in range(2):
        for number in range(parts):
            for index in range(planes):
                pieces[number][part, pl.ds(index, ROWS, stride=planes), :] = total_ref[
                    part, number * planes + index
                ]


def vmem():
    return pl.BlockSpec(memory_space=pltpu.VMEM)


def smem():
    return pl.BlockSpec(memory_space=pltpu.SMEM)


def anywhere():
    return pl.BlockSpec(memory_space=pl.ANY)


def float_array(*shape):
    return jax.ShapeDtypeStruct(shape, jnp.float32)


def shifted(value, axis_name, count, shift):
    return lax.ppermute(value, axis_name, [((index + shift) % count, index) for index in range(count)])


def per_device(parts, blocks, orbitals, local_potential, atom_sites, host_point, fields):
    norb = orbitals.shape[2]
    planes, points = local_potential.shape
    width = planes * parts
    share = norb // parts
    owned = fields.shape[1]
    atoms = atom_sites.shape[0]
    kinds = 2 * atoms
    here = lax.axis_index("grid").astype(jnp.int32)[None]
    params = pltpu.CompilerParams(vmem_limit_bytes=LIMIT)

    def rows_of(value):
        lead = value.shape[:-2]
        value = value.reshape(*lead, planes, ROWS, LANES)
        return jnp.swapaxes(value, -3, -2).reshape(*lead, ROWS * planes, LANES)

    def planes_of(value):
        lead = value.shape[:-2]
        value = value.reshape(*lead, ROWS, planes, LANES)
        return jnp.swapaxes(value, -3, -2)

    field_blocks = [fields] + [shifted(fields, "macro", blocks, step) for step in range(1, blocks)]

    piece = float_array(2, ROWS * planes, LANES)
    packed = pl.pallas_call(
        functools.partial(pack_kernel, parts, share),
        out_shape=[piece] * (parts * share),
        in_specs=[smem(), anywhere()],
        out_specs=[anywhere()] * (parts * share),
        scratch_shapes=[pltpu.SemaphoreType.DMA((parts * share,))],
        compiler_params=params,
    )(here, rows_of(orbitals[0]))
    arrived = []
    potentials = [local_potential]
    for orbital in range(share):
        row = [packed[orbital]]
        for part in range(1, parts):
            row.append(shifted(packed[part * share + orbital], "grid", parts, -part % parts))
        arrived.append(row)
        if orbital == 0:
            for part in range(1, parts):
                potentials.append(shifted(local_potential, "grid", parts, part))
    arrived = [[row[0]] + row[:0:-1] for row in arrived]
    potential = jnp.concatenate(
        [value.reshape(planes, ROWS, LANES) for value in potentials], axis=0
    )

    tables = pl.pallas_call(
        functools.partial(tables_kernel, atoms, planes),
        out_shape=[
            jax.ShapeDtypeStruct((2 * LANES, 4 * LANES), jnp.bfloat16),
            jax.ShapeDtypeStruct((2 * LANES, LANES), jnp.bfloat16),
            float_array(width, ROWS, LANES),
            float_array(width, ROWS, LANES),
            float_array(5, ROWS, LANES),
        ],
        in_specs=[smem(), smem(), vmem()],
        out_specs=[vmem()] * 5,
        compiler_params=params,
    )(atom_sites, here, stencil_weights(width))

    block = lax.axis_index("macro").astype(jnp.int32)
    scalars = pl.pallas_call(
        functools.partial(vector_kernel, blocks),
        out_shape=float_array(2),
        in_specs=[smem()] + [vmem()] * blocks,
        out_specs=smem(),
        compiler_params=params,
    )(jnp.stack([host_point[0], block]), *field_blocks)

    scratch = [
        pltpu.VMEM((2 * width * ROWS, 2 * LANES), jnp.bfloat16),
        pltpu.VMEM((2 * width * ROWS, 4 * LANES), jnp.float32),
        pltpu.VMEM((2, width, ROWS, LANES), jnp.float32),
        pltpu.VMEM((2, width, ROWS, LANES), jnp.float32),
        pltpu.VMEM((2 * width * ROWS, 2 * LANES), jnp.bfloat16),
        pltpu.VMEM((width, ROWS, LANES), jnp.float32),
    ]
    cell = float_array(2, width, ROWS, LANES)
    cell_scratch = pltpu.VMEM((2, width, ROWS, LANES), jnp.float32)
    sums_shape = float_array(2, ROWS, LANES)
    cost = pl.CostEstimate(flops=3 * 2 * 512 * 256 * 256 * ORDER, bytes_accessed=2 * 1024 * 1024, transcendentals=0)

    sums = jnp.zeros((2, ROWS, LANES), jnp.float32)
    moved = []
    for orbital in range(share):
        psi, sums = pl.pallas_call(
            functools.partial(first_kernel, parts, kinds),
            out_shape=[cell, sums_shape],
            in_specs=[smem()] + [vmem()] * (parts + 7),
            out_specs=[vmem()] * 2,
            scratch_shapes=[cell_scratch] + scratch,
            compiler_params=params,
            cost_estimate=cost,
        )(scalars, *arrived[orbital], potential, *tables, sums)
        moved.append(psi)
    first_sums = sums
    seen = [first_sums] + [shifted(first_sums, "grid", parts, part) for part in range(1, parts)]

    sums = jnp.zeros((2, ROWS, LANES), jnp.float32)
    returned = [None] * (parts * share)
    for orbital in range(share):
        *pieces, sums, vector_value = pl.pallas_call(
            functools.partial(second_kernel, parts, kinds, float(width**3 * norb)),
            out_shape=[piece] * parts + [sums_shape, float_array(1)],
            in_specs=[smem()] + [vmem()] * (parts + 8),
            out_specs=[vmem()] * (parts + 1) + [smem()],
            scratch_shapes=[cell_scratch, cell_scratch] + scratch,
            compiler_params=params,
            cost_estimate=cost,
        )(scalars, *seen, moved[orbital], potential, *tables, sums)
        returned[orbital] = pieces[0]
        for part in range(1, parts):
            returned[part * share + orbital] = shifted(pieces[part], "grid", parts, -part % parts)
    second_sums = sums

    unpacked = pl.pallas_call(
        functools.partial(unpack_kernel, parts, share),
        out_shape=float_array(2, norb, ROWS * planes, LANES),
        in_specs=[smem()] + [anywhere()] * (parts * share),
        out_specs=anywhere(),
        scratch_shapes=[pltpu.SemaphoreType.DMA((parts * share,))],
        compiler_params=params,
    )(here, *returned)
    orbitals_out = planes_of(unpacked).reshape(2, norb, planes, points)

    length = blocks * owned
    positions = lax.broadcasted_iota(jnp.int32, (length,), 0)
    values = jnp.stack([scalars[0], vector_value[0]])
    flows = jnp.stack([jnp.sum(first_sums[0]), jnp.sum(second_sums[0])])
    densities = jnp.stack([jnp.sum(first_sums[1]), jnp.sum(second_sums[1])])
    currents = (flows + values * densities) / (width**3 * norb)
    sources = lax.psum(
        jnp.where(positions[None] == host_point[0], currents[:, None], 0.0), ("macro", "grid")
    )
    turned = jnp.concatenate(field_blocks, axis=1)
    start = block * owned
    whole = lax.dynamic_slice_in_dim(
        jnp.concatenate([turned, turned], axis=1), length - start, length, axis=1
    )
    previous, present = whole[0], whole[1]
    for step in range(STEPS):
        rim = jnp.pad(present, 1)
        following = (
            2.0 * present
            - previous
            + courant_square * (rim[2:] - 2.0 * present + rim[:-2])
            - source_weight * sources[step]
        )
        previous, present = present, following
    fields_out = lax.dynamic_slice_in_dim(jnp.stack([previous, present]), start, owned, axis=1)
    return orbitals_out[None], fields_out


def solution(mesh):
    in_specs = (
        P("macro", None, None, "grid", None),
        P("grid", None),
        P(),
        P("macro"),
        P(None, "macro"),
    )
    out_specs = (P("macro", None, None, "grid", None), P(None, "macro"))
    return jax.shard_map(
        functools.partial(per_device, mesh.shape["grid"], mesh.shape["macro"]),
        mesh=mesh,
        in_specs=in_specs,
        out_specs=out_specs,
        check_vma=False,
    )
```

time: 586 us -> 153 us (0.26)
  the two profiles are of different devices: /device:TPU:17 before, /device:TPU:0 now
where the time goes in v1:
time: 153 us; the launch traced here: 152 us
  starting transfers between devices  56.6 us (37%)
  blocking collectives  39.4 us (26%)
  Pallas kernels  37.4 us (24%)
  waiting for transfers between devices  9.77 us (6%)
  other arithmetic  5.39 us (4%)
  local copies, waits for them, and re-layouts  2.2 us (1%)
    ppermute x37, starting transfers between devices, shifted(): lax.ppermute(value, axis_name, [((index + shift) % count, index) for inde...  56.6 us
    psum x1, blocking collectives, per_device(): lax.psum(jnp.where(positions[None] == host_point[0], currents[:, None], 0...  39.4 us
    pallas_call x4, Pallas kernels, per_device(): pl.pallas_call(functools.partial(second_kernel, parts, kinds, float(width...  17.2 us
    pallas_call x4, Pallas kernels, per_device(): pl.pallas_call(functools.partial(first_kernel, parts, kinds), out_shape=[...  16.1 us
    ppermute x37, waiting for transfers between devices, shifted(): lax.ppermute(value, axis_name, [((index + shift) % count, index) for inde...  9.77 us
    div x1, other arithmetic, per_device(): currents = (flows + values * densities) / (width ** 3 * norb)  3.19 us
  transfers between devices with their start and end apart: 37, of which 6 were waited for; matrix products, arithmetic and copies ran while one was open for 1% of the time, Pallas kernels for 10%

profile of v1, /device:TPU:0, one launch (start us, length us, event | category | flops | bytes accessed | tf_op | source)
XLA Modules:
  0.0 152.3 jit_solution(12820805466995046653)
XLA Ops:
  1.1 2.6 %collective-permute-start.5 = (f32[2,64]{1,0:T(2,128)}, f32[2,64]{1,0:T(2,128)S(1)}, u32[]{:S(2)}, u32[]{:S(2)}) collective-permute-start(f32[2,64]{1,0:T(2,128)} %refs_0_.1), channel_id=1, source_target_pairs={{24,0},{28,4},{0,8},{4,12},{8,16},{12,20},{16,24},{20,28},{25,1},{... | collective-permute-start | bytes 1544 | tf_op jit(solution)/shard_map/ppermute | solution.py:361
  3.7 2.4 %collective-permute-start.4 = (f32[2,64]{1,0:T(2,128)}, f32[2,64]{1,0:T(2,128)S(1)}, u32[]{:S(2)}, u32[]{:S(2)}) collective-permute-start(f32[2,64]{1,0:T(2,128)} %refs_0_.1), channel_id=1, source_target_pairs={{20,0},{24,4},{28,8},{0,12},{4,16},{8,20},{12,24},{16,28},{21,1},{... | collective-permute-start | bytes 1544 | tf_op jit(solution)/shard_map/ppermute | solution.py:361
  11.8 2.3 %collective-permute-start = (f32[2,64]{1,0:T(2,128)S(1)}, f32[2,64]{1,0:T(2,128)S(1)}, u32[]{:S(2)}, u32[]{:S(2)}) collective-permute-start(f32[2,64]{1,0:T(2,128)S(1)} %copy-done.2), channel_id=1, source_target_pairs={{4,0},{8,4},{12,8},{16,12},{20,16},{24,20},{28,24},{0,28},{5,1},{9... | collective-permute-start | bytes 1544 | tf_op jit(solution)/shard_map/ppermute | solution.py:361
  15.1 3.7 %collective-permute-start.10 = (f32[8,1024]{1,0:T(8,128)S(1)}, f32[8,1024]{1,0:T(8,128)S(1)}, u32[]{:S(2)}, u32[]{:S(2)}) collective-permute-start(f32[8,1024]{1,0:T(8,128)S(1)} %copy-done.3), channel_id=1, source_target_pairs={{1,0},{2,1},{3,2},{0,3},{5,4},{6,5},{7,6},{4,7},{9,8},{10,9},{11,1... | collective-permute-start | bytes 98312 | tf_op jit(solution)/shard_map/ppermute | solution.py:361
  19.8 2.9 %collective-permute-start.7 = (f32[2,64,128]{2,1,0:T(8,128)S(1)}, f32[2,64,128]{2,1,0:T(8,128)S(1)}, u32[]{:S(2)}, u32[]{:S(2)}) collective-permute-start(f32[2,64,128]{2,1,0:T(8,128)S(1)} %get-tuple-element.53), channel_id=1, source_target_pairs={{1,0},{2,1},{3,2},{0,3},{5,4},{6,5},{7,6},{4,7},{9,8},{10,9},{11,1... | collective-permute-start | bytes 196616 | tf_op jit(solution)/shard_map/ppermute | solution.py:361
  29.3 3.3 %collective-permute-done.19.refs_1_ = f32[2,64,128]{2,1,0:T(8,128)S(1)} collective-permute-done((f32[2,64,128]{2,1,0:T(8,128)S(1)}, f32[2,64,128]{2,1,0:T(8,128)S(1)}, u32[]{:S(2)}, u32[]{:S(2)}) %collective-permute-start.19) | collective-permute-done | bytes 65568 | tf_op jit(solution)/shard_map/ppermute | solution.py:361
  36.4 4.0 %shard_map.80 = (f32[2,32,8,128]{3,2,1,0:T(8,128)S(1)}, f32[2,8,128]{2,1,0:T(8,128)S(1)}) custom-call(f32[2]{0:T(128)S(1)} %shard_map.77.scalar_ref, f32[2,64,128]{2,1,0:T(8,128)S(1)} %get-tuple-element.69.refs_0_, f32[2,64,128]{2,1,0:T(8,128)S(1)} %collective-permute-done.19.refs_1_, f32[2,64,128]{2,1,0:T(8,128)S(1)} %collective-permute-done.20.refs_2_, ...), custom_call_target="tpu_custom_call" | custom-call | flops 805306368 | bytes 2097152 | tf_op jit(solution)/shard_map/pallas_call | solution.py:450
  40.4 2.8 %collective-permute-start.13 = (f32[2,64,128]{2,1,0:T(8,128)S(1)}, f32[2,64,128]{2,1,0:T(8,128)S(1)}, u32[]{:S(2)}, u32[]{:S(2)}) collective-permute-start(f32[2,64,128]{2,1,0:T(8,128)S(1)} %get-tuple-element.62), channel_id=1, source_target_pairs={{1,0},{2,1},{3,2},{0,3},{5,4},{6,5},{7,6},{4,7},{9,8},{10,9},{11,1... | collective-permute-start | bytes 196616 | tf_op jit(solution)/shard_map/ppermute | solution.py:361
  44.4 4.0 %shard_map.81 = (f32[2,32,8,128]{3,2,1,0:T(8,128)S(1)}, f32[2,8,128]{2,1,0:T(8,128)S(1)}) custom-call(f32[2]{0:T(128)S(1)} %shard_map.77.scalar_ref, f32[2,64,128]{2,1,0:T(8,128)S(1)} %get-tuple-element.65.refs_0_, f32[2,64,128]{2,1,0:T(8,128)S(1)} %collective-permute-done.16.refs_1_, f32[2,64,128]{2,1,0:T(8,128)S(1)} %collective-permute-done.17.refs_2_, ...), custom_call_target="tpu_custom_call" | custom-call | flops 805306368 | bytes 2097152 | tf_op jit(solution)/shard_map/pallas_call | solution.py:450
  48.4 2.4 %collective-permute-start.9 = (f32[2,64,128]{2,1,0:T(8,128)S(1)}, f32[2,64,128]{2,1,0:T(8,128)S(1)}, u32[]{:S(2)}, u32[]{:S(2)}) collective-permute-start(f32[2,64,128]{2,1,0:T(8,128)S(1)} %get-tuple-element.55), channel_id=1, source_target_pairs={{3,0},{0,1},{1,2},{2,3},{7,4},{4,5},{5,6},{6,7},{11,8},{8,9},{9,10... | collective-permute-start | bytes 196616 | tf_op jit(solution)/shard_map/ppermute | solution.py:361
  50.8 4.0 %shard_map.82 = (f32[2,32,8,128]{3,2,1,0:T(8,128)S(1)}, f32[2,8,128]{2,1,0:T(8,128)S(1)}) custom-call(f32[2]{0:T(128)S(1)} %shard_map.77.scalar_ref, f32[2,64,128]{2,1,0:T(8,128)S(1)} %get-tuple-element.61.refs_0_, f32[2,64,128]{2,1,0:T(8,128)S(1)} %collective-permute-done.13.refs_1_, f32[2,64,128]{2,1,0:T(8,128)S(1)} %collective-permute-done.14.refs_2_, ...), custom_call_target="tpu_custom_call" | custom-call | flops 805306368 | bytes 2097152 | tf_op jit(solution)/shard_map/pallas_call | solution.py:450
  54.9 4.0 %shard_map.83 = (f32[2,32,8,128]{3,2,1,0:T(8,128)S(1)}, f32[2,8,128]{2,1,0:T(8,128)S(1)}) custom-call(f32[2]{0:T(128)S(1)} %shard_map.77.scalar_ref, f32[2,64,128]{2,1,0:T(8,128)S(1)} %get-tuple-element.52.refs_0_, f32[2,64,128]{2,1,0:T(8,128)S(1)} %collective-permute-done.7.refs_1_, f32[2,64,128]{2,1,0:T(8,128)S(1)} %collective-permute-done.8.refs_2_, ...), custom_call_target="tpu_custom_call" | custom-call | flops 805306368 | bytes 2097152 | tf_op jit(solution)/shard_map/pallas_call | solution.py:450
  61.2 2.7 %collective-permute-start.22 = (f32[2,8,128]{2,1,0:T(8,128)S(1)}, f32[2,8,128]{2,1,0:T(8,128)S(1)}, u32[]{:S(2)}, u32[]{:S(2)}) collective-permute-start(f32[2,8,128]{2,1,0:T(8,128)S(1)} %get-tuple-element.76.refs_0_), channel_id=1, source_target_pairs={{1,0},{2,1},{3,2},{0,3},{5,4},{6,5},{7,6},{4,7},{9,8},{10,9},{11,1... | collective-permute-start | bytes 24584 | tf_op jit(solution)/shard_map/ppermute | solution.py:361
  65.3 4.3 %shard_map.84 = (f32[2,64,128]{2,1,0:T(8,128)S(1)}, f32[2,64,128]{2,1,0:T(8,128)S(1)}, f32[2,64,128]{2,1,0:T(8,128)S(1)}, f32[2,64,128]{2,1,0:T(8,128)S(1)}, f32[2,8,128]{2,1,0:T(8,128)S(1)}, /*index=5*/f32[1]{0:T(128)}) custom-call(f32[2]{0:T(128)S(1)} %shard_map.77.scalar_ref, f32[2,8,128]{2,1,0:T(8,128)S(1)} %get-tuple-element.76.refs_0_, ...), custom_call_target="tpu_custom_call" | custom-call | flops 805306368 | bytes 2097152 | tf_op jit(solution)/shard_map/pallas_call | solution.py:466
  69.5 4.3 %shard_map.85 = (f32[2,64,128]{2,1,0:T(8,128)S(1)}, f32[2,64,128]{2,1,0:T(8,128)S(1)}, f32[2,64,128]{2,1,0:T(8,128)S(1)}, f32[2,64,128]{2,1,0:T(8,128)S(1)}, f32[2,8,128]{2,1,0:T(8,128)S(1)}, /*index=5*/f32[1]{0:T(128)}) custom-call(f32[2]{0:T(128)S(1)} %shard_map.77.scalar_ref, f32[2,8,128]{2,1,0:T(8,128)S(1)} %get-tuple-element.76.refs_0_, ...), custom_call_target="tpu_custom_call" | custom-call | flops 805306368 | bytes 2097152 | tf_op jit(solution)/shard_map/pallas_call | solution.py:466
  73.8 4.3 %shard_map.86 = (f32[2,64,128]{2,1,0:T(8,128)S(1)}, f32[2,64,128]{2,1,0:T(8,128)S(1)}, f32[2,64,128]{2,1,0:T(8,128)S(1)}, f32[2,64,128]{2,1,0:T(8,128)S(1)}, f32[2,8,128]{2,1,0:T(8,128)S(1)}, /*index=5*/f32[1]{0:T(128)}) custom-call(f32[2]{0:T(128)S(1)} %shard_map.77.scalar_ref, f32[2,8,128]{2,1,0:T(8,128)S(1)} %get-tuple-element.76.refs_0_, ...), custom_call_target="tpu_custom_call" | custom-call | flops 805306368 | bytes 2097152 | tf_op jit(solution)/shard_map/pallas_call | solution.py:466
  78.2 4.3 %shard_map.87 = (f32[2,64,128]{2,1,0:T(8,128)S(1)}, f32[2,64,128]{2,1,0:T(8,128)S(1)}, f32[2,64,128]{2,1,0:T(8,128)S(1)}, f32[2,64,128]{2,1,0:T(8,128)S(1)}, f32[2,8,128]{2,1,0:T(8,128)S(1)}, /*index=5*/f32[1]{0:T(128)}) custom-call(f32[2]{0:T(128)S(1)} %shard_map.77.scalar_ref, f32[2,8,128]{2,1,0:T(8,128)S(1)} %get-tuple-element.76.refs_0_, ...), custom_call_target="tpu_custom_call" | custom-call | flops 805306368 | bytes 2097152 | tf_op jit(solution)/shard_map/pallas_call | solution.py:466
  83.1 3.2 %fusion.11 = f32[2]{0:T(128)S(1)} fusion(f32[1]{0:T(128)} %bitcast.12, f32[1]{0:T(128)} %bitcast.11, f32[1]{0:T(128)} %get-tuple-element.101, f32[1]{0:T(128)S(1)} %bitcast.38, f32[1]{0:T(128)} %bitcast.14, f32[1]{0:T(128)} %bitcast.13), kind=kLoop, calls=%fused_computation.32 | loop fusion | flops 12 | bytes 32 | tf_op jit(solution)/shard_map/div | solution.py:495
  86.3 39.4 %psum.7 = f32[2,512]{1,0:T(2,128)S(1)} all-reduce(f32[2,512]{1,0:T(2,128)S(1)} %broadcast_select_fusion), channel_id=1, replica_groups=mesh['macro'=8,'grid'=4] {'macro','grid'}, use_global_device_ids=true, to_apply=%region_4.5 | all-reduce | flops 1024 | bytes 8192 | tf_op jit(solution)/shard_map/psum | solution.py:496
  128.8 2.8 %collective-permute-start.36 = (f32[2,64,128]{2,1,0:T(8,128)S(1)}, f32[2,64,128]{2,1,0:T(8,128)S(1)}, u32[]{:S(2)}, u32[]{:S(2)}) collective-permute-start(f32[2,64,128]{2,1,0:T(8,128)S(1)} %get-tuple-element.99), channel_id=1, source_target_pairs={{1,0},{2,1},{3,2},{0,3},{5,4},{6,5},{7,6},{4,7},{9,8},{10,9},{11,1... | collective-permute-start | bytes 196616 | tf_op jit(solution)/shard_map/ppermute | solution.py:361
  133.0 2.6 %collective-permute-start.35 = (f32[2,64,128]{2,1,0:T(8,128)S(1)}, f32[2,64,128]{2,1,0:T(8,128)S(1)}, u32[]{:S(2)}, u32[]{:S(2)}) collective-permute-start(f32[2,64,128]{2,1,0:T(8,128)S(1)} %get-tuple-element.98), channel_id=1, source_target_pairs={{1,0},{2,1},{3,2},{0,3},{5,4},{6,5},{7,6},{4,7},{9,8},{10,9},{11,1... | collective-permute-start | bytes 196616 | tf_op jit(solution)/shard_map/ppermute | solution.py:361
  136.3 4.0 %collective-permute-start.30 = (f32[2,64,128]{2,1,0:T(8,128)S(1)}, f32[2,64,128]{2,1,0:T(8,128)S(1)}, u32[]{:S(2)}, u32[]{:S(2)}) collective-permute-start(f32[2,64,128]{2,1,0:T(8,128)S(1)} %get-tuple-element.93), channel_id=1, source_target_pairs={{2,0},{3,1},{0,2},{1,3},{6,4},{7,5},{4,6},{5,7},{10,8},{11,9},{8,1... | collective-permute-start | bytes 196616 | tf_op jit(solution)/shard_map/ppermute | solution.py:361
  140.2 2.9 %collective-permute-start.34 = (f32[2,64,128]{2,1,0:T(8,128)S(1)}, f32[2,64,128]{2,1,0:T(8,128)S(1)}, u32[]{:S(2)}, u32[]{:S(2)}) collective-permute-start(f32[2,64,128]{2,1,0:T(8,128)S(1)} %get-tuple-element.97), channel_id=1, source_target_pairs={{1,0},{2,1},{3,2},{0,3},{5,4},{6,5},{7,6},{4,7},{9,8},{10,9},{11,1... | collective-permute-start | bytes 196616 | tf_op jit(solution)/shard_map/ppermute | solution.py:361
  143.2 2.4 %collective-permute-start.29 = (f32[2,64,128]{2,1,0:T(8,128)S(1)}, f32[2,64,128]{2,1,0:T(8,128)S(1)}, u32[]{:S(2)}, u32[]{:S(2)}) collective-permute-start(f32[2,64,128]{2,1,0:T(8,128)S(1)} %get-tuple-element.92), channel_id=1, source_target_pairs={{2,0},{3,1},{0,2},{1,3},{6,4},{7,5},{4,6},{5,7},{10,8},{11,9},{8,1... | collective-permute-start | bytes 196616 | tf_op jit(solution)/shard_map/ppermute | solution.py:361
  (91 shorter events, 35.3 us)
Async XLA Ops:
  0.6 9.7 %collective-permute-start.6 = (f32[2,64]{1,0:T(2,128)}, f32[2,64]{1,0:T(2,128)S(1)}, u32[]{:S(2)}, u32[]{:S(2)}) collective-permute-start(f32[2,64]{1,0:T(2,128)} %refs_0_.1), channel_id=1, source_target_pairs={{28,0},{0,4},{4,8},{8,12},{12,16},{16,20},{20,24},{24,28},{29,1},{... | collective-permute-start | bytes 1544 | tf_op jit(solution)/shard_map/ppermute | solution.py:361
  1.1 10.7 %collective-permute-start.5 = (f32[2,64]{1,0:T(2,128)}, f32[2,64]{1,0:T(2,128)S(1)}, u32[]{:S(2)}, u32[]{:S(2)}) collective-permute-start(f32[2,64]{1,0:T(2,128)} %refs_0_.1), channel_id=1, source_target_pairs={{24,0},{28,4},{0,8},{4,12},{8,16},{12,20},{16,24},{20,28},{25,1},{... | collective-permute-start | bytes 1544 | tf_op jit(solution)/shard_map/ppermute | solution.py:361
  3.7 11.4 %collective-permute-start.4 = (f32[2,64]{1,0:T(2,128)}, f32[2,64]{1,0:T(2,128)S(1)}, u32[]{:S(2)}, u32[]{:S(2)}) collective-permute-start(f32[2,64]{1,0:T(2,128)} %refs_0_.1), channel_id=1, source_target_pairs={{20,0},{24,4},{28,8},{0,12},{4,16},{8,20},{12,24},{16,28},{21,1},{... | collective-permute-start | bytes 1544 | tf_op jit(solution)/shard_map/ppermute | solution.py:361
  6.1 12.7 %collective-permute-start.3 = (f32[2,64]{1,0:T(2,128)}, f32[2,64]{1,0:T(2,128)S(1)}, u32[]{:S(2)}, u32[]{:S(2)}) collective-permute-start(f32[2,64]{1,0:T(2,128)} %refs_0_.1), channel_id=1, source_target_pairs={{16,0},{20,4},{24,8},{28,12},{0,16},{4,20},{8,24},{12,28},{17,1},{... | collective-permute-start | bytes 1544 | tf_op jit(solution)/shard_map/ppermute | solution.py:361
  6.6 12.2 %collective-permute-start.2 = (f32[2,64]{1,0:T(2,128)}, f32[2,64]{1,0:T(2,128)S(1)}, u32[]{:S(2)}, u32[]{:S(2)}) collective-permute-start(f32[2,64]{1,0:T(2,128)} %refs_0_.1), channel_id=1, source_target_pairs={{12,0},{16,4},{20,8},{24,12},{28,16},{0,20},{4,24},{8,28},{13,1},{... | collective-permute-start | bytes 1544 | tf_op jit(solution)/shard_map/ppermute | solution.py:361
  10.3 9.5 %collective-permute-start.1 = (f32[2,64]{1,0:T(2,128)S(1)}, f32[2,64]{1,0:T(2,128)S(1)}, u32[]{:S(2)}, u32[]{:S(2)}) collective-permute-start(f32[2,64]{1,0:T(2,128)S(1)} %copy-done.2), channel_id=1, source_target_pairs={{8,0},{12,4},{16,8},{20,12},{24,16},{28,20},{0,24},{4,28},{9,1},{1... | collective-permute-start | bytes 1544 | tf_op jit(solution)/shard_map/ppermute | solution.py:361
  11.8 10.8 %collective-permute-start = (f32[2,64]{1,0:T(2,128)S(1)}, f32[2,64]{1,0:T(2,128)S(1)}, u32[]{:S(2)}, u32[]{:S(2)}) collective-permute-start(f32[2,64]{1,0:T(2,128)S(1)} %copy-done.2), channel_id=1, source_target_pairs={{4,0},{8,4},{12,8},{16,12},{20,16},{24,20},{28,24},{0,28},{5,1},{9... | collective-permute-start | bytes 1544 | tf_op jit(solution)/shard_map/ppermute | solution.py:361
  15.1 11.0 %collective-permute-start.10 = (f32[8,1024]{1,0:T(8,128)S(1)}, f32[8,1024]{1,0:T(8,128)S(1)}, u32[]{:S(2)}, u32[]{:S(2)}) collective-permute-start(f32[8,1024]{1,0:T(8,128)S(1)} %copy-done.3), channel_id=1, source_target_pairs={{1,0},{2,1},{3,2},{0,3},{5,4},{6,5},{7,6},{4,7},{9,8},{10,9},{11,1... | collective-permute-start | bytes 98312 | tf_op jit(solution)/shard_map/ppermute | solution.py:361
  18.8 8.5 %collective-permute-start.12 = (f32[8,1024]{1,0:T(8,128)S(1)}, f32[8,1024]{1,0:T(8,128)S(1)}, u32[]{:S(2)}, u32[]{:S(2)}) collective-permute-start(f32[8,1024]{1,0:T(8,128)S(1)} %copy-done.3), channel_id=1, source_target_pairs={{3,0},{0,1},{1,2},{2,3},{7,4},{4,5},{5,6},{6,7},{11,8},{8,9},{9,10... | collective-permute-start | bytes 98312 | tf_op jit(solution)/shard_map/ppermute | solution.py:361
  18.8 8.4 %collective-permute-start.11 = (f32[8,1024]{1,0:T(8,128)S(1)}, f32[8,1024]{1,0:T(8,128)S(1)}, u32[]{:S(2)}, u32[]{:S(2)}) collective-permute-start(f32[8,1024]{1,0:T(8,128)S(1)} %copy-done.3), channel_id=1, source_target_pairs={{2,0},{3,1},{0,2},{1,3},{6,4},{7,5},{4,6},{5,7},{10,8},{11,9},{8,1... | collective-permute-start | bytes 98312 | tf_op jit(solution)/shard_map/ppermute | solution.py:361
  19.8 35.0 %collective-permute-start.7 = (f32[2,64,128]{2,1,0:T(8,128)S(1)}, f32[2,64,128]{2,1,0:T(8,128)S(1)}, u32[]{:S(2)}, u32[]{:S(2)}) collective-permute-start(f32[2,64,128]{2,1,0:T(8,128)S(1)} %get-tuple-element.53), channel_id=1, source_target_pairs={{1,0},{2,1},{3,2},{0,3},{5,4},{6,5},{7,6},{4,7},{9,8},{10,9},{11,1... | collective-permute-start | bytes 196616 | tf_op jit(solution)/shard_map/ppermute | solution.py:361
  22.7 32.2 %collective-permute-start.8 = (f32[2,64,128]{2,1,0:T(8,128)S(1)}, f32[2,64,128]{2,1,0:T(8,128)S(1)}, u32[]{:S(2)}, u32[]{:S(2)}) collective-permute-start(f32[2,64,128]{2,1,0:T(8,128)S(1)} %get-tuple-element.54), channel_id=1, source_target_pairs={{2,0},{3,1},{0,2},{1,3},{6,4},{7,5},{4,6},{5,7},{10,8},{11,9},{8,1... | collective-permute-start | bytes 196616 | tf_op jit(solution)/shard_map/ppermute | solution.py:361
  27.2 8.2 %collective-permute-start.20 = (f32[2,64,128]{2,1,0:T(8,128)S(1)}, f32[2,64,128]{2,1,0:T(8,128)S(1)}, u32[]{:S(2)}, u32[]{:S(2)}) collective-permute-start(f32[2,64,128]{2,1,0:T(8,128)S(1)} %get-tuple-element.71), channel_id=1, source_target_pairs={{2,0},{3,1},{0,2},{1,3},{6,4},{7,5},{4,6},{5,7},{10,8},{11,9},{8,1... | collective-permute-start | bytes 196616 | tf_op jit(solution)/shard_map/ppermute | solution.py:361
  27.3 8.1 %collective-permute-start.21 = (f32[2,64,128]{2,1,0:T(8,128)S(1)}, f32[2,64,128]{2,1,0:T(8,128)S(1)}, u32[]{:S(2)}, u32[]{:S(2)}) collective-permute-start(f32[2,64,128]{2,1,0:T(8,128)S(1)} %get-tuple-element.72), channel_id=1, source_target_pairs={{3,0},{0,1},{1,2},{2,3},{7,4},{4,5},{5,6},{6,7},{11,8},{8,9},{9,10... | collective-permute-start | bytes 196616 | tf_op jit(solution)/shard_map/ppermute | solution.py:361
  35.3 7.9 %collective-permute-start.17 = (f32[2,64,128]{2,1,0:T(8,128)S(1)}, f32[2,64,128]{2,1,0:T(8,128)S(1)}, u32[]{:S(2)}, u32[]{:S(2)}) collective-permute-start(f32[2,64,128]{2,1,0:T(8,128)S(1)} %get-tuple-element.67), channel_id=1, source_target_pairs={{2,0},{3,1},{0,2},{1,3},{6,4},{7,5},{4,6},{5,7},{10,8},{11,9},{8,1... | collective-permute-start | bytes 196616 | tf_op jit(solution)/shard_map/ppermute | solution.py:361
  35.3 9.0 %collective-permute-start.18 = (f32[2,64,128]{2,1,0:T(8,128)S(1)}, f32[2,64,128]{2,1,0:T(8,128)S(1)}, u32[]{:S(2)}, u32[]{:S(2)}) collective-permute-start(f32[2,64,128]{2,1,0:T(8,128)S(1)} %get-tuple-element.68), channel_id=1, source_target_pairs={{3,0},{0,1},{1,2},{2,3},{7,4},{4,5},{5,6},{6,7},{11,8},{8,9},{9,10... | collective-permute-start | bytes 196616 | tf_op jit(solution)/shard_map/ppermute | solution.py:361
  40.4 8.0 %collective-permute-start.13 = (f32[2,64,128]{2,1,0:T(8,128)S(1)}, f32[2,64,128]{2,1,0:T(8,128)S(1)}, u32[]{:S(2)}, u32[]{:S(2)}) collective-permute-start(f32[2,64,128]{2,1,0:T(8,128)S(1)} %get-tuple-element.62), channel_id=1, source_target_pairs={{1,0},{2,1},{3,2},{0,3},{5,4},{6,5},{7,6},{4,7},{9,8},{10,9},{11,1... | collective-permute-start | bytes 196616 | tf_op jit(solution)/shard_map/ppermute | solution.py:361
  127.9 8.2 %collective-permute-start.32 = (f32[2,64,128]{2,1,0:T(8,128)S(1)}, f32[2,64,128]{2,1,0:T(8,128)S(1)}, u32[]{:S(2)}, u32[]{:S(2)}) collective-permute-start(f32[2,64,128]{2,1,0:T(8,128)S(1)} %get-tuple-element.95), channel_id=1, source_target_pairs={{2,0},{3,1},{0,2},{1,3},{6,4},{7,5},{4,6},{5,7},{10,8},{11,9},{8,1... | collective-permute-start | bytes 196616 | tf_op jit(solution)/shard_map/ppermute | solution.py:361
  131.7 8.6 %collective-permute-start.27 = (f32[2,64,128]{2,1,0:T(8,128)S(1)}, f32[2,64,128]{2,1,0:T(8,128)S(1)}, u32[]{:S(2)}, u32[]{:S(2)}) collective-permute-start(f32[2,64,128]{2,1,0:T(8,128)S(1)} %get-tuple-element.90), channel_id=1, source_target_pairs={{3,0},{0,1},{1,2},{2,3},{7,4},{4,5},{5,6},{6,7},{11,8},{8,9},{9,10... | collective-permute-start | bytes 196616 | tf_op jit(solution)/shard_map/ppermute | solution.py:361
  131.7 11.5 %collective-permute-start.31 = (f32[2,64,128]{2,1,0:T(8,128)S(1)}, f32[2,64,128]{2,1,0:T(8,128)S(1)}, u32[]{:S(2)}, u32[]{:S(2)}) collective-permute-start(f32[2,64,128]{2,1,0:T(8,128)S(1)} %get-tuple-element.94), channel_id=1, source_target_pairs={{2,0},{3,1},{0,2},{1,3},{6,4},{7,5},{4,6},{5,7},{10,8},{11,9},{8,1... | collective-permute-start | bytes 196616 | tf_op jit(solution)/shard_map/ppermute | solution.py:361
  133.0 10.2 %collective-permute-start.35 = (f32[2,64,128]{2,1,0:T(8,128)S(1)}, f32[2,64,128]{2,1,0:T(8,128)S(1)}, u32[]{:S(2)}, u32[]{:S(2)}) collective-permute-start(f32[2,64,128]{2,1,0:T(8,128)S(1)} %get-tuple-element.98), channel_id=1, source_target_pairs={{1,0},{2,1},{3,2},{0,3},{5,4},{6,5},{7,6},{4,7},{9,8},{10,9},{11,1... | collective-permute-start | bytes 196616 | tf_op jit(solution)/shard_map/ppermute | solution.py:361
  136.1 9.5 %collective-permute-start.26 = (f32[2,64,128]{2,1,0:T(8,128)S(1)}, f32[2,64,128]{2,1,0:T(8,128)S(1)}, u32[]{:S(2)}, u32[]{:S(2)}) collective-permute-start(f32[2,64,128]{2,1,0:T(8,128)S(1)} %get-tuple-element.89), channel_id=1, source_target_pairs={{3,0},{0,1},{1,2},{2,3},{7,4},{4,5},{5,6},{6,7},{11,8},{8,9},{9,10... | collective-permute-start | bytes 196616 | tf_op jit(solution)/shard_map/ppermute | solution.py:361
  136.3 11.8 %collective-permute-start.30 = (f32[2,64,128]{2,1,0:T(8,128)S(1)}, f32[2,64,128]{2,1,0:T(8,128)S(1)}, u32[]{:S(2)}, u32[]{:S(2)}) collective-permute-start(f32[2,64,128]{2,1,0:T(8,128)S(1)} %get-tuple-element.93), channel_id=1, source_target_pairs={{2,0},{3,1},{0,2},{1,3},{6,4},{7,5},{4,6},{5,7},{10,8},{11,9},{8,1... | collective-permute-start | bytes 196616 | tf_op jit(solution)/shard_map/ppermute | solution.py:361
  143.2 8.1 %collective-permute-start.29 = (f32[2,64,128]{2,1,0:T(8,128)S(1)}, f32[2,64,128]{2,1,0:T(8,128)S(1)}, u32[]{:S(2)}, u32[]{:S(2)}) collective-permute-start(f32[2,64,128]{2,1,0:T(8,128)S(1)} %get-tuple-element.92), channel_id=1, source_target_pairs={{2,0},{3,1},{0,2},{1,3},{6,4},{7,5},{4,6},{5,7},{10,8},{11,9},{8,1... | collective-permute-start | bytes 196616 | tf_op jit(solution)/shard_map/ppermute | solution.py:361
  (18 other events, 98.5 us)

commit v2 on v1

v2 whole, which is shorter than its diff:
```python
import functools

import jax
import jax.numpy as jnp
import numpy as np
from jax import lax
from jax.experimental import pallas as pl
from jax.experimental.pallas import tpu as pltpu
from jax.sharding import PartitionSpec as P

ORDER = 4
STEPS = 2
spacing = 0.3206
time_step = 0.02
courant_square = 0.81
source_weight = 0.1
radial_strength = 0.3
polar_strength = -0.2
projector_width = 2.5

SECOND = (-14350.0, 8064.0, -1008.0, 128.0, -9.0)
FIRST = (672.0, -168.0, 32.0, -3.0)
KINETIC = 1.0 / (2.0 * 5040.0 * spacing * spacing)
SLOPE = 1.0 / (840.0 * spacing)

LANES = 128
ROWS = 8
LIMIT = 24 * 1024 * 1024


def stencil_weights(width):
    group = LANES // width
    total = np.zeros((LANES, 3 * LANES), np.float32)
    for y_in in range(group):
        for z_in in range(width):
            for y_out in range(group):
                for part, step in enumerate((0, group, -group)):
                    reach = abs(step + y_in - y_out)
                    if 1 <= reach <= 4:
                        total[y_in * width + z_in, part * LANES + y_out * width + z_in] += SECOND[reach]
            for reach in range(1, 5):
                for z_out in ((z_in + reach) % width, (z_in - reach) % width):
                    total[y_in * width + z_in, y_in * width + z_out] += SECOND[reach]
    return jnp.asarray(np.concatenate([total, total], axis=0), jnp.bfloat16)


def periodic(distance, width):
    return ((distance + width // 2) & (width - 1)) - width // 2


def bell_of(offset):
    distance = offset.astype(jnp.float32)
    bell = jnp.exp(-0.5 * distance * distance / (projector_width * projector_width))
    return bell, distance / projector_width * bell


def tables_kernel(atoms, site_ref, stencil_ref, near_ref, far_ref, zy_ref, xbell_ref, xslope_ref, y_ref):
    width = xbell_ref.shape[0]
    kinds = 2 * atoms
    group = LANES // width

    def site_of(column, axis_number):
        atom = (column % kinds) // 2
        position = jnp.zeros(column.shape, jnp.int32)
        for number in range(atoms):
            position = jnp.where(atom == number, site_ref[number, axis_number], position)
        return position

    def factor(coordinate, column):
        bell, slope = bell_of(periodic(coordinate - site_of(column, 2), width))
        value = jnp.where(column % 2 == 0, bell, slope)
        high = value.astype(jnp.bfloat16).astype(jnp.float32)
        return jnp.where(column % LANES < LANES // 2, high, value - high)

    def groups_agree(point, column):
        return (point % LANES) // width == (column // kinds) % group

    shape = (2 * LANES, LANES)
    first = lax.broadcasted_iota(jnp.int32, shape, 0)
    last = lax.broadcasted_iota(jnp.int32, shape, 1)
    near_ref[:, :LANES] = stencil_ref[:, :LANES]
    far_ref[...] = stencil_ref[:, LANES:]
    inward = jnp.where(groups_agree(first, last), factor(first % width, last), 0.0)
    near_ref[:, LANES:] = inward.astype(jnp.bfloat16)
    outward = jnp.where(groups_agree(last, first), factor(last % width, first), 0.0)
    zy_ref[...] = outward.astype(jnp.bfloat16)

    shape = (width, ROWS, LANES)
    plane = lax.broadcasted_iota(jnp.int32, shape, 0)
    column = lax.broadcasted_iota(jnp.int32, shape, 2)
    bell, slope = bell_of(periodic(plane - site_of(column, 0), width))
    xbell_ref[...] = bell
    xslope_ref[...] = slope

    shape = (ROWS, LANES)
    column = lax.broadcasted_iota(jnp.int32, shape, 1)
    row = lax.broadcasted_iota(jnp.int32, shape, 0) * group + (column // kinds) % group
    bell, slope = bell_of(periodic(row - site_of(column, 1), width))
    scale = -1.0 / KINETIC
    even = column % 2 == 0
    y_ref[0] = bell
    y_ref[1] = slope
    y_ref[2] = bell * jnp.where(even, scale * radial_strength, scale * polar_strength)
    y_ref[3] = bell * jnp.where(even, scale * polar_strength, 0.0)
    y_ref[4] = slope * jnp.where(even, scale * polar_strength, 0.0)


def vector_kernel(host_ref, seen_ref, out_ref):
    blocks, _, owned = seen_ref.shape
    host = host_ref[0]
    position = lax.broadcasted_iota(jnp.int32, (blocks, owned), 0) * owned + lax.broadcasted_iota(
        jnp.int32, (blocks, owned), 1
    )
    before, now = seen_ref[:, 0, :], seen_ref[:, 1, :]
    present = jnp.sum(jnp.where(position == host, now, 0.0))
    previous = jnp.sum(jnp.where(position == host, before, 0.0))
    beside = jnp.sum(jnp.where((position == host - 1) | (position == host + 1), now, 0.0))
    out_ref[0] = present
    out_ref[1] = 2.0 * present - previous + courant_square * (beside - 2.0 * present)


def pack_kernel(parts, share, count, first, with_potential, source_ref, *refs):
    out_ref, sems = refs[-2:]
    copies = []
    for owner in range(parts):
        for part in range(2):
            copies.append(
                (source_ref.at[part, pl.ds(owner * share + first, count)], out_ref.at[owner, pl.ds(part * count, count)])
            )
        if with_potential:
            copies.append((refs[0], out_ref.at[owner, 2 * count]))
    copies = [
        pltpu.make_async_copy(source, target, sems.at[number]) for number, (source, target) in enumerate(copies)
    ]
    for copy in copies:
        copy.start()
    for copy in copies:
        copy.wait()


def unpack_kernel(parts, share, count, first, piece_ref, *refs):
    out_ref, sems = refs[-2:]
    copies = []
    for owner in range(parts):
        for part in range(2):
            copies.append(
                pltpu.make_async_copy(
                    piece_ref.at[owner, pl.ds(part * count, count)],
                    out_ref.at[part, pl.ds(owner * share + first, count)],
                    sems.at[2 * owner + part],
                )
            )
    for copy in copies:
        copy.start()
    for copy in copies:
        copy.wait()


def total_of_groups(value, kinds):
    for shift in (4, 2, 1):
        value = value + pltpu.roll(value, shift, 0)
    shift = LANES // 2
    while shift >= kinds:
        value = value + pltpu.roll(value, shift, 1)
        shift //= 2
    return value


def propagate_in_kernel(
    count, vector_value, field_ref, total_ref, potential_ref, tables, scratch, width, kinds
):
    near_ref, far_ref, zy_ref, xbell_ref, xslope_ref, y_ref = tables
    split_ref, first_ref, second_ref, partial_ref, drift_ref, spread_ref, diagonal_ref = scratch
    diagonal_ref[...] = (3.0 * SECOND[0] - 0.5 * vector_value * vector_value / KINETIC) - potential_ref[
        ...
    ] * (1.0 / KINETIC)
    block = ROWS
    slab = block * ROWS
    cell_rows = width * ROWS
    numbers = [(orbital, part, part * count + orbital) for orbital in range(count) for part in range(2)]

    def split(planes):
        rows = planes.reshape(slab, LANES)
        high = rows.astype(jnp.bfloat16)
        low = (rows - high.astype(jnp.float32)).astype(jnp.bfloat16)
        return high, low

    def store_split(ref, number, start, planes):
        rows = pl.ds(number * cell_rows + start * ROWS, slab)
        high, low = split(planes)
        ref[rows, :LANES] = high
        ref[rows, LANES:] = low

    for number in range(2 * count):
        for start in range(0, width, block):
            store_split(split_ref, number, start, field_ref[number, start : start + block])

    def one_order(order, carry):
        inverse = jnp.where(order == 1, 1.0, jnp.where(order == 2, 0.5, jnp.where(order == 3, 1.0 / 3.0, 0.25)))
        step_scale = inverse * time_step
        kinetic = step_scale * KINETIC
        drift = step_scale * SLOPE * vector_value
        slopes = [drift * weight for weight in FIRST]
        outers = {}
        for orbital in range(count):
            for part in range(2):
                number = part * count + orbital
                rows = pl.ds(number * cell_rows, cell_rows)
                first_ref[rows, :] = jnp.dot(
                    split_ref[rows, :], near_ref[...], preferred_element_type=jnp.float32
                )
                bells = [jnp.zeros((ROWS, LANES), jnp.float32) for _ in range(2)]
                inclines = [jnp.zeros((ROWS, LANES), jnp.float32) for _ in range(2)]
                for plane in range(width):
                    inner = first_ref[pl.ds(number * cell_rows + plane * ROWS, ROWS), LANES:]
                    turn = plane % 2
                    bells[turn] = bells[turn] + inner * xbell_ref[plane]
                    inclines[turn] = inclines[turn] + inner * xslope_ref[plane]
                bell = bells[0] + bells[1]
                incline = inclines[0] + inclines[1]
                first = total_of_groups(bell * y_ref[0], kinds)
                second = total_of_groups(incline * y_ref[0], kinds)
                third = total_of_groups(bell * y_ref[1], kinds)
                outers[number] = (first * y_ref[2] + third * y_ref[4], second * y_ref[3])
        for orbital in range(count):
            for part in range(2):
                number = part * count + orbital
                rows = pl.ds(number * cell_rows, cell_rows)
                second_ref[rows, :] = jnp.dot(
                    split_ref[rows, :], far_ref[...], preferred_element_type=jnp.float32
                )
                for start in range(0, width, block):
                    near = {
                        plane: field_ref[number, plane % width] for plane in range(start - 4, start + block + 4)
                    }
                    for plane in range(start, start + block):
                        line = pl.ds(number * cell_rows + plane * ROWS, ROWS)
                        total = first_ref[line, :LANES]
                        total = total + pltpu.roll(second_ref[line, :LANES], ROWS - 1, 0)
                        total = total + pltpu.roll(second_ref[line, LANES:], 1, 0)
                        total = total + diagonal_ref[plane] * near[plane]
                        moved = None
                        for reach in range(1, 5):
                            ahead, behind = near[plane + reach], near[plane - reach]
                            total = total + SECOND[reach] * (ahead + behind)
                            term = slopes[reach - 1] * (ahead - behind)
                            moved = term if moved is None else moved + term
                        partial_ref[number, plane] = total
                        drift_ref[number, plane] = moved
        for orbital in range(count):
            for part in range(2):
                number = part * count + orbital
                rows = pl.ds(number * cell_rows, cell_rows)
                for start in range(0, width, block):
                    spread = (
                        xbell_ref[start : start + block] * outers[number][0][None]
                        + xslope_ref[start : start + block] * outers[number][1][None]
                    )
                    store_split(spread_ref, number, start, spread)
                first_ref[rows, :LANES] = jnp.dot(
                    spread_ref[rows, :], zy_ref[...], preferred_element_type=jnp.float32
                )
            real, imaginary = orbital, count + orbital
            for start in range(0, width, block):
                images = []
                for number in (real, imaginary):
                    rows = pl.ds(number * cell_rows + start * ROWS, slab)
                    images.append(
                        partial_ref[number, start : start + block]
                        + first_ref[rows, :LANES].reshape(block, ROWS, LANES)
                    )
                new = (
                    -kinetic * images[1] - drift_ref[real, start : start + block],
                    kinetic * images[0] - drift_ref[imaginary, start : start + block],
                )
                for number, value in zip((real, imaginary), new):
                    field_ref[number, start : start + block] = value
                    total_ref[number, start : start + block] += value
                    store_split(split_ref, number, start, value)
        return carry

    lax.fori_loop(1, ORDER + 1, one_order, 0)


def sums_in_kernel(count, total_ref, width):
    flow = jnp.zeros((ROWS, LANES), jnp.float32)
    density = jnp.zeros((ROWS, LANES), jnp.float32)
    for orbital in range(count):
        for plane in range(width):
            real = total_ref[orbital, plane]
            imaginary = total_ref[count + orbital, plane]
            moved = None
            for reach in range(1, 5):
                ahead = total_ref[count + orbital, (plane + reach) % width]
                behind = total_ref[count + orbital, (plane - reach) % width]
                term = FIRST[reach - 1] * (ahead - behind)
                moved = term if moved is None else moved + term
            flow = flow + real * moved
            density = density + (real * real + imaginary * imaginary)
    return (2.0 * SLOPE) * flow, density


def first_kernel(parts, count, kinds, copies, scalar_ref, piece_ref, *refs):
    opening = piece_ref.shape[1] > 2 * count
    if opening:
        *tables, total_ref, out_ref, potential_ref, field_ref = refs[:10]
        scratch = refs[10:]
    else:
        potential_ref, *tables, sums_ref, total_ref, out_ref, field_ref = refs[:11]
        scratch = refs[11:]
    width = total_ref.shape[1]
    planes = width // parts
    for owner in range(parts):
        for index in range(planes):
            rows = pl.ds(index, ROWS, stride=planes)
            plane = owner * planes + index
            for number in range(2 * count):
                value = piece_ref[owner, number, rows, :]
                field_ref[number, plane] = value
                total_ref[number, plane] = value
            if opening:
                potential_ref[plane] = piece_ref[owner, 2 * count, rows, :]
    propagate_in_kernel(
        count, scalar_ref[0], field_ref, total_ref, potential_ref, tables, scratch, width, kinds
    )
    flow, density = sums_in_kernel(count, total_ref, width)
    if not opening:
        flow, density = sums_ref[0, 0] + flow, sums_ref[0, 1] + density
    for copy in range(copies):
        out_ref[copy, 0] = flow
        out_ref[copy, 1] = density


def second_kernel(parts, count, kinds, points, copies, scalar_ref, seen_ref, *refs):
    psi_ref, potential_ref, *tables, sums_ref, piece_ref, out_ref, field_ref, total_ref = refs[:13]
    scratch = refs[13:]
    width = total_ref.shape[1]
    planes = width // parts
    seen = [seen_ref[owner] for owner in range(parts)]
    seen = functools.reduce(lambda left, right: left + right, seen)
    current = (jnp.sum(seen[0]) + scalar_ref[0] * jnp.sum(seen[1])) * (1.0 / points)
    vector_value = scalar_ref[1] - source_weight * current
    field_ref[...] = psi_ref[...]
    total_ref[...] = psi_ref[...]
    propagate_in_kernel(
        count, vector_value, field_ref, total_ref, potential_ref, tables, scratch, width, kinds
    )
    flow, density = sums_in_kernel(count, total_ref, width)
    flow, density = sums_ref[0, 0] + flow, sums_ref[0, 1] + density
    if copies == 1:
        out_ref[0, 0] = flow
        out_ref[0, 1] = density
    else:
        row = lax.broadcasted_iota(jnp.int32, (ROWS, LANES), 0)
        own = sums_ref[1, 0] + scalar_ref[0] * sums_ref[1, 1]
        following = flow + vector_value * density
        message = jnp.where(
            row == 0,
            jnp.sum(own, axis=0, keepdims=True) * (1.0 / points),
            jnp.where(row == 1, jnp.sum(following, axis=0, keepdims=True) * (1.0 / points), scalar_ref[2]),
        )
        for copy in range(copies):
            out_ref[copy] = message
    for owner in range(parts):
        for number in range(2 * count):
            for index in range(planes):
                piece_ref[owner, number, pl.ds(index, ROWS, stride=planes), :] = total_ref[
                    number, owner * planes + index
                ]


def vmem():
    return pl.BlockSpec(memory_space=pltpu.VMEM)


def smem():
    return pl.BlockSpec(memory_space=pltpu.SMEM)


def anywhere():
    return pl.BlockSpec(memory_space=pl.ANY)


def float_array(*shape):
    return jax.ShapeDtypeStruct(shape, jnp.float32)


def exchanged(value, axes):
    return lax.all_to_all(value, axes, split_axis=0, concat_axis=0, tiled=True)


def per_device(parts, blocks, orbitals, local_potential, atom_sites, host_point, fields):
    norb = orbitals.shape[2]
    planes, points = local_potential.shape
    width = planes * parts
    share = norb // parts
    count = min(2, share)
    chunks = share // count
    owned = fields.shape[1]
    atoms = atom_sites.shape[0]
    kinds = 2 * atoms
    held = ROWS * planes
    total_points = float(width**3 * norb)
    params = pltpu.CompilerParams(vmem_limit_bytes=LIMIT)

    def rows_of(value):
        lead = value.shape[:-2]
        value = value.reshape(*lead, planes, ROWS, LANES)
        return jnp.swapaxes(value, -3, -2).reshape(*lead, held, LANES)

    def planes_of(value):
        lead = value.shape[:-2]
        value = value.reshape(*lead, ROWS, planes, LANES)
        return jnp.swapaxes(value, -3, -2)

    source = rows_of(orbitals[0])
    arrived = []
    for chunk in range(chunks):
        extra = [rows_of(local_potential)] if chunk == 0 else []
        packed = pl.pallas_call(
            functools.partial(pack_kernel, parts, share, count, chunk * count, chunk == 0),
            out_shape=float_array(parts, 2 * count + len(extra), held, LANES),
            in_specs=[anywhere()] * (1 + len(extra)),
            out_specs=anywhere(),
            scratch_shapes=[pltpu.SemaphoreType.DMA((parts * (2 + len(extra)),))],
            compiler_params=params,
        )(source, *extra)
        arrived.append(exchanged(packed, "grid"))
        if chunk == 0:
            seen_fields = exchanged(jnp.broadcast_to(fields[None], (blocks, 2, owned)), "macro")

    tables = pl.pallas_call(
        functools.partial(tables_kernel, atoms),
        out_shape=[
            jax.ShapeDtypeStruct((2 * LANES, 2 * LANES), jnp.bfloat16),
            jax.ShapeDtypeStruct((2 * LANES, 2 * LANES), jnp.bfloat16),
            jax.ShapeDtypeStruct((2 * LANES, LANES), jnp.bfloat16),
            float_array(width, ROWS, LANES),
            float_array(width, ROWS, LANES),
            float_array(5, ROWS, LANES),
        ],
        in_specs=[smem(), vmem()],
        out_specs=[vmem()] * 6,
        compiler_params=params,
    )(atom_sites, stencil_weights(width))

    near_scalars = pl.pallas_call(
        vector_kernel,
        out_shape=float_array(2),
        in_specs=[smem(), vmem()],
        out_specs=smem(),
        compiler_params=params,
    )(host_point, seen_fields)
    scalars = jnp.concatenate([near_scalars, host_point.astype(jnp.float32)])

    rows = 2 * count * width * ROWS
    cell_scratch = pltpu.VMEM((2 * count, width, ROWS, LANES), jnp.float32)
    scratch = [
        pltpu.VMEM((rows, 2 * LANES), jnp.bfloat16),
        pltpu.VMEM((rows, 2 * LANES), jnp.float32),
        pltpu.VMEM((rows, 2 * LANES), jnp.float32),
        cell_scratch,
        cell_scratch,
        pltpu.VMEM((rows, 2 * LANES), jnp.bfloat16),
        pltpu.VMEM((width, ROWS, LANES), jnp.float32),
    ]
    cell = float_array(2 * count, width, ROWS, LANES)
    cost = pl.CostEstimate(
        flops=count * 3 * 2 * 512 * 256 * 256 * ORDER, bytes_accessed=4 * 1024 * 1024, transcendentals=0
    )

    potential, sums = None, None
    moved = []
    for chunk in range(chunks):
        copies = parts if chunk == chunks - 1 else 1
        inputs = [scalars, arrived[chunk]]
        outputs = [cell, float_array(copies, 2, ROWS, LANES)]
        if chunk == 0:
            inputs += list(tables)
            outputs += [float_array(width, ROWS, LANES)]
        else:
            inputs += [potential, *tables, sums]
        psi, sums, *rest = pl.pallas_call(
            functools.partial(first_kernel, parts, count, kinds, copies),
            out_shape=outputs,
            in_specs=[smem()] + [vmem()] * (len(inputs) - 1),
            out_specs=[vmem()] * len(outputs),
            scratch_shapes=[cell_scratch] + scratch,
            compiler_params=params,
            cost_estimate=cost,
        )(*inputs)
        if chunk == 0:
            potential = rest[0]
        moved.append(psi)
    own_sums = sums[:1]
    seen = exchanged(sums, "grid")

    sums = jnp.concatenate([jnp.zeros_like(own_sums), own_sums])
    result = None
    for chunk in range(chunks):
        last = chunk == chunks - 1
        copies = blocks * parts if last else 1
        if last and chunks > 1:
            sums = jnp.concatenate([sums, own_sums])
        pieces, sums = pl.pallas_call(
            functools.partial(second_kernel, parts, count, kinds, total_points, copies),
            out_shape=[
                float_array(parts, 2 * count, held, LANES),
                float_array(copies, ROWS, LANES) if last else float_array(1, 2, ROWS, LANES),
            ],
            in_specs=[smem()] + [vmem()] * 10,
            out_specs=[vmem()] * 2,
            scratch_shapes=[cell_scratch, cell_scratch] + scratch,
            compiler_params=params,
            cost_estimate=cost,
        )(scalars, seen, moved[chunk], potential, *tables, sums)
        returned = exchanged(pieces, "grid")
        result = pl.pallas_call(
            functools.partial(unpack_kernel, parts, share, count, chunk * count),
            out_shape=float_array(2, norb, held, LANES),
            in_specs=[anywhere()] * (1 if chunk == 0 else 2),
            out_specs=anywhere(),
            scratch_shapes=[pltpu.SemaphoreType.DMA((2 * parts,))],
            input_output_aliases={} if chunk == 0 else {1: 0},
            compiler_params=params,
        )(*([returned] if chunk == 0 else [returned, result]))
    orbitals_out = planes_of(result).reshape(2, norb, planes, points)

    messages = exchanged(sums, ("macro", "grid")).reshape(blocks, parts, ROWS, LANES)
    currents = jnp.sum(messages[:, :, :2], axis=(1, 3))
    hosts = messages[:, 0, 2, 0].astype(jnp.int32)
    length = blocks * owned
    positions = lax.broadcasted_iota(jnp.int32, (length,), 0)
    sources = jnp.sum(
        jnp.where(positions[None, None] == hosts[:, None, None], currents[:, :, None], 0.0), axis=0
    )
    whole = jnp.swapaxes(seen_fields, 0, 1).reshape(2, length)
    previous, present = whole[0], whole[1]
    for step in range(STEPS):
        rim = jnp.pad(present, 1)
        following = (
            2.0 * present
            - previous
            + courant_square * (rim[2:] - 2.0 * present + rim[:-2])
            - source_weight * sources[step]
        )
        previous, present = present, following
    start = lax.axis_index("macro") * owned
    fields_out = lax.dynamic_slice_in_dim(jnp.stack([previous, present]), start, owned, axis=1)
    return orbitals_out[None], fields_out


def solution(mesh):
    in_specs = (
        P("macro", None, None, "grid", None),
        P("grid", None),
        P(),
        P("macro"),
        P(None, "macro"),
    )
    out_specs = (P("macro", None, None, "grid", None), P(None, "macro"))
    return jax.shard_map(
        functools.partial(per_device, mesh.shape["grid"], mesh.shape["macro"]),
        mesh=mesh,
        in_specs=in_specs,
        out_specs=out_specs,
        check_vma=False,
    )
```

time: 153 us -> 126 us (0.82)
  waiting for transfers between devices: 9.77 us -> 54 us
  starting transfers between devices: 56.6 us -> 23.7 us
  blocking collectives: 39.4 us -> 10.1 us
  Pallas kernels: 37.4 us -> 29.8 us
  other arithmetic: 5.39 us -> 1.81 us
  local copies, waits for them, and re-layouts: 2.2 us -> 4.35 us
    ppermute x37 -> x0, starting transfers between devices: 56.6 us -> none  [shifted(): lax.ppermute(value, axis_name, [((index + shift) % count, index) for inde...]
    all_to_all x0 -> x6, waiting for transfers between devices: none -> 54 us  [exchanged(): return lax.all_to_all(value, axes, split_axis=0, concat_axis=0, tiled=True)]
    psum x1 -> x0, blocking collectives: 39.4 us -> none  [per_device(): lax.psum(jnp.where(positions[None] == host_point[0], currents[:, None], 0...]
    all_to_all x0 -> x6, starting transfers between devices: none -> 23.7 us  [exchanged(): return lax.all_to_all(value, axes, split_axis=0, concat_axis=0, tiled=True)]
    all_to_all x0 -> x1, blocking collectives: none -> 10.1 us  [exchanged(): return lax.all_to_all(value, axes, split_axis=0, concat_axis=0, tiled=True)]
    ppermute x37 -> x0, waiting for transfers between devices: 9.77 us -> none  [shifted(): lax.ppermute(value, axis_name, [((index + shift) % count, index) for inde...]
    pallas_call x12 -> x10, Pallas kernels: 37.4 us -> 29.8 us  [the longest x2 12.7 us: per_device(): pl.pallas_call(functools.partial(second_kernel, parts, count, kinds, tota...]
    div x1 -> x0, other arithmetic: 3.19 us -> none  [per_device(): currents = (flows + values * densities) / (width ** 3 * norb)]
  transfers between devices with their start and end apart: 37 -> 6, of which waited for: 6 -> 6; matrix products, arithmetic and copies ran while one was open for 1% -> 3% of each run, Pallas kernels for 10% -> 8%
where the time goes in v2:
time: 126 us; the launch traced here: 125 us
  waiting for transfers between devices  54 us (43%)
  Pallas kernels  29.8 us (24%)
  starting transfers between devices  23.7 us (19%)
  blocking collectives  10.1 us (8%)
  local copies, waits for them, and re-layouts  4.35 us (3%)
  other arithmetic  1.81 us (1%)
  between operations  1.44 us (1%)
    all_to_all x6, waiting for transfers between devices, exchanged(): return lax.all_to_all(value, axes, split_axis=0, concat_axis=0, tiled=True)  54 us
    all_to_all x6, starting transfers between devices, exchanged(): return lax.all_to_all(value, axes, split_axis=0, concat_axis=0, tiled=True)  23.7 us
    pallas_call x2, Pallas kernels, per_device(): pl.pallas_call(functools.partial(second_kernel, parts, count, kinds, tota...  12.7 us
    pallas_call x2, Pallas kernels, per_device(): pl.pallas_call(functools.partial(first_kernel, parts, count, kinds, copie...  11.9 us
    all_to_all x1, blocking collectives, exchanged(): return lax.all_to_all(value, axes, split_axis=0, concat_axis=0, tiled=True)  10.1 us
  transfers between devices with their start and end apart: 6, of which 6 were waited for; matrix products, arithmetic and copies ran while one was open for 3% of the time, Pallas kernels for 8%

profile of v2, /device:TPU:0, one launch (start us, length us, event | category | flops | bytes accessed | tf_op | source)
XLA Modules:
  0.0 125.1 jit_solution(3850168097109851218)
XLA Ops:
  2.0 5.2 %all-to-all-start = ((f32[8,1,128]{2,1,0:T(1,128)}), f32[8,1,128]{2,1,0:T(1,128)S(1)}, u32[]{:S(2)}, u32[]{:S(2)}) async-start(f32[8,1,128]{2,1,0:T(1,128)} %reshape.75), calls=%async_computation | async-start | bytes 8192 | tf_op jit(solution)/shard_map/all_to_all | solution.py:389
  7.2 1.2 copy-done
  8.4 0.9 shard_map.79
  9.3 2.5 %all-to-all-done = f32[8,1,128]{2,1,0:T(1,128)S(1)} async-done(((f32[8,1,128]{2,1,0:T(1,128)}), f32[8,1,128]{2,1,0:T(1,128)S(1)}, u32[]{:S(2)}, u32[]{:S(2)}) %all-to-all-start) | async-done | bytes 4128 | tf_op jit(solution)/shard_map/all_to_all | solution.py:389
  11.8 4.9 %all-to-all-start.2 = ((f32[4,5,64,128]{3,2,1,0:T(8,128)}), f32[4,5,64,128]{3,2,1,0:T(8,128)S(1)}, u32[]{:S(2)}, u32[]{:S(2)}) async-start(f32[4,5,64,128]{3,2,1,0:T(8,128)} %shard_map.79), calls=%async_computation.2 | async-start | bytes 1310720 | tf_op jit(solution)/shard_map/all_to_all | solution.py:389
  16.7 0.9 shard_map.78
  17.6 16.4 %all-to-all-done.2.piece_ref = f32[4,5,64,128]{3,2,1,0:T(8,128)S(1)} async-done(((f32[4,5,64,128]{3,2,1,0:T(8,128)}), f32[4,5,64,128]{3,2,1,0:T(8,128)S(1)}, u32[]{:S(2)}, u32[]{:S(2)}) %all-to-all-start.2) | async-done | bytes 655392 | tf_op jit(solution)/shard_map/all_to_all | solution.py:389
  34.0 3.5 %all-to-all-start.1 = ((f32[4,4,64,128]{3,2,1,0:T(8,128)}), f32[4,4,64,128]{3,2,1,0:T(8,128)S(1)}, u32[]{:S(2)}, u32[]{:S(2)}) async-start(f32[4,4,64,128]{3,2,1,0:T(8,128)} %shard_map.78), calls=%async_computation.1 | async-start | bytes 1048576 | tf_op jit(solution)/shard_map/all_to_all | solution.py:389
  38.2 1.0 shard_map.80
  40.5 0.7 shard_map.77
  41.3 5.7 %shard_map.81 = (f32[4,32,8,128]{3,2,1,0:T(8,128)S(1)}, f32[1,2,8,128]{3,2,1,0:T(8,128)S(1)}, f32[32,8,128]{2,1,0:T(8,128)S(1)}) custom-call(f32[3]{0:T(128)S(1)} %pad_maximum_fusion.1.scalar_ref, f32[4,5,64,128]{3,2,1,0:T(8,128)S(1)} %all-to-all-done.2.piece_ref, bf16[256,256]{1,0:T(8,128)(2,1)S(1)} %get-tuple-element.17.refs_0_.refs_1_.refs_2_, ...), custom_call_target="tpu_custom_call" | custom-call | flops 1610612736 | bytes 4194304 | tf_op jit(solution)/shard_map/pallas_call | solution.py:483
  46.9 4.5 %all-to-all-done.1.piece_ref = f32[4,4,64,128]{3,2,1,0:T(8,128)S(1)} async-done(((f32[4,4,64,128]{3,2,1,0:T(8,128)}), f32[4,4,64,128]{3,2,1,0:T(8,128)S(1)}, u32[]{:S(2)}, u32[]{:S(2)}) %all-to-all-start.1) | async-done | bytes 524320 | tf_op jit(solution)/shard_map/all_to_all | solution.py:389
  51.4 6.3 %shard_map.82 = (f32[4,32,8,128]{3,2,1,0:T(8,128)S(1)}, f32[4,2,8,128]{3,2,1,0:T(8,128)}) custom-call(f32[3]{0:T(128)S(1)} %pad_maximum_fusion.1.scalar_ref, f32[4,4,64,128]{3,2,1,0:T(8,128)S(1)} %all-to-all-done.1.piece_ref, f32[32,8,128]{2,1,0:T(8,128)S(1)} %get-tuple-element.23.refs_0_.refs_1_, ...), custom_call_target="tpu_custom_call" | custom-call | flops 1610612736 | bytes 4194304 | tf_op jit(solution)/shard_map/pallas_call | solution.py:483
  57.7 3.3 %all-to-all-start.3 = ((f32[4,2,8,128]{3,2,1,0:T(8,128)}), f32[4,2,8,128]{3,2,1,0:T(8,128)S(1)}, u32[]{:S(2)}, u32[]{:S(2)}) async-start(f32[4,2,8,128]{3,2,1,0:T(8,128)} %get-tuple-element.25), calls=%async_computation.3 | async-start | bytes 65536 | tf_op jit(solution)/shard_map/all_to_all | solution.py:389
  61.6 4.9 %all-to-all-done.3.seen_ref = f32[4,2,8,128]{3,2,1,0:T(8,128)S(1)} async-done(((f32[4,2,8,128]{3,2,1,0:T(8,128)}), f32[4,2,8,128]{3,2,1,0:T(8,128)S(1)}, u32[]{:S(2)}, u32[]{:S(2)}) %all-to-all-start.3) | async-done | bytes 32800 | tf_op jit(solution)/shard_map/all_to_all | solution.py:389
  66.6 6.3 %shard_map.83 = (f32[4,4,64,128]{3,2,1,0:T(8,128)}, f32[1,2,8,128]{3,2,1,0:T(8,128)S(1)}) custom-call(f32[3]{0:T(128)S(1)} %pad_maximum_fusion.1.scalar_ref, f32[4,2,8,128]{3,2,1,0:T(8,128)S(1)} %all-to-all-done.3.seen_ref, f32[4,32,8,128]{3,2,1,0:T(8,128)S(1)} %get-tuple-element.27.refs_0_, f32[32,8,128]{2,1,0:T(8,128)S(1)} %get-tuple-element.23.refs_0_.refs_1_, ...), custom_call_target="tpu_custom_call" | custom-call | flops 1610612736 | bytes 4194304 | tf_op jit(solution)/shard_map/pallas_call | solution.py:505
  72.9 6.3 %shard_map.84 = (f32[4,4,64,128]{3,2,1,0:T(8,128)}, f32[32,8,128]{2,1,0:T(8,128)S(1)}) custom-call(f32[3]{0:T(128)S(1)} %pad_maximum_fusion.1.scalar_ref, f32[4,2,8,128]{3,2,1,0:T(8,128)S(1)} %all-to-all-done.3.seen_ref, f32[4,32,8,128]{3,2,1,0:T(8,128)S(1)} %get-tuple-element.26.refs_0_, f32[32,8,128]{2,1,0:T(8,128)S(1)} %get-tuple-element.23.refs_0_.refs_1_, ...), custom_call_target="tpu_custom_call" | custom-call | flops 1610612736 | bytes 4194304 | tf_op jit(solution)/shard_map/pallas_call | solution.py:505
  79.2 10.1 %all_to_all.35 = f32[32,8,128]{2,1,0:T(8,128)S(1)} all-to-all(f32[32,8,128]{2,1,0:T(8,128)S(1)} %get-tuple-element.31), channel_id=1, replica_groups=mesh['macro'=8,'grid'=4] {'macro','grid'}, dimensions={0} | all-to-all | bytes 262144 | tf_op jit(solution)/shard_map/all_to_all | solution.py:389
  89.3 3.5 %all-to-all-start.5 = ((f32[4,4,64,128]{3,2,1,0:T(8,128)}), f32[4,4,64,128]{3,2,1,0:T(8,128)S(1)}, u32[]{:S(2)}, u32[]{:S(2)}) async-start(f32[4,4,64,128]{3,2,1,0:T(8,128)} %get-tuple-element.30), calls=%async_computation.5 | async-start | bytes 1048576 | tf_op jit(solution)/shard_map/all_to_all | solution.py:389
  93.3 13.5 %all-to-all-done.5.piece_ref = f32[4,4,64,128]{3,2,1,0:T(8,128)S(1)} async-done(((f32[4,4,64,128]{3,2,1,0:T(8,128)}), f32[4,4,64,128]{3,2,1,0:T(8,128)S(1)}, u32[]{:S(2)}, u32[]{:S(2)}) %all-to-all-start.5) | async-done | bytes 524320 | tf_op jit(solution)/shard_map/all_to_all | solution.py:389
  106.9 3.5 %all-to-all-start.4 = ((f32[4,4,64,128]{3,2,1,0:T(8,128)}), f32[4,4,64,128]{3,2,1,0:T(8,128)S(1)}, u32[]{:S(2)}, u32[]{:S(2)}) async-start(f32[4,4,64,128]{3,2,1,0:T(8,128)} %get-tuple-element.29), calls=%async_computation.4 | async-start | bytes 1048576 | tf_op jit(solution)/shard_map/all_to_all | solution.py:389
  111.2 0.8 shard_map.85.refs_0_
  112.1 12.2 %all-to-all-done.4.piece_ref = f32[4,4,64,128]{3,2,1,0:T(8,128)S(1)} async-done(((f32[4,4,64,128]{3,2,1,0:T(8,128)}), f32[4,4,64,128]{3,2,1,0:T(8,128)S(1)}, u32[]{:S(2)}, u32[]{:S(2)}) %all-to-all-start.4) | async-done | bytes 524320 | tf_op jit(solution)/shard_map/all_to_all | solution.py:389
  124.3 0.8 shard_map.86
  (33 shorter events, 4.9 us)
Async XLA Ops:
  0.6 6.5 %copy-start.3 = (f32[8,1024]{1,0:T(8,128)S(1)}, f32[8,1024]{1,0:T(8,128)}, u32[]{:S(2)}) copy-start(f32[8,1024]{1,0:T(8,128)} %param.7) | copy-start | bytes 98308
  2.0 9.8 %all-to-all-start = ((f32[8,1,128]{2,1,0:T(1,128)}), f32[8,1,128]{2,1,0:T(1,128)S(1)}, u32[]{:S(2)}, u32[]{:S(2)}) async-start(f32[8,1,128]{2,1,0:T(1,128)} %reshape.75), calls=%async_computation | async-start | bytes 8192 | tf_op jit(solution)/shard_map/all_to_all | solution.py:389
  7.2 1.2 copy-start
  9.3 7.4 %copy-start.1 = (f32[1,2,16,8,1024]{4,3,2,1,0:T(8,128)S(1)}, f32[1,2,16,8,1024]{4,3,2,1,0:T(8,128)}, u32[]{:S(2)}) copy-start(f32[1,2,16,8,1024]{4,3,2,1,0:T(8,128)} %param.6) | copy-start | bytes 3145732
  11.8 22.1 %all-to-all-start.2 = ((f32[4,5,64,128]{3,2,1,0:T(8,128)}), f32[4,5,64,128]{3,2,1,0:T(8,128)S(1)}, u32[]{:S(2)}, u32[]{:S(2)}) async-start(f32[4,5,64,128]{3,2,1,0:T(8,128)} %shard_map.79), calls=%async_computation.2 | async-start | bytes 1310720 | tf_op jit(solution)/shard_map/all_to_all | solution.py:389
  17.6 20.6 %copy-start.2 = (bf16[256,384]{1,0:T(8,128)(2,1)S(1)}, bf16[256,384]{1,0:T(8,128)(2,1)}, u32[]{:S(2)}) copy-start(bf16[256,384]{1,0:T(8,128)(2,1)} %constant.24.clone.stencil_ref) | copy-start | bytes 589828
  34.0 17.4 %all-to-all-start.1 = ((f32[4,4,64,128]{3,2,1,0:T(8,128)}), f32[4,4,64,128]{3,2,1,0:T(8,128)S(1)}, u32[]{:S(2)}, u32[]{:S(2)}) async-start(f32[4,4,64,128]{3,2,1,0:T(8,128)} %shard_map.78), calls=%async_computation.1 | async-start | bytes 1048576 | tf_op jit(solution)/shard_map/all_to_all | solution.py:389
  37.5 0.7 copy-start.4
  57.7 8.9 %all-to-all-start.3 = ((f32[4,2,8,128]{3,2,1,0:T(8,128)}), f32[4,2,8,128]{3,2,1,0:T(8,128)S(1)}, u32[]{:S(2)}, u32[]{:S(2)}) async-start(f32[4,2,8,128]{3,2,1,0:T(8,128)} %get-tuple-element.25), calls=%async_computation.3 | async-start | bytes 65536 | tf_op jit(solution)/shard_map/all_to_all | solution.py:389
  89.3 17.5 %all-to-all-start.5 = ((f32[4,4,64,128]{3,2,1,0:T(8,128)}), f32[4,4,64,128]{3,2,1,0:T(8,128)S(1)}, u32[]{:S(2)}, u32[]{:S(2)}) async-start(f32[4,4,64,128]{3,2,1,0:T(8,128)} %get-tuple-element.30), calls=%async_computation.5 | async-start | bytes 1048576 | tf_op jit(solution)/shard_map/all_to_all | solution.py:389
  106.9 17.4 %all-to-all-start.4 = ((f32[4,4,64,128]{3,2,1,0:T(8,128)}), f32[4,4,64,128]{3,2,1,0:T(8,128)S(1)}, u32[]{:S(2)}, u32[]{:S(2)}) async-start(f32[4,4,64,128]{3,2,1,0:T(8,128)} %get-tuple-element.29), calls=%async_computation.4 | async-start | bytes 1048576 | tf_op jit(solution)/shard_map/all_to_all | solution.py:389

commit v3 on v2

v3 whole, which is shorter than its diff:
```python
import functools

import jax
import jax.numpy as jnp
import numpy as np
from jax import lax
from jax.experimental import pallas as pl
from jax.experimental.pallas import tpu as pltpu
from jax.sharding import PartitionSpec as P

ORDER = 4
STEPS = 2
spacing = 0.3206
time_step = 0.02
courant_square = 0.81
source_weight = 0.1
radial_strength = 0.3
polar_strength = -0.2
projector_width = 2.5

SECOND = (-14350.0, 8064.0, -1008.0, 128.0, -9.0)
FIRST = (672.0, -168.0, 32.0, -3.0)
KINETIC = 1.0 / (2.0 * 5040.0 * spacing * spacing)
SLOPE = 1.0 / (840.0 * spacing)

LANES = 128
ROWS = 8
LIMIT = 24 * 1024 * 1024


def stencil_weights(width):
    group = LANES // width
    total = np.zeros((LANES, 3 * LANES), np.float32)
    for y_in in range(group):
        for z_in in range(width):
            for y_out in range(group):
                for part, step in enumerate((0, group, -group)):
                    reach = abs(step + y_in - y_out)
                    if 1 <= reach <= 4:
                        total[y_in * width + z_in, part * LANES + y_out * width + z_in] += SECOND[reach]
            for reach in range(1, 5):
                for z_out in ((z_in + reach) % width, (z_in - reach) % width):
                    total[y_in * width + z_in, y_in * width + z_out] += SECOND[reach]
    return jnp.asarray(np.concatenate([total, total], axis=0), jnp.bfloat16)


def periodic(distance, width):
    return ((distance + width // 2) & (width - 1)) - width // 2


def bell_of(offset):
    distance = offset.astype(jnp.float32)
    bell = jnp.exp(-0.5 * distance * distance / (projector_width * projector_width))
    return bell, distance / projector_width * bell


def tables_kernel(atoms, site_ref, stencil_ref, near_ref, far_ref, zy_ref, xbell_ref, xslope_ref, y_ref):
    width = xbell_ref.shape[0]
    kinds = 2 * atoms
    group = LANES // width

    def site_of(column, axis_number):
        atom = (column % kinds) // 2
        position = jnp.zeros(column.shape, jnp.int32)
        for number in range(atoms):
            position = jnp.where(atom == number, site_ref[number, axis_number], position)
        return position

    def factor(coordinate, column):
        bell, slope = bell_of(periodic(coordinate - site_of(column, 2), width))
        value = jnp.where(column % 2 == 0, bell, slope)
        high = value.astype(jnp.bfloat16).astype(jnp.float32)
        return jnp.where(column % LANES < LANES // 2, high, value - high)

    def groups_agree(point, column):
        return (point % LANES) // width == (column // kinds) % group

    shape = (2 * LANES, LANES)
    first = lax.broadcasted_iota(jnp.int32, shape, 0)
    last = lax.broadcasted_iota(jnp.int32, shape, 1)
    near_ref[:, :LANES] = stencil_ref[:, :LANES]
    far_ref[...] = stencil_ref[:, LANES:]
    inward = jnp.where(groups_agree(first, last), factor(first % width, last), 0.0)
    near_ref[:, LANES:] = inward.astype(jnp.bfloat16)
    outward = jnp.where(groups_agree(last, first), factor(last % width, first), 0.0)
    zy_ref[...] = outward.astype(jnp.bfloat16)

    shape = (width, ROWS, LANES)
    plane = lax.broadcasted_iota(jnp.int32, shape, 0)
    column = lax.broadcasted_iota(jnp.int32, shape, 2)
    bell, slope = bell_of(periodic(plane - site_of(column, 0), width))
    xbell_ref[...] = bell
    xslope_ref[...] = slope

    shape = (ROWS, LANES)
    column = lax.broadcasted_iota(jnp.int32, shape, 1)
    row = lax.broadcasted_iota(jnp.int32, shape, 0) * group + (column // kinds) % group
    bell, slope = bell_of(periodic(row - site_of(column, 1), width))
    scale = -1.0 / KINETIC
    even = column % 2 == 0
    y_ref[0] = bell
    y_ref[1] = slope
    y_ref[2] = bell * jnp.where(even, scale * radial_strength, scale * polar_strength)
    y_ref[3] = bell * jnp.where(even, scale * polar_strength, 0.0)
    y_ref[4] = slope * jnp.where(even, scale * polar_strength, 0.0)


def vector_kernel(blocks, host_ref, here_ref, *refs):
    out_ref = refs[blocks]
    owned = refs[0].shape[1]
    host = host_ref[0]
    place = lax.broadcasted_iota(jnp.int32, (1, owned), 1)
    present = jnp.zeros((1, owned), jnp.float32)
    previous, beside = present, present
    for number in range(blocks):
        position = place + lax.rem(here_ref[0] + number, blocks) * owned
        before, now = refs[number][0:1, :], refs[number][1:2, :]
        present = present + jnp.where(position == host, now, 0.0)
        previous = previous + jnp.where(position == host, before, 0.0)
        beside = beside + jnp.where((position == host - 1) | (position == host + 1), now, 0.0)
    present = jnp.sum(present)
    out_ref[0] = present
    out_ref[1] = 2.0 * present - jnp.sum(previous) + courant_square * (jnp.sum(beside) - 2.0 * present)
    out_ref[2] = host.astype(jnp.float32)


def run_copies(pairs, sems):
    copies = [
        pltpu.make_async_copy(source, target, sems.at[number]) for number, (source, target) in enumerate(pairs)
    ]
    for copy in copies:
        copy.start()
    for copy in copies:
        copy.wait()


def pack_kernel(parts, share, count, first, source_ref, potential_ref, out_ref, sems):
    pairs = []
    for owner in range(parts):
        pairs.append((potential_ref, out_ref.at[owner, 2 * count]))
        for part in range(2):
            source = source_ref.at[part, pl.ds(owner * share + first, count)]
            pairs.append((source, out_ref.at[owner, pl.ds(part * count, count)]))
    run_copies(pairs, sems)


def pack_pieces_kernel(parts, share, count, first, here_ref, source_ref, *refs):
    pairs = []
    for step in range(parts):
        owner = lax.rem(here_ref[0] + step, parts)
        for part in range(2):
            source = source_ref.at[part, pl.ds(owner * share + first, count)]
            pairs.append((source, refs[step].at[pl.ds(part * count, count)]))
    run_copies(pairs, refs[parts])


def unpack_kernel(parts, share, count, first, piece_ref, *refs):
    out_ref, sems = refs[-2:]
    pairs = []
    for owner in range(parts):
        for part in range(2):
            target = out_ref.at[part, pl.ds(owner * share + first, count)]
            pairs.append((piece_ref.at[owner, pl.ds(part * count, count)], target))
    run_copies(pairs, sems)


def unpack_pieces_kernel(parts, share, count, first, here_ref, *refs):
    out_ref, sems = refs[parts:]
    pairs = []
    for step in range(parts):
        owner = lax.rem(here_ref[0] + parts - step, parts)
        for part in range(2):
            target = out_ref.at[part, pl.ds(owner * share + first, count)]
            pairs.append((refs[step].at[pl.ds(part * count, count)], target))
    run_copies(pairs, sems)


def fold(values):
    while len(values) > 1:
        half = len(values) // 2
        values = [values[number] + values[number + half] for number in range(half)]
    return values[0]


def total_of_groups(value, kinds):
    for shift in (4, 2, 1):
        value = value + pltpu.roll(value, shift, 0)
    shift = LANES // 2
    while shift >= kinds:
        value = value + pltpu.roll(value, shift, 1)
        shift //= 2
    return value


def propagate_in_kernel(
    count, vector_value, field_ref, total_ref, potential_ref, tables, scratch, width, kinds
):
    near_ref, far_ref, zy_ref, xbell_ref, xslope_ref, y_ref = tables
    split_ref, first_ref, second_ref, partial_ref, drift_ref, spread_ref, diagonal_ref = scratch
    diagonal_ref[...] = (3.0 * SECOND[0] - 0.5 * vector_value * vector_value / KINETIC) - potential_ref[
        ...
    ] * (1.0 / KINETIC)
    block = ROWS
    slab = block * ROWS
    cell_rows = width * ROWS

    def split(planes):
        rows = planes.reshape(slab, LANES)
        high = rows.astype(jnp.bfloat16)
        low = (rows - high.astype(jnp.float32)).astype(jnp.bfloat16)
        return high, low

    def store_split(ref, number, start, planes):
        rows = pl.ds(number * cell_rows + start * ROWS, slab)
        high, low = split(planes)
        ref[rows, :LANES] = high
        ref[rows, LANES:] = low

    for number in range(2 * count):
        for start in range(0, width, block):
            store_split(split_ref, number, start, field_ref[number, start : start + block])

    def one_order(order, carry):
        inverse = jnp.where(order == 1, 1.0, jnp.where(order == 2, 0.5, jnp.where(order == 3, 1.0 / 3.0, 0.25)))
        step_scale = inverse * time_step
        kinetic = step_scale * KINETIC
        drift = step_scale * SLOPE * vector_value
        slopes = [drift * weight for weight in FIRST]
        outers = {}
        for orbital in range(count):
            rows = pl.ds(2 * orbital * cell_rows, 2 * cell_rows)
            first_ref[rows, :] = jnp.dot(split_ref[rows, :], near_ref[...], preferred_element_type=jnp.float32)
            for number in (2 * orbital, 2 * orbital + 1):
                bells = [jnp.zeros((ROWS, LANES), jnp.float32) for _ in range(2)]
                inclines = [jnp.zeros((ROWS, LANES), jnp.float32) for _ in range(2)]
                for plane in range(width):
                    inner = first_ref[pl.ds(number * cell_rows + plane * ROWS, ROWS), LANES:]
                    turn = plane % 2
                    bells[turn] = bells[turn] + inner * xbell_ref[plane]
                    inclines[turn] = inclines[turn] + inner * xslope_ref[plane]
                bell = bells[0] + bells[1]
                incline = inclines[0] + inclines[1]
                first = total_of_groups(bell * y_ref[0], kinds)
                second = total_of_groups(incline * y_ref[0], kinds)
                third = total_of_groups(bell * y_ref[1], kinds)
                outers[number] = (first * y_ref[2] + third * y_ref[4], second * y_ref[3])
        for orbital in range(count):
            rows = pl.ds(2 * orbital * cell_rows, 2 * cell_rows)
            second_ref[rows, :] = jnp.dot(split_ref[rows, :], far_ref[...], preferred_element_type=jnp.float32)
            for start in range(0, width, block):
                for number in (2 * orbital, 2 * orbital + 1):
                    near = {
                        plane: field_ref[number, plane % width] for plane in range(start - 4, start + block + 4)
                    }
                    for plane in range(start, start + block):
                        line = pl.ds(number * cell_rows + plane * ROWS, ROWS)
                        total = first_ref[line, :LANES]
                        total = total + pltpu.roll(second_ref[line, :LANES], ROWS - 1, 0)
                        total = total + pltpu.roll(second_ref[line, LANES:], 1, 0)
                        total = total + diagonal_ref[plane] * near[plane]
                        moved = None
                        for reach in range(1, 5):
                            ahead, behind = near[plane + reach], near[plane - reach]
                            total = total + SECOND[reach] * (ahead + behind)
                            term = slopes[reach - 1] * (ahead - behind)
                            moved = term if moved is None else moved + term
                        partial_ref[number, plane] = total
                        drift_ref[number, plane] = moved
        for orbital in range(count):
            real, imaginary = 2 * orbital, 2 * orbital + 1
            for start in range(0, width, block):
                xbell = xbell_ref[start : start + block]
                xslope = xslope_ref[start : start + block]
                for number in (real, imaginary):
                    spread = xbell * outers[number][0][None] + xslope * outers[number][1][None]
                    store_split(spread_ref, number, start, spread)
            rows = pl.ds(real * cell_rows, 2 * cell_rows)
            first_ref[rows, :LANES] = jnp.dot(
                spread_ref[rows, :], zy_ref[...], preferred_element_type=jnp.float32
            )
            for start in range(0, width, block):
                images = []
                for number in (real, imaginary):
                    rows = pl.ds(number * cell_rows + start * ROWS, slab)
                    images.append(
                        partial_ref[number, start : start + block]
                        + first_ref[rows, :LANES].reshape(block, ROWS, LANES)
                    )
                new = (
                    -kinetic * images[1] - drift_ref[real, start : start + block],
                    kinetic * images[0] - drift_ref[imaginary, start : start + block],
                )
                for number, value in zip((real, imaginary), new):
                    field_ref[number, start : start + block] = value
                    total_ref[number, start : start + block] += value
                    store_split(split_ref, number, start, value)
        return carry

    lax.fori_loop(1, ORDER + 1, one_order, 0)


def sums_in_kernel(count, total_ref, width):
    flow = jnp.zeros((ROWS, LANES), jnp.float32)
    density = jnp.zeros((ROWS, LANES), jnp.float32)
    for orbital in range(count):
        for plane in range(width):
            real = total_ref[2 * orbital, plane]
            imaginary = total_ref[2 * orbital + 1, plane]
            moved = None
            for reach in range(1, 5):
                ahead = total_ref[2 * orbital + 1, (plane + reach) % width]
                behind = total_ref[2 * orbital + 1, (plane - reach) % width]
                term = FIRST[reach - 1] * (ahead - behind)
                moved = term if moved is None else moved + term
            flow = flow + real * moved
            density = density + (real * real + imaginary * imaginary)
    return (2.0 * SLOPE) * flow, density


def first_kernel(parts, count, kinds, opening, scalar_ref, *refs):
    if opening:
        piece_ref, *tables, total_ref, out_ref, potential_ref, field_ref = refs[:11]
        scratch = refs[11:]
    else:
        here_ref, pieces, refs = refs[0], refs[1 : 1 + parts], refs[1 + parts :]
        potential_ref, *tables, sums_ref, total_ref, out_ref, field_ref = refs[:11]
        scratch = refs[11:]
    width = total_ref.shape[1]
    planes = width // parts
    for step in range(parts):
        if opening:
            piece, start = piece_ref.at[step], step * planes
        else:
            piece, start = pieces[step], lax.rem(here_ref[0] + parts - step, parts) * planes
        for index in range(planes):
            rows = pl.ds(index, ROWS, stride=planes)
            for orbital in range(count):
                for part in range(2):
                    value = piece[part * count + orbital, rows, :]
                    field_ref[2 * orbital + part, start + index] = value
                    total_ref[2 * orbital + part, start + index] = value
            if opening:
                potential_ref[start + index] = piece[2 * count, rows, :]
    propagate_in_kernel(
        count, scalar_ref[0], field_ref, total_ref, potential_ref, tables, scratch, width, kinds
    )
    flow, density = sums_in_kernel(count, total_ref, width)
    if not opening:
        flow, density = sums_ref[0] + flow, sums_ref[1] + density
    out_ref[0] = flow
    out_ref[1] = density


def second_kernel(parts, count, kinds, points, opening, copies, scalar_ref, *refs):
    if opening:
        here_ref, seen, refs = refs[0], refs[1 : 1 + parts], refs[1 + parts :]
    else:
        vector_ref, first_sums_ref, sums_ref, *refs = refs
    psi_ref, potential_ref, *tables = refs[:8]
    refs = refs[8:]
    if copies and opening:
        first_sums_ref = seen[0]
    if opening and not copies:
        pieces, vector_ref, refs = refs[:parts], refs[parts], refs[parts + 1 :]
    else:
        piece_ref, *refs = refs
    out_ref, field_ref, total_ref = refs[:3]
    scratch = refs[3:]
    width = total_ref.shape[1]
    planes = width // parts
    if opening:
        flow = jnp.sum(fold([ref[0] for ref in seen]))
        density = jnp.sum(fold([ref[1] for ref in seen]))
        current = (flow + scalar_ref[0] * density) * (1.0 / points)
        vector_value = scalar_ref[1] - source_weight * current
        if not copies:
            vector_ref[0] = vector_value
    else:
        vector_value = vector_ref[0]
    field_ref[...] = psi_ref[...]
    total_ref[...] = psi_ref[...]
    propagate_in_kernel(
        count, vector_value, field_ref, total_ref, potential_ref, tables, scratch, width, kinds
    )
    for step in range(parts):
        if copies:
            piece, start = piece_ref.at[step], step * planes
        else:
            piece, start = pieces[step], lax.rem(here_ref[0] + step, parts) * planes
        for index in range(planes):
            rows = pl.ds(index, ROWS, stride=planes)
            for orbital in range(count):
                for part in range(2):
                    piece[part * count + orbital, rows, :] = total_ref[2 * orbital + part, start + index]
    flow, density = sums_in_kernel(count, total_ref, width)
    if not opening:
        flow, density = sums_ref[0] + flow, sums_ref[1] + density
    if copies:
        row = lax.broadcasted_iota(jnp.int32, (ROWS, LANES), 0)
        own = first_sums_ref[0] + scalar_ref[0] * first_sums_ref[1]
        own = jnp.sum(own, axis=0, keepdims=True) * (1.0 / points)
        new = jnp.sum(flow + vector_value * density, axis=0, keepdims=True) * (1.0 / points)
        message = jnp.where(row == 0, own, jnp.where(row == 1, new, scalar_ref[2]))
        for copy in range(copies):
            out_ref[copy] = message
    else:
        out_ref[0] = flow
        out_ref[1] = density


def vmem():
    return pl.BlockSpec(memory_space=pltpu.VMEM)


def smem():
    return pl.BlockSpec(memory_space=pltpu.SMEM)


def anywhere():
    return pl.BlockSpec(memory_space=pl.ANY)


def hbm():
    return pl.BlockSpec(memory_space=pltpu.HBM)


def float_array(*shape):
    return jax.ShapeDtypeStruct(shape, jnp.float32)


def exchanged(value, axes):
    return lax.all_to_all(value, axes, split_axis=0, concat_axis=0, tiled=True)


def shifted(value, axis_name, count, shift):
    return lax.ppermute(value, axis_name, [((index + shift) % count, index) for index in range(count)])


def per_device(parts, blocks, orbitals, local_potential, atom_sites, host_point, fields):
    norb = orbitals.shape[2]
    planes, points = local_potential.shape
    width = planes * parts
    share = norb // parts
    last_count = 1 if share > 1 else 0
    main_count = share - last_count
    owned = fields.shape[1]
    atoms = atom_sites.shape[0]
    kinds = 2 * atoms
    held = ROWS * planes
    total_points = float(width**3 * norb)
    here = lax.axis_index("grid").astype(jnp.int32)[None]
    block = lax.axis_index("macro").astype(jnp.int32)
    params = pltpu.CompilerParams(vmem_limit_bytes=LIMIT)

    def rows_of(value):
        lead = value.shape[:-2]
        value = value.reshape(*lead, planes, ROWS, LANES)
        return jnp.swapaxes(value, -3, -2).reshape(*lead, held, LANES)

    def planes_of(value):
        lead = value.shape[:-2]
        value = value.reshape(*lead, ROWS, planes, LANES)
        return jnp.swapaxes(value, -3, -2)

    source = rows_of(orbitals[0])
    packed = pl.pallas_call(
        functools.partial(pack_kernel, parts, share, main_count, 0),
        out_shape=float_array(parts, 2 * main_count + 1, held, LANES),
        in_specs=[hbm(), hbm()],
        out_specs=anywhere(),
        scratch_shapes=[pltpu.SemaphoreType.DMA((parts * 3,))],
        compiler_params=params,
    )(source, rows_of(local_potential))
    main = exchanged(packed, "grid")
    fields, source, packed = lax.optimization_barrier((fields, source, packed))
    if last_count:
        last = pl.pallas_call(
            functools.partial(pack_pieces_kernel, parts, share, last_count, main_count),
            out_shape=[float_array(2 * last_count, held, LANES)] * parts,
            in_specs=[smem(), hbm()],
            out_specs=[anywhere()] * parts,
            scratch_shapes=[pltpu.SemaphoreType.DMA((parts * 2,))],
            compiler_params=params,
        )(here, source)
        last = [last[0]] + [shifted(last[step], "grid", parts, -step) for step in range(1, parts)]
    field_blocks = [fields] + [shifted(fields, "macro", blocks, step) for step in range(1, blocks)]

    tables = pl.pallas_call(
        functools.partial(tables_kernel, atoms),
        out_shape=[
            jax.ShapeDtypeStruct((2 * LANES, 2 * LANES), jnp.bfloat16),
            jax.ShapeDtypeStruct((2 * LANES, 2 * LANES), jnp.bfloat16),
            jax.ShapeDtypeStruct((2 * LANES, LANES), jnp.bfloat16),
            float_array(width, ROWS, LANES),
            float_array(width, ROWS, LANES),
            float_array(5, ROWS, LANES),
        ],
        in_specs=[smem(), vmem()],
        out_specs=[vmem()] * 6,
        compiler_params=params,
    )(atom_sites, stencil_weights(width))

    scalars = pl.pallas_call(
        functools.partial(vector_kernel, blocks),
        out_shape=float_array(3),
        in_specs=[smem(), smem()] + [vmem()] * blocks,
        out_specs=smem(),
        compiler_params=params,
    )(host_point, block[None], *field_blocks)

    def micro_call(kernel, count, inputs, scalar_inputs, outputs, scalar_outputs, cells):
        rows = 2 * count * width * ROWS
        cell = pltpu.VMEM((2 * count, width, ROWS, LANES), jnp.float32)
        return pl.pallas_call(
            kernel,
            out_shape=outputs,
            in_specs=[smem() if number < scalar_inputs else vmem() for number in range(len(inputs))],
            out_specs=[smem() if number in scalar_outputs else vmem() for number in range(len(outputs))],
            scratch_shapes=[cell] * cells
            + [
                pltpu.VMEM((rows, 2 * LANES), jnp.bfloat16),
                pltpu.VMEM((rows, 2 * LANES), jnp.float32),
                pltpu.VMEM((rows, 2 * LANES), jnp.float32),
                cell,
                cell,
                pltpu.VMEM((rows, 2 * LANES), jnp.bfloat16),
                pltpu.VMEM((width, ROWS, LANES), jnp.float32),
            ],
            compiler_params=params,
            cost_estimate=pl.CostEstimate(
                flops=count * 3 * 2 * 512 * 256 * 256 * ORDER, bytes_accessed=4 * 1024 * 1024, transcendentals=0
            ),
        )(*inputs)

    def cells_of(count):
        return float_array(2 * count, width, ROWS, LANES)

    sums_shape = float_array(2, ROWS, LANES)
    main_psi, sums, potential = micro_call(
        functools.partial(first_kernel, parts, main_count, kinds, True),
        main_count,
        [scalars, main, *tables],
        1,
        [cells_of(main_count), sums_shape, float_array(width, ROWS, LANES)],
        (),
        1,
    )
    if last_count:
        last_psi, sums = micro_call(
            functools.partial(first_kernel, parts, last_count, kinds, False),
            last_count,
            [scalars, here, *last, potential, *tables, sums],
            2,
            [cells_of(last_count), sums_shape],
            (),
            1,
        )
    seen = [sums] + [shifted(sums, "grid", parts, step) for step in range(1, parts)]

    everyone = blocks * parts
    pieces_shape = float_array(parts, 2 * main_count, held, LANES)
    messages_shape = float_array(everyone, ROWS, LANES)
    whole_shape = float_array(2, norb, held, LANES)
    if last_count:
        *pieces, vector_value, second_sums = micro_call(
            functools.partial(second_kernel, parts, last_count, kinds, total_points, True, 0),
            last_count,
            [scalars, here, *seen, last_psi, potential, *tables],
            2,
            [float_array(2 * last_count, held, LANES)] * parts + [float_array(1), sums_shape],
            (parts,),
            2,
        )
        pieces = [pieces[0]] + [shifted(pieces[step], "grid", parts, -step) for step in range(1, parts)]
        main_pieces, messages = micro_call(
            functools.partial(second_kernel, parts, main_count, kinds, total_points, False, everyone),
            main_count,
            [scalars, vector_value, sums, second_sums, main_psi, potential, *tables],
            2,
            [pieces_shape, messages_shape],
            (),
            2,
        )
    else:
        main_pieces, messages = micro_call(
            functools.partial(second_kernel, parts, main_count, kinds, total_points, True, everyone),
            main_count,
            [scalars, here, *seen, main_psi, potential, *tables],
            2,
            [pieces_shape, messages_shape],
            (),
            2,
        )
    returned = exchanged(main_pieces, "grid")
    result = []
    if last_count:
        result = pl.pallas_call(
            functools.partial(unpack_pieces_kernel, parts, share, last_count, main_count),
            out_shape=whole_shape,
            in_specs=[smem()] + [anywhere()] * parts,
            out_specs=hbm(),
            scratch_shapes=[pltpu.SemaphoreType.DMA((parts * 2,))],
            compiler_params=params,
        )(here, *pieces)
        result, messages = lax.optimization_barrier((result, messages))
        result = [result]
    result = pl.pallas_call(
        functools.partial(unpack_kernel, parts, share, main_count, 0),
        out_shape=whole_shape,
        in_specs=[anywhere()] + [hbm()] * len(result),
        out_specs=hbm(),
        scratch_shapes=[pltpu.SemaphoreType.DMA((parts * 2,))],
        input_output_aliases={1: 0} if result else {},
        compiler_params=params,
    )(returned, *result)
    orbitals_out = planes_of(result).reshape(2, norb, planes, points)

    messages = exchanged(messages, ("macro", "grid")).reshape(blocks, parts, ROWS, LANES)
    currents = jnp.sum(messages[:, :, :2], axis=(1, 3))
    hosts = messages[:, 0, 2, 0].astype(jnp.int32)
    length = blocks * owned
    start = block * owned
    positions = lax.broadcasted_iota(jnp.int32, (length,), 0)
    sources = jnp.sum(
        jnp.where(positions[None, None] == hosts[:, None, None], currents[:, :, None], 0.0), axis=0
    )
    turned = jnp.concatenate(field_blocks, axis=1)
    whole = lax.dynamic_slice_in_dim(
        jnp.concatenate([turned, turned], axis=1), length - start, length, axis=1
    )
    previous, present = whole[0], whole[1]
    for step in range(STEPS):
        rim = jnp.pad(present, 1)
        following = (
            2.0 * present
            - previous
            + courant_square * (rim[2:] - 2.0 * present + rim[:-2])
            - source_weight * sources[step]
        )
        previous, present = present, following
    fields_out = lax.dynamic_slice_in_dim(jnp.stack([previous, present]), start, owned, axis=1)
    return orbitals_out[None], fields_out


def solution(mesh):
    in_specs = (
        P("macro", None, None, "grid", None),
        P("grid", None),
        P(),
        P("macro"),
        P(None, "macro"),
    )
    out_specs = (P("macro", None, None, "grid", None), P(None, "macro"))
    return jax.shard_map(
        functools.partial(per_device, mesh.shape["grid"], mesh.shape["macro"]),
        mesh=mesh,
        in_specs=in_specs,
        out_specs=out_specs,
        check_vma=False,
    )
```

time: 126 us -> 111 us (0.88)
  waiting for transfers between devices: 54 us -> 38.5 us
  starting transfers between devices: 23.7 us -> 36.7 us
  blocking collectives: 10.1 us -> 0 us
  local copies, waits for them, and re-layouts: 4.35 us -> 2.45 us
    ppermute x0 -> x16, starting transfers between devices: none -> 22.5 us  [shifted(): lax.ppermute(value, axis_name, [((index + shift) % count, index) for inde...]
    all_to_all x6 -> x3, waiting for transfers between devices: 54 us -> 36.2 us  [exchanged(): return lax.all_to_all(value, axes, split_axis=0, concat_axis=0, tiled=True)]
    all_to_all x1 -> x0, blocking collectives: 10.1 us -> none  [exchanged(): return lax.all_to_all(value, axes, split_axis=0, concat_axis=0, tiled=True)]
    all_to_all x6 -> x3, starting transfers between devices: 23.7 us -> 14.2 us  [exchanged(): return lax.all_to_all(value, axes, split_axis=0, concat_axis=0, tiled=True)]
    ppermute x0 -> x16, waiting for transfers between devices: none -> 2.24 us  [shifted(): lax.ppermute(value, axis_name, [((index + shift) % count, index) for inde...]
  transfers between devices with their start and end apart: 6 -> 19, of which waited for: 6 -> 5; matrix products, arithmetic and copies ran while one was open for 3% -> 1% of each run, Pallas kernels for 8% -> 18%
where the time goes in v3:
time: 111 us
  waiting for transfers between devices  38.5 us (35%)
  starting transfers between devices  36.7 us (33%)
  Pallas kernels  30.6 us (28%)
  local copies, waits for them, and re-layouts  2.45 us (2%)
  between operations  1.49 us (1%)
    all_to_all x3, waiting for transfers between devices, exchanged(): return lax.all_to_all(value, axes, split_axis=0, concat_axis=0, tiled=True)  36.2 us
    pallas_call x4, Pallas kernels, micro_call(): pl.pallas_call(kernel, out_shape=outputs, in_specs=[smem() if number < sc...  25.7 us
    ppermute x16, starting transfers between devices, shifted(): lax.ppermute(value, axis_name, [((index + shift) % count, index) for inde...  22.5 us
    all_to_all x3, starting transfers between devices, exchanged(): return lax.all_to_all(value, axes, split_axis=0, concat_axis=0, tiled=True)  14.2 us
    ppermute x16, waiting for transfers between devices, shifted(): lax.ppermute(value, axis_name, [((index + shift) % count, index) for inde...  2.24 us
  transfers between devices with their start and end apart: 19, of which 5 were waited for; matrix products, arithmetic and copies ran while one was open for 1% of the time, Pallas kernels for 18%

profile of v3, /device:TPU:0, one launch (start us, length us, event | category | flops | bytes accessed | tf_op | source)
XLA Modules:
  0.0 110.8 jit_solution(5342895422869568148)
XLA Ops:
  0.6 1.2 %copy-done = f32[1,2,16,8,1024]{4,3,2,1,0:T(8,128)S(1)} copy-done((f32[1,2,16,8,1024]{4,3,2,1,0:T(8,128)S(1)}, f32[1,2,16,8,1024]{4,3,2,1,0:T(8,128)}, u32[]{:S(2)}) %copy-start) | copy-done | bytes 1048600
  2.6 1.0 shard_map.77
  3.7 6.5 %all-to-all-start = ((f32[4,7,64,128]{3,2,1,0:T(8,128)}), f32[4,7,64,128]{3,2,1,0:T(8,128)S(1)}, u32[]{:S(2)}, u32[]{:S(2)}) async-start(f32[4,7,64,128]{3,2,1,0:T(8,128)} %shard_map.77), calls=%async_computation | async-start | bytes 1835008 | tf_op jit(solution)/shard_map/all_to_all | solution.py:432
  10.1 1.5 %collective-permute-start.5 = (f32[2,64]{1,0:T(2,128)S(1)}, f32[2,64]{1,0:T(2,128)S(1)}, u32[]{:S(2)}, u32[]{:S(2)}) collective-permute-start(f32[2,64]{1,0:T(2,128)S(1)} %copy-done.4), channel_id=1, source_target_pairs={{24,0},{28,4},{0,8},{4,12},{8,16},{12,20},{16,24},{20,28},{25,1},{... | collective-permute-start | bytes 1544 | tf_op jit(solution)/shard_map/ppermute | solution.py:436
  11.7 2.4 %collective-permute-start.4 = (f32[2,64]{1,0:T(2,128)S(1)}, f32[2,64]{1,0:T(2,128)S(1)}, u32[]{:S(2)}, u32[]{:S(2)}) collective-permute-start(f32[2,64]{1,0:T(2,128)S(1)} %copy-done.4), channel_id=1, source_target_pairs={{20,0},{24,4},{28,8},{0,12},{4,16},{8,20},{12,24},{16,28},{21,1},{... | collective-permute-start | bytes 1544 | tf_op jit(solution)/shard_map/ppermute | solution.py:436
  16.9 1.5 %collective-permute-start.1 = (f32[2,64]{1,0:T(2,128)S(1)}, f32[2,64]{1,0:T(2,128)S(1)}, u32[]{:S(2)}, u32[]{:S(2)}) collective-permute-start(f32[2,64]{1,0:T(2,128)S(1)} %copy-done.4), channel_id=1, source_target_pairs={{8,0},{12,4},{16,8},{20,12},{24,16},{28,20},{0,24},{4,28},{9,1},{1... | collective-permute-start | bytes 1544 | tf_op jit(solution)/shard_map/ppermute | solution.py:436
  18.4 2.3 %collective-permute-start = (f32[2,64]{1,0:T(2,128)S(1)}, f32[2,64]{1,0:T(2,128)S(1)}, u32[]{:S(2)}, u32[]{:S(2)}) collective-permute-start(f32[2,64]{1,0:T(2,128)S(1)} %copy-done.4), channel_id=1, source_target_pairs={{4,0},{8,4},{12,8},{16,12},{20,16},{24,20},{28,24},{0,28},{5,1},{9... | collective-permute-start | bytes 1544 | tf_op jit(solution)/shard_map/ppermute | solution.py:436
  20.7 2.0 %collective-permute-start.7 = (f32[2,64,128]{2,1,0:T(8,128)S(1)}, f32[2,64,128]{2,1,0:T(8,128)S(1)}, u32[]{:S(2)}, u32[]{:S(2)}) collective-permute-start(f32[2,64,128]{2,1,0:T(8,128)S(1)} %get-tuple-element.32), channel_id=1, source_target_pairs={{3,0},{0,1},{1,2},{2,3},{7,4},{4,5},{5,6},{6,7},{11,8},{8,9},{9,10... | collective-permute-start | bytes 196616 | tf_op jit(solution)/shard_map/ppermute | solution.py:436
  22.7 2.4 %collective-permute-start.8 = (f32[2,64,128]{2,1,0:T(8,128)S(1)}, f32[2,64,128]{2,1,0:T(8,128)S(1)}, u32[]{:S(2)}, u32[]{:S(2)}) collective-permute-start(f32[2,64,128]{2,1,0:T(8,128)S(1)} %get-tuple-element.33), channel_id=1, source_target_pairs={{2,0},{3,1},{0,2},{1,3},{6,4},{7,5},{4,6},{5,7},{10,8},{11,9},{8,1... | collective-permute-start | bytes 196616 | tf_op jit(solution)/shard_map/ppermute | solution.py:436
  25.1 1.5 %collective-permute-start.9 = (f32[2,64,128]{2,1,0:T(8,128)S(1)}, f32[2,64,128]{2,1,0:T(8,128)S(1)}, u32[]{:S(2)}, u32[]{:S(2)}) collective-permute-start(f32[2,64,128]{2,1,0:T(8,128)S(1)} %get-tuple-element.34), channel_id=1, source_target_pairs={{1,0},{2,1},{3,2},{0,3},{5,4},{6,5},{7,6},{4,7},{9,8},{10,9},{11,1... | collective-permute-start | bytes 196616 | tf_op jit(solution)/shard_map/ppermute | solution.py:436
  27.3 9.6 %all-to-all-done.refs_0_ = f32[4,7,64,128]{3,2,1,0:T(8,128)S(1)} async-done(((f32[4,7,64,128]{3,2,1,0:T(8,128)}), f32[4,7,64,128]{3,2,1,0:T(8,128)S(1)}, u32[]{:S(2)}, u32[]{:S(2)}) %all-to-all-start) | async-done | bytes 917536 | tf_op jit(solution)/shard_map/all_to_all | solution.py:432
  36.9 8.1 %shard_map.81 = (f32[6,32,8,128]{3,2,1,0:T(8,128)S(1)}, f32[2,8,128]{2,1,0:T(8,128)S(1)}, f32[32,8,128]{2,1,0:T(8,128)S(1)}) custom-call(f32[3]{0:T(128)S(1)} %shard_map.78.scalar_ref, f32[4,7,64,128]{3,2,1,0:T(8,128)S(1)} %all-to-all-done.refs_0_, bf16[256,256]{1,0:T(8,128)(2,1)S(1)} %get-tuple-element.35.refs_1_.refs_6_.refs_7_.refs_5_, ...), custom_call_target="tpu_custom_call" | custom-call | flops 2415919104 | bytes 4194304 | tf_op jit(solution)/shard_map/pallas_call | solution.py:514
  45.0 3.8 %shard_map.82 = (f32[2,32,8,128]{3,2,1,0:T(8,128)S(1)}, f32[2,8,128]{2,1,0:T(8,128)S(1)}) custom-call(f32[3]{0:T(128)S(1)} %shard_map.78.scalar_ref, s32[1]{0:T(128)} %bitcast.9.here_ref.refs_0_, f32[2,64,128]{2,1,0:T(8,128)S(1)} %get-tuple-element.31.refs_1_, f32[2,64,128]{2,1,0:T(8,128)S(1)} %collective-permute-done.7.refs_2_, ...), custom_call_target="tpu_custom_call" | custom-call | flops 805306368 | bytes 4194304 | tf_op jit(solution)/shard_map/pallas_call | solution.py:514
  48.9 2.4 %collective-permute-start.11 = (f32[2,8,128]{2,1,0:T(8,128)S(1)}, f32[2,8,128]{2,1,0:T(8,128)S(1)}, u32[]{:S(2)}, u32[]{:S(2)}) collective-permute-start(f32[2,8,128]{2,1,0:T(8,128)S(1)} %get-tuple-element.43.refs_1_), channel_id=1, source_target_pairs={{2,0},{3,1},{0,2},{1,3},{6,4},{7,5},{4,6},{5,7},{10,8},{11,9},{8,1... | collective-permute-start | bytes 24584 | tf_op jit(solution)/shard_map/ppermute | solution.py:436
  51.3 1.4 %collective-permute-start.10 = (f32[2,8,128]{2,1,0:T(8,128)S(1)}, f32[2,8,128]{2,1,0:T(8,128)S(1)}, u32[]{:S(2)}, u32[]{:S(2)}) collective-permute-start(f32[2,8,128]{2,1,0:T(8,128)S(1)} %get-tuple-element.43.refs_1_), channel_id=1, source_target_pairs={{1,0},{2,1},{3,2},{0,3},{5,4},{6,5},{7,6},{4,7},{9,8},{10,9},{11,1... | collective-permute-start | bytes 24584 | tf_op jit(solution)/shard_map/ppermute | solution.py:436
  52.7 1.6 %collective-permute-done.12.refs_4_ = f32[2,8,128]{2,1,0:T(8,128)S(1)} collective-permute-done((f32[2,8,128]{2,1,0:T(8,128)S(1)}, f32[2,8,128]{2,1,0:T(8,128)S(1)}, u32[]{:S(2)}, u32[]{:S(2)}) %collective-permute-start.12) | collective-permute-done | bytes 8224 | tf_op jit(solution)/shard_map/ppermute | solution.py:436
  54.9 4.3 %shard_map.83 = (f32[2,64,128]{2,1,0:T(8,128)S(1)}, f32[2,64,128]{2,1,0:T(8,128)S(1)}, f32[2,64,128]{2,1,0:T(8,128)S(1)}, f32[2,64,128]{2,1,0:T(8,128)S(1)}, f32[1]{0:T(128)}, /*index=5*/f32[2,8,128]{2,1,0:T(8,128)S(1)}) custom-call(f32[3]{0:T(128)S(1)} %shard_map.78.scalar_ref, s32[1]{0:T(128)} %bitcast.9.here_ref.refs_0_, ...), custom_call_target="tpu_custom_call" | custom-call | flops 805306368 | bytes 4194304 | tf_op jit(solution)/shard_map/pallas_call | solution.py:514
  59.2 2.1 %collective-permute-start.13 = (f32[2,64,128]{2,1,0:T(8,128)S(1)}, f32[2,64,128]{2,1,0:T(8,128)S(1)}, u32[]{:S(2)}, u32[]{:S(2)}) collective-permute-start(f32[2,64,128]{2,1,0:T(8,128)S(1)} %get-tuple-element.50), channel_id=1, source_target_pairs={{3,0},{0,1},{1,2},{2,3},{7,4},{4,5},{5,6},{6,7},{11,8},{8,9},{9,10... | collective-permute-start | bytes 196616 | tf_op jit(solution)/shard_map/ppermute | solution.py:436
  61.3 1.8 %collective-permute-start.14 = (f32[2,64,128]{2,1,0:T(8,128)S(1)}, f32[2,64,128]{2,1,0:T(8,128)S(1)}, u32[]{:S(2)}, u32[]{:S(2)}) collective-permute-start(f32[2,64,128]{2,1,0:T(8,128)S(1)} %get-tuple-element.51), channel_id=1, source_target_pairs={{2,0},{3,1},{0,2},{1,3},{6,4},{7,5},{4,6},{5,7},{10,8},{11,9},{8,1... | collective-permute-start | bytes 196616 | tf_op jit(solution)/shard_map/ppermute | solution.py:436
  63.7 9.5 %shard_map.84 = (f32[4,6,64,128]{3,2,1,0:T(8,128)}, f32[32,8,128]{2,1,0:T(8,128)}) custom-call(f32[3]{0:T(128)S(1)} %shard_map.78.scalar_ref, f32[1]{0:T(128)} %get-tuple-element.45.refs_0_, f32[2,8,128]{2,1,0:T(8,128)S(1)} %get-tuple-element.43.refs_1_, f32[2,8,128]{2,1,0:T(8,128)S(1)} %get-tuple-element.46.refs_2_, ...), custom_call_target="tpu_custom_call" | custom-call | flops 2415919104 | bytes 4194304 | tf_op jit(solution)/shard_map/pallas_call | solution.py:514
  74.1 4.2 %all-to-all-start.2 = ((f32[32,8,128]{2,1,0:T(8,128)}), f32[32,8,128]{2,1,0:T(8,128)S(1)}, u32[]{:S(2)}, u32[]{:S(2)}) async-start(f32[32,8,128]{2,1,0:T(8,128)} %get-tuple-element.55), calls=%async_computation.2 | async-start | bytes 262144 | tf_op jit(solution)/shard_map/all_to_all | solution.py:432
  78.5 8.2 %all-to-all-done.2 = f32[32,8,128]{2,1,0:T(8,128)S(1)} async-done(((f32[32,8,128]{2,1,0:T(8,128)}), f32[32,8,128]{2,1,0:T(8,128)S(1)}, u32[]{:S(2)}, u32[]{:S(2)}) %all-to-all-start.2) | async-done | bytes 131104 | tf_op jit(solution)/shard_map/all_to_all | solution.py:432
  86.7 3.5 %all-to-all-start.1 = ((f32[4,6,64,128]{3,2,1,0:T(8,128)}), f32[4,6,64,128]{3,2,1,0:T(8,128)S(1)}, u32[]{:S(2)}, u32[]{:S(2)}) async-start(f32[4,6,64,128]{3,2,1,0:T(8,128)} %get-tuple-element.48), calls=%async_computation.1 | async-start | bytes 1572864 | tf_op jit(solution)/shard_map/all_to_all | solution.py:432
  91.4 18.4 %all-to-all-done.1.piece_ref = f32[4,6,64,128]{3,2,1,0:T(8,128)S(1)} async-done(((f32[4,6,64,128]{3,2,1,0:T(8,128)}), f32[4,6,64,128]{3,2,1,0:T(8,128)S(1)}, u32[]{:S(2)}, u32[]{:S(2)}) %all-to-all-start.1) | async-done | bytes 786464 | tf_op jit(solution)/shard_map/all_to_all | solution.py:432
  (50 shorter events, 8.1 us)
Async XLA Ops:
  0.6 1.2 %copy-start = (f32[1,2,16,8,1024]{4,3,2,1,0:T(8,128)S(1)}, f32[1,2,16,8,1024]{4,3,2,1,0:T(8,128)}, u32[]{:S(2)}) copy-start(f32[1,2,16,8,1024]{4,3,2,1,0:T(8,128)} %param.6) | copy-start | bytes 3145732
  1.9 0.8 copy-start.3
  3.6 6.5 %copy-start.4 = (f32[2,64]{1,0:T(2,128)S(1)}, f32[2,64]{1,0:T(2,128)}, u32[]{:S(2)}) copy-start(f32[2,64]{1,0:T(2,128)} %refs_0_) | copy-start | bytes 1540
  3.6 11.8 %copy-start.2 = (bf16[256,384]{1,0:T(8,128)(2,1)S(1)}, bf16[256,384]{1,0:T(8,128)(2,1)}, u32[]{:S(2)}) copy-start(bf16[256,384]{1,0:T(8,128)(2,1)} %constant.29.clone.stencil_ref) | copy-start | bytes 589828
  3.7 12.8 %copy-start.1 = (f32[1,2,16,8,1024]{4,3,2,1,0:T(8,128)S(1)}, f32[1,2,16,8,1024]{4,3,2,1,0:T(8,128)}, u32[]{:S(2)}) copy-start(f32[1,2,16,8,1024]{4,3,2,1,0:T(8,128)} %param.6) | copy-start | bytes 3145732
  3.7 33.2 %all-to-all-start = ((f32[4,7,64,128]{3,2,1,0:T(8,128)}), f32[4,7,64,128]{3,2,1,0:T(8,128)S(1)}, u32[]{:S(2)}, u32[]{:S(2)}) async-start(f32[4,7,64,128]{3,2,1,0:T(8,128)} %shard_map.77), calls=%async_computation | async-start | bytes 1835008 | tf_op jit(solution)/shard_map/all_to_all | solution.py:432
  10.1 6.7 %collective-permute-start.6 = (f32[2,64]{1,0:T(2,128)S(1)}, f32[2,64]{1,0:T(2,128)S(1)}, u32[]{:S(2)}, u32[]{:S(2)}) collective-permute-start(f32[2,64]{1,0:T(2,128)S(1)} %copy-done.4), channel_id=1, source_target_pairs={{28,0},{0,4},{4,8},{8,12},{12,16},{16,20},{20,24},{24,28},{29,1},{... | collective-permute-start | bytes 1544 | tf_op jit(solution)/shard_map/ppermute | solution.py:436
  10.1 8.2 %collective-permute-start.5 = (f32[2,64]{1,0:T(2,128)S(1)}, f32[2,64]{1,0:T(2,128)S(1)}, u32[]{:S(2)}, u32[]{:S(2)}) collective-permute-start(f32[2,64]{1,0:T(2,128)S(1)} %copy-done.4), channel_id=1, source_target_pairs={{24,0},{28,4},{0,8},{4,12},{8,16},{12,20},{16,24},{20,28},{25,1},{... | collective-permute-start | bytes 1544 | tf_op jit(solution)/shard_map/ppermute | solution.py:436
  11.7 9.0 %collective-permute-start.4 = (f32[2,64]{1,0:T(2,128)S(1)}, f32[2,64]{1,0:T(2,128)S(1)}, u32[]{:S(2)}, u32[]{:S(2)}) collective-permute-start(f32[2,64]{1,0:T(2,128)S(1)} %copy-done.4), channel_id=1, source_target_pairs={{20,0},{24,4},{28,8},{0,12},{4,16},{8,20},{12,24},{16,28},{21,1},{... | collective-permute-start | bytes 1544 | tf_op jit(solution)/shard_map/ppermute | solution.py:436
  14.1 8.7 %collective-permute-start.3 = (f32[2,64]{1,0:T(2,128)S(1)}, f32[2,64]{1,0:T(2,128)S(1)}, u32[]{:S(2)}, u32[]{:S(2)}) collective-permute-start(f32[2,64]{1,0:T(2,128)S(1)} %copy-done.4), channel_id=1, source_target_pairs={{16,0},{20,4},{24,8},{28,12},{0,16},{4,20},{8,24},{12,28},{17,1},{... | collective-permute-start | bytes 1544 | tf_op jit(solution)/shard_map/ppermute | solution.py:436
  14.6 10.5 %collective-permute-start.2 = (f32[2,64]{1,0:T(2,128)S(1)}, f32[2,64]{1,0:T(2,128)S(1)}, u32[]{:S(2)}, u32[]{:S(2)}) collective-permute-start(f32[2,64]{1,0:T(2,128)S(1)} %copy-done.4), channel_id=1, source_target_pairs={{12,0},{16,4},{20,8},{24,12},{28,16},{0,20},{4,24},{8,28},{13,1},{... | collective-permute-start | bytes 1544 | tf_op jit(solution)/shard_map/ppermute | solution.py:436
  16.9 9.7 %collective-permute-start.1 = (f32[2,64]{1,0:T(2,128)S(1)}, f32[2,64]{1,0:T(2,128)S(1)}, u32[]{:S(2)}, u32[]{:S(2)}) collective-permute-start(f32[2,64]{1,0:T(2,128)S(1)} %copy-done.4), channel_id=1, source_target_pairs={{8,0},{12,4},{16,8},{20,12},{24,16},{28,20},{0,24},{4,28},{9,1},{1... | collective-permute-start | bytes 1544 | tf_op jit(solution)/shard_map/ppermute | solution.py:436
  18.4 8.2 %collective-permute-start = (f32[2,64]{1,0:T(2,128)S(1)}, f32[2,64]{1,0:T(2,128)S(1)}, u32[]{:S(2)}, u32[]{:S(2)}) collective-permute-start(f32[2,64]{1,0:T(2,128)S(1)} %copy-done.4), channel_id=1, source_target_pairs={{4,0},{8,4},{12,8},{16,12},{20,16},{24,20},{28,24},{0,28},{5,1},{9... | collective-permute-start | bytes 1544 | tf_op jit(solution)/shard_map/ppermute | solution.py:436
  20.7 24.3 %collective-permute-start.7 = (f32[2,64,128]{2,1,0:T(8,128)S(1)}, f32[2,64,128]{2,1,0:T(8,128)S(1)}, u32[]{:S(2)}, u32[]{:S(2)}) collective-permute-start(f32[2,64,128]{2,1,0:T(8,128)S(1)} %get-tuple-element.32), channel_id=1, source_target_pairs={{3,0},{0,1},{1,2},{2,3},{7,4},{4,5},{5,6},{6,7},{11,8},{8,9},{9,10... | collective-permute-start | bytes 196616 | tf_op jit(solution)/shard_map/ppermute | solution.py:436
  22.7 22.3 %collective-permute-start.8 = (f32[2,64,128]{2,1,0:T(8,128)S(1)}, f32[2,64,128]{2,1,0:T(8,128)S(1)}, u32[]{:S(2)}, u32[]{:S(2)}) collective-permute-start(f32[2,64,128]{2,1,0:T(8,128)S(1)} %get-tuple-element.33), channel_id=1, source_target_pairs={{2,0},{3,1},{0,2},{1,3},{6,4},{7,5},{4,6},{5,7},{10,8},{11,9},{8,1... | collective-permute-start | bytes 196616 | tf_op jit(solution)/shard_map/ppermute | solution.py:436
  25.1 19.9 %collective-permute-start.9 = (f32[2,64,128]{2,1,0:T(8,128)S(1)}, f32[2,64,128]{2,1,0:T(8,128)S(1)}, u32[]{:S(2)}, u32[]{:S(2)}) collective-permute-start(f32[2,64,128]{2,1,0:T(8,128)S(1)} %get-tuple-element.34), channel_id=1, source_target_pairs={{1,0},{2,1},{3,2},{0,3},{5,4},{6,5},{7,6},{4,7},{9,8},{10,9},{11,1... | collective-permute-start | bytes 196616 | tf_op jit(solution)/shard_map/ppermute | solution.py:436
  48.8 5.5 %collective-permute-start.12 = (f32[2,8,128]{2,1,0:T(8,128)S(1)}, f32[2,8,128]{2,1,0:T(8,128)S(1)}, u32[]{:S(2)}, u32[]{:S(2)}) collective-permute-start(f32[2,8,128]{2,1,0:T(8,128)S(1)} %get-tuple-element.43.refs_1_), channel_id=1, source_target_pairs={{3,0},{0,1},{1,2},{2,3},{7,4},{4,5},{5,6},{6,7},{11,8},{8,9},{9,10... | collective-permute-start | bytes 24584 | tf_op jit(solution)/shard_map/ppermute | solution.py:436
  48.9 5.4 %collective-permute-start.11 = (f32[2,8,128]{2,1,0:T(8,128)S(1)}, f32[2,8,128]{2,1,0:T(8,128)S(1)}, u32[]{:S(2)}, u32[]{:S(2)}) collective-permute-start(f32[2,8,128]{2,1,0:T(8,128)S(1)} %get-tuple-element.43.refs_1_), channel_id=1, source_target_pairs={{2,0},{3,1},{0,2},{1,3},{6,4},{7,5},{4,6},{5,7},{10,8},{11,9},{8,1... | collective-permute-start | bytes 24584 | tf_op jit(solution)/shard_map/ppermute | solution.py:436
  51.3 3.7 %collective-permute-start.10 = (f32[2,8,128]{2,1,0:T(8,128)S(1)}, f32[2,8,128]{2,1,0:T(8,128)S(1)}, u32[]{:S(2)}, u32[]{:S(2)}) collective-permute-start(f32[2,8,128]{2,1,0:T(8,128)S(1)} %get-tuple-element.43.refs_1_), channel_id=1, source_target_pairs={{1,0},{2,1},{3,2},{0,3},{5,4},{6,5},{7,6},{4,7},{9,8},{10,9},{11,1... | collective-permute-start | bytes 24584 | tf_op jit(solution)/shard_map/ppermute | solution.py:436
  59.2 14.0 %collective-permute-start.13 = (f32[2,64,128]{2,1,0:T(8,128)S(1)}, f32[2,64,128]{2,1,0:T(8,128)S(1)}, u32[]{:S(2)}, u32[]{:S(2)}) collective-permute-start(f32[2,64,128]{2,1,0:T(8,128)S(1)} %get-tuple-element.50), channel_id=1, source_target_pairs={{3,0},{0,1},{1,2},{2,3},{7,4},{4,5},{5,6},{6,7},{11,8},{8,9},{9,10... | collective-permute-start | bytes 196616 | tf_op jit(solution)/shard_map/ppermute | solution.py:436
  61.3 12.0 %collective-permute-start.14 = (f32[2,64,128]{2,1,0:T(8,128)S(1)}, f32[2,64,128]{2,1,0:T(8,128)S(1)}, u32[]{:S(2)}, u32[]{:S(2)}) collective-permute-start(f32[2,64,128]{2,1,0:T(8,128)S(1)} %get-tuple-element.51), channel_id=1, source_target_pairs={{2,0},{3,1},{0,2},{1,3},{6,4},{7,5},{4,6},{5,7},{10,8},{11,9},{8,1... | collective-permute-start | bytes 196616 | tf_op jit(solution)/shard_map/ppermute | solution.py:436
  63.1 10.2 %collective-permute-start.15 = (f32[2,64,128]{2,1,0:T(8,128)S(1)}, f32[2,64,128]{2,1,0:T(8,128)S(1)}, u32[]{:S(2)}, u32[]{:S(2)}) collective-permute-start(f32[2,64,128]{2,1,0:T(8,128)S(1)} %get-tuple-element.52), channel_id=1, source_target_pairs={{1,0},{2,1},{3,2},{0,3},{5,4},{6,5},{7,6},{4,7},{9,8},{10,9},{11,1... | collective-permute-start | bytes 196616 | tf_op jit(solution)/shard_map/ppermute | solution.py:436
  74.1 12.6 %all-to-all-start.2 = ((f32[32,8,128]{2,1,0:T(8,128)}), f32[32,8,128]{2,1,0:T(8,128)S(1)}, u32[]{:S(2)}, u32[]{:S(2)}) async-start(f32[32,8,128]{2,1,0:T(8,128)} %get-tuple-element.55), calls=%async_computation.2 | async-start | bytes 262144 | tf_op jit(solution)/shard_map/all_to_all | solution.py:432
  86.7 23.2 %all-to-all-start.1 = ((f32[4,6,64,128]{3,2,1,0:T(8,128)}), f32[4,6,64,128]{3,2,1,0:T(8,128)S(1)}, u32[]{:S(2)}, u32[]{:S(2)}) async-start(f32[4,6,64,128]{3,2,1,0:T(8,128)} %get-tuple-element.48), calls=%async_computation.1 | async-start | bytes 1572864 | tf_op jit(solution)/shard_map/all_to_all | solution.py:432
  (1 other events, 0.7 us)

commit v4 on v3

--- a/solution.py
+++ b/solution.py
@@ -165,7 +165,7 @@
 
 
 def unpack_pieces_kernel(parts, share, count, first, here_ref, *refs):
-    out_ref, sems = refs[parts:]
+    out_ref, sems = refs[-2:]
     pairs = []
     for step in range(parts):
         owner = lax.rem(here_ref[0] + parts - step, parts)
@@ -351,19 +351,22 @@
     out_ref[1] = density
 
 
-def second_kernel(parts, count, kinds, points, opening, copies, scalar_ref, *refs):
+def second_kernel(parts, count, kinds, points, opening, permuted, copies, scalar_ref, *refs):
+    if permuted:
+        here_ref, *refs = refs
     if opening:
-        here_ref, seen, refs = refs[0], refs[1 : 1 + parts], refs[1 + parts :]
+        seen, refs = refs[:parts], refs[parts:]
+        first_sums_ref = seen[0]
     else:
         vector_ref, first_sums_ref, sums_ref, *refs = refs
     psi_ref, potential_ref, *tables = refs[:8]
     refs = refs[8:]
-    if copies and opening:
-        first_sums_ref = seen[0]
-    if opening and not copies:
-        pieces, vector_ref, refs = refs[:parts], refs[parts], refs[parts + 1 :]
+    if permuted:
+        pieces, refs = refs[:parts], refs[parts:]
     else:
         piece_ref, *refs = refs
+    if opening and not copies:
+        vector_ref, *refs = refs
     out_ref, field_ref, total_ref = refs[:3]
     scratch = refs[3:]
     width = total_ref.shape[1]
@@ -383,10 +386,10 @@
         count, vector_value, field_ref, total_ref, potential_ref, tables, scratch, width, kinds
     )
     for step in range(parts):
-        if copies:
+        if permuted:
+            piece, start = pieces[step], lax.rem(here_ref[0] + step, parts) * planes
+        else:
             piece, start = piece_ref.at[step], step * planes
-        else:
-            piece, start = pieces[step], lax.rem(here_ref[0] + step, parts) * planes
         for index in range(planes):
             rows = pl.ds(index, ROWS, stride=planes)
             for orbital in range(count):
@@ -441,7 +444,7 @@
     planes, points = local_potential.shape
     width = planes * parts
     share = norb // parts
-    last_count = 1 if share > 1 else 0
+    last_count = share // 2
     main_count = share - last_count
     owned = fields.shape[1]
     atoms = atom_sites.shape[0]
@@ -561,61 +564,53 @@
     pieces_shape = float_array(parts, 2 * main_count, held, LANES)
     messages_shape = float_array(everyone, ROWS, LANES)
     whole_shape = float_array(2, norb, held, LANES)
+    main_pieces, *rest = micro_call(
+        functools.partial(
+            second_kernel, parts, main_count, kinds, total_points, True, False, 0 if last_count else everyone
+        ),
+        main_count,
+        [scalars, *seen, main_psi, potential, *tables],
+        1,
+        [pieces_shape] + ([float_array(1), sums_shape] if last_count else [messages_shape]),
+        (1,) if last_count else (),
+        2,
+    )
+    returned = exchanged(main_pieces, "grid")
+    messages = rest[-1]
     if last_count:
-        *pieces, vector_value, second_sums = micro_call(
-            functools.partial(second_kernel, parts, last_count, kinds, total_points, True, 0),
+        vector_value, second_sums = rest
+        *pieces, messages = micro_call(
+            functools.partial(second_kernel, parts, last_count, kinds, total_points, False, True, everyone),
             last_count,
-            [scalars, here, *seen, last_psi, potential, *tables],
-            2,
-            [float_array(2 * last_count, held, LANES)] * parts + [float_array(1), sums_shape],
-            (parts,),
+            [scalars, here, vector_value, sums, second_sums, last_psi, potential, *tables],
+            3,
+            [float_array(2 * last_count, held, LANES)] * parts + [messages_shape],
+            (),
             2,
         )
         pieces = [pieces[0]] + [shifted(pieces[step], "grid", parts, -step) for step in range(1, parts)]
-        main_pieces, messages = micro_call(
-            functools.partial(second_kernel, parts, main_count, kinds, total_points, False, everyone),
-            main_count,
-            [scalars, vector_value, sums, second_sums, main_psi, potential, *tables],
-            2,
-            [pieces_shape, messages_shape],
-            (),
-            2,
-        )
-    else:
-        main_pieces, messages = micro_call(
-            functools.partial(second_kernel, parts, main_count, kinds, total_points, True, everyone),
-            main_count,
-            [scalars, here, *seen, main_psi, potential, *tables],
-            2,
-            [pieces_shape, messages_shape],
-            (),
-            2,
-        )
-    returned = exchanged(main_pieces, "grid")
-    result = []
+    result = pl.pallas_call(
+        functools.partial(unpack_kernel, parts, share, main_count, 0),
+        out_shape=whole_shape,
+        in_specs=[anywhere()],
+        out_specs=hbm(),
+        scratch_shapes=[pltpu.SemaphoreType.DMA((parts * 2,))],
+        compiler_params=params,
+    )(returned)
+    result, messages = lax.optimization_barrier((result, messages))
+    messages = exchanged(messages, ("macro", "grid")).reshape(blocks, parts, ROWS, LANES)
     if last_count:
         result = pl.pallas_call(
             functools.partial(unpack_pieces_kernel, parts, share, last_count, main_count),
             out_shape=whole_shape,
-            in_specs=[smem()] + [anywhere()] * parts,
+            in_specs=[smem()] + [anywhere()] * parts + [hbm()],
             out_specs=hbm(),
             scratch_shapes=[pltpu.SemaphoreType.DMA((parts * 2,))],
+            input_output_aliases={1 + parts: 0},
             compiler_params=params,
-        )(here, *pieces)
-        result, messages = lax.optimization_barrier((result, messages))
-        result = [result]
-    result = pl.pallas_call(
-        functools.partial(unpack_kernel, parts, share, main_count, 0),
-        out_shape=whole_shape,
-        in_specs=[anywhere()] + [hbm()] * len(result),
-        out_specs=hbm(),
-        scratch_shapes=[pltpu.SemaphoreType.DMA((parts * 2,))],
-        input_output_aliases={1: 0} if result else {},
-        compiler_params=params,
-    )(returned, *result)
+        )(here, *pieces, result)
     orbitals_out = planes_of(result).reshape(2, norb, planes, points)
 
-    messages = exchanged(messages, ("macro", "grid")).reshape(blocks, parts, ROWS, LANES)
     currents = jnp.sum(messages[:, :, :2], axis=(1, 3))
     hosts = messages[:, 0, 2, 0].astype(jnp.int32)
     length = blocks * owned

time: 111 us -> 96.1 us (0.87)
  waiting for transfers between devices: 38.5 us -> 22.5 us
  starting transfers between devices: 36.7 us -> 38.4 us
    all_to_all x3, waiting for transfers between devices: 36.2 us -> 10.8 us  [exchanged(): return lax.all_to_all(value, axes, split_axis=0, concat_axis=0, tiled=True)]
    ppermute x16, waiting for transfers between devices: 2.24 us -> 11.8 us  [shifted(): lax.ppermute(value, axis_name, [((index + shift) % count, index) for inde...]
    ppermute x16, starting transfers between devices: 22.5 us -> 23.7 us  [shifted(): lax.ppermute(value, axis_name, [((index + shift) % count, index) for inde...]
  transfers between devices with their start and end apart: 19 -> 19, of which waited for: 5 -> 6; matrix products, arithmetic and copies ran while one was open for 1% -> 0% of each run, Pallas kernels for 18% -> 17%
where the time goes in v4:
time: 96.1 us; the launch traced here: 95.7 us
  starting transfers between devices  38.4 us (40%)
  Pallas kernels  29.8 us (31%)
  waiting for transfers between devices  22.5 us (23%)
  local copies, waits for them, and re-layouts  2.45 us (3%)
  between operations  1.49 us (2%)
  other arithmetic  1.07 us (1%)
    pallas_call x4, Pallas kernels, micro_call(): pl.pallas_call(kernel, out_shape=outputs, in_specs=[smem() if number < sc...  24.7 us
    ppermute x16, starting transfers between devices, shifted(): lax.ppermute(value, axis_name, [((index + shift) % count, index) for inde...  23.7 us
    all_to_all x3, starting transfers between devices, exchanged(): return lax.all_to_all(value, axes, split_axis=0, concat_axis=0, tiled=True)  14.7 us
    ppermute x16, waiting for transfers between devices, shifted(): lax.ppermute(value, axis_name, [((index + shift) % count, index) for inde...  11.8 us
    all_to_all x3, waiting for transfers between devices, exchanged(): return lax.all_to_all(value, axes, split_axis=0, concat_axis=0, tiled=True)  10.8 us
    unnamed x14, local copies, waits for them, and re-layouts  2.17 us
  transfers between devices with their start and end apart: 19, of which 6 were waited for; matrix products, arithmetic and copies ran while one was open for 0% of the time, Pallas kernels for 17%

profile of v4, /device:TPU:0, one launch (start us, length us, event | category | flops | bytes accessed | tf_op | source)
XLA Modules:
  0.0 95.7 jit_solution(13205155178737734002)
XLA Ops:
  3.6 6.5 %all-to-all-start = ((f32[4,5,64,128]{3,2,1,0:T(8,128)}), f32[4,5,64,128]{3,2,1,0:T(8,128)S(1)}, u32[]{:S(2)}, u32[]{:S(2)}) async-start(f32[4,5,64,128]{3,2,1,0:T(8,128)} %shard_map.77), calls=%async_computation | async-start | bytes 1310720 | tf_op jit(solution)/shard_map/all_to_all | solution.py:435
  10.1 1.5 %collective-permute-start.5 = (f32[2,64]{1,0:T(2,128)S(1)}, f32[2,64]{1,0:T(2,128)S(1)}, u32[]{:S(2)}, u32[]{:S(2)}) collective-permute-start(f32[2,64]{1,0:T(2,128)S(1)} %copy-done.4), channel_id=1, source_target_pairs={{24,0},{28,4},{0,8},{4,12},{8,16},{12,20},{16,24},{20,28},{25,1},{... | collective-permute-start | bytes 1544 | tf_op jit(solution)/shard_map/ppermute | solution.py:439
  11.6 2.4 %collective-permute-start.4 = (f32[2,64]{1,0:T(2,128)S(1)}, f32[2,64]{1,0:T(2,128)S(1)}, u32[]{:S(2)}, u32[]{:S(2)}) collective-permute-start(f32[2,64]{1,0:T(2,128)S(1)} %copy-done.4), channel_id=1, source_target_pairs={{20,0},{24,4},{28,8},{0,12},{4,16},{8,20},{12,24},{16,28},{21,1},{... | collective-permute-start | bytes 1544 | tf_op jit(solution)/shard_map/ppermute | solution.py:439
  17.1 1.5 %collective-permute-start.1 = (f32[2,64]{1,0:T(2,128)S(1)}, f32[2,64]{1,0:T(2,128)S(1)}, u32[]{:S(2)}, u32[]{:S(2)}) collective-permute-start(f32[2,64]{1,0:T(2,128)S(1)} %copy-done.4), channel_id=1, source_target_pairs={{8,0},{12,4},{16,8},{20,12},{24,16},{28,20},{0,24},{4,28},{9,1},{1... | collective-permute-start | bytes 1544 | tf_op jit(solution)/shard_map/ppermute | solution.py:439
  18.6 2.3 %collective-permute-start = (f32[2,64]{1,0:T(2,128)S(1)}, f32[2,64]{1,0:T(2,128)S(1)}, u32[]{:S(2)}, u32[]{:S(2)}) collective-permute-start(f32[2,64]{1,0:T(2,128)S(1)} %copy-done.4), channel_id=1, source_target_pairs={{4,0},{8,4},{12,8},{16,12},{20,16},{24,20},{28,24},{0,28},{5,1},{9... | collective-permute-start | bytes 1544 | tf_op jit(solution)/shard_map/ppermute | solution.py:439
  20.9 2.0 %collective-permute-start.7 = (f32[4,64,128]{2,1,0:T(8,128)S(1)}, f32[4,64,128]{2,1,0:T(8,128)S(1)}, u32[]{:S(2)}, u32[]{:S(2)}) collective-permute-start(f32[4,64,128]{2,1,0:T(8,128)S(1)} %get-tuple-element.32), channel_id=1, source_target_pairs={{3,0},{0,1},{1,2},{2,3},{7,4},{4,5},{5,6},{6,7},{11,8},{8,9},{9,10... | collective-permute-start | bytes 393224 | tf_op jit(solution)/shard_map/ppermute | solution.py:439
  23.0 2.4 %collective-permute-start.8 = (f32[4,64,128]{2,1,0:T(8,128)S(1)}, f32[4,64,128]{2,1,0:T(8,128)S(1)}, u32[]{:S(2)}, u32[]{:S(2)}) collective-permute-start(f32[4,64,128]{2,1,0:T(8,128)S(1)} %get-tuple-element.33), channel_id=1, source_target_pairs={{2,0},{3,1},{0,2},{1,3},{6,4},{7,5},{4,6},{5,7},{10,8},{11,9},{8,1... | collective-permute-start | bytes 393224 | tf_op jit(solution)/shard_map/ppermute | solution.py:439
  25.3 1.5 %collective-permute-start.9 = (f32[4,64,128]{2,1,0:T(8,128)S(1)}, f32[4,64,128]{2,1,0:T(8,128)S(1)}, u32[]{:S(2)}, u32[]{:S(2)}) collective-permute-start(f32[4,64,128]{2,1,0:T(8,128)S(1)} %get-tuple-element.34), channel_id=1, source_target_pairs={{1,0},{2,1},{3,2},{0,3},{5,4},{6,5},{7,6},{4,7},{9,8},{10,9},{11,1... | collective-permute-start | bytes 393224 | tf_op jit(solution)/shard_map/ppermute | solution.py:439
  27.5 6.5 %all-to-all-done.refs_0_ = f32[4,5,64,128]{3,2,1,0:T(8,128)S(1)} async-done(((f32[4,5,64,128]{3,2,1,0:T(8,128)}), f32[4,5,64,128]{3,2,1,0:T(8,128)S(1)}, u32[]{:S(2)}, u32[]{:S(2)}) %all-to-all-start) | async-done | bytes 655392 | tf_op jit(solution)/shard_map/all_to_all | solution.py:435
  34.1 5.7 %shard_map.81 = (f32[4,32,8,128]{3,2,1,0:T(8,128)S(1)}, f32[2,8,128]{2,1,0:T(8,128)S(1)}, f32[32,8,128]{2,1,0:T(8,128)S(1)}) custom-call(f32[3]{0:T(128)S(1)} %shard_map.78.scalar_ref, f32[4,5,64,128]{3,2,1,0:T(8,128)S(1)} %all-to-all-done.refs_0_, bf16[256,256]{1,0:T(8,128)(2,1)S(1)} %get-tuple-element.35.refs_1_.refs_6_, ...), custom_call_target="tpu_custom_call" | custom-call | flops 1610612736 | bytes 4194304 | tf_op jit(solution)/shard_map/pallas_call | solution.py:517
  39.8 5.7 %shard_map.82 = (f32[4,32,8,128]{3,2,1,0:T(8,128)S(1)}, f32[2,8,128]{2,1,0:T(8,128)S(1)}) custom-call(f32[3]{0:T(128)S(1)} %shard_map.78.scalar_ref, s32[1]{0:T(128)} %bitcast.here_ref.refs_0_, f32[4,64,128]{2,1,0:T(8,128)S(1)} %get-tuple-element.31.refs_1_, f32[4,64,128]{2,1,0:T(8,128)S(1)} %collective-permute-done.7.refs_2_, ...), custom_call_target="tpu_custom_call" | custom-call | flops 1610612736 | bytes 4194304 | tf_op jit(solution)/shard_map/pallas_call | solution.py:517
  45.5 2.4 %collective-permute-start.11 = (f32[2,8,128]{2,1,0:T(8,128)S(1)}, f32[2,8,128]{2,1,0:T(8,128)S(1)}, u32[]{:S(2)}, u32[]{:S(2)}) collective-permute-start(f32[2,8,128]{2,1,0:T(8,128)S(1)} %get-tuple-element.43.refs_0_.refs_2_), channel_id=1, source_target_pairs={{2,0},{3,1},{0,2},{1,3},{6,4},{7,5},{4,6},{5,7},{10,8},{11,9},{8,1... | collective-permute-start | bytes 24584 | tf_op jit(solution)/shard_map/ppermute | solution.py:439
  47.9 1.4 %collective-permute-start.10 = (f32[2,8,128]{2,1,0:T(8,128)S(1)}, f32[2,8,128]{2,1,0:T(8,128)S(1)}, u32[]{:S(2)}, u32[]{:S(2)}) collective-permute-start(f32[2,8,128]{2,1,0:T(8,128)S(1)} %get-tuple-element.43.refs_0_.refs_2_), channel_id=1, source_target_pairs={{1,0},{2,1},{3,2},{0,3},{5,4},{6,5},{7,6},{4,7},{9,8},{10,9},{11,1... | collective-permute-start | bytes 24584 | tf_op jit(solution)/shard_map/ppermute | solution.py:439
  49.3 1.6 %collective-permute-done.12.refs_3_ = f32[2,8,128]{2,1,0:T(8,128)S(1)} collective-permute-done((f32[2,8,128]{2,1,0:T(8,128)S(1)}, f32[2,8,128]{2,1,0:T(8,128)S(1)}, u32[]{:S(2)}, u32[]{:S(2)}) %collective-permute-start.12) | collective-permute-done | bytes 8224 | tf_op jit(solution)/shard_map/ppermute | solution.py:439
  51.6 6.4 %shard_map.83 = (f32[4,4,64,128]{3,2,1,0:T(8,128)}, f32[1]{0:T(128)}, f32[2,8,128]{2,1,0:T(8,128)S(1)}) custom-call(f32[3]{0:T(128)S(1)} %shard_map.78.scalar_ref, f32[2,8,128]{2,1,0:T(8,128)S(1)} %get-tuple-element.43.refs_0_.refs_2_, f32[2,8,128]{2,1,0:T(8,128)S(1)} %collective-permute-done.10.refs_1_, f32[2,8,128]{2,1,0:T(8,128)S(1)} %collective-permute-done.11.refs_2_, ...), custom_call_target="tpu_custom_call" | custom-call | flops 1610612736 | bytes 4194304 | tf_op jit(solution)/shard_map/pallas_call | solution.py:517
  58.0 4.5 %all-to-all-start.1 = ((f32[4,4,64,128]{3,2,1,0:T(8,128)}), f32[4,4,64,128]{3,2,1,0:T(8,128)S(1)}, u32[]{:S(2)}, u32[]{:S(2)}) async-start(f32[4,4,64,128]{3,2,1,0:T(8,128)} %get-tuple-element.52), calls=%async_computation.1 | async-start | bytes 1048576 | tf_op jit(solution)/shard_map/all_to_all | solution.py:435
  62.5 7.0 %shard_map.84 = (f32[4,64,128]{2,1,0:T(8,128)S(1)}, f32[4,64,128]{2,1,0:T(8,128)S(1)}, f32[4,64,128]{2,1,0:T(8,128)S(1)}, f32[4,64,128]{2,1,0:T(8,128)S(1)}, f32[32,8,128]{2,1,0:T(8,128)}) custom-call(f32[3]{0:T(128)S(1)} %shard_map.78.scalar_ref, s32[1]{0:T(128)} %bitcast.here_ref.refs_0_, f32[1]{0:T(128)} %get-tuple-element.45.refs_1_, ...), custom_call_target="tpu_custom_call" | custom-call | flops 1610612736 | bytes 4194304 | tf_op jit(solution)/shard_map/pallas_call | solution.py:517
  69.4 4.2 %all-to-all-done.1.piece_ref = f32[4,4,64,128]{3,2,1,0:T(8,128)S(1)} async-done(((f32[4,4,64,128]{3,2,1,0:T(8,128)}), f32[4,4,64,128]{3,2,1,0:T(8,128)S(1)}, u32[]{:S(2)}, u32[]{:S(2)}) %all-to-all-start.1) | async-done | bytes 524320 | tf_op jit(solution)/shard_map/all_to_all | solution.py:435
  74.5 3.7 %all-to-all-start.2 = ((f32[32,8,128]{2,1,0:T(8,128)}), f32[32,8,128]{2,1,0:T(8,128)S(1)}, u32[]{:S(2)}, u32[]{:S(2)}) async-start(f32[32,8,128]{2,1,0:T(8,128)} %get-tuple-element.55), calls=%async_computation.2 | async-start | bytes 262144 | tf_op jit(solution)/shard_map/all_to_all | solution.py:435
  78.2 1.8 %collective-permute-start.13 = (f32[4,64,128]{2,1,0:T(8,128)S(1)}, f32[4,64,128]{2,1,0:T(8,128)S(1)}, u32[]{:S(2)}, u32[]{:S(2)}) collective-permute-start(f32[4,64,128]{2,1,0:T(8,128)S(1)} %get-tuple-element.49), channel_id=1, source_target_pairs={{3,0},{0,1},{1,2},{2,3},{7,4},{4,5},{5,6},{6,7},{11,8},{8,9},{9,10... | collective-permute-start | bytes 393224 | tf_op jit(solution)/shard_map/ppermute | solution.py:439
  80.1 2.4 %collective-permute-start.14 = (f32[4,64,128]{2,1,0:T(8,128)S(1)}, f32[4,64,128]{2,1,0:T(8,128)S(1)}, u32[]{:S(2)}, u32[]{:S(2)}) collective-permute-start(f32[4,64,128]{2,1,0:T(8,128)S(1)} %get-tuple-element.50), channel_id=1, source_target_pairs={{2,0},{3,1},{0,2},{1,3},{6,4},{7,5},{4,6},{5,7},{10,8},{11,9},{8,1... | collective-permute-start | bytes 393224 | tf_op jit(solution)/shard_map/ppermute | solution.py:439
  82.5 1.4 %collective-permute-start.15 = (f32[4,64,128]{2,1,0:T(8,128)S(1)}, f32[4,64,128]{2,1,0:T(8,128)S(1)}, u32[]{:S(2)}, u32[]{:S(2)}) collective-permute-start(f32[4,64,128]{2,1,0:T(8,128)S(1)} %get-tuple-element.51), channel_id=1, source_target_pairs={{1,0},{2,1},{3,2},{0,3},{5,4},{6,5},{7,6},{4,7},{9,8},{10,9},{11,1... | collective-permute-start | bytes 393224 | tf_op jit(solution)/shard_map/ppermute | solution.py:439
  84.1 4.3 %collective-permute-done.13.refs_1_ = f32[4,64,128]{2,1,0:T(8,128)S(1)} collective-permute-done((f32[4,64,128]{2,1,0:T(8,128)S(1)}, f32[4,64,128]{2,1,0:T(8,128)S(1)}, u32[]{:S(2)}, u32[]{:S(2)}) %collective-permute-start.13) | collective-permute-done | bytes 131104 | tf_op jit(solution)/shard_map/ppermute | solution.py:439
  88.3 5.2 %collective-permute-done.14.refs_2_ = f32[4,64,128]{2,1,0:T(8,128)S(1)} collective-permute-done((f32[4,64,128]{2,1,0:T(8,128)S(1)}, f32[4,64,128]{2,1,0:T(8,128)S(1)}, u32[]{:S(2)}, u32[]{:S(2)}) %collective-permute-start.14) | collective-permute-done | bytes 131104 | tf_op jit(solution)/shard_map/ppermute | solution.py:439
  (50 shorter events, 9.9 us)
Async XLA Ops:
  0.6 1.2 %copy-start = (f32[1,2,16,8,1024]{4,3,2,1,0:T(8,128)S(1)}, f32[1,2,16,8,1024]{4,3,2,1,0:T(8,128)}, u32[]{:S(2)}) copy-start(f32[1,2,16,8,1024]{4,3,2,1,0:T(8,128)} %param.6) | copy-start | bytes 3145732
  1.9 0.8 copy-start.3
  3.5 6.5 %copy-start.4 = (f32[2,64]{1,0:T(2,128)S(1)}, f32[2,64]{1,0:T(2,128)}, u32[]{:S(2)}) copy-start(f32[2,64]{1,0:T(2,128)} %refs_0_) | copy-start | bytes 1540
  3.6 11.8 %copy-start.2 = (bf16[256,384]{1,0:T(8,128)(2,1)S(1)}, bf16[256,384]{1,0:T(8,128)(2,1)}, u32[]{:S(2)}) copy-start(bf16[256,384]{1,0:T(8,128)(2,1)} %constant.29.clone.stencil_ref) | copy-start | bytes 589828
  3.6 12.8 %copy-start.1 = (f32[1,2,16,8,1024]{4,3,2,1,0:T(8,128)S(1)}, f32[1,2,16,8,1024]{4,3,2,1,0:T(8,128)}, u32[]{:S(2)}) copy-start(f32[1,2,16,8,1024]{4,3,2,1,0:T(8,128)} %param.6) | copy-start | bytes 3145732
  3.6 30.5 %all-to-all-start = ((f32[4,5,64,128]{3,2,1,0:T(8,128)}), f32[4,5,64,128]{3,2,1,0:T(8,128)S(1)}, u32[]{:S(2)}, u32[]{:S(2)}) async-start(f32[4,5,64,128]{3,2,1,0:T(8,128)} %shard_map.77), calls=%async_computation | async-start | bytes 1310720 | tf_op jit(solution)/shard_map/all_to_all | solution.py:435
  10.0 7.1 %collective-permute-start.6 = (f32[2,64]{1,0:T(2,128)S(1)}, f32[2,64]{1,0:T(2,128)S(1)}, u32[]{:S(2)}, u32[]{:S(2)}) collective-permute-start(f32[2,64]{1,0:T(2,128)S(1)} %copy-done.4), channel_id=1, source_target_pairs={{28,0},{0,4},{4,8},{8,12},{12,16},{16,20},{20,24},{24,28},{29,1},{... | collective-permute-start | bytes 1544 | tf_op jit(solution)/shard_map/ppermute | solution.py:439
  10.1 8.6 %collective-permute-start.5 = (f32[2,64]{1,0:T(2,128)S(1)}, f32[2,64]{1,0:T(2,128)S(1)}, u32[]{:S(2)}, u32[]{:S(2)}) collective-permute-start(f32[2,64]{1,0:T(2,128)S(1)} %copy-done.4), channel_id=1, source_target_pairs={{24,0},{28,4},{0,8},{4,12},{8,16},{12,20},{16,24},{20,28},{25,1},{... | collective-permute-start | bytes 1544 | tf_op jit(solution)/shard_map/ppermute | solution.py:439
  11.6 9.3 %collective-permute-start.4 = (f32[2,64]{1,0:T(2,128)S(1)}, f32[2,64]{1,0:T(2,128)S(1)}, u32[]{:S(2)}, u32[]{:S(2)}) collective-permute-start(f32[2,64]{1,0:T(2,128)S(1)} %copy-done.4), channel_id=1, source_target_pairs={{20,0},{24,4},{28,8},{0,12},{4,16},{8,20},{12,24},{16,28},{21,1},{... | collective-permute-start | bytes 1544 | tf_op jit(solution)/shard_map/ppermute | solution.py:439
  14.0 9.0 %collective-permute-start.3 = (f32[2,64]{1,0:T(2,128)S(1)}, f32[2,64]{1,0:T(2,128)S(1)}, u32[]{:S(2)}, u32[]{:S(2)}) collective-permute-start(f32[2,64]{1,0:T(2,128)S(1)} %copy-done.4), channel_id=1, source_target_pairs={{16,0},{20,4},{24,8},{28,12},{0,16},{4,20},{8,24},{12,28},{17,1},{... | collective-permute-start | bytes 1544 | tf_op jit(solution)/shard_map/ppermute | solution.py:439
  14.5 10.9 %collective-permute-start.2 = (f32[2,64]{1,0:T(2,128)S(1)}, f32[2,64]{1,0:T(2,128)S(1)}, u32[]{:S(2)}, u32[]{:S(2)}) collective-permute-start(f32[2,64]{1,0:T(2,128)S(1)} %copy-done.4), channel_id=1, source_target_pairs={{12,0},{16,4},{20,8},{24,12},{28,16},{0,20},{4,24},{8,28},{13,1},{... | collective-permute-start | bytes 1544 | tf_op jit(solution)/shard_map/ppermute | solution.py:439
  17.1 9.7 %collective-permute-start.1 = (f32[2,64]{1,0:T(2,128)S(1)}, f32[2,64]{1,0:T(2,128)S(1)}, u32[]{:S(2)}, u32[]{:S(2)}) collective-permute-start(f32[2,64]{1,0:T(2,128)S(1)} %copy-done.4), channel_id=1, source_target_pairs={{8,0},{12,4},{16,8},{20,12},{24,16},{28,20},{0,24},{4,28},{9,1},{1... | collective-permute-start | bytes 1544 | tf_op jit(solution)/shard_map/ppermute | solution.py:439
  18.6 8.2 %collective-permute-start = (f32[2,64]{1,0:T(2,128)S(1)}, f32[2,64]{1,0:T(2,128)S(1)}, u32[]{:S(2)}, u32[]{:S(2)}) collective-permute-start(f32[2,64]{1,0:T(2,128)S(1)} %copy-done.4), channel_id=1, source_target_pairs={{4,0},{8,4},{12,8},{16,12},{20,16},{24,20},{28,24},{0,28},{5,1},{9... | collective-permute-start | bytes 1544 | tf_op jit(solution)/shard_map/ppermute | solution.py:439
  20.9 18.8 %collective-permute-start.7 = (f32[4,64,128]{2,1,0:T(8,128)S(1)}, f32[4,64,128]{2,1,0:T(8,128)S(1)}, u32[]{:S(2)}, u32[]{:S(2)}) collective-permute-start(f32[4,64,128]{2,1,0:T(8,128)S(1)} %get-tuple-element.32), channel_id=1, source_target_pairs={{3,0},{0,1},{1,2},{2,3},{7,4},{4,5},{5,6},{6,7},{11,8},{8,9},{9,10... | collective-permute-start | bytes 393224 | tf_op jit(solution)/shard_map/ppermute | solution.py:439
  23.0 16.8 %collective-permute-start.8 = (f32[4,64,128]{2,1,0:T(8,128)S(1)}, f32[4,64,128]{2,1,0:T(8,128)S(1)}, u32[]{:S(2)}, u32[]{:S(2)}) collective-permute-start(f32[4,64,128]{2,1,0:T(8,128)S(1)} %get-tuple-element.33), channel_id=1, source_target_pairs={{2,0},{3,1},{0,2},{1,3},{6,4},{7,5},{4,6},{5,7},{10,8},{11,9},{8,1... | collective-permute-start | bytes 393224 | tf_op jit(solution)/shard_map/ppermute | solution.py:439
  25.3 14.5 %collective-permute-start.9 = (f32[4,64,128]{2,1,0:T(8,128)S(1)}, f32[4,64,128]{2,1,0:T(8,128)S(1)}, u32[]{:S(2)}, u32[]{:S(2)}) collective-permute-start(f32[4,64,128]{2,1,0:T(8,128)S(1)} %get-tuple-element.34), channel_id=1, source_target_pairs={{1,0},{2,1},{3,2},{0,3},{5,4},{6,5},{7,6},{4,7},{9,8},{10,9},{11,1... | collective-permute-start | bytes 393224 | tf_op jit(solution)/shard_map/ppermute | solution.py:439
  45.5 5.5 %collective-permute-start.12 = (f32[2,8,128]{2,1,0:T(8,128)S(1)}, f32[2,8,128]{2,1,0:T(8,128)S(1)}, u32[]{:S(2)}, u32[]{:S(2)}) collective-permute-start(f32[2,8,128]{2,1,0:T(8,128)S(1)} %get-tuple-element.43.refs_0_.refs_2_), channel_id=1, source_target_pairs={{3,0},{0,1},{1,2},{2,3},{7,4},{4,5},{5,6},{6,7},{11,8},{8,9},{9,10... | collective-permute-start | bytes 24584 | tf_op jit(solution)/shard_map/ppermute | solution.py:439
  45.5 5.4 %collective-permute-start.11 = (f32[2,8,128]{2,1,0:T(8,128)S(1)}, f32[2,8,128]{2,1,0:T(8,128)S(1)}, u32[]{:S(2)}, u32[]{:S(2)}) collective-permute-start(f32[2,8,128]{2,1,0:T(8,128)S(1)} %get-tuple-element.43.refs_0_.refs_2_), channel_id=1, source_target_pairs={{2,0},{3,1},{0,2},{1,3},{6,4},{7,5},{4,6},{5,7},{10,8},{11,9},{8,1... | collective-permute-start | bytes 24584 | tf_op jit(solution)/shard_map/ppermute | solution.py:439
  47.9 3.7 %collective-permute-start.10 = (f32[2,8,128]{2,1,0:T(8,128)S(1)}, f32[2,8,128]{2,1,0:T(8,128)S(1)}, u32[]{:S(2)}, u32[]{:S(2)}) collective-permute-start(f32[2,8,128]{2,1,0:T(8,128)S(1)} %get-tuple-element.43.refs_0_.refs_2_), channel_id=1, source_target_pairs={{1,0},{2,1},{3,2},{0,3},{5,4},{6,5},{7,6},{4,7},{9,8},{10,9},{11,1... | collective-permute-start | bytes 24584 | tf_op jit(solution)/shard_map/ppermute | solution.py:439
  58.0 15.7 %all-to-all-start.1 = ((f32[4,4,64,128]{3,2,1,0:T(8,128)}), f32[4,4,64,128]{3,2,1,0:T(8,128)S(1)}, u32[]{:S(2)}, u32[]{:S(2)}) async-start(f32[4,4,64,128]{3,2,1,0:T(8,128)} %get-tuple-element.52), calls=%async_computation.1 | async-start | bytes 1048576 | tf_op jit(solution)/shard_map/all_to_all | solution.py:435
  74.5 19.9 %all-to-all-start.2 = ((f32[32,8,128]{2,1,0:T(8,128)}), f32[32,8,128]{2,1,0:T(8,128)S(1)}, u32[]{:S(2)}, u32[]{:S(2)}) async-start(f32[32,8,128]{2,1,0:T(8,128)} %get-tuple-element.55), calls=%async_computation.2 | async-start | bytes 262144 | tf_op jit(solution)/shard_map/all_to_all | solution.py:435
  78.2 10.1 %collective-permute-start.13 = (f32[4,64,128]{2,1,0:T(8,128)S(1)}, f32[4,64,128]{2,1,0:T(8,128)S(1)}, u32[]{:S(2)}, u32[]{:S(2)}) collective-permute-start(f32[4,64,128]{2,1,0:T(8,128)S(1)} %get-tuple-element.49), channel_id=1, source_target_pairs={{3,0},{0,1},{1,2},{2,3},{7,4},{4,5},{5,6},{6,7},{11,8},{8,9},{9,10... | collective-permute-start | bytes 393224 | tf_op jit(solution)/shard_map/ppermute | solution.py:439
  80.1 13.5 %collective-permute-start.14 = (f32[4,64,128]{2,1,0:T(8,128)S(1)}, f32[4,64,128]{2,1,0:T(8,128)S(1)}, u32[]{:S(2)}, u32[]{:S(2)}) collective-permute-start(f32[4,64,128]{2,1,0:T(8,128)S(1)} %get-tuple-element.50), channel_id=1, source_target_pairs={{2,0},{3,1},{0,2},{1,3},{6,4},{7,5},{4,6},{5,7},{10,8},{11,9},{8,1... | collective-permute-start | bytes 393224 | tf_op jit(solution)/shard_map/ppermute | solution.py:439
  82.5 11.1 %collective-permute-start.15 = (f32[4,64,128]{2,1,0:T(8,128)S(1)}, f32[4,64,128]{2,1,0:T(8,128)S(1)}, u32[]{:S(2)}, u32[]{:S(2)}) collective-permute-start(f32[4,64,128]{2,1,0:T(8,128)S(1)} %get-tuple-element.51), channel_id=1, source_target_pairs={{1,0},{2,1},{3,2},{0,3},{5,4},{6,5},{7,6},{4,7},{9,8},{10,9},{11,1... | collective-permute-start | bytes 393224 | tf_op jit(solution)/shard_map/ppermute | solution.py:439
  (1 other events, 0.7 us)

commit v5 on v4

--- a/solution.py
+++ b/solution.py
@@ -26,6 +26,7 @@
 LANES = 128
 ROWS = 8
 LIMIT = 24 * 1024 * 1024
+WHOLE = 60 * 1024 * 1024
 
 
 def stencil_weights(width):
@@ -161,17 +162,6 @@
         for part in range(2):
             target = out_ref.at[part, pl.ds(owner * share + first, count)]
             pairs.append((piece_ref.at[owner, pl.ds(part * count, count)], target))
-    run_copies(pairs, sems)
-
-
-def unpack_pieces_kernel(parts, share, count, first, here_ref, *refs):
-    out_ref, sems = refs[-2:]
-    pairs = []
-    for step in range(parts):
-        owner = lax.rem(here_ref[0] + parts - step, parts)
-        for part in range(2):
-            target = out_ref.at[part, pl.ds(owner * share + first, count)]
-            pairs.append((refs[step].at[pl.ds(part * count, count)], target))
     run_copies(pairs, sems)
 
 
@@ -351,9 +341,7 @@
     out_ref[1] = density
 
 
-def second_kernel(parts, count, kinds, points, opening, permuted, copies, scalar_ref, *refs):
-    if permuted:
-        here_ref, *refs = refs
+def second_kernel(parts, count, kinds, points, opening, closing, scalar_ref, *refs):
     if opening:
         seen, refs = refs[:parts], refs[parts:]
         first_sums_ref = seen[0]
@@ -361,11 +349,8 @@
         vector_ref, first_sums_ref, sums_ref, *refs = refs
     psi_ref, potential_ref, *tables = refs[:8]
     refs = refs[8:]
-    if permuted:
-        pieces, refs = refs[:parts], refs[parts:]
-    else:
-        piece_ref, *refs = refs
-    if opening and not copies:
+    piece_ref, *refs = refs
+    if opening and not closing:
         vector_ref, *refs = refs
     out_ref, field_ref, total_ref = refs[:3]
     scratch = refs[3:]
@@ -376,7 +361,7 @@
         density = jnp.sum(fold([ref[1] for ref in seen]))
         current = (flow + scalar_ref[0] * density) * (1.0 / points)
         vector_value = scalar_ref[1] - source_weight * current
-        if not copies:
+        if not closing:
             vector_ref[0] = vector_value
     else:
         vector_value = vector_ref[0]
@@ -386,10 +371,7 @@
         count, vector_value, field_ref, total_ref, potential_ref, tables, scratch, width, kinds
     )
     for step in range(parts):
-        if permuted:
-            piece, start = pieces[step], lax.rem(here_ref[0] + step, parts) * planes
-        else:
-            piece, start = piece_ref.at[step], step * planes
+        piece, start = piece_ref.at[step], step * planes
         for index in range(planes):
             rows = pl.ds(index, ROWS, stride=planes)
             for orbital in range(count):
@@ -398,17 +380,39 @@
     flow, density = sums_in_kernel(count, total_ref, width)
     if not opening:
         flow, density = sums_ref[0] + flow, sums_ref[1] + density
-    if copies:
+    if closing:
         row = lax.broadcasted_iota(jnp.int32, (ROWS, LANES), 0)
         own = first_sums_ref[0] + scalar_ref[0] * first_sums_ref[1]
         own = jnp.sum(own, axis=0, keepdims=True) * (1.0 / points)
         new = jnp.sum(flow + vector_value * density, axis=0, keepdims=True) * (1.0 / points)
-        message = jnp.where(row == 0, own, jnp.where(row == 1, new, scalar_ref[2]))
-        for copy in range(copies):
-            out_ref[copy] = message
+        host = scalar_ref[2] * (1.0 / parts)
+        out_ref[...] = jnp.where(row == 0, own, jnp.where(row == 1, new, host))
     else:
         out_ref[0] = flow
         out_ref[1] = density
+
+
+def fields_kernel(blocks, owned, here_ref, window_ref, *refs):
+    messages, out_ref = refs[:blocks], refs[blocks]
+    edge = (LANES - owned) // 2
+    length = blocks * owned
+    position = lax.broadcasted_iota(jnp.int32, (1, LANES), 1) + (here_ref[0] * owned - edge)
+    inside = (position >= 0) & (position < length)
+    previous = jnp.where(inside, window_ref[0:1, :], 0.0)
+    present = jnp.where(inside, window_ref[1:2, :], 0.0)
+    place = position.astype(jnp.float32)
+    for step in range(STEPS):
+        source = jnp.zeros((1, LANES), jnp.float32)
+        for message in messages:
+            current = jnp.sum(message[step : step + 1, :])
+            source = source + jnp.where(place == message[2:3, :], current, 0.0)
+        beside = pltpu.roll(present, 1, 1) + pltpu.roll(present, LANES - 1, 1)
+        following = (
+            2.0 * present - previous + courant_square * (beside - 2.0 * present) - source_weight * source
+        )
+        previous, present = present, jnp.where(inside, following, 0.0)
+    out_ref[0:1, :] = pltpu.roll(previous, LANES - edge, 1)[:, :owned]
+    out_ref[1:2, :] = pltpu.roll(present, LANES - edge, 1)[:, :owned]
 
 
 def vmem():
@@ -454,6 +458,7 @@
     here = lax.axis_index("grid").astype(jnp.int32)[None]
     block = lax.axis_index("macro").astype(jnp.int32)
     params = pltpu.CompilerParams(vmem_limit_bytes=LIMIT)
+    whole_params = pltpu.CompilerParams(vmem_limit_bytes=WHOLE)
 
     def rows_of(value):
         lead = value.shape[:-2]
@@ -472,20 +477,10 @@
         in_specs=[hbm(), hbm()],
         out_specs=anywhere(),
         scratch_shapes=[pltpu.SemaphoreType.DMA((parts * 3,))],
-        compiler_params=params,
+        compiler_params=whole_params,
     )(source, rows_of(local_potential))
     main = exchanged(packed, "grid")
-    fields, source, packed = lax.optimization_barrier((fields, source, packed))
-    if last_count:
-        last = pl.pallas_call(
-            functools.partial(pack_pieces_kernel, parts, share, last_count, main_count),
-            out_shape=[float_array(2 * last_count, held, LANES)] * parts,
-            in_specs=[smem(), hbm()],
-            out_specs=[anywhere()] * parts,
-            scratch_shapes=[pltpu.SemaphoreType.DMA((parts * 2,))],
-            compiler_params=params,
-        )(here, source)
-        last = [last[0]] + [shifted(last[step], "grid", parts, -step) for step in range(1, parts)]
+    fields, packed = lax.optimization_barrier((fields, packed))
     field_blocks = [fields] + [shifted(fields, "macro", blocks, step) for step in range(1, blocks)]
 
     tables = pl.pallas_call(
@@ -510,6 +505,22 @@
         out_specs=smem(),
         compiler_params=params,
     )(host_point, block[None], *field_blocks)
+
+    source, scalars = lax.optimization_barrier((source, scalars))
+    if last_count:
+        last = pl.pallas_call(
+            functools.partial(pack_pieces_kernel, parts, share, last_count, main_count),
+            out_shape=[float_array(2 * last_count, held, LANES)] * parts,
+            in_specs=[smem(), hbm()],
+            out_specs=[anywhere()] * parts,
+            scratch_shapes=[pltpu.SemaphoreType.DMA((parts * 2,))],
+            compiler_params=whole_params,
+        )(here, source)
+        last = [last[0]] + [shifted(last[step], "grid", parts, -step) for step in range(1, parts)]
+    edge = (LANES - owned) // 2
+    window = jnp.concatenate(
+        [field_blocks[-1][:, owned - edge :], field_blocks[0], field_blocks[1 % blocks][:, :edge]], axis=1
+    )
 
     def micro_call(kernel, count, inputs, scalar_inputs, outputs, scalar_outputs, cells):
         rows = 2 * count * width * ROWS
@@ -560,80 +571,59 @@
         )
     seen = [sums] + [shifted(sums, "grid", parts, step) for step in range(1, parts)]
 
-    everyone = blocks * parts
-    pieces_shape = float_array(parts, 2 * main_count, held, LANES)
-    messages_shape = float_array(everyone, ROWS, LANES)
     whole_shape = float_array(2, norb, held, LANES)
+    message_shape = float_array(ROWS, LANES)
+    result = []
+
+    def give_back(pieces, count, first):
+        return pl.pallas_call(
+            functools.partial(unpack_kernel, parts, share, count, first),
+            out_shape=whole_shape,
+            in_specs=[anywhere()] + [hbm()] * len(result),
+            out_specs=hbm(),
+            scratch_shapes=[pltpu.SemaphoreType.DMA((parts * 2,))],
+            input_output_aliases={1: 0} if result else {},
+            compiler_params=params,
+        )(exchanged(pieces, "grid"), *result)
+
     main_pieces, *rest = micro_call(
-        functools.partial(
-            second_kernel, parts, main_count, kinds, total_points, True, False, 0 if last_count else everyone
-        ),
+        functools.partial(second_kernel, parts, main_count, kinds, total_points, True, not last_count),
         main_count,
         [scalars, *seen, main_psi, potential, *tables],
         1,
-        [pieces_shape] + ([float_array(1), sums_shape] if last_count else [messages_shape]),
+        [float_array(parts, 2 * main_count, held, LANES)]
+        + ([float_array(1), sums_shape] if last_count else [message_shape]),
         (1,) if last_count else (),
         2,
     )
-    returned = exchanged(main_pieces, "grid")
-    messages = rest[-1]
+    result = [give_back(main_pieces, main_count, 0)]
+    message = rest[-1]
     if last_count:
         vector_value, second_sums = rest
-        *pieces, messages = micro_call(
-            functools.partial(second_kernel, parts, last_count, kinds, total_points, False, True, everyone),
+        last_pieces, message = micro_call(
+            functools.partial(second_kernel, parts, last_count, kinds, total_points, False, True),
             last_count,
-            [scalars, here, vector_value, sums, second_sums, last_psi, potential, *tables],
-            3,
-            [float_array(2 * last_count, held, LANES)] * parts + [messages_shape],
+            [scalars, vector_value, sums, second_sums, last_psi, potential, *tables],
+            2,
+            [float_array(parts, 2 * last_count, held, LANES), message_shape],
             (),
             2,
         )
-        pieces = [pieces[0]] + [shifted(pieces[step], "grid", parts, -step) for step in range(1, parts)]
-    result = pl.pallas_call(
-        functools.partial(unpack_kernel, parts, share, main_count, 0),
-        out_shape=whole_shape,
-        in_specs=[anywhere()],
-        out_specs=hbm(),
-        scratch_shapes=[pltpu.SemaphoreType.DMA((parts * 2,))],
+        first_result, message = lax.optimization_barrier((result[0], message))
+        result = [first_result]
+        result = [give_back(last_pieces, last_count, main_count)]
+    result = result[0]
+    orbitals_out = planes_of(result).reshape(2, norb, planes, points)
+
+    message = fold([message] + [shifted(message, "grid", parts, step) for step in range(1, parts)])
+    messages = [message] + [shifted(message, "macro", blocks, step) for step in range(1, blocks)]
+    fields_out = pl.pallas_call(
+        functools.partial(fields_kernel, blocks, owned),
+        out_shape=float_array(2, owned),
+        in_specs=[smem()] + [vmem()] * (1 + blocks),
+        out_specs=vmem(),
         compiler_params=params,
-    )(returned)
-    result, messages = lax.optimization_barrier((result, messages))
-    messages = exchanged(messages, ("macro", "grid")).reshape(blocks, parts, ROWS, LANES)
-    if last_count:
-        result = pl.pallas_call(
-            functools.partial(unpack_pieces_kernel, parts, share, last_count, main_count),
-            out_shape=whole_shape,
-            in_specs=[smem()] + [anywhere()] * parts + [hbm()],
-            out_specs=hbm(),
-            scratch_shapes=[pltpu.SemaphoreType.DMA((parts * 2,))],
-            input_output_aliases={1 + parts: 0},
-            compiler_params=params,
-        )(here, *pieces, result)
-    orbitals_out = planes_of(result).reshape(2, norb, planes, points)
-
-    currents = jnp.sum(messages[:, :, :2], axis=(1, 3))
-    hosts = messages[:, 0, 2, 0].astype(jnp.int32)
-    length = blocks * owned
-    start = block * owned
-    positions = lax.broadcasted_iota(jnp.int32, (length,), 0)
-    sources = jnp.sum(
-        jnp.where(positions[None, None] == hosts[:, None, None], currents[:, :, None], 0.0), axis=0
-    )
-    turned = jnp.concatenate(field_blocks, axis=1)
-    whole = lax.dynamic_slice_in_dim(
-        jnp.concatenate([turned, turned], axis=1), length - start, length, axis=1
-    )
-    previous, present = whole[0], whole[1]
-    for step in range(STEPS):
-        rim = jnp.pad(present, 1)
-        following = (
-            2.0 * present
-            - previous
-            + courant_square * (rim[2:] - 2.0 * present + rim[:-2])
-            - source_weight * sources[step]
-        )
-        previous, present = present, following
-    fields_out = lax.dynamic_slice_in_dim(jnp.stack([previous, present]), start, owned, axis=1)
+    )(block[None], window, *messages)
     return orbitals_out[None], fields_out
 
 

time: 96.1 us -> 135 us (1.40)
  Pallas kernels: 29.8 us -> 67.1 us
  starting transfers between devices: 38.4 us -> 45.6 us
  waiting for transfers between devices: 22.5 us -> 20.1 us
  local copies, waits for them, and re-layouts: 2.45 us -> 0.17 us
    pallas_call x1, Pallas kernels: 0.92 us -> 21.1 us  [per_device(): pl.pallas_call(functools.partial(pack_kernel, parts, share, main_count, 0...]
    pallas_call x1, Pallas kernels: 0.78 us -> 17.1 us  [per_device(): pl.pallas_call(functools.partial(pack_pieces_kernel, parts, share, last_c...]
    ppermute x16 -> x23, starting transfers between devices: 23.7 us -> 32.2 us  [shifted(): lax.ppermute(value, axis_name, [((index + shift) % count, index) for inde...]
    all_to_all x3, waiting for transfers between devices: 10.8 us -> 6.26 us  [exchanged(): return lax.all_to_all(value, axes, split_axis=0, concat_axis=0, tiled=True)]
    ppermute x16 -> x23, waiting for transfers between devices: 11.8 us -> 13.8 us  [shifted(): lax.ppermute(value, axis_name, [((index + shift) % count, index) for inde...]
    unnamed x14 -> x9, local copies, waits for them, and re-layouts: 2.17 us -> 0.1 us
  transfers between devices with their start and end apart: 19 -> 26, of which waited for: 6 -> 8; matrix products, arithmetic and copies ran while one was open for 0% -> 0% of each run, Pallas kernels for 17% -> 25%
where the time goes in v5:
time: 135 us
  Pallas kernels  67.1 us (50%)
  starting transfers between devices  45.6 us (34%)
  waiting for transfers between devices  20.1 us (15%)
  between operations  1.48 us (1%)
    ppermute x23, starting transfers between devices, shifted(): lax.ppermute(value, axis_name, [((index + shift) % count, index) for inde...  32.2 us
    pallas_call x4, Pallas kernels, micro_call(): pl.pallas_call(kernel, out_shape=outputs, in_specs=[smem() if number < sc...  24.7 us
    pallas_call x1, Pallas kernels, per_device(): pl.pallas_call(functools.partial(pack_kernel, parts, share, main_count, 0...  21.1 us
    pallas_call x1, Pallas kernels, per_device(): pl.pallas_call(functools.partial(pack_pieces_kernel, parts, share, last_c...  17.1 us
    ppermute x23, waiting for transfers between devices, shifted(): lax.ppermute(value, axis_name, [((index + shift) % count, index) for inde...  13.8 us
    all_to_all x3, starting transfers between devices, exchanged(): return lax.all_to_all(value, axes, split_axis=0, concat_axis=0, tiled=True)  13.4 us
    all_to_all x3, waiting for transfers between devices, exchanged(): return lax.all_to_all(value, axes, split_axis=0, concat_axis=0, tiled=True)  6.26 us
  transfers between devices with their start and end apart: 26, of which 8 were waited for; matrix products, arithmetic and copies ran while one was open for 0% of the time, Pallas kernels for 25%

profile of v5, /device:TPU:0, one launch (start us, length us, event | category | flops | bytes accessed | tf_op | source)
XLA Modules:
  0.0 134.6 jit_solution(12106076681967077245)
XLA Ops:
  0.6 21.1 %shard_map.77 = f32[4,5,64,128]{3,2,1,0:T(8,128)} custom-call(f32[2,16,64,128]{3,2,1,0:T(8,128)} %bitcast.19, f32[64,128]{1,0:T(8,128)} %bitcast.22), custom_call_target="tpu_custom_call" | custom-call | tf_op jit(solution)/shard_map/pallas_call | solution.py:474
  21.7 6.5 %all-to-all-start = ((f32[4,5,64,128]{3,2,1,0:T(8,128)}), f32[4,5,64,128]{3,2,1,0:T(8,128)S(1)}, u32[]{:S(2)}, u32[]{:S(2)}) async-start(f32[4,5,64,128]{3,2,1,0:T(8,128)} %shard_map.77), calls=%async_computation | async-start | bytes 1310720 | tf_op jit(solution)/shard_map/all_to_all | solution.py:439
  28.2 1.5 %collective-permute-start.5 = (f32[2,64]{1,0:T(2,128)S(1)}, f32[2,64]{1,0:T(2,128)S(1)}, u32[]{:S(2)}, u32[]{:S(2)}) collective-permute-start(f32[2,64]{1,0:T(2,128)S(1)} %copy-done.1), channel_id=1, source_target_pairs={{24,0},{28,4},{0,8},{4,12},{8,16},{12,20},{16,24},{20,28},{25,1},{... | collective-permute-start | bytes 1544 | tf_op jit(solution)/shard_map/ppermute | solution.py:443
  29.7 2.4 %collective-permute-start.4 = (f32[2,64]{1,0:T(2,128)S(1)}, f32[2,64]{1,0:T(2,128)S(1)}, u32[]{:S(2)}, u32[]{:S(2)}) collective-permute-start(f32[2,64]{1,0:T(2,128)S(1)} %copy-done.1), channel_id=1, source_target_pairs={{20,0},{24,4},{28,8},{0,12},{4,16},{8,20},{12,24},{16,28},{21,1},{... | collective-permute-start | bytes 1544 | tf_op jit(solution)/shard_map/ppermute | solution.py:443
  34.2 2.3 %collective-permute-start = (f32[2,64]{1,0:T(2,128)S(1)}, f32[2,64]{1,0:T(2,128)S(1)}, u32[]{:S(2)}, u32[]{:S(2)}) collective-permute-start(f32[2,64]{1,0:T(2,128)S(1)} %copy-done.1), channel_id=1, source_target_pairs={{4,0},{8,4},{12,8},{16,12},{20,16},{24,20},{28,24},{0,28},{5,1},{9... | collective-permute-start | bytes 1544 | tf_op jit(solution)/shard_map/ppermute | solution.py:443
  39.0 17.1 %shard_map.79 = (f32[4,64,128]{2,1,0:T(8,128)}, f32[4,64,128]{2,1,0:T(8,128)}, f32[4,64,128]{2,1,0:T(8,128)}, f32[4,64,128]{2,1,0:T(8,128)}) custom-call(s32[1]{0:T(128)} %bitcast.9.here_ref.refs_0_, f32[2,16,64,128]{3,2,1,0:T(8,128)} %bitcast.20), custom_call_target="tpu_custom_call" | custom-call | tf_op jit(solution)/shard_map/pallas_call | solution.py:511
  56.1 2.1 %collective-permute-start.7 = (f32[4,64,128]{2,1,0:T(8,128)}, f32[4,64,128]{2,1,0:T(8,128)S(1)}, u32[]{:S(2)}, u32[]{:S(2)}) collective-permute-start(f32[4,64,128]{2,1,0:T(8,128)} %get-tuple-element.31), channel_id=1, source_target_pairs={{3,0},{0,1},{1,2},{2,3},{7,4},{4,5},{5,6},{6,7},{11,8},{8,9},{9,10... | collective-permute-start | bytes 393224 | tf_op jit(solution)/shard_map/ppermute | solution.py:443
  58.1 2.4 %collective-permute-start.8 = (f32[4,64,128]{2,1,0:T(8,128)}, f32[4,64,128]{2,1,0:T(8,128)S(1)}, u32[]{:S(2)}, u32[]{:S(2)}) collective-permute-start(f32[4,64,128]{2,1,0:T(8,128)} %get-tuple-element.32), channel_id=1, source_target_pairs={{2,0},{3,1},{0,2},{1,3},{6,4},{7,5},{4,6},{5,7},{10,8},{11,9},{8,1... | collective-permute-start | bytes 393224 | tf_op jit(solution)/shard_map/ppermute | solution.py:443
  62.0 5.7 %shard_map.81 = (f32[4,32,8,128]{3,2,1,0:T(8,128)S(1)}, f32[2,8,128]{2,1,0:T(8,128)S(1)}, f32[32,8,128]{2,1,0:T(8,128)S(1)}) custom-call(f32[3]{0:T(128)S(1)} %shard_map.78.scalar_ref, f32[4,5,64,128]{3,2,1,0:T(8,128)S(1)} %all-to-all-done.refs_0_, bf16[256,256]{1,0:T(8,128)(2,1)S(1)} %get-tuple-element.34.refs_1_.refs_6_.refs_5_, ...), custom_call_target="tpu_custom_call" | custom-call | flops 1610612736 | bytes 4194304 | tf_op jit(solution)/shard_map/pallas_call | solution.py:528
  67.7 2.0 %collective-permute-done.8.refs_3_ = f32[4,64,128]{2,1,0:T(8,128)S(1)} collective-permute-done((f32[4,64,128]{2,1,0:T(8,128)}, f32[4,64,128]{2,1,0:T(8,128)S(1)}, u32[]{:S(2)}, u32[]{:S(2)}) %collective-permute-start.8) | collective-permute-done | bytes 131104 | tf_op jit(solution)/shard_map/ppermute | solution.py:443
  69.7 5.7 %shard_map.82 = (f32[4,32,8,128]{3,2,1,0:T(8,128)S(1)}, f32[2,8,128]{2,1,0:T(8,128)S(1)}) custom-call(f32[3]{0:T(128)S(1)} %shard_map.78.scalar_ref, s32[1]{0:T(128)} %bitcast.9.here_ref.refs_0_, f32[4,64,128]{2,1,0:T(8,128)S(1)} %copy-done.2, f32[4,64,128]{2,1,0:T(8,128)S(1)} %collective-permute-done.7.refs_2_, ...), custom_call_target="tpu_custom_call" | custom-call | flops 1610612736 | bytes 4194304 | tf_op jit(solution)/shard_map/pallas_call | solution.py:528
  75.3 3.4 %collective-permute-start.12 = (f32[2,8,128]{2,1,0:T(8,128)S(1)}, f32[2,8,128]{2,1,0:T(8,128)S(1)}, u32[]{:S(2)}, u32[]{:S(2)}) collective-permute-start(f32[2,8,128]{2,1,0:T(8,128)S(1)} %get-tuple-element.42.refs_0_.refs_1_), channel_id=1, source_target_pairs={{3,0},{0,1},{1,2},{2,3},{7,4},{4,5},{5,6},{6,7},{11,8},{8,9},{9,10... | collective-permute-start | bytes 24584 | tf_op jit(solution)/shard_map/ppermute | solution.py:443
  78.7 2.0 %collective-permute-start.11 = (f32[2,8,128]{2,1,0:T(8,128)S(1)}, f32[2,8,128]{2,1,0:T(8,128)S(1)}, u32[]{:S(2)}, u32[]{:S(2)}) collective-permute-start(f32[2,8,128]{2,1,0:T(8,128)S(1)} %get-tuple-element.42.refs_0_.refs_1_), channel_id=1, source_target_pairs={{2,0},{3,1},{0,2},{1,3},{6,4},{7,5},{4,6},{5,7},{10,8},{11,9},{8,1... | collective-permute-start | bytes 24584 | tf_op jit(solution)/shard_map/ppermute | solution.py:443
  84.4 6.4 %shard_map.83 = (f32[4,4,64,128]{3,2,1,0:T(8,128)}, f32[1]{0:T(128)}, f32[2,8,128]{2,1,0:T(8,128)S(1)}) custom-call(f32[3]{0:T(128)S(1)} %shard_map.78.scalar_ref, f32[2,8,128]{2,1,0:T(8,128)S(1)} %get-tuple-element.42.refs_0_.refs_1_, f32[2,8,128]{2,1,0:T(8,128)S(1)} %collective-permute-done.10.refs_1_, f32[2,8,128]{2,1,0:T(8,128)S(1)} %collective-permute-done.11.refs_2_, ...), custom_call_target="tpu_custom_call" | custom-call | flops 1610612736 | bytes 4194304 | tf_op jit(solution)/shard_map/pallas_call | solution.py:528
  90.7 3.5 %all-to-all-start.2 = ((f32[4,4,64,128]{3,2,1,0:T(8,128)}), f32[4,4,64,128]{3,2,1,0:T(8,128)S(1)}, u32[]{:S(2)}, u32[]{:S(2)}) async-start(f32[4,4,64,128]{3,2,1,0:T(8,128)} %get-tuple-element.48), calls=%async_computation.2 | async-start | bytes 1048576 | tf_op jit(solution)/shard_map/all_to_all | solution.py:439
  94.2 7.0 %shard_map.84 = (f32[4,4,64,128]{3,2,1,0:T(8,128)}, f32[8,128]{1,0:T(8,128)S(1)}) custom-call(f32[3]{0:T(128)S(1)} %shard_map.78.scalar_ref, f32[1]{0:T(128)} %get-tuple-element.44.refs_0_, f32[2,8,128]{2,1,0:T(8,128)S(1)} %get-tuple-element.42.refs_0_.refs_1_, f32[2,8,128]{2,1,0:T(8,128)S(1)} %get-tuple-element.45.refs_2_, ...), custom_call_target="tpu_custom_call" | custom-call | flops 1610612736 | bytes 4194304 | tf_op jit(solution)/shard_map/pallas_call | solution.py:528
  101.2 6.3 %all-to-all-done.2.piece_ref = f32[4,4,64,128]{3,2,1,0:T(8,128)S(1)} async-done(((f32[4,4,64,128]{3,2,1,0:T(8,128)}), f32[4,4,64,128]{3,2,1,0:T(8,128)S(1)}, u32[]{:S(2)}, u32[]{:S(2)}) %all-to-all-start.2) | async-done | bytes 524320 | tf_op jit(solution)/shard_map/all_to_all | solution.py:439
  107.5 3.5 %all-to-all-start.1 = ((f32[4,4,64,128]{3,2,1,0:T(8,128)}), f32[4,4,64,128]{3,2,1,0:T(8,128)S(1)}, u32[]{:S(2)}, u32[]{:S(2)}) async-start(f32[4,4,64,128]{3,2,1,0:T(8,128)} %get-tuple-element.47), calls=%async_computation.1 | async-start | bytes 1048576 | tf_op jit(solution)/shard_map/all_to_all | solution.py:439
  111.8 2.0 %collective-permute-start.15 = (f32[8,128]{1,0:T(8,128)S(1)}, f32[8,128]{1,0:T(8,128)S(1)}, u32[]{:S(2)}, u32[]{:S(2)}) collective-permute-start(f32[8,128]{1,0:T(8,128)S(1)} %get-tuple-element.51), channel_id=1, source_target_pairs={{3,0},{0,1},{1,2},{2,3},{7,4},{4,5},{5,6},{6,7},{11,8},{8,9},{9,10... | collective-permute-start | bytes 12296 | tf_op jit(solution)/shard_map/ppermute | solution.py:443
  113.9 1.9 %collective-permute-start.14 = (f32[8,128]{1,0:T(8,128)S(1)}, f32[8,128]{1,0:T(8,128)S(1)}, u32[]{:S(2)}, u32[]{:S(2)}) collective-permute-start(f32[8,128]{1,0:T(8,128)S(1)} %get-tuple-element.51), channel_id=1, source_target_pairs={{1,0},{2,1},{3,2},{0,3},{5,4},{6,5},{7,6},{4,7},{9,8},{10,9},{11,1... | collective-permute-start | bytes 12296 | tf_op jit(solution)/shard_map/ppermute | solution.py:443
  116.8 6.3 %collective-permute-done.15 = f32[8,128]{1,0:T(8,128)S(1)} collective-permute-done((f32[8,128]{1,0:T(8,128)S(1)}, f32[8,128]{1,0:T(8,128)S(1)}, u32[]{:S(2)}, u32[]{:S(2)}) %collective-permute-start.15) | collective-permute-done | bytes 4128 | tf_op jit(solution)/shard_map/ppermute | solution.py:443
  123.1 1.9 %collective-permute-done.13 = f32[8,128]{1,0:T(8,128)S(1)} collective-permute-done((f32[8,128]{1,0:T(8,128)S(1)}, f32[8,128]{1,0:T(8,128)S(1)}, u32[]{:S(2)}, u32[]{:S(2)}) %collective-permute-start.13) | collective-permute-done | bytes 4128 | tf_op jit(solution)/shard_map/ppermute | solution.py:443
  127.8 1.5 %collective-permute-start.19 = (f32[8,128]{1,0:T(8,128)S(1)}, f32[8,128]{1,0:T(8,128)S(1)}, u32[]{:S(2)}, u32[]{:S(2)}) collective-permute-start(f32[8,128]{1,0:T(8,128)S(1)} %add_add_fusion.refs_0_), channel_id=1, source_target_pairs={{16,0},{20,4},{24,8},{28,12},{0,16},{4,20},{8,24},{12,28},{17,1},{... | collective-permute-start | bytes 12296 | tf_op jit(solution)/shard_map/ppermute | solution.py:443
  129.3 1.8 %collective-permute-start.17 = (f32[8,128]{1,0:T(8,128)S(1)}, f32[8,128]{1,0:T(8,128)S(1)}, u32[]{:S(2)}, u32[]{:S(2)}) collective-permute-start(f32[8,128]{1,0:T(8,128)S(1)} %add_add_fusion.refs_0_), channel_id=1, source_target_pairs={{8,0},{12,4},{16,8},{20,12},{24,16},{28,20},{0,24},{4,28},{9,1},{1... | collective-permute-start | bytes 12296 | tf_op jit(solution)/shard_map/ppermute | solution.py:443
  (51 shorter events, 17.2 us)
Async XLA Ops:
  21.7 40.3 %all-to-all-start = ((f32[4,5,64,128]{3,2,1,0:T(8,128)}), f32[4,5,64,128]{3,2,1,0:T(8,128)S(1)}, u32[]{:S(2)}, u32[]{:S(2)}) async-start(f32[4,5,64,128]{3,2,1,0:T(8,128)} %shard_map.77), calls=%async_computation | async-start | bytes 1310720 | tf_op jit(solution)/shard_map/all_to_all | solution.py:439
  28.2 4.5 %collective-permute-start.6 = (f32[2,64]{1,0:T(2,128)S(1)}, f32[2,64]{1,0:T(2,128)S(1)}, u32[]{:S(2)}, u32[]{:S(2)}) collective-permute-start(f32[2,64]{1,0:T(2,128)S(1)} %copy-done.1), channel_id=1, source_target_pairs={{28,0},{0,4},{4,8},{8,12},{12,16},{16,20},{20,24},{24,28},{29,1},{... | collective-permute-start | bytes 1544 | tf_op jit(solution)/shard_map/ppermute | solution.py:443
  28.2 6.0 %collective-permute-start.5 = (f32[2,64]{1,0:T(2,128)S(1)}, f32[2,64]{1,0:T(2,128)S(1)}, u32[]{:S(2)}, u32[]{:S(2)}) collective-permute-start(f32[2,64]{1,0:T(2,128)S(1)} %copy-done.1), channel_id=1, source_target_pairs={{24,0},{28,4},{0,8},{4,12},{8,16},{12,20},{16,24},{20,28},{25,1},{... | collective-permute-start | bytes 1544 | tf_op jit(solution)/shard_map/ppermute | solution.py:443
  29.7 8.5 %collective-permute-start.4 = (f32[2,64]{1,0:T(2,128)S(1)}, f32[2,64]{1,0:T(2,128)S(1)}, u32[]{:S(2)}, u32[]{:S(2)}) collective-permute-start(f32[2,64]{1,0:T(2,128)S(1)} %copy-done.1), channel_id=1, source_target_pairs={{20,0},{24,4},{28,8},{0,12},{4,16},{8,20},{12,24},{16,28},{21,1},{... | collective-permute-start | bytes 1544 | tf_op jit(solution)/shard_map/ppermute | solution.py:443
  32.1 6.1 %collective-permute-start.3 = (f32[2,64]{1,0:T(2,128)S(1)}, f32[2,64]{1,0:T(2,128)S(1)}, u32[]{:S(2)}, u32[]{:S(2)}) collective-permute-start(f32[2,64]{1,0:T(2,128)S(1)} %copy-done.1), channel_id=1, source_target_pairs={{16,0},{20,4},{24,8},{28,12},{0,16},{4,20},{8,24},{12,28},{17,1},{... | collective-permute-start | bytes 1544 | tf_op jit(solution)/shard_map/ppermute | solution.py:443
  32.6 5.6 %collective-permute-start.2 = (f32[2,64]{1,0:T(2,128)S(1)}, f32[2,64]{1,0:T(2,128)S(1)}, u32[]{:S(2)}, u32[]{:S(2)}) collective-permute-start(f32[2,64]{1,0:T(2,128)S(1)} %copy-done.1), channel_id=1, source_target_pairs={{12,0},{16,4},{20,8},{24,12},{28,16},{0,20},{4,24},{8,28},{13,1},{... | collective-permute-start | bytes 1544 | tf_op jit(solution)/shard_map/ppermute | solution.py:443
  32.7 5.5 %collective-permute-start.1 = (f32[2,64]{1,0:T(2,128)S(1)}, f32[2,64]{1,0:T(2,128)S(1)}, u32[]{:S(2)}, u32[]{:S(2)}) collective-permute-start(f32[2,64]{1,0:T(2,128)S(1)} %copy-done.1), channel_id=1, source_target_pairs={{8,0},{12,4},{16,8},{20,12},{24,16},{28,20},{0,24},{4,28},{9,1},{1... | collective-permute-start | bytes 1544 | tf_op jit(solution)/shard_map/ppermute | solution.py:443
  34.2 4.1 %collective-permute-start = (f32[2,64]{1,0:T(2,128)S(1)}, f32[2,64]{1,0:T(2,128)S(1)}, u32[]{:S(2)}, u32[]{:S(2)}) collective-permute-start(f32[2,64]{1,0:T(2,128)S(1)} %copy-done.1), channel_id=1, source_target_pairs={{4,0},{8,4},{12,8},{16,12},{20,16},{24,20},{28,24},{0,28},{5,1},{9... | collective-permute-start | bytes 1544 | tf_op jit(solution)/shard_map/ppermute | solution.py:443
  56.1 11.6 %collective-permute-start.7 = (f32[4,64,128]{2,1,0:T(8,128)}, f32[4,64,128]{2,1,0:T(8,128)S(1)}, u32[]{:S(2)}, u32[]{:S(2)}) collective-permute-start(f32[4,64,128]{2,1,0:T(8,128)} %get-tuple-element.31), channel_id=1, source_target_pairs={{3,0},{0,1},{1,2},{2,3},{7,4},{4,5},{5,6},{6,7},{11,8},{8,9},{9,10... | collective-permute-start | bytes 393224 | tf_op jit(solution)/shard_map/ppermute | solution.py:443
  58.1 11.5 %collective-permute-start.8 = (f32[4,64,128]{2,1,0:T(8,128)}, f32[4,64,128]{2,1,0:T(8,128)S(1)}, u32[]{:S(2)}, u32[]{:S(2)}) collective-permute-start(f32[4,64,128]{2,1,0:T(8,128)} %get-tuple-element.32), channel_id=1, source_target_pairs={{2,0},{3,1},{0,2},{1,3},{6,4},{7,5},{4,6},{5,7},{10,8},{11,9},{8,1... | collective-permute-start | bytes 393224 | tf_op jit(solution)/shard_map/ppermute | solution.py:443
  60.5 9.2 %collective-permute-start.9 = (f32[4,64,128]{2,1,0:T(8,128)}, f32[4,64,128]{2,1,0:T(8,128)S(1)}, u32[]{:S(2)}, u32[]{:S(2)}) collective-permute-start(f32[4,64,128]{2,1,0:T(8,128)} %get-tuple-element.33), channel_id=1, source_target_pairs={{1,0},{2,1},{3,2},{0,3},{5,4},{6,5},{7,6},{4,7},{9,8},{10,9},{11,1... | collective-permute-start | bytes 393224 | tf_op jit(solution)/shard_map/ppermute | solution.py:443
  75.3 6.5 %collective-permute-start.12 = (f32[2,8,128]{2,1,0:T(8,128)S(1)}, f32[2,8,128]{2,1,0:T(8,128)S(1)}, u32[]{:S(2)}, u32[]{:S(2)}) collective-permute-start(f32[2,8,128]{2,1,0:T(8,128)S(1)} %get-tuple-element.42.refs_0_.refs_1_), channel_id=1, source_target_pairs={{3,0},{0,1},{1,2},{2,3},{7,4},{4,5},{5,6},{6,7},{11,8},{8,9},{9,10... | collective-permute-start | bytes 24584 | tf_op jit(solution)/shard_map/ppermute | solution.py:443
  78.7 4.5 %collective-permute-start.11 = (f32[2,8,128]{2,1,0:T(8,128)S(1)}, f32[2,8,128]{2,1,0:T(8,128)S(1)}, u32[]{:S(2)}, u32[]{:S(2)}) collective-permute-start(f32[2,8,128]{2,1,0:T(8,128)S(1)} %get-tuple-element.42.refs_0_.refs_1_), channel_id=1, source_target_pairs={{2,0},{3,1},{0,2},{1,3},{6,4},{7,5},{4,6},{5,7},{10,8},{11,9},{8,1... | collective-permute-start | bytes 24584 | tf_op jit(solution)/shard_map/ppermute | solution.py:443
  90.7 16.8 %all-to-all-start.2 = ((f32[4,4,64,128]{3,2,1,0:T(8,128)}), f32[4,4,64,128]{3,2,1,0:T(8,128)S(1)}, u32[]{:S(2)}, u32[]{:S(2)}) async-start(f32[4,4,64,128]{3,2,1,0:T(8,128)} %get-tuple-element.48), calls=%async_computation.2 | async-start | bytes 1048576 | tf_op jit(solution)/shard_map/all_to_all | solution.py:439
  107.5 25.0 %all-to-all-start.1 = ((f32[4,4,64,128]{3,2,1,0:T(8,128)}), f32[4,4,64,128]{3,2,1,0:T(8,128)S(1)}, u32[]{:S(2)}, u32[]{:S(2)}) async-start(f32[4,4,64,128]{3,2,1,0:T(8,128)} %get-tuple-element.47), calls=%async_computation.1 | async-start | bytes 1048576 | tf_op jit(solution)/shard_map/all_to_all | solution.py:439
  111.8 11.3 %collective-permute-start.15 = (f32[8,128]{1,0:T(8,128)S(1)}, f32[8,128]{1,0:T(8,128)S(1)}, u32[]{:S(2)}, u32[]{:S(2)}) collective-permute-start(f32[8,128]{1,0:T(8,128)S(1)} %get-tuple-element.51), channel_id=1, source_target_pairs={{3,0},{0,1},{1,2},{2,3},{7,4},{4,5},{5,6},{6,7},{11,8},{8,9},{9,10... | collective-permute-start | bytes 12296 | tf_op jit(solution)/shard_map/ppermute | solution.py:443
  113.9 9.3 %collective-permute-start.14 = (f32[8,128]{1,0:T(8,128)S(1)}, f32[8,128]{1,0:T(8,128)S(1)}, u32[]{:S(2)}, u32[]{:S(2)}) collective-permute-start(f32[8,128]{1,0:T(8,128)S(1)} %get-tuple-element.51), channel_id=1, source_target_pairs={{1,0},{2,1},{3,2},{0,3},{5,4},{6,5},{7,6},{4,7},{9,8},{10,9},{11,1... | collective-permute-start | bytes 12296 | tf_op jit(solution)/shard_map/ppermute | solution.py:443
  115.7 9.3 %collective-permute-start.13 = (f32[8,128]{1,0:T(8,128)S(1)}, f32[8,128]{1,0:T(8,128)S(1)}, u32[]{:S(2)}, u32[]{:S(2)}) collective-permute-start(f32[8,128]{1,0:T(8,128)S(1)} %get-tuple-element.51), channel_id=1, source_target_pairs={{2,0},{3,1},{0,2},{1,3},{6,4},{7,5},{4,6},{5,7},{10,8},{11,9},{8,1... | collective-permute-start | bytes 12296 | tf_op jit(solution)/shard_map/ppermute | solution.py:443
  125.0 4.2 %collective-permute-start.22 = (f32[8,128]{1,0:T(8,128)S(1)}, f32[8,128]{1,0:T(8,128)S(1)}, u32[]{:S(2)}, u32[]{:S(2)}) collective-permute-start(f32[8,128]{1,0:T(8,128)S(1)} %add_add_fusion.refs_0_), channel_id=1, source_target_pairs={{28,0},{0,4},{4,8},{8,12},{12,16},{16,20},{20,24},{24,28},{29,1},{... | collective-permute-start | bytes 12296 | tf_op jit(solution)/shard_map/ppermute | solution.py:443
  125.0 6.0 %collective-permute-start.21 = (f32[8,128]{1,0:T(8,128)S(1)}, f32[8,128]{1,0:T(8,128)S(1)}, u32[]{:S(2)}, u32[]{:S(2)}) collective-permute-start(f32[8,128]{1,0:T(8,128)S(1)} %add_add_fusion.refs_0_), channel_id=1, source_target_pairs={{24,0},{28,4},{0,8},{4,12},{8,16},{12,20},{16,24},{20,28},{25,1},{... | collective-permute-start | bytes 12296 | tf_op jit(solution)/shard_map/ppermute | solution.py:443
  126.4 7.0 %collective-permute-start.20 = (f32[8,128]{1,0:T(8,128)S(1)}, f32[8,128]{1,0:T(8,128)S(1)}, u32[]{:S(2)}, u32[]{:S(2)}) collective-permute-start(f32[8,128]{1,0:T(8,128)S(1)} %add_add_fusion.refs_0_), channel_id=1, source_target_pairs={{20,0},{24,4},{28,8},{0,12},{4,16},{8,20},{12,24},{16,28},{21,1},{... | collective-permute-start | bytes 12296 | tf_op jit(solution)/shard_map/ppermute | solution.py:443
  127.8 5.6 %collective-permute-start.19 = (f32[8,128]{1,0:T(8,128)S(1)}, f32[8,128]{1,0:T(8,128)S(1)}, u32[]{:S(2)}, u32[]{:S(2)}) collective-permute-start(f32[8,128]{1,0:T(8,128)S(1)} %add_add_fusion.refs_0_), channel_id=1, source_target_pairs={{16,0},{20,4},{24,8},{28,12},{0,16},{4,20},{8,24},{12,28},{17,1},{... | collective-permute-start | bytes 12296 | tf_op jit(solution)/shard_map/ppermute | solution.py:443
  129.2 4.1 %collective-permute-start.18 = (f32[8,128]{1,0:T(8,128)S(1)}, f32[8,128]{1,0:T(8,128)S(1)}, u32[]{:S(2)}, u32[]{:S(2)}) collective-permute-start(f32[8,128]{1,0:T(8,128)S(1)} %add_add_fusion.refs_0_), channel_id=1, source_target_pairs={{12,0},{16,4},{20,8},{24,12},{28,16},{0,20},{4,24},{8,28},{13,1},{... | collective-permute-start | bytes 12296 | tf_op jit(solution)/shard_map/ppermute | solution.py:443
  129.3 4.1 %collective-permute-start.17 = (f32[8,128]{1,0:T(8,128)S(1)}, f32[8,128]{1,0:T(8,128)S(1)}, u32[]{:S(2)}, u32[]{:S(2)}) collective-permute-start(f32[8,128]{1,0:T(8,128)S(1)} %add_add_fusion.refs_0_), channel_id=1, source_target_pairs={{8,0},{12,4},{16,8},{20,12},{24,16},{28,20},{0,24},{4,28},{9,1},{1... | collective-permute-start | bytes 12296 | tf_op jit(solution)/shard_map/ppermute | solution.py:443
  (6 other events, 40.5 us)

commit v6 on v5

--- a/solution.py
+++ b/solution.py
@@ -475,7 +475,7 @@
         functools.partial(pack_kernel, parts, share, main_count, 0),
         out_shape=float_array(parts, 2 * main_count + 1, held, LANES),
         in_specs=[hbm(), hbm()],
-        out_specs=anywhere(),
+        out_specs=vmem(),
         scratch_shapes=[pltpu.SemaphoreType.DMA((parts * 3,))],
         compiler_params=whole_params,
     )(source, rows_of(local_potential))
@@ -512,7 +512,7 @@
             functools.partial(pack_pieces_kernel, parts, share, last_count, main_count),
             out_shape=[float_array(2 * last_count, held, LANES)] * parts,
             in_specs=[smem(), hbm()],
-            out_specs=[anywhere()] * parts,
+            out_specs=[vmem()] * parts,
             scratch_shapes=[pltpu.SemaphoreType.DMA((parts * 2,))],
             compiler_params=whole_params,
         )(here, source)

time: 135 us -> 101 us (0.75)
  Pallas kernels: 67.1 us -> 33 us
    pallas_call x1, Pallas kernels: 21.1 us -> 2.06 us  [per_device(): pl.pallas_call(functools.partial(pack_kernel, parts, share, main_count, 0...]
    pallas_call x1, Pallas kernels: 17.1 us -> 1.93 us  [per_device(): pl.pallas_call(functools.partial(pack_pieces_kernel, parts, share, last_c...]
  transfers between devices with their start and end apart: 26 -> 26, of which waited for: 8 -> 8; matrix products, arithmetic and copies ran while one was open for 0% -> 0% of each run, Pallas kernels for 25% -> 18%
where the time goes in v6:
time: 101 us; the launch traced here: 99.9 us
  starting transfers between devices  45.1 us (45%)
  Pallas kernels  33 us (33%)
  waiting for transfers between devices  20.1 us (20%)
  between operations  1.47 us (1%)
    ppermute x23, starting transfers between devices, shifted(): lax.ppermute(value, axis_name, [((index + shift) % count, index) for inde...  31.7 us
    pallas_call x4, Pallas kernels, micro_call(): pl.pallas_call(kernel, out_shape=outputs, in_specs=[smem() if number < sc...  24.7 us
    ppermute x23, waiting for transfers between devices, shifted(): lax.ppermute(value, axis_name, [((index + shift) % count, index) for inde...  13.8 us
    all_to_all x3, starting transfers between devices, exchanged(): return lax.all_to_all(value, axes, split_axis=0, concat_axis=0, tiled=True)  13.4 us
    all_to_all x3, waiting for transfers between devices, exchanged(): return lax.all_to_all(value, axes, split_axis=0, concat_axis=0, tiled=True)  6.26 us
    pallas_call x1, Pallas kernels, per_device(): pl.pallas_call(functools.partial(pack_kernel, parts, share, main_count, 0...  2.06 us
  transfers between devices with their start and end apart: 26, of which 8 were waited for; matrix products, arithmetic and copies ran while one was open for 0% of the time, Pallas kernels for 18%

profile of v6, /device:TPU:0, one launch (start us, length us, event | category | flops | bytes accessed | tf_op | source)
XLA Modules:
  0.0 99.9 jit_solution(5996234504181173180)
XLA Ops:
  0.6 2.1 %shard_map.77 = f32[4,5,64,128]{3,2,1,0:T(8,128)} custom-call(f32[2,16,64,128]{3,2,1,0:T(8,128)} %bitcast.19, f32[64,128]{1,0:T(8,128)} %bitcast.22), custom_call_target="tpu_custom_call" | custom-call | tf_op jit(solution)/shard_map/pallas_call | solution.py:474
  2.7 6.5 %all-to-all-start = ((f32[4,5,64,128]{3,2,1,0:T(8,128)}), f32[4,5,64,128]{3,2,1,0:T(8,128)S(1)}, u32[]{:S(2)}, u32[]{:S(2)}) async-start(f32[4,5,64,128]{3,2,1,0:T(8,128)} %shard_map.77), calls=%async_computation | async-start | bytes 1310720 | tf_op jit(solution)/shard_map/all_to_all | solution.py:439
  9.2 1.5 %collective-permute-start.5 = (f32[2,64]{1,0:T(2,128)S(1)}, f32[2,64]{1,0:T(2,128)S(1)}, u32[]{:S(2)}, u32[]{:S(2)}) collective-permute-start(f32[2,64]{1,0:T(2,128)S(1)} %copy-done.1), channel_id=1, source_target_pairs={{24,0},{28,4},{0,8},{4,12},{8,16},{12,20},{16,24},{20,28},{25,1},{... | collective-permute-start | bytes 1544 | tf_op jit(solution)/shard_map/ppermute | solution.py:443
  10.7 2.4 %collective-permute-start.4 = (f32[2,64]{1,0:T(2,128)S(1)}, f32[2,64]{1,0:T(2,128)S(1)}, u32[]{:S(2)}, u32[]{:S(2)}) collective-permute-start(f32[2,64]{1,0:T(2,128)S(1)} %copy-done.1), channel_id=1, source_target_pairs={{20,0},{24,4},{28,8},{0,12},{4,16},{8,20},{12,24},{16,28},{21,1},{... | collective-permute-start | bytes 1544 | tf_op jit(solution)/shard_map/ppermute | solution.py:443
  15.2 2.3 %collective-permute-start = (f32[2,64]{1,0:T(2,128)S(1)}, f32[2,64]{1,0:T(2,128)S(1)}, u32[]{:S(2)}, u32[]{:S(2)}) collective-permute-start(f32[2,64]{1,0:T(2,128)S(1)} %copy-done.1), channel_id=1, source_target_pairs={{4,0},{8,4},{12,8},{16,12},{20,16},{24,20},{28,24},{0,28},{5,1},{9... | collective-permute-start | bytes 1544 | tf_op jit(solution)/shard_map/ppermute | solution.py:443
  20.0 1.9 %shard_map.79 = (f32[4,64,128]{2,1,0:T(8,128)}, f32[4,64,128]{2,1,0:T(8,128)}, f32[4,64,128]{2,1,0:T(8,128)}, f32[4,64,128]{2,1,0:T(8,128)}) custom-call(s32[1]{0:T(128)} %bitcast.9.here_ref.refs_0_, f32[2,16,64,128]{3,2,1,0:T(8,128)} %bitcast.20), custom_call_target="tpu_custom_call" | custom-call | tf_op jit(solution)/shard_map/pallas_call | solution.py:511
  21.9 2.1 %collective-permute-start.7 = (f32[4,64,128]{2,1,0:T(8,128)}, f32[4,64,128]{2,1,0:T(8,128)S(1)}, u32[]{:S(2)}, u32[]{:S(2)}) collective-permute-start(f32[4,64,128]{2,1,0:T(8,128)} %get-tuple-element.31), channel_id=1, source_target_pairs={{3,0},{0,1},{1,2},{2,3},{7,4},{4,5},{5,6},{6,7},{11,8},{8,9},{9,10... | collective-permute-start | bytes 393224 | tf_op jit(solution)/shard_map/ppermute | solution.py:443
  24.0 2.4 %collective-permute-start.8 = (f32[4,64,128]{2,1,0:T(8,128)}, f32[4,64,128]{2,1,0:T(8,128)S(1)}, u32[]{:S(2)}, u32[]{:S(2)}) collective-permute-start(f32[4,64,128]{2,1,0:T(8,128)} %get-tuple-element.32), channel_id=1, source_target_pairs={{2,0},{3,1},{0,2},{1,3},{6,4},{7,5},{4,6},{5,7},{10,8},{11,9},{8,1... | collective-permute-start | bytes 393224 | tf_op jit(solution)/shard_map/ppermute | solution.py:443
  27.8 5.7 %shard_map.81 = (f32[4,32,8,128]{3,2,1,0:T(8,128)S(1)}, f32[2,8,128]{2,1,0:T(8,128)S(1)}, f32[32,8,128]{2,1,0:T(8,128)S(1)}) custom-call(f32[3]{0:T(128)S(1)} %shard_map.78.scalar_ref, f32[4,5,64,128]{3,2,1,0:T(8,128)S(1)} %all-to-all-done.refs_0_, bf16[256,256]{1,0:T(8,128)(2,1)S(1)} %get-tuple-element.34.refs_1_.refs_6_.refs_5_, ...), custom_call_target="tpu_custom_call" | custom-call | flops 1610612736 | bytes 4194304 | tf_op jit(solution)/shard_map/pallas_call | solution.py:528
  33.6 2.0 %collective-permute-done.8.refs_3_ = f32[4,64,128]{2,1,0:T(8,128)S(1)} collective-permute-done((f32[4,64,128]{2,1,0:T(8,128)}, f32[4,64,128]{2,1,0:T(8,128)S(1)}, u32[]{:S(2)}, u32[]{:S(2)}) %collective-permute-start.8) | collective-permute-done | bytes 131104 | tf_op jit(solution)/shard_map/ppermute | solution.py:443
  35.5 5.7 %shard_map.82 = (f32[4,32,8,128]{3,2,1,0:T(8,128)S(1)}, f32[2,8,128]{2,1,0:T(8,128)S(1)}) custom-call(f32[3]{0:T(128)S(1)} %shard_map.78.scalar_ref, s32[1]{0:T(128)} %bitcast.9.here_ref.refs_0_, f32[4,64,128]{2,1,0:T(8,128)S(1)} %copy-done.2, f32[4,64,128]{2,1,0:T(8,128)S(1)} %collective-permute-done.7.refs_2_, ...), custom_call_target="tpu_custom_call" | custom-call | flops 1610612736 | bytes 4194304 | tf_op jit(solution)/shard_map/pallas_call | solution.py:528
  41.2 3.4 %collective-permute-start.12 = (f32[2,8,128]{2,1,0:T(8,128)S(1)}, f32[2,8,128]{2,1,0:T(8,128)S(1)}, u32[]{:S(2)}, u32[]{:S(2)}) collective-permute-start(f32[2,8,128]{2,1,0:T(8,128)S(1)} %get-tuple-element.42.refs_0_.refs_1_), channel_id=1, source_target_pairs={{3,0},{0,1},{1,2},{2,3},{7,4},{4,5},{5,6},{6,7},{11,8},{8,9},{9,10... | collective-permute-start | bytes 24584 | tf_op jit(solution)/shard_map/ppermute | solution.py:443
  44.6 2.0 %collective-permute-start.11 = (f32[2,8,128]{2,1,0:T(8,128)S(1)}, f32[2,8,128]{2,1,0:T(8,128)S(1)}, u32[]{:S(2)}, u32[]{:S(2)}) collective-permute-start(f32[2,8,128]{2,1,0:T(8,128)S(1)} %get-tuple-element.42.refs_0_.refs_1_), channel_id=1, source_target_pairs={{2,0},{3,1},{0,2},{1,3},{6,4},{7,5},{4,6},{5,7},{10,8},{11,9},{8,1... | collective-permute-start | bytes 24584 | tf_op jit(solution)/shard_map/ppermute | solution.py:443
  50.2 6.4 %shard_map.83 = (f32[4,4,64,128]{3,2,1,0:T(8,128)}, f32[1]{0:T(128)}, f32[2,8,128]{2,1,0:T(8,128)S(1)}) custom-call(f32[3]{0:T(128)S(1)} %shard_map.78.scalar_ref, f32[2,8,128]{2,1,0:T(8,128)S(1)} %get-tuple-element.42.refs_0_.refs_1_, f32[2,8,128]{2,1,0:T(8,128)S(1)} %collective-permute-done.10.refs_1_, f32[2,8,128]{2,1,0:T(8,128)S(1)} %collective-permute-done.11.refs_2_, ...), custom_call_target="tpu_custom_call" | custom-call | flops 1610612736 | bytes 4194304 | tf_op jit(solution)/shard_map/pallas_call | solution.py:528
  56.6 3.5 %all-to-all-start.2 = ((f32[4,4,64,128]{3,2,1,0:T(8,128)}), f32[4,4,64,128]{3,2,1,0:T(8,128)S(1)}, u32[]{:S(2)}, u32[]{:S(2)}) async-start(f32[4,4,64,128]{3,2,1,0:T(8,128)} %get-tuple-element.48), calls=%async_computation.2 | async-start | bytes 1048576 | tf_op jit(solution)/shard_map/all_to_all | solution.py:439
  60.1 7.0 %shard_map.84 = (f32[4,4,64,128]{3,2,1,0:T(8,128)}, f32[8,128]{1,0:T(8,128)S(1)}) custom-call(f32[3]{0:T(128)S(1)} %shard_map.78.scalar_ref, f32[1]{0:T(128)} %get-tuple-element.44.refs_0_, f32[2,8,128]{2,1,0:T(8,128)S(1)} %get-tuple-element.42.refs_0_.refs_1_, f32[2,8,128]{2,1,0:T(8,128)S(1)} %get-tuple-element.45.refs_2_, ...), custom_call_target="tpu_custom_call" | custom-call | flops 1610612736 | bytes 4194304 | tf_op jit(solution)/shard_map/pallas_call | solution.py:528
  67.1 6.3 %all-to-all-done.2.piece_ref = f32[4,4,64,128]{3,2,1,0:T(8,128)S(1)} async-done(((f32[4,4,64,128]{3,2,1,0:T(8,128)}), f32[4,4,64,128]{3,2,1,0:T(8,128)S(1)}, u32[]{:S(2)}, u32[]{:S(2)}) %all-to-all-start.2) | async-done | bytes 524320 | tf_op jit(solution)/shard_map/all_to_all | solution.py:439
  73.4 3.5 %all-to-all-start.1 = ((f32[4,4,64,128]{3,2,1,0:T(8,128)}), f32[4,4,64,128]{3,2,1,0:T(8,128)S(1)}, u32[]{:S(2)}, u32[]{:S(2)}) async-start(f32[4,4,64,128]{3,2,1,0:T(8,128)} %get-tuple-element.47), calls=%async_computation.1 | async-start | bytes 1048576 | tf_op jit(solution)/shard_map/all_to_all | solution.py:439
  77.7 2.0 %collective-permute-start.15 = (f32[8,128]{1,0:T(8,128)S(1)}, f32[8,128]{1,0:T(8,128)S(1)}, u32[]{:S(2)}, u32[]{:S(2)}) collective-permute-start(f32[8,128]{1,0:T(8,128)S(1)} %get-tuple-element.51), channel_id=1, source_target_pairs={{3,0},{0,1},{1,2},{2,3},{7,4},{4,5},{5,6},{6,7},{11,8},{8,9},{9,10... | collective-permute-start | bytes 12296 | tf_op jit(solution)/shard_map/ppermute | solution.py:443
  79.7 1.9 %collective-permute-start.14 = (f32[8,128]{1,0:T(8,128)S(1)}, f32[8,128]{1,0:T(8,128)S(1)}, u32[]{:S(2)}, u32[]{:S(2)}) collective-permute-start(f32[8,128]{1,0:T(8,128)S(1)} %get-tuple-element.51), channel_id=1, source_target_pairs={{1,0},{2,1},{3,2},{0,3},{5,4},{6,5},{7,6},{4,7},{9,8},{10,9},{11,1... | collective-permute-start | bytes 12296 | tf_op jit(solution)/shard_map/ppermute | solution.py:443
  82.7 6.3 %collective-permute-done.15 = f32[8,128]{1,0:T(8,128)S(1)} collective-permute-done((f32[8,128]{1,0:T(8,128)S(1)}, f32[8,128]{1,0:T(8,128)S(1)}, u32[]{:S(2)}, u32[]{:S(2)}) %collective-permute-start.15) | collective-permute-done | bytes 4128 | tf_op jit(solution)/shard_map/ppermute | solution.py:443
  89.0 1.9 %collective-permute-done.13 = f32[8,128]{1,0:T(8,128)S(1)} collective-permute-done((f32[8,128]{1,0:T(8,128)S(1)}, f32[8,128]{1,0:T(8,128)S(1)}, u32[]{:S(2)}, u32[]{:S(2)}) %collective-permute-start.13) | collective-permute-done | bytes 4128 | tf_op jit(solution)/shard_map/ppermute | solution.py:443
  92.2 2.9 %collective-permute-start.19 = (f32[8,128]{1,0:T(8,128)S(1)}, f32[8,128]{1,0:T(8,128)S(1)}, u32[]{:S(2)}, u32[]{:S(2)}) collective-permute-start(f32[8,128]{1,0:T(8,128)S(1)} %add_add_fusion.refs_0_), channel_id=1, source_target_pairs={{16,0},{20,4},{24,8},{28,12},{0,16},{4,20},{8,24},{12,28},{17,1},{... | collective-permute-start | bytes 12296 | tf_op jit(solution)/shard_map/ppermute | solution.py:443
  95.1 1.8 %collective-permute-start.17 = (f32[8,128]{1,0:T(8,128)S(1)}, f32[8,128]{1,0:T(8,128)S(1)}, u32[]{:S(2)}, u32[]{:S(2)}) collective-permute-start(f32[8,128]{1,0:T(8,128)S(1)} %add_add_fusion.refs_0_), channel_id=1, source_target_pairs={{8,0},{12,4},{16,8},{20,12},{24,16},{28,20},{0,24},{4,28},{9,1},{1... | collective-permute-start | bytes 12296 | tf_op jit(solution)/shard_map/ppermute | solution.py:443
  (51 shorter events, 15.3 us)
Async XLA Ops:
  2.7 25.1 %all-to-all-start = ((f32[4,5,64,128]{3,2,1,0:T(8,128)}), f32[4,5,64,128]{3,2,1,0:T(8,128)S(1)}, u32[]{:S(2)}, u32[]{:S(2)}) async-start(f32[4,5,64,128]{3,2,1,0:T(8,128)} %shard_map.77), calls=%async_computation | async-start | bytes 1310720 | tf_op jit(solution)/shard_map/all_to_all | solution.py:439
  9.2 4.5 %collective-permute-start.6 = (f32[2,64]{1,0:T(2,128)S(1)}, f32[2,64]{1,0:T(2,128)S(1)}, u32[]{:S(2)}, u32[]{:S(2)}) collective-permute-start(f32[2,64]{1,0:T(2,128)S(1)} %copy-done.1), channel_id=1, source_target_pairs={{28,0},{0,4},{4,8},{8,12},{12,16},{16,20},{20,24},{24,28},{29,1},{... | collective-permute-start | bytes 1544 | tf_op jit(solution)/shard_map/ppermute | solution.py:443
  9.2 6.0 %collective-permute-start.5 = (f32[2,64]{1,0:T(2,128)S(1)}, f32[2,64]{1,0:T(2,128)S(1)}, u32[]{:S(2)}, u32[]{:S(2)}) collective-permute-start(f32[2,64]{1,0:T(2,128)S(1)} %copy-done.1), channel_id=1, source_target_pairs={{24,0},{28,4},{0,8},{4,12},{8,16},{12,20},{16,24},{20,28},{25,1},{... | collective-permute-start | bytes 1544 | tf_op jit(solution)/shard_map/ppermute | solution.py:443
  10.7 8.5 %collective-permute-start.4 = (f32[2,64]{1,0:T(2,128)S(1)}, f32[2,64]{1,0:T(2,128)S(1)}, u32[]{:S(2)}, u32[]{:S(2)}) collective-permute-start(f32[2,64]{1,0:T(2,128)S(1)} %copy-done.1), channel_id=1, source_target_pairs={{20,0},{24,4},{28,8},{0,12},{4,16},{8,20},{12,24},{16,28},{21,1},{... | collective-permute-start | bytes 1544 | tf_op jit(solution)/shard_map/ppermute | solution.py:443
  13.1 6.1 %collective-permute-start.3 = (f32[2,64]{1,0:T(2,128)S(1)}, f32[2,64]{1,0:T(2,128)S(1)}, u32[]{:S(2)}, u32[]{:S(2)}) collective-permute-start(f32[2,64]{1,0:T(2,128)S(1)} %copy-done.1), channel_id=1, source_target_pairs={{16,0},{20,4},{24,8},{28,12},{0,16},{4,20},{8,24},{12,28},{17,1},{... | collective-permute-start | bytes 1544 | tf_op jit(solution)/shard_map/ppermute | solution.py:443
  13.6 5.6 %collective-permute-start.2 = (f32[2,64]{1,0:T(2,128)S(1)}, f32[2,64]{1,0:T(2,128)S(1)}, u32[]{:S(2)}, u32[]{:S(2)}) collective-permute-start(f32[2,64]{1,0:T(2,128)S(1)} %copy-done.1), channel_id=1, source_target_pairs={{12,0},{16,4},{20,8},{24,12},{28,16},{0,20},{4,24},{8,28},{13,1},{... | collective-permute-start | bytes 1544 | tf_op jit(solution)/shard_map/ppermute | solution.py:443
  13.7 5.5 %collective-permute-start.1 = (f32[2,64]{1,0:T(2,128)S(1)}, f32[2,64]{1,0:T(2,128)S(1)}, u32[]{:S(2)}, u32[]{:S(2)}) collective-permute-start(f32[2,64]{1,0:T(2,128)S(1)} %copy-done.1), channel_id=1, source_target_pairs={{8,0},{12,4},{16,8},{20,12},{24,16},{28,20},{0,24},{4,28},{9,1},{1... | collective-permute-start | bytes 1544 | tf_op jit(solution)/shard_map/ppermute | solution.py:443
  15.2 4.1 %collective-permute-start = (f32[2,64]{1,0:T(2,128)S(1)}, f32[2,64]{1,0:T(2,128)S(1)}, u32[]{:S(2)}, u32[]{:S(2)}) collective-permute-start(f32[2,64]{1,0:T(2,128)S(1)} %copy-done.1), channel_id=1, source_target_pairs={{4,0},{8,4},{12,8},{16,12},{20,16},{24,20},{28,24},{0,28},{5,1},{9... | collective-permute-start | bytes 1544 | tf_op jit(solution)/shard_map/ppermute | solution.py:443
  21.9 11.6 %collective-permute-start.7 = (f32[4,64,128]{2,1,0:T(8,128)}, f32[4,64,128]{2,1,0:T(8,128)S(1)}, u32[]{:S(2)}, u32[]{:S(2)}) collective-permute-start(f32[4,64,128]{2,1,0:T(8,128)} %get-tuple-element.31), channel_id=1, source_target_pairs={{3,0},{0,1},{1,2},{2,3},{7,4},{4,5},{5,6},{6,7},{11,8},{8,9},{9,10... | collective-permute-start | bytes 393224 | tf_op jit(solution)/shard_map/ppermute | solution.py:443
  24.0 11.5 %collective-permute-start.8 = (f32[4,64,128]{2,1,0:T(8,128)}, f32[4,64,128]{2,1,0:T(8,128)S(1)}, u32[]{:S(2)}, u32[]{:S(2)}) collective-permute-start(f32[4,64,128]{2,1,0:T(8,128)} %get-tuple-element.32), channel_id=1, source_target_pairs={{2,0},{3,1},{0,2},{1,3},{6,4},{7,5},{4,6},{5,7},{10,8},{11,9},{8,1... | collective-permute-start | bytes 393224 | tf_op jit(solution)/shard_map/ppermute | solution.py:443
  26.4 9.2 %collective-permute-start.9 = (f32[4,64,128]{2,1,0:T(8,128)}, f32[4,64,128]{2,1,0:T(8,128)S(1)}, u32[]{:S(2)}, u32[]{:S(2)}) collective-permute-start(f32[4,64,128]{2,1,0:T(8,128)} %get-tuple-element.33), channel_id=1, source_target_pairs={{1,0},{2,1},{3,2},{0,3},{5,4},{6,5},{7,6},{4,7},{9,8},{10,9},{11,1... | collective-permute-start | bytes 393224 | tf_op jit(solution)/shard_map/ppermute | solution.py:443
  41.2 6.5 %collective-permute-start.12 = (f32[2,8,128]{2,1,0:T(8,128)S(1)}, f32[2,8,128]{2,1,0:T(8,128)S(1)}, u32[]{:S(2)}, u32[]{:S(2)}) collective-permute-start(f32[2,8,128]{2,1,0:T(8,128)S(1)} %get-tuple-element.42.refs_0_.refs_1_), channel_id=1, source_target_pairs={{3,0},{0,1},{1,2},{2,3},{7,4},{4,5},{5,6},{6,7},{11,8},{8,9},{9,10... | collective-permute-start | bytes 24584 | tf_op jit(solution)/shard_map/ppermute | solution.py:443
  44.6 4.5 %collective-permute-start.11 = (f32[2,8,128]{2,1,0:T(8,128)S(1)}, f32[2,8,128]{2,1,0:T(8,128)S(1)}, u32[]{:S(2)}, u32[]{:S(2)}) collective-permute-start(f32[2,8,128]{2,1,0:T(8,128)S(1)} %get-tuple-element.42.refs_0_.refs_1_), channel_id=1, source_target_pairs={{2,0},{3,1},{0,2},{1,3},{6,4},{7,5},{4,6},{5,7},{10,8},{11,9},{8,1... | collective-permute-start | bytes 24584 | tf_op jit(solution)/shard_map/ppermute | solution.py:443
  46.6 3.7 %collective-permute-start.10 = (f32[2,8,128]{2,1,0:T(8,128)S(1)}, f32[2,8,128]{2,1,0:T(8,128)S(1)}, u32[]{:S(2)}, u32[]{:S(2)}) collective-permute-start(f32[2,8,128]{2,1,0:T(8,128)S(1)} %get-tuple-element.42.refs_0_.refs_1_), channel_id=1, source_target_pairs={{1,0},{2,1},{3,2},{0,3},{5,4},{6,5},{7,6},{4,7},{9,8},{10,9},{11,1... | collective-permute-start | bytes 24584 | tf_op jit(solution)/shard_map/ppermute | solution.py:443
  56.6 16.8 %all-to-all-start.2 = ((f32[4,4,64,128]{3,2,1,0:T(8,128)}), f32[4,4,64,128]{3,2,1,0:T(8,128)S(1)}, u32[]{:S(2)}, u32[]{:S(2)}) async-start(f32[4,4,64,128]{3,2,1,0:T(8,128)} %get-tuple-element.48), calls=%async_computation.2 | async-start | bytes 1048576 | tf_op jit(solution)/shard_map/all_to_all | solution.py:439
  73.4 24.5 %all-to-all-start.1 = ((f32[4,4,64,128]{3,2,1,0:T(8,128)}), f32[4,4,64,128]{3,2,1,0:T(8,128)S(1)}, u32[]{:S(2)}, u32[]{:S(2)}) async-start(f32[4,4,64,128]{3,2,1,0:T(8,128)} %get-tuple-element.47), calls=%async_computation.1 | async-start | bytes 1048576 | tf_op jit(solution)/shard_map/all_to_all | solution.py:439
  77.7 11.3 %collective-permute-start.15 = (f32[8,128]{1,0:T(8,128)S(1)}, f32[8,128]{1,0:T(8,128)S(1)}, u32[]{:S(2)}, u32[]{:S(2)}) collective-permute-start(f32[8,128]{1,0:T(8,128)S(1)} %get-tuple-element.51), channel_id=1, source_target_pairs={{3,0},{0,1},{1,2},{2,3},{7,4},{4,5},{5,6},{6,7},{11,8},{8,9},{9,10... | collective-permute-start | bytes 12296 | tf_op jit(solution)/shard_map/ppermute | solution.py:443
  79.7 9.3 %collective-permute-start.14 = (f32[8,128]{1,0:T(8,128)S(1)}, f32[8,128]{1,0:T(8,128)S(1)}, u32[]{:S(2)}, u32[]{:S(2)}) collective-permute-start(f32[8,128]{1,0:T(8,128)S(1)} %get-tuple-element.51), channel_id=1, source_target_pairs={{1,0},{2,1},{3,2},{0,3},{5,4},{6,5},{7,6},{4,7},{9,8},{10,9},{11,1... | collective-permute-start | bytes 12296 | tf_op jit(solution)/shard_map/ppermute | solution.py:443
  81.6 9.3 %collective-permute-start.13 = (f32[8,128]{1,0:T(8,128)S(1)}, f32[8,128]{1,0:T(8,128)S(1)}, u32[]{:S(2)}, u32[]{:S(2)}) collective-permute-start(f32[8,128]{1,0:T(8,128)S(1)} %get-tuple-element.51), channel_id=1, source_target_pairs={{2,0},{3,1},{0,2},{1,3},{6,4},{7,5},{4,6},{5,7},{10,8},{11,9},{8,1... | collective-permute-start | bytes 12296 | tf_op jit(solution)/shard_map/ppermute | solution.py:443
  90.9 4.2 %collective-permute-start.22 = (f32[8,128]{1,0:T(8,128)S(1)}, f32[8,128]{1,0:T(8,128)S(1)}, u32[]{:S(2)}, u32[]{:S(2)}) collective-permute-start(f32[8,128]{1,0:T(8,128)S(1)} %add_add_fusion.refs_0_), channel_id=1, source_target_pairs={{28,0},{0,4},{4,8},{8,12},{12,16},{16,20},{20,24},{24,28},{29,1},{... | collective-permute-start | bytes 12296 | tf_op jit(solution)/shard_map/ppermute | solution.py:443
  90.9 6.0 %collective-permute-start.21 = (f32[8,128]{1,0:T(8,128)S(1)}, f32[8,128]{1,0:T(8,128)S(1)}, u32[]{:S(2)}, u32[]{:S(2)}) collective-permute-start(f32[8,128]{1,0:T(8,128)S(1)} %add_add_fusion.refs_0_), channel_id=1, source_target_pairs={{24,0},{28,4},{0,8},{4,12},{8,16},{12,20},{16,24},{20,28},{25,1},{... | collective-permute-start | bytes 12296 | tf_op jit(solution)/shard_map/ppermute | solution.py:443
  92.2 6.5 %collective-permute-start.20 = (f32[8,128]{1,0:T(8,128)S(1)}, f32[8,128]{1,0:T(8,128)S(1)}, u32[]{:S(2)}, u32[]{:S(2)}) collective-permute-start(f32[8,128]{1,0:T(8,128)S(1)} %add_add_fusion.refs_0_), channel_id=1, source_target_pairs={{20,0},{24,4},{28,8},{0,12},{4,16},{8,20},{12,24},{16,28},{21,1},{... | collective-permute-start | bytes 12296 | tf_op jit(solution)/shard_map/ppermute | solution.py:443
  92.2 6.5 %collective-permute-start.19 = (f32[8,128]{1,0:T(8,128)S(1)}, f32[8,128]{1,0:T(8,128)S(1)}, u32[]{:S(2)}, u32[]{:S(2)}) collective-permute-start(f32[8,128]{1,0:T(8,128)S(1)} %add_add_fusion.refs_0_), channel_id=1, source_target_pairs={{16,0},{20,4},{24,8},{28,12},{0,16},{4,20},{8,24},{12,28},{17,1},{... | collective-permute-start | bytes 12296 | tf_op jit(solution)/shard_map/ppermute | solution.py:443
  95.1 3.6 %collective-permute-start.17 = (f32[8,128]{1,0:T(8,128)S(1)}, f32[8,128]{1,0:T(8,128)S(1)}, u32[]{:S(2)}, u32[]{:S(2)}) collective-permute-start(f32[8,128]{1,0:T(8,128)S(1)} %add_add_fusion.refs_0_), channel_id=1, source_target_pairs={{8,0},{12,4},{16,8},{20,12},{24,16},{28,20},{0,24},{4,28},{9,1},{1... | collective-permute-start | bytes 12296 | tf_op jit(solution)/shard_map/ppermute | solution.py:443
  (6 other events, 40.0 us)

commit v7 on v6

--- a/solution.py
+++ b/solution.py
@@ -609,13 +609,13 @@
             (),
             2,
         )
-        first_result, message = lax.optimization_barrier((result[0], message))
-        result = [first_result]
+    message = fold([message] + [shifted(message, "grid", parts, step) for step in range(1, parts)])
+    if last_count:
+        last_pieces, message = lax.optimization_barrier((last_pieces, message))
         result = [give_back(last_pieces, last_count, main_count)]
     result = result[0]
     orbitals_out = planes_of(result).reshape(2, norb, planes, points)
 
-    message = fold([message] + [shifted(message, "grid", parts, step) for step in range(1, parts)])
     messages = [message] + [shifted(message, "macro", blocks, step) for step in range(1, blocks)]
     fields_out = pl.pallas_call(
         functools.partial(fields_kernel, blocks, owned),

time: 101 us -> 93.4 us (0.925)
  waiting for transfers between devices: 20.1 us -> 9.89 us
  starting transfers between devices: 45.1 us -> 47.3 us
    all_to_all x3, waiting for transfers between devices: 6.26 us -> 0.01 us  [exchanged(): return lax.all_to_all(value, axes, split_axis=0, concat_axis=0, tiled=True)]
    ppermute x23, waiting for transfers between devices: 13.8 us -> 9.88 us  [shifted(): lax.ppermute(value, axis_name, [((index + shift) % count, index) for inde...]
    ppermute x23, starting transfers between devices: 31.7 us -> 33.9 us  [shifted(): lax.ppermute(value, axis_name, [((index + shift) % count, index) for inde...]
  transfers between devices with their start and end apart: 26 -> 26, of which waited for: 8 -> 9; matrix products, arithmetic and copies ran while one was open for 0% -> 0% of each run, Pallas kernels for 18% -> 20%
where the time goes in v7:
time: 93.4 us; the launch traced here: 92 us
  starting transfers between devices  47.3 us (51%)
  Pallas kernels  33 us (35%)
  waiting for transfers between devices  9.89 us (11%)
  between operations  1.46 us (2%)
    ppermute x23, starting transfers between devices, shifted(): lax.ppermute(value, axis_name, [((index + shift) % count, index) for inde...  33.9 us
    pallas_call x4, Pallas kernels, micro_call(): pl.pallas_call(kernel, out_shape=outputs, in_specs=[smem() if number < sc...  24.8 us
    all_to_all x3, starting transfers between devices, exchanged(): return lax.all_to_all(value, axes, split_axis=0, concat_axis=0, tiled=True)  13.4 us
    ppermute x23, waiting for transfers between devices, shifted(): lax.ppermute(value, axis_name, [((index + shift) % count, index) for inde...  9.88 us
    pallas_call x1, Pallas kernels, per_device(): pl.pallas_call(functools.partial(pack_kernel, parts, share, main_count, 0...  2.06 us
    pallas_call x1, Pallas kernels, per_device(): pl.pallas_call(functools.partial(pack_pieces_kernel, parts, share, last_c...  1.93 us
  transfers between devices with their start and end apart: 26, of which 9 were waited for; matrix products, arithmetic and copies ran while one was open for 0% of the time, Pallas kernels for 20%

profile of v7, /device:TPU:0, one launch (start us, length us, event | category | flops | bytes accessed | tf_op | source)
XLA Modules:
  0.0 92.0 jit_solution(158943897090409701)
XLA Ops:
  0.6 2.1 %shard_map.77 = f32[4,5,64,128]{3,2,1,0:T(8,128)} custom-call(f32[2,16,64,128]{3,2,1,0:T(8,128)} %bitcast.19, f32[64,128]{1,0:T(8,128)} %bitcast.22), custom_call_target="tpu_custom_call" | custom-call | tf_op jit(solution)/shard_map/pallas_call | solution.py:474
  2.7 6.5 %all-to-all-start = ((f32[4,5,64,128]{3,2,1,0:T(8,128)}), f32[4,5,64,128]{3,2,1,0:T(8,128)S(1)}, u32[]{:S(2)}, u32[]{:S(2)}) async-start(f32[4,5,64,128]{3,2,1,0:T(8,128)} %shard_map.77), calls=%async_computation | async-start | bytes 1310720 | tf_op jit(solution)/shard_map/all_to_all | solution.py:439
  9.2 1.5 %collective-permute-start.5 = (f32[2,64]{1,0:T(2,128)S(1)}, f32[2,64]{1,0:T(2,128)S(1)}, u32[]{:S(2)}, u32[]{:S(2)}) collective-permute-start(f32[2,64]{1,0:T(2,128)S(1)} %copy-done.1), channel_id=1, source_target_pairs={{24,0},{28,4},{0,8},{4,12},{8,16},{12,20},{16,24},{20,28},{25,1},{... | collective-permute-start | bytes 1544 | tf_op jit(solution)/shard_map/ppermute | solution.py:443
  10.7 2.4 %collective-permute-start.4 = (f32[2,64]{1,0:T(2,128)S(1)}, f32[2,64]{1,0:T(2,128)S(1)}, u32[]{:S(2)}, u32[]{:S(2)}) collective-permute-start(f32[2,64]{1,0:T(2,128)S(1)} %copy-done.1), channel_id=1, source_target_pairs={{20,0},{24,4},{28,8},{0,12},{4,16},{8,20},{12,24},{16,28},{21,1},{... | collective-permute-start | bytes 1544 | tf_op jit(solution)/shard_map/ppermute | solution.py:443
  13.7 1.4 %collective-permute-start.1 = (f32[2,64]{1,0:T(2,128)S(1)}, f32[2,64]{1,0:T(2,128)S(1)}, u32[]{:S(2)}, u32[]{:S(2)}) collective-permute-start(f32[2,64]{1,0:T(2,128)S(1)} %copy-done.1), channel_id=1, source_target_pairs={{8,0},{12,4},{16,8},{20,12},{24,16},{28,20},{0,24},{4,28},{9,1},{1... | collective-permute-start | bytes 1544 | tf_op jit(solution)/shard_map/ppermute | solution.py:443
  15.2 2.3 %collective-permute-start = (f32[2,64]{1,0:T(2,128)S(1)}, f32[2,64]{1,0:T(2,128)S(1)}, u32[]{:S(2)}, u32[]{:S(2)}) collective-permute-start(f32[2,64]{1,0:T(2,128)S(1)} %copy-done.1), channel_id=1, source_target_pairs={{4,0},{8,4},{12,8},{16,12},{20,16},{24,20},{28,24},{0,28},{5,1},{9... | collective-permute-start | bytes 1544 | tf_op jit(solution)/shard_map/ppermute | solution.py:443
  20.0 1.9 %shard_map.79 = (f32[4,64,128]{2,1,0:T(8,128)}, f32[4,64,128]{2,1,0:T(8,128)}, f32[4,64,128]{2,1,0:T(8,128)}, f32[4,64,128]{2,1,0:T(8,128)}) custom-call(s32[1]{0:T(128)} %bitcast.9.here_ref.refs_0_, f32[2,16,64,128]{3,2,1,0:T(8,128)} %bitcast.20), custom_call_target="tpu_custom_call" | custom-call | tf_op jit(solution)/shard_map/pallas_call | solution.py:511
  21.9 2.1 %collective-permute-start.7 = (f32[4,64,128]{2,1,0:T(8,128)}, f32[4,64,128]{2,1,0:T(8,128)S(1)}, u32[]{:S(2)}, u32[]{:S(2)}) collective-permute-start(f32[4,64,128]{2,1,0:T(8,128)} %get-tuple-element.31), channel_id=1, source_target_pairs={{3,0},{0,1},{1,2},{2,3},{7,4},{4,5},{5,6},{6,7},{11,8},{8,9},{9,10... | collective-permute-start | bytes 393224 | tf_op jit(solution)/shard_map/ppermute | solution.py:443
  24.0 2.4 %collective-permute-start.8 = (f32[4,64,128]{2,1,0:T(8,128)}, f32[4,64,128]{2,1,0:T(8,128)S(1)}, u32[]{:S(2)}, u32[]{:S(2)}) collective-permute-start(f32[4,64,128]{2,1,0:T(8,128)} %get-tuple-element.32), channel_id=1, source_target_pairs={{2,0},{3,1},{0,2},{1,3},{6,4},{7,5},{4,6},{5,7},{10,8},{11,9},{8,1... | collective-permute-start | bytes 393224 | tf_op jit(solution)/shard_map/ppermute | solution.py:443
  26.4 1.5 %collective-permute-start.9 = (f32[4,64,128]{2,1,0:T(8,128)}, f32[4,64,128]{2,1,0:T(8,128)S(1)}, u32[]{:S(2)}, u32[]{:S(2)}) collective-permute-start(f32[4,64,128]{2,1,0:T(8,128)} %get-tuple-element.33), channel_id=1, source_target_pairs={{1,0},{2,1},{3,2},{0,3},{5,4},{6,5},{7,6},{4,7},{9,8},{10,9},{11,1... | collective-permute-start | bytes 393224 | tf_op jit(solution)/shard_map/ppermute | solution.py:443
  27.8 5.7 %shard_map.81 = (f32[4,32,8,128]{3,2,1,0:T(8,128)S(1)}, f32[2,8,128]{2,1,0:T(8,128)S(1)}, f32[32,8,128]{2,1,0:T(8,128)S(1)}) custom-call(f32[3]{0:T(128)S(1)} %shard_map.78.scalar_ref, f32[4,5,64,128]{3,2,1,0:T(8,128)S(1)} %all-to-all-done.refs_0_, bf16[256,256]{1,0:T(8,128)(2,1)S(1)} %get-tuple-element.34.refs_1_.refs_6_.refs_5_, ...), custom_call_target="tpu_custom_call" | custom-call | flops 1610612736 | bytes 4194304 | tf_op jit(solution)/shard_map/pallas_call | solution.py:528
  33.6 2.0 %collective-permute-done.8.refs_3_ = f32[4,64,128]{2,1,0:T(8,128)S(1)} collective-permute-done((f32[4,64,128]{2,1,0:T(8,128)}, f32[4,64,128]{2,1,0:T(8,128)S(1)}, u32[]{:S(2)}, u32[]{:S(2)}) %collective-permute-start.8) | collective-permute-done | bytes 131104 | tf_op jit(solution)/shard_map/ppermute | solution.py:443
  35.5 5.7 %shard_map.82 = (f32[4,32,8,128]{3,2,1,0:T(8,128)S(1)}, f32[2,8,128]{2,1,0:T(8,128)S(1)}) custom-call(f32[3]{0:T(128)S(1)} %shard_map.78.scalar_ref, s32[1]{0:T(128)} %bitcast.9.here_ref.refs_0_, f32[4,64,128]{2,1,0:T(8,128)S(1)} %copy-done.2, f32[4,64,128]{2,1,0:T(8,128)S(1)} %collective-permute-done.7.refs_2_, ...), custom_call_target="tpu_custom_call" | custom-call | flops 1610612736 | bytes 4194304 | tf_op jit(solution)/shard_map/pallas_call | solution.py:528
  41.3 3.4 %collective-permute-start.12 = (f32[2,8,128]{2,1,0:T(8,128)S(1)}, f32[2,8,128]{2,1,0:T(8,128)S(1)}, u32[]{:S(2)}, u32[]{:S(2)}) collective-permute-start(f32[2,8,128]{2,1,0:T(8,128)S(1)} %get-tuple-element.42.refs_0_.refs_1_), channel_id=1, source_target_pairs={{3,0},{0,1},{1,2},{2,3},{7,4},{4,5},{5,6},{6,7},{11,8},{8,9},{9,10... | collective-permute-start | bytes 24584 | tf_op jit(solution)/shard_map/ppermute | solution.py:443
  44.6 2.0 %collective-permute-start.11 = (f32[2,8,128]{2,1,0:T(8,128)S(1)}, f32[2,8,128]{2,1,0:T(8,128)S(1)}, u32[]{:S(2)}, u32[]{:S(2)}) collective-permute-start(f32[2,8,128]{2,1,0:T(8,128)S(1)} %get-tuple-element.42.refs_0_.refs_1_), channel_id=1, source_target_pairs={{2,0},{3,1},{0,2},{1,3},{6,4},{7,5},{4,6},{5,7},{10,8},{11,9},{8,1... | collective-permute-start | bytes 24584 | tf_op jit(solution)/shard_map/ppermute | solution.py:443
  50.3 6.4 %shard_map.83 = (f32[4,4,64,128]{3,2,1,0:T(8,128)}, f32[1]{0:T(128)}, f32[2,8,128]{2,1,0:T(8,128)S(1)}) custom-call(f32[3]{0:T(128)S(1)} %shard_map.78.scalar_ref, f32[2,8,128]{2,1,0:T(8,128)S(1)} %get-tuple-element.42.refs_0_.refs_1_, f32[2,8,128]{2,1,0:T(8,128)S(1)} %collective-permute-done.10.refs_1_, f32[2,8,128]{2,1,0:T(8,128)S(1)} %collective-permute-done.11.refs_2_, ...), custom_call_target="tpu_custom_call" | custom-call | flops 1610612736 | bytes 4194304 | tf_op jit(solution)/shard_map/pallas_call | solution.py:528
  56.7 3.5 %all-to-all-start.2 = ((f32[4,4,64,128]{3,2,1,0:T(8,128)}), f32[4,4,64,128]{3,2,1,0:T(8,128)S(1)}, u32[]{:S(2)}, u32[]{:S(2)}) async-start(f32[4,4,64,128]{3,2,1,0:T(8,128)} %get-tuple-element.50), calls=%async_computation.2 | async-start | bytes 1048576 | tf_op jit(solution)/shard_map/all_to_all | solution.py:439
  60.2 7.0 %shard_map.84 = (f32[4,4,64,128]{3,2,1,0:T(8,128)}, f32[8,128]{1,0:T(8,128)S(1)}) custom-call(f32[3]{0:T(128)S(1)} %shard_map.78.scalar_ref, f32[1]{0:T(128)} %get-tuple-element.44.refs_0_, f32[2,8,128]{2,1,0:T(8,128)S(1)} %get-tuple-element.42.refs_0_.refs_1_, f32[2,8,128]{2,1,0:T(8,128)S(1)} %get-tuple-element.45.refs_2_, ...), custom_call_target="tpu_custom_call" | custom-call | flops 1610612736 | bytes 4194304 | tf_op jit(solution)/shard_map/pallas_call | solution.py:528
  67.2 2.0 %collective-permute-start.15 = (f32[8,128]{1,0:T(8,128)S(1)}, f32[8,128]{1,0:T(8,128)S(1)}, u32[]{:S(2)}, u32[]{:S(2)}) collective-permute-start(f32[8,128]{1,0:T(8,128)S(1)} %get-tuple-element.48), channel_id=1, source_target_pairs={{3,0},{0,1},{1,2},{2,3},{7,4},{4,5},{5,6},{6,7},{11,8},{8,9},{9,10... | collective-permute-start | bytes 12296 | tf_op jit(solution)/shard_map/ppermute | solution.py:443
  69.2 1.8 %collective-permute-start.14 = (f32[8,128]{1,0:T(8,128)S(1)}, f32[8,128]{1,0:T(8,128)S(1)}, u32[]{:S(2)}, u32[]{:S(2)}) collective-permute-start(f32[8,128]{1,0:T(8,128)S(1)} %get-tuple-element.48), channel_id=1, source_target_pairs={{1,0},{2,1},{3,2},{0,3},{5,4},{6,5},{7,6},{4,7},{9,8},{10,9},{11,1... | collective-permute-start | bytes 12296 | tf_op jit(solution)/shard_map/ppermute | solution.py:443
  73.2 2.3 %collective-permute-done.13 = f32[8,128]{1,0:T(8,128)S(1)} collective-permute-done((f32[8,128]{1,0:T(8,128)S(1)}, f32[8,128]{1,0:T(8,128)S(1)}, u32[]{:S(2)}, u32[]{:S(2)}) %collective-permute-start.13) | collective-permute-done | bytes 4128 | tf_op jit(solution)/shard_map/ppermute | solution.py:443
  75.5 3.5 %all-to-all-start.1 = ((f32[4,4,64,128]{3,2,1,0:T(8,128)}), f32[4,4,64,128]{3,2,1,0:T(8,128)S(1)}, u32[]{:S(2)}, u32[]{:S(2)}) async-start(f32[4,4,64,128]{3,2,1,0:T(8,128)} %get-tuple-element.49), calls=%async_computation.1 | async-start | bytes 1048576 | tf_op jit(solution)/shard_map/all_to_all | solution.py:439
  80.3 3.9 %collective-permute-start.20 = (f32[8,128]{1,0:T(8,128)S(1)}, f32[8,128]{1,0:T(8,128)S(1)}, u32[]{:S(2)}, u32[]{:S(2)}) collective-permute-start(f32[8,128]{1,0:T(8,128)S(1)} %add_add_fusion.refs_0_), channel_id=1, source_target_pairs={{20,0},{24,4},{28,8},{0,12},{4,16},{8,20},{12,24},{16,28},{21,1},{... | collective-permute-start | bytes 12296 | tf_op jit(solution)/shard_map/ppermute | solution.py:443
  86.0 2.1 %collective-permute-start.16 = (f32[8,128]{1,0:T(8,128)S(1)}, f32[8,128]{1,0:T(8,128)S(1)}, u32[]{:S(2)}, u32[]{:S(2)}) collective-permute-start(f32[8,128]{1,0:T(8,128)S(1)} %add_add_fusion.refs_0_), channel_id=1, source_target_pairs={{4,0},{8,4},{12,8},{16,12},{20,16},{24,20},{28,24},{0,28},{5,1},{9... | collective-permute-start | bytes 12296 | tf_op jit(solution)/shard_map/ppermute | solution.py:443
  (51 shorter events, 15.2 us)
Async XLA Ops:
  2.7 25.1 %all-to-all-start = ((f32[4,5,64,128]{3,2,1,0:T(8,128)}), f32[4,5,64,128]{3,2,1,0:T(8,128)S(1)}, u32[]{:S(2)}, u32[]{:S(2)}) async-start(f32[4,5,64,128]{3,2,1,0:T(8,128)} %shard_map.77), calls=%async_computation | async-start | bytes 1310720 | tf_op jit(solution)/shard_map/all_to_all | solution.py:439
  9.2 4.5 %collective-permute-start.6 = (f32[2,64]{1,0:T(2,128)S(1)}, f32[2,64]{1,0:T(2,128)S(1)}, u32[]{:S(2)}, u32[]{:S(2)}) collective-permute-start(f32[2,64]{1,0:T(2,128)S(1)} %copy-done.1), channel_id=1, source_target_pairs={{28,0},{0,4},{4,8},{8,12},{12,16},{16,20},{20,24},{24,28},{29,1},{... | collective-permute-start | bytes 1544 | tf_op jit(solution)/shard_map/ppermute | solution.py:443
  9.2 6.0 %collective-permute-start.5 = (f32[2,64]{1,0:T(2,128)S(1)}, f32[2,64]{1,0:T(2,128)S(1)}, u32[]{:S(2)}, u32[]{:S(2)}) collective-permute-start(f32[2,64]{1,0:T(2,128)S(1)} %copy-done.1), channel_id=1, source_target_pairs={{24,0},{28,4},{0,8},{4,12},{8,16},{12,20},{16,24},{20,28},{25,1},{... | collective-permute-start | bytes 1544 | tf_op jit(solution)/shard_map/ppermute | solution.py:443
  10.7 8.5 %collective-permute-start.4 = (f32[2,64]{1,0:T(2,128)S(1)}, f32[2,64]{1,0:T(2,128)S(1)}, u32[]{:S(2)}, u32[]{:S(2)}) collective-permute-start(f32[2,64]{1,0:T(2,128)S(1)} %copy-done.1), channel_id=1, source_target_pairs={{20,0},{24,4},{28,8},{0,12},{4,16},{8,20},{12,24},{16,28},{21,1},{... | collective-permute-start | bytes 1544 | tf_op jit(solution)/shard_map/ppermute | solution.py:443
  13.1 6.1 %collective-permute-start.3 = (f32[2,64]{1,0:T(2,128)S(1)}, f32[2,64]{1,0:T(2,128)S(1)}, u32[]{:S(2)}, u32[]{:S(2)}) collective-permute-start(f32[2,64]{1,0:T(2,128)S(1)} %copy-done.1), channel_id=1, source_target_pairs={{16,0},{20,4},{24,8},{28,12},{0,16},{4,20},{8,24},{12,28},{17,1},{... | collective-permute-start | bytes 1544 | tf_op jit(solution)/shard_map/ppermute | solution.py:443
  13.6 5.6 %collective-permute-start.2 = (f32[2,64]{1,0:T(2,128)S(1)}, f32[2,64]{1,0:T(2,128)S(1)}, u32[]{:S(2)}, u32[]{:S(2)}) collective-permute-start(f32[2,64]{1,0:T(2,128)S(1)} %copy-done.1), channel_id=1, source_target_pairs={{12,0},{16,4},{20,8},{24,12},{28,16},{0,20},{4,24},{8,28},{13,1},{... | collective-permute-start | bytes 1544 | tf_op jit(solution)/shard_map/ppermute | solution.py:443
  13.7 5.5 %collective-permute-start.1 = (f32[2,64]{1,0:T(2,128)S(1)}, f32[2,64]{1,0:T(2,128)S(1)}, u32[]{:S(2)}, u32[]{:S(2)}) collective-permute-start(f32[2,64]{1,0:T(2,128)S(1)} %copy-done.1), channel_id=1, source_target_pairs={{8,0},{12,4},{16,8},{20,12},{24,16},{28,20},{0,24},{4,28},{9,1},{1... | collective-permute-start | bytes 1544 | tf_op jit(solution)/shard_map/ppermute | solution.py:443
  15.2 4.1 %collective-permute-start = (f32[2,64]{1,0:T(2,128)S(1)}, f32[2,64]{1,0:T(2,128)S(1)}, u32[]{:S(2)}, u32[]{:S(2)}) collective-permute-start(f32[2,64]{1,0:T(2,128)S(1)} %copy-done.1), channel_id=1, source_target_pairs={{4,0},{8,4},{12,8},{16,12},{20,16},{24,20},{28,24},{0,28},{5,1},{9... | collective-permute-start | bytes 1544 | tf_op jit(solution)/shard_map/ppermute | solution.py:443
  21.9 11.6 %collective-permute-start.7 = (f32[4,64,128]{2,1,0:T(8,128)}, f32[4,64,128]{2,1,0:T(8,128)S(1)}, u32[]{:S(2)}, u32[]{:S(2)}) collective-permute-start(f32[4,64,128]{2,1,0:T(8,128)} %get-tuple-element.31), channel_id=1, source_target_pairs={{3,0},{0,1},{1,2},{2,3},{7,4},{4,5},{5,6},{6,7},{11,8},{8,9},{9,10... | collective-permute-start | bytes 393224 | tf_op jit(solution)/shard_map/ppermute | solution.py:443
  24.0 11.5 %collective-permute-start.8 = (f32[4,64,128]{2,1,0:T(8,128)}, f32[4,64,128]{2,1,0:T(8,128)S(1)}, u32[]{:S(2)}, u32[]{:S(2)}) collective-permute-start(f32[4,64,128]{2,1,0:T(8,128)} %get-tuple-element.32), channel_id=1, source_target_pairs={{2,0},{3,1},{0,2},{1,3},{6,4},{7,5},{4,6},{5,7},{10,8},{11,9},{8,1... | collective-permute-start | bytes 393224 | tf_op jit(solution)/shard_map/ppermute | solution.py:443
  26.4 9.2 %collective-permute-start.9 = (f32[4,64,128]{2,1,0:T(8,128)}, f32[4,64,128]{2,1,0:T(8,128)S(1)}, u32[]{:S(2)}, u32[]{:S(2)}) collective-permute-start(f32[4,64,128]{2,1,0:T(8,128)} %get-tuple-element.33), channel_id=1, source_target_pairs={{1,0},{2,1},{3,2},{0,3},{5,4},{6,5},{7,6},{4,7},{9,8},{10,9},{11,1... | collective-permute-start | bytes 393224 | tf_op jit(solution)/shard_map/ppermute | solution.py:443
  41.3 6.5 %collective-permute-start.12 = (f32[2,8,128]{2,1,0:T(8,128)S(1)}, f32[2,8,128]{2,1,0:T(8,128)S(1)}, u32[]{:S(2)}, u32[]{:S(2)}) collective-permute-start(f32[2,8,128]{2,1,0:T(8,128)S(1)} %get-tuple-element.42.refs_0_.refs_1_), channel_id=1, source_target_pairs={{3,0},{0,1},{1,2},{2,3},{7,4},{4,5},{5,6},{6,7},{11,8},{8,9},{9,10... | collective-permute-start | bytes 24584 | tf_op jit(solution)/shard_map/ppermute | solution.py:443
  44.6 4.5 %collective-permute-start.11 = (f32[2,8,128]{2,1,0:T(8,128)S(1)}, f32[2,8,128]{2,1,0:T(8,128)S(1)}, u32[]{:S(2)}, u32[]{:S(2)}) collective-permute-start(f32[2,8,128]{2,1,0:T(8,128)S(1)} %get-tuple-element.42.refs_0_.refs_1_), channel_id=1, source_target_pairs={{2,0},{3,1},{0,2},{1,3},{6,4},{7,5},{4,6},{5,7},{10,8},{11,9},{8,1... | collective-permute-start | bytes 24584 | tf_op jit(solution)/shard_map/ppermute | solution.py:443
  46.6 3.7 %collective-permute-start.10 = (f32[2,8,128]{2,1,0:T(8,128)S(1)}, f32[2,8,128]{2,1,0:T(8,128)S(1)}, u32[]{:S(2)}, u32[]{:S(2)}) collective-permute-start(f32[2,8,128]{2,1,0:T(8,128)S(1)} %get-tuple-element.42.refs_0_.refs_1_), channel_id=1, source_target_pairs={{1,0},{2,1},{3,2},{0,3},{5,4},{6,5},{7,6},{4,7},{9,8},{10,9},{11,1... | collective-permute-start | bytes 24584 | tf_op jit(solution)/shard_map/ppermute | solution.py:443
  56.7 18.8 %all-to-all-start.2 = ((f32[4,4,64,128]{3,2,1,0:T(8,128)}), f32[4,4,64,128]{3,2,1,0:T(8,128)S(1)}, u32[]{:S(2)}, u32[]{:S(2)}) async-start(f32[4,4,64,128]{3,2,1,0:T(8,128)} %get-tuple-element.50), calls=%async_computation.2 | async-start | bytes 1048576 | tf_op jit(solution)/shard_map/all_to_all | solution.py:439
  67.2 5.5 %collective-permute-start.15 = (f32[8,128]{1,0:T(8,128)S(1)}, f32[8,128]{1,0:T(8,128)S(1)}, u32[]{:S(2)}, u32[]{:S(2)}) collective-permute-start(f32[8,128]{1,0:T(8,128)S(1)} %get-tuple-element.48), channel_id=1, source_target_pairs={{3,0},{0,1},{1,2},{2,3},{7,4},{4,5},{5,6},{6,7},{11,8},{8,9},{9,10... | collective-permute-start | bytes 12296 | tf_op jit(solution)/shard_map/ppermute | solution.py:443
  69.2 4.0 %collective-permute-start.14 = (f32[8,128]{1,0:T(8,128)S(1)}, f32[8,128]{1,0:T(8,128)S(1)}, u32[]{:S(2)}, u32[]{:S(2)}) collective-permute-start(f32[8,128]{1,0:T(8,128)S(1)} %get-tuple-element.48), channel_id=1, source_target_pairs={{1,0},{2,1},{3,2},{0,3},{5,4},{6,5},{7,6},{4,7},{9,8},{10,9},{11,1... | collective-permute-start | bytes 12296 | tf_op jit(solution)/shard_map/ppermute | solution.py:443
  71.0 4.5 %collective-permute-start.13 = (f32[8,128]{1,0:T(8,128)S(1)}, f32[8,128]{1,0:T(8,128)S(1)}, u32[]{:S(2)}, u32[]{:S(2)}) collective-permute-start(f32[8,128]{1,0:T(8,128)S(1)} %get-tuple-element.48), channel_id=1, source_target_pairs={{2,0},{3,1},{0,2},{1,3},{6,4},{7,5},{4,6},{5,7},{10,8},{11,9},{8,1... | collective-permute-start | bytes 12296 | tf_op jit(solution)/shard_map/ppermute | solution.py:443
  75.5 15.6 %all-to-all-start.1 = ((f32[4,4,64,128]{3,2,1,0:T(8,128)}), f32[4,4,64,128]{3,2,1,0:T(8,128)S(1)}, u32[]{:S(2)}, u32[]{:S(2)}) async-start(f32[4,4,64,128]{3,2,1,0:T(8,128)} %get-tuple-element.49), calls=%async_computation.1 | async-start | bytes 1048576 | tf_op jit(solution)/shard_map/all_to_all | solution.py:439
  79.0 5.8 %collective-permute-start.22 = (f32[8,128]{1,0:T(8,128)S(1)}, f32[8,128]{1,0:T(8,128)S(1)}, u32[]{:S(2)}, u32[]{:S(2)}) collective-permute-start(f32[8,128]{1,0:T(8,128)S(1)} %add_add_fusion.refs_0_), channel_id=1, source_target_pairs={{28,0},{0,4},{4,8},{8,12},{12,16},{16,20},{20,24},{24,28},{29,1},{... | collective-permute-start | bytes 12296 | tf_op jit(solution)/shard_map/ppermute | solution.py:443
  79.1 6.9 %collective-permute-start.21 = (f32[8,128]{1,0:T(8,128)S(1)}, f32[8,128]{1,0:T(8,128)S(1)}, u32[]{:S(2)}, u32[]{:S(2)}) collective-permute-start(f32[8,128]{1,0:T(8,128)S(1)} %add_add_fusion.refs_0_), channel_id=1, source_target_pairs={{24,0},{28,4},{0,8},{4,12},{8,16},{12,20},{16,24},{20,28},{25,1},{... | collective-permute-start | bytes 12296 | tf_op jit(solution)/shard_map/ppermute | solution.py:443
  80.3 7.9 %collective-permute-start.20 = (f32[8,128]{1,0:T(8,128)S(1)}, f32[8,128]{1,0:T(8,128)S(1)}, u32[]{:S(2)}, u32[]{:S(2)}) collective-permute-start(f32[8,128]{1,0:T(8,128)S(1)} %add_add_fusion.refs_0_), channel_id=1, source_target_pairs={{20,0},{24,4},{28,8},{0,12},{4,16},{8,20},{12,24},{16,28},{21,1},{... | collective-permute-start | bytes 12296 | tf_op jit(solution)/shard_map/ppermute | solution.py:443
  84.2 4.0 %collective-permute-start.19 = (f32[8,128]{1,0:T(8,128)S(1)}, f32[8,128]{1,0:T(8,128)S(1)}, u32[]{:S(2)}, u32[]{:S(2)}) collective-permute-start(f32[8,128]{1,0:T(8,128)S(1)} %add_add_fusion.refs_0_), channel_id=1, source_target_pairs={{16,0},{20,4},{24,8},{28,12},{0,16},{4,20},{8,24},{12,28},{17,1},{... | collective-permute-start | bytes 12296 | tf_op jit(solution)/shard_map/ppermute | solution.py:443
  84.2 4.0 %collective-permute-start.18 = (f32[8,128]{1,0:T(8,128)S(1)}, f32[8,128]{1,0:T(8,128)S(1)}, u32[]{:S(2)}, u32[]{:S(2)}) collective-permute-start(f32[8,128]{1,0:T(8,128)S(1)} %add_add_fusion.refs_0_), channel_id=1, source_target_pairs={{12,0},{16,4},{20,8},{24,12},{28,16},{0,20},{4,24},{8,28},{13,1},{... | collective-permute-start | bytes 12296 | tf_op jit(solution)/shard_map/ppermute | solution.py:443
  (6 other events, 41.1 us)

commit v8 on v7

--- a/solution.py
+++ b/solution.py
@@ -183,10 +183,10 @@
 
 
 def propagate_in_kernel(
-    count, vector_value, field_ref, total_ref, potential_ref, tables, scratch, width, kinds
+    count, vector_value, source_ref, field_ref, total_ref, potential_ref, tables, scratch, width, kinds
 ):
     near_ref, far_ref, zy_ref, xbell_ref, xslope_ref, y_ref = tables
-    split_ref, first_ref, second_ref, partial_ref, drift_ref, spread_ref, diagonal_ref = scratch
+    split_ref, first_ref, second_ref, partial_ref, spread_ref, diagonal_ref = scratch
     diagonal_ref[...] = (3.0 * SECOND[0] - 0.5 * vector_value * vector_value / KINETIC) - potential_ref[
         ...
     ] * (1.0 / KINETIC)
@@ -208,7 +208,11 @@
 
     for number in range(2 * count):
         for start in range(0, width, block):
-            store_split(split_ref, number, start, field_ref[number, start : start + block])
+            planes = source_ref[number, start : start + block]
+            store_split(split_ref, number, start, planes)
+            if source_ref is not field_ref:
+                field_ref[number, start : start + block] = planes
+                total_ref[number, start : start + block] = planes
 
     def one_order(order, carry):
         inverse = jnp.where(order == 1, 1.0, jnp.where(order == 2, 0.5, jnp.where(order == 3, 1.0 / 3.0, 0.25)))
@@ -233,29 +237,33 @@
                 first = total_of_groups(bell * y_ref[0], kinds)
                 second = total_of_groups(incline * y_ref[0], kinds)
                 third = total_of_groups(bell * y_ref[1], kinds)
-                outers[number] = (first * y_ref[2] + third * y_ref[4], second * y_ref[3])
+                outers[number] = (kinetic * (first * y_ref[2] + third * y_ref[4]), kinetic * (second * y_ref[3]))
         for orbital in range(count):
             rows = pl.ds(2 * orbital * cell_rows, 2 * cell_rows)
             second_ref[rows, :] = jnp.dot(split_ref[rows, :], far_ref[...], preferred_element_type=jnp.float32)
             for start in range(0, width, block):
-                for number in (2 * orbital, 2 * orbital + 1):
-                    near = {
-                        plane: field_ref[number, plane % width] for plane in range(start - 4, start + block + 4)
-                    }
-                    for plane in range(start, start + block):
-                        line = pl.ds(number * cell_rows + plane * ROWS, ROWS)
+                near = [
+                    {plane: field_ref[number, plane % width] for plane in range(start - 4, start + block + 4)}
+                    for number in (2 * orbital, 2 * orbital + 1)
+                ]
+                for plane in range(start, start + block):
+                    images, drifts = [], []
+                    for part in range(2):
+                        line = pl.ds((2 * orbital + part) * cell_rows + plane * ROWS, ROWS)
                         total = first_ref[line, :LANES]
                         total = total + pltpu.roll(second_ref[line, :LANES], ROWS - 1, 0)
                         total = total + pltpu.roll(second_ref[line, LANES:], 1, 0)
-                        total = total + diagonal_ref[plane] * near[plane]
+                        total = total + diagonal_ref[plane] * near[part][plane]
                         moved = None
                         for reach in range(1, 5):
-                            ahead, behind = near[plane + reach], near[plane - reach]
+                            ahead, behind = near[part][plane + reach], near[part][plane - reach]
                             total = total + SECOND[reach] * (ahead + behind)
                             term = slopes[reach - 1] * (ahead - behind)
                             moved = term if moved is None else moved + term
-                        partial_ref[number, plane] = total
-                        drift_ref[number, plane] = moved
+                        images.append(kinetic * total)
+                        drifts.append(moved)
+                    partial_ref[2 * orbital, plane] = -images[1] - drifts[0]
+                    partial_ref[2 * orbital + 1, plane] = images[0] - drifts[1]
         for orbital in range(count):
             real, imaginary = 2 * orbital, 2 * orbital + 1
             for start in range(0, width, block):
@@ -269,16 +277,13 @@
                 spread_ref[rows, :], zy_ref[...], preferred_element_type=jnp.float32
             )
             for start in range(0, width, block):
-                images = []
-                for number in (real, imaginary):
-                    rows = pl.ds(number * cell_rows + start * ROWS, slab)
-                    images.append(
-                        partial_ref[number, start : start + block]
-                        + first_ref[rows, :LANES].reshape(block, ROWS, LANES)
-                    )
+                spreads = [
+                    first_ref[pl.ds(number * cell_rows + start * ROWS, slab), :LANES].reshape(block, ROWS, LANES)
+                    for number in (real, imaginary)
+                ]
                 new = (
-                    -kinetic * images[1] - drift_ref[real, start : start + block],
-                    kinetic * images[0] - drift_ref[imaginary, start : start + block],
+                    partial_ref[real, start : start + block] - spreads[1],
+                    partial_ref[imaginary, start : start + block] + spreads[0],
                 )
                 for number, value in zip((real, imaginary), new):
                     field_ref[number, start : start + block] = value
@@ -292,18 +297,20 @@
 def sums_in_kernel(count, total_ref, width):
     flow = jnp.zeros((ROWS, LANES), jnp.float32)
     density = jnp.zeros((ROWS, LANES), jnp.float32)
+    block = ROWS
     for orbital in range(count):
-        for plane in range(width):
-            real = total_ref[2 * orbital, plane]
-            imaginary = total_ref[2 * orbital + 1, plane]
-            moved = None
-            for reach in range(1, 5):
-                ahead = total_ref[2 * orbital + 1, (plane + reach) % width]
-                behind = total_ref[2 * orbital + 1, (plane - reach) % width]
-                term = FIRST[reach - 1] * (ahead - behind)
-                moved = term if moved is None else moved + term
-            flow = flow + real * moved
-            density = density + (real * real + imaginary * imaginary)
+        for start in range(0, width, block):
+            near = {
+                plane: total_ref[2 * orbital + 1, plane % width] for plane in range(start - 4, start + block + 4)
+            }
+            for plane in range(start, start + block):
+                real, imaginary = total_ref[2 * orbital, plane], near[plane]
+                moved = None
+                for reach in range(1, 5):
+                    term = FIRST[reach - 1] * (near[plane + reach] - near[plane - reach])
+                    moved = term if moved is None else moved + term
+                flow = flow + real * moved
+                density = density + (real * real + imaginary * imaginary)
     return (2.0 * SLOPE) * flow, density
 
 
@@ -332,7 +339,7 @@
             if opening:
                 potential_ref[start + index] = piece[2 * count, rows, :]
     propagate_in_kernel(
-        count, scalar_ref[0], field_ref, total_ref, potential_ref, tables, scratch, width, kinds
+        count, scalar_ref[0], field_ref, field_ref, total_ref, potential_ref, tables, scratch, width, kinds
     )
     flow, density = sums_in_kernel(count, total_ref, width)
     if not opening:
@@ -365,10 +372,8 @@
             vector_ref[0] = vector_value
     else:
         vector_value = vector_ref[0]
-    field_ref[...] = psi_ref[...]
-    total_ref[...] = psi_ref[...]
     propagate_in_kernel(
-        count, vector_value, field_ref, total_ref, potential_ref, tables, scratch, width, kinds
+        count, vector_value, psi_ref, field_ref, total_ref, potential_ref, tables, scratch, width, kinds
     )
     for step in range(parts):
         piece, start = piece_ref.at[step], step * planes
@@ -535,7 +540,6 @@
                 pltpu.VMEM((rows, 2 * LANES), jnp.bfloat16),
                 pltpu.VMEM((rows, 2 * LANES), jnp.float32),
                 pltpu.VMEM((rows, 2 * LANES), jnp.float32),
-                cell,
                 cell,
                 pltpu.VMEM((rows, 2 * LANES), jnp.bfloat16),
                 pltpu.VMEM((width, ROWS, LANES), jnp.float32),

time: 93.4 us -> 93.4 us (level)
  no operation moved by 1% of the time
where the time goes in v8:
time: 93.4 us; the launch traced here: 91.9 us
  starting transfers between devices  47.3 us (51%)
  Pallas kernels  33 us (35%)
  waiting for transfers between devices  9.87 us (11%)
  between operations  1.46 us (2%)
    ppermute x23, starting transfers between devices, shifted(): lax.ppermute(value, axis_name, [((index + shift) % count, index) for inde...  33.9 us
    pallas_call x4, Pallas kernels, micro_call(): pl.pallas_call(kernel, out_shape=outputs, in_specs=[smem() if number < sc...  24.8 us
    all_to_all x3, starting transfers between devices, exchanged(): return lax.all_to_all(value, axes, split_axis=0, concat_axis=0, tiled=True)  13.4 us
    ppermute x23, waiting for transfers between devices, shifted(): lax.ppermute(value, axis_name, [((index + shift) % count, index) for inde...  9.86 us
    pallas_call x1, Pallas kernels, per_device(): pl.pallas_call(functools.partial(pack_kernel, parts, share, main_count, 0...  2.06 us
    pallas_call x1, Pallas kernels, per_device(): pl.pallas_call(functools.partial(pack_pieces_kernel, parts, share, last_c...  1.93 us
  transfers between devices with their start and end apart: 26, of which 9 were waited for; matrix products, arithmetic and copies ran while one was open for 0% of the time, Pallas kernels for 20%

profile of v8, /device:TPU:0, one launch (start us, length us, event | category | flops | bytes accessed | tf_op | source)
XLA Modules:
  0.0 91.9 jit_solution(675446193779217636)
XLA Ops:
  0.6 2.1 %shard_map.77 = f32[4,5,64,128]{3,2,1,0:T(8,128)} custom-call(f32[2,16,64,128]{3,2,1,0:T(8,128)} %bitcast.19, f32[64,128]{1,0:T(8,128)} %bitcast.22), custom_call_target="tpu_custom_call" | custom-call | tf_op jit(solution)/shard_map/pallas_call | solution.py:479
  2.7 6.5 %all-to-all-start = ((f32[4,5,64,128]{3,2,1,0:T(8,128)}), f32[4,5,64,128]{3,2,1,0:T(8,128)S(1)}, u32[]{:S(2)}, u32[]{:S(2)}) async-start(f32[4,5,64,128]{3,2,1,0:T(8,128)} %shard_map.77), calls=%async_computation | async-start | bytes 1310720 | tf_op jit(solution)/shard_map/all_to_all | solution.py:444
  9.2 1.5 %collective-permute-start.5 = (f32[2,64]{1,0:T(2,128)S(1)}, f32[2,64]{1,0:T(2,128)S(1)}, u32[]{:S(2)}, u32[]{:S(2)}) collective-permute-start(f32[2,64]{1,0:T(2,128)S(1)} %copy-done.1), channel_id=1, source_target_pairs={{24,0},{28,4},{0,8},{4,12},{8,16},{12,20},{16,24},{20,28},{25,1},{... | collective-permute-start | bytes 1544 | tf_op jit(solution)/shard_map/ppermute | solution.py:448
  10.7 2.4 %collective-permute-start.4 = (f32[2,64]{1,0:T(2,128)S(1)}, f32[2,64]{1,0:T(2,128)S(1)}, u32[]{:S(2)}, u32[]{:S(2)}) collective-permute-start(f32[2,64]{1,0:T(2,128)S(1)} %copy-done.1), channel_id=1, source_target_pairs={{20,0},{24,4},{28,8},{0,12},{4,16},{8,20},{12,24},{16,28},{21,1},{... | collective-permute-start | bytes 1544 | tf_op jit(solution)/shard_map/ppermute | solution.py:448
  13.7 1.4 %collective-permute-start.1 = (f32[2,64]{1,0:T(2,128)S(1)}, f32[2,64]{1,0:T(2,128)S(1)}, u32[]{:S(2)}, u32[]{:S(2)}) collective-permute-start(f32[2,64]{1,0:T(2,128)S(1)} %copy-done.1), channel_id=1, source_target_pairs={{8,0},{12,4},{16,8},{20,12},{24,16},{28,20},{0,24},{4,28},{9,1},{1... | collective-permute-start | bytes 1544 | tf_op jit(solution)/shard_map/ppermute | solution.py:448
  15.2 2.3 %collective-permute-start = (f32[2,64]{1,0:T(2,128)S(1)}, f32[2,64]{1,0:T(2,128)S(1)}, u32[]{:S(2)}, u32[]{:S(2)}) collective-permute-start(f32[2,64]{1,0:T(2,128)S(1)} %copy-done.1), channel_id=1, source_target_pairs={{4,0},{8,4},{12,8},{16,12},{20,16},{24,20},{28,24},{0,28},{5,1},{9... | collective-permute-start | bytes 1544 | tf_op jit(solution)/shard_map/ppermute | solution.py:448
  20.0 1.9 %shard_map.79 = (f32[4,64,128]{2,1,0:T(8,128)}, f32[4,64,128]{2,1,0:T(8,128)}, f32[4,64,128]{2,1,0:T(8,128)}, f32[4,64,128]{2,1,0:T(8,128)}) custom-call(s32[1]{0:T(128)} %bitcast.9.here_ref.refs_0_, f32[2,16,64,128]{3,2,1,0:T(8,128)} %bitcast.20), custom_call_target="tpu_custom_call" | custom-call | tf_op jit(solution)/shard_map/pallas_call | solution.py:516
  21.9 2.1 %collective-permute-start.7 = (f32[4,64,128]{2,1,0:T(8,128)}, f32[4,64,128]{2,1,0:T(8,128)S(1)}, u32[]{:S(2)}, u32[]{:S(2)}) collective-permute-start(f32[4,64,128]{2,1,0:T(8,128)} %get-tuple-element.31), channel_id=1, source_target_pairs={{3,0},{0,1},{1,2},{2,3},{7,4},{4,5},{5,6},{6,7},{11,8},{8,9},{9,10... | collective-permute-start | bytes 393224 | tf_op jit(solution)/shard_map/ppermute | solution.py:448
  24.0 2.4 %collective-permute-start.8 = (f32[4,64,128]{2,1,0:T(8,128)}, f32[4,64,128]{2,1,0:T(8,128)S(1)}, u32[]{:S(2)}, u32[]{:S(2)}) collective-permute-start(f32[4,64,128]{2,1,0:T(8,128)} %get-tuple-element.32), channel_id=1, source_target_pairs={{2,0},{3,1},{0,2},{1,3},{6,4},{7,5},{4,6},{5,7},{10,8},{11,9},{8,1... | collective-permute-start | bytes 393224 | tf_op jit(solution)/shard_map/ppermute | solution.py:448
  26.4 1.5 %collective-permute-start.9 = (f32[4,64,128]{2,1,0:T(8,128)}, f32[4,64,128]{2,1,0:T(8,128)S(1)}, u32[]{:S(2)}, u32[]{:S(2)}) collective-permute-start(f32[4,64,128]{2,1,0:T(8,128)} %get-tuple-element.33), channel_id=1, source_target_pairs={{1,0},{2,1},{3,2},{0,3},{5,4},{6,5},{7,6},{4,7},{9,8},{10,9},{11,1... | collective-permute-start | bytes 393224 | tf_op jit(solution)/shard_map/ppermute | solution.py:448
  27.8 5.7 %shard_map.81 = (f32[4,32,8,128]{3,2,1,0:T(8,128)S(1)}, f32[2,8,128]{2,1,0:T(8,128)S(1)}, f32[32,8,128]{2,1,0:T(8,128)S(1)}) custom-call(f32[3]{0:T(128)S(1)} %shard_map.78.scalar_ref, f32[4,5,64,128]{3,2,1,0:T(8,128)S(1)} %all-to-all-done.refs_0_, bf16[256,256]{1,0:T(8,128)(2,1)S(1)} %get-tuple-element.34.refs_1_.refs_6_.refs_5_, ...), custom_call_target="tpu_custom_call" | custom-call | flops 1610612736 | bytes 4194304 | tf_op jit(solution)/shard_map/pallas_call | solution.py:533
  33.6 2.0 %collective-permute-done.8.refs_3_ = f32[4,64,128]{2,1,0:T(8,128)S(1)} collective-permute-done((f32[4,64,128]{2,1,0:T(8,128)}, f32[4,64,128]{2,1,0:T(8,128)S(1)}, u32[]{:S(2)}, u32[]{:S(2)}) %collective-permute-start.8) | collective-permute-done | bytes 131104 | tf_op jit(solution)/shard_map/ppermute | solution.py:448
  35.5 5.7 %shard_map.82 = (f32[4,32,8,128]{3,2,1,0:T(8,128)S(1)}, f32[2,8,128]{2,1,0:T(8,128)S(1)}) custom-call(f32[3]{0:T(128)S(1)} %shard_map.78.scalar_ref, s32[1]{0:T(128)} %bitcast.9.here_ref.refs_0_, f32[4,64,128]{2,1,0:T(8,128)S(1)} %copy-done.2, f32[4,64,128]{2,1,0:T(8,128)S(1)} %collective-permute-done.7.refs_2_, ...), custom_call_target="tpu_custom_call" | custom-call | flops 1610612736 | bytes 4194304 | tf_op jit(solution)/shard_map/pallas_call | solution.py:533
  41.3 3.4 %collective-permute-start.12 = (f32[2,8,128]{2,1,0:T(8,128)S(1)}, f32[2,8,128]{2,1,0:T(8,128)S(1)}, u32[]{:S(2)}, u32[]{:S(2)}) collective-permute-start(f32[2,8,128]{2,1,0:T(8,128)S(1)} %get-tuple-element.42.refs_0_.refs_1_), channel_id=1, source_target_pairs={{3,0},{0,1},{1,2},{2,3},{7,4},{4,5},{5,6},{6,7},{11,8},{8,9},{9,10... | collective-permute-start | bytes 24584 | tf_op jit(solution)/shard_map/ppermute | solution.py:448
  44.6 2.0 %collective-permute-start.11 = (f32[2,8,128]{2,1,0:T(8,128)S(1)}, f32[2,8,128]{2,1,0:T(8,128)S(1)}, u32[]{:S(2)}, u32[]{:S(2)}) collective-permute-start(f32[2,8,128]{2,1,0:T(8,128)S(1)} %get-tuple-element.42.refs_0_.refs_1_), channel_id=1, source_target_pairs={{2,0},{3,1},{0,2},{1,3},{6,4},{7,5},{4,6},{5,7},{10,8},{11,9},{8,1... | collective-permute-start | bytes 24584 | tf_op jit(solution)/shard_map/ppermute | solution.py:448
  50.3 6.4 %shard_map.83 = (f32[4,4,64,128]{3,2,1,0:T(8,128)}, f32[1]{0:T(128)}, f32[2,8,128]{2,1,0:T(8,128)S(1)}) custom-call(f32[3]{0:T(128)S(1)} %shard_map.78.scalar_ref, f32[2,8,128]{2,1,0:T(8,128)S(1)} %get-tuple-element.42.refs_0_.refs_1_, f32[2,8,128]{2,1,0:T(8,128)S(1)} %collective-permute-done.10.refs_1_, f32[2,8,128]{2,1,0:T(8,128)S(1)} %collective-permute-done.11.refs_2_, ...), custom_call_target="tpu_custom_call" | custom-call | flops 1610612736 | bytes 4194304 | tf_op jit(solution)/shard_map/pallas_call | solution.py:533
  56.7 3.5 %all-to-all-start.2 = ((f32[4,4,64,128]{3,2,1,0:T(8,128)}), f32[4,4,64,128]{3,2,1,0:T(8,128)S(1)}, u32[]{:S(2)}, u32[]{:S(2)}) async-start(f32[4,4,64,128]{3,2,1,0:T(8,128)} %get-tuple-element.50), calls=%async_computation.2 | async-start | bytes 1048576 | tf_op jit(solution)/shard_map/all_to_all | solution.py:444
  60.2 7.0 %shard_map.84 = (f32[4,4,64,128]{3,2,1,0:T(8,128)}, f32[8,128]{1,0:T(8,128)S(1)}) custom-call(f32[3]{0:T(128)S(1)} %shard_map.78.scalar_ref, f32[1]{0:T(128)} %get-tuple-element.44.refs_0_, f32[2,8,128]{2,1,0:T(8,128)S(1)} %get-tuple-element.42.refs_0_.refs_1_, f32[2,8,128]{2,1,0:T(8,128)S(1)} %get-tuple-element.45.refs_2_, ...), custom_call_target="tpu_custom_call" | custom-call | flops 1610612736 | bytes 4194304 | tf_op jit(solution)/shard_map/pallas_call | solution.py:533
  67.2 2.0 %collective-permute-start.15 = (f32[8,128]{1,0:T(8,128)S(1)}, f32[8,128]{1,0:T(8,128)S(1)}, u32[]{:S(2)}, u32[]{:S(2)}) collective-permute-start(f32[8,128]{1,0:T(8,128)S(1)} %get-tuple-element.48), channel_id=1, source_target_pairs={{3,0},{0,1},{1,2},{2,3},{7,4},{4,5},{5,6},{6,7},{11,8},{8,9},{9,10... | collective-permute-start | bytes 12296 | tf_op jit(solution)/shard_map/ppermute | solution.py:448
  69.2 1.8 %collective-permute-start.14 = (f32[8,128]{1,0:T(8,128)S(1)}, f32[8,128]{1,0:T(8,128)S(1)}, u32[]{:S(2)}, u32[]{:S(2)}) collective-permute-start(f32[8,128]{1,0:T(8,128)S(1)} %get-tuple-element.48), channel_id=1, source_target_pairs={{1,0},{2,1},{3,2},{0,3},{5,4},{6,5},{7,6},{4,7},{9,8},{10,9},{11,1... | collective-permute-start | bytes 12296 | tf_op jit(solution)/shard_map/ppermute | solution.py:448
  73.2 2.3 %collective-permute-done.13 = f32[8,128]{1,0:T(8,128)S(1)} collective-permute-done((f32[8,128]{1,0:T(8,128)S(1)}, f32[8,128]{1,0:T(8,128)S(1)}, u32[]{:S(2)}, u32[]{:S(2)}) %collective-permute-start.13) | collective-permute-done | bytes 4128 | tf_op jit(solution)/shard_map/ppermute | solution.py:448
  75.5 3.5 %all-to-all-start.1 = ((f32[4,4,64,128]{3,2,1,0:T(8,128)}), f32[4,4,64,128]{3,2,1,0:T(8,128)S(1)}, u32[]{:S(2)}, u32[]{:S(2)}) async-start(f32[4,4,64,128]{3,2,1,0:T(8,128)} %get-tuple-element.49), calls=%async_computation.1 | async-start | bytes 1048576 | tf_op jit(solution)/shard_map/all_to_all | solution.py:444
  80.3 3.9 %collective-permute-start.20 = (f32[8,128]{1,0:T(8,128)S(1)}, f32[8,128]{1,0:T(8,128)S(1)}, u32[]{:S(2)}, u32[]{:S(2)}) collective-permute-start(f32[8,128]{1,0:T(8,128)S(1)} %add_add_fusion.refs_0_), channel_id=1, source_target_pairs={{20,0},{24,4},{28,8},{0,12},{4,16},{8,20},{12,24},{16,28},{21,1},{... | collective-permute-start | bytes 12296 | tf_op jit(solution)/shard_map/ppermute | solution.py:448
  86.0 2.1 %collective-permute-start.16 = (f32[8,128]{1,0:T(8,128)S(1)}, f32[8,128]{1,0:T(8,128)S(1)}, u32[]{:S(2)}, u32[]{:S(2)}) collective-permute-start(f32[8,128]{1,0:T(8,128)S(1)} %add_add_fusion.refs_0_), channel_id=1, source_target_pairs={{4,0},{8,4},{12,8},{16,12},{20,16},{24,20},{28,24},{0,28},{5,1},{9... | collective-permute-start | bytes 12296 | tf_op jit(solution)/shard_map/ppermute | solution.py:448
  (51 shorter events, 15.3 us)
Async XLA Ops:
  2.7 25.1 %all-to-all-start = ((f32[4,5,64,128]{3,2,1,0:T(8,128)}), f32[4,5,64,128]{3,2,1,0:T(8,128)S(1)}, u32[]{:S(2)}, u32[]{:S(2)}) async-start(f32[4,5,64,128]{3,2,1,0:T(8,128)} %shard_map.77), calls=%async_computation | async-start | bytes 1310720 | tf_op jit(solution)/shard_map/all_to_all | solution.py:444
  9.2 4.5 %collective-permute-start.6 = (f32[2,64]{1,0:T(2,128)S(1)}, f32[2,64]{1,0:T(2,128)S(1)}, u32[]{:S(2)}, u32[]{:S(2)}) collective-permute-start(f32[2,64]{1,0:T(2,128)S(1)} %copy-done.1), channel_id=1, source_target_pairs={{28,0},{0,4},{4,8},{8,12},{12,16},{16,20},{20,24},{24,28},{29,1},{... | collective-permute-start | bytes 1544 | tf_op jit(solution)/shard_map/ppermute | solution.py:448
  9.2 6.0 %collective-permute-start.5 = (f32[2,64]{1,0:T(2,128)S(1)}, f32[2,64]{1,0:T(2,128)S(1)}, u32[]{:S(2)}, u32[]{:S(2)}) collective-permute-start(f32[2,64]{1,0:T(2,128)S(1)} %copy-done.1), channel_id=1, source_target_pairs={{24,0},{28,4},{0,8},{4,12},{8,16},{12,20},{16,24},{20,28},{25,1},{... | collective-permute-start | bytes 1544 | tf_op jit(solution)/shard_map/ppermute | solution.py:448
  10.7 8.5 %collective-permute-start.4 = (f32[2,64]{1,0:T(2,128)S(1)}, f32[2,64]{1,0:T(2,128)S(1)}, u32[]{:S(2)}, u32[]{:S(2)}) collective-permute-start(f32[2,64]{1,0:T(2,128)S(1)} %copy-done.1), channel_id=1, source_target_pairs={{20,0},{24,4},{28,8},{0,12},{4,16},{8,20},{12,24},{16,28},{21,1},{... | collective-permute-start | bytes 1544 | tf_op jit(solution)/shard_map/ppermute | solution.py:448
  13.1 6.1 %collective-permute-start.3 = (f32[2,64]{1,0:T(2,128)S(1)}, f32[2,64]{1,0:T(2,128)S(1)}, u32[]{:S(2)}, u32[]{:S(2)}) collective-permute-start(f32[2,64]{1,0:T(2,128)S(1)} %copy-done.1), channel_id=1, source_target_pairs={{16,0},{20,4},{24,8},{28,12},{0,16},{4,20},{8,24},{12,28},{17,1},{... | collective-permute-start | bytes 1544 | tf_op jit(solution)/shard_map/ppermute | solution.py:448
  13.6 5.6 %collective-permute-start.2 = (f32[2,64]{1,0:T(2,128)S(1)}, f32[2,64]{1,0:T(2,128)S(1)}, u32[]{:S(2)}, u32[]{:S(2)}) collective-permute-start(f32[2,64]{1,0:T(2,128)S(1)} %copy-done.1), channel_id=1, source_target_pairs={{12,0},{16,4},{20,8},{24,12},{28,16},{0,20},{4,24},{8,28},{13,1},{... | collective-permute-start | bytes 1544 | tf_op jit(solution)/shard_map/ppermute | solution.py:448
  13.7 5.5 %collective-permute-start.1 = (f32[2,64]{1,0:T(2,128)S(1)}, f32[2,64]{1,0:T(2,128)S(1)}, u32[]{:S(2)}, u32[]{:S(2)}) collective-permute-start(f32[2,64]{1,0:T(2,128)S(1)} %copy-done.1), channel_id=1, source_target_pairs={{8,0},{12,4},{16,8},{20,12},{24,16},{28,20},{0,24},{4,28},{9,1},{1... | collective-permute-start | bytes 1544 | tf_op jit(solution)/shard_map/ppermute | solution.py:448
  15.2 4.1 %collective-permute-start = (f32[2,64]{1,0:T(2,128)S(1)}, f32[2,64]{1,0:T(2,128)S(1)}, u32[]{:S(2)}, u32[]{:S(2)}) collective-permute-start(f32[2,64]{1,0:T(2,128)S(1)} %copy-done.1), channel_id=1, source_target_pairs={{4,0},{8,4},{12,8},{16,12},{20,16},{24,20},{28,24},{0,28},{5,1},{9... | collective-permute-start | bytes 1544 | tf_op jit(solution)/shard_map/ppermute | solution.py:448
  21.9 11.6 %collective-permute-start.7 = (f32[4,64,128]{2,1,0:T(8,128)}, f32[4,64,128]{2,1,0:T(8,128)S(1)}, u32[]{:S(2)}, u32[]{:S(2)}) collective-permute-start(f32[4,64,128]{2,1,0:T(8,128)} %get-tuple-element.31), channel_id=1, source_target_pairs={{3,0},{0,1},{1,2},{2,3},{7,4},{4,5},{5,6},{6,7},{11,8},{8,9},{9,10... | collective-permute-start | bytes 393224 | tf_op jit(solution)/shard_map/ppermute | solution.py:448
  24.0 11.5 %collective-permute-start.8 = (f32[4,64,128]{2,1,0:T(8,128)}, f32[4,64,128]{2,1,0:T(8,128)S(1)}, u32[]{:S(2)}, u32[]{:S(2)}) collective-permute-start(f32[4,64,128]{2,1,0:T(8,128)} %get-tuple-element.32), channel_id=1, source_target_pairs={{2,0},{3,1},{0,2},{1,3},{6,4},{7,5},{4,6},{5,7},{10,8},{11,9},{8,1... | collective-permute-start | bytes 393224 | tf_op jit(solution)/shard_map/ppermute | solution.py:448
  26.4 9.2 %collective-permute-start.9 = (f32[4,64,128]{2,1,0:T(8,128)}, f32[4,64,128]{2,1,0:T(8,128)S(1)}, u32[]{:S(2)}, u32[]{:S(2)}) collective-permute-start(f32[4,64,128]{2,1,0:T(8,128)} %get-tuple-element.33), channel_id=1, source_target_pairs={{1,0},{2,1},{3,2},{0,3},{5,4},{6,5},{7,6},{4,7},{9,8},{10,9},{11,1... | collective-permute-start | bytes 393224 | tf_op jit(solution)/shard_map/ppermute | solution.py:448
  41.3 6.5 %collective-permute-start.12 = (f32[2,8,128]{2,1,0:T(8,128)S(1)}, f32[2,8,128]{2,1,0:T(8,128)S(1)}, u32[]{:S(2)}, u32[]{:S(2)}) collective-permute-start(f32[2,8,128]{2,1,0:T(8,128)S(1)} %get-tuple-element.42.refs_0_.refs_1_), channel_id=1, source_target_pairs={{3,0},{0,1},{1,2},{2,3},{7,4},{4,5},{5,6},{6,7},{11,8},{8,9},{9,10... | collective-permute-start | bytes 24584 | tf_op jit(solution)/shard_map/ppermute | solution.py:448
  44.6 4.5 %collective-permute-start.11 = (f32[2,8,128]{2,1,0:T(8,128)S(1)}, f32[2,8,128]{2,1,0:T(8,128)S(1)}, u32[]{:S(2)}, u32[]{:S(2)}) collective-permute-start(f32[2,8,128]{2,1,0:T(8,128)S(1)} %get-tuple-element.42.refs_0_.refs_1_), channel_id=1, source_target_pairs={{2,0},{3,1},{0,2},{1,3},{6,4},{7,5},{4,6},{5,7},{10,8},{11,9},{8,1... | collective-permute-start | bytes 24584 | tf_op jit(solution)/shard_map/ppermute | solution.py:448
  46.6 3.7 %collective-permute-start.10 = (f32[2,8,128]{2,1,0:T(8,128)S(1)}, f32[2,8,128]{2,1,0:T(8,128)S(1)}, u32[]{:S(2)}, u32[]{:S(2)}) collective-permute-start(f32[2,8,128]{2,1,0:T(8,128)S(1)} %get-tuple-element.42.refs_0_.refs_1_), channel_id=1, source_target_pairs={{1,0},{2,1},{3,2},{0,3},{5,4},{6,5},{7,6},{4,7},{9,8},{10,9},{11,1... | collective-permute-start | bytes 24584 | tf_op jit(solution)/shard_map/ppermute | solution.py:448
  56.7 18.8 %all-to-all-start.2 = ((f32[4,4,64,128]{3,2,1,0:T(8,128)}), f32[4,4,64,128]{3,2,1,0:T(8,128)S(1)}, u32[]{:S(2)}, u32[]{:S(2)}) async-start(f32[4,4,64,128]{3,2,1,0:T(8,128)} %get-tuple-element.50), calls=%async_computation.2 | async-start | bytes 1048576 | tf_op jit(solution)/shard_map/all_to_all | solution.py:444
  67.2 5.5 %collective-permute-start.15 = (f32[8,128]{1,0:T(8,128)S(1)}, f32[8,128]{1,0:T(8,128)S(1)}, u32[]{:S(2)}, u32[]{:S(2)}) collective-permute-start(f32[8,128]{1,0:T(8,128)S(1)} %get-tuple-element.48), channel_id=1, source_target_pairs={{3,0},{0,1},{1,2},{2,3},{7,4},{4,5},{5,6},{6,7},{11,8},{8,9},{9,10... | collective-permute-start | bytes 12296 | tf_op jit(solution)/shard_map/ppermute | solution.py:448
  69.2 4.0 %collective-permute-start.14 = (f32[8,128]{1,0:T(8,128)S(1)}, f32[8,128]{1,0:T(8,128)S(1)}, u32[]{:S(2)}, u32[]{:S(2)}) collective-permute-start(f32[8,128]{1,0:T(8,128)S(1)} %get-tuple-element.48), channel_id=1, source_target_pairs={{1,0},{2,1},{3,2},{0,3},{5,4},{6,5},{7,6},{4,7},{9,8},{10,9},{11,1... | collective-permute-start | bytes 12296 | tf_op jit(solution)/shard_map/ppermute | solution.py:448
  71.0 4.5 %collective-permute-start.13 = (f32[8,128]{1,0:T(8,128)S(1)}, f32[8,128]{1,0:T(8,128)S(1)}, u32[]{:S(2)}, u32[]{:S(2)}) collective-permute-start(f32[8,128]{1,0:T(8,128)S(1)} %get-tuple-element.48), channel_id=1, source_target_pairs={{2,0},{3,1},{0,2},{1,3},{6,4},{7,5},{4,6},{5,7},{10,8},{11,9},{8,1... | collective-permute-start | bytes 12296 | tf_op jit(solution)/shard_map/ppermute | solution.py:448
  75.5 15.6 %all-to-all-start.1 = ((f32[4,4,64,128]{3,2,1,0:T(8,128)}), f32[4,4,64,128]{3,2,1,0:T(8,128)S(1)}, u32[]{:S(2)}, u32[]{:S(2)}) async-start(f32[4,4,64,128]{3,2,1,0:T(8,128)} %get-tuple-element.49), calls=%async_computation.1 | async-start | bytes 1048576 | tf_op jit(solution)/shard_map/all_to_all | solution.py:444
  79.0 5.8 %collective-permute-start.22 = (f32[8,128]{1,0:T(8,128)S(1)}, f32[8,128]{1,0:T(8,128)S(1)}, u32[]{:S(2)}, u32[]{:S(2)}) collective-permute-start(f32[8,128]{1,0:T(8,128)S(1)} %add_add_fusion.refs_0_), channel_id=1, source_target_pairs={{28,0},{0,4},{4,8},{8,12},{12,16},{16,20},{20,24},{24,28},{29,1},{... | collective-permute-start | bytes 12296 | tf_op jit(solution)/shard_map/ppermute | solution.py:448
  79.1 6.9 %collective-permute-start.21 = (f32[8,128]{1,0:T(8,128)S(1)}, f32[8,128]{1,0:T(8,128)S(1)}, u32[]{:S(2)}, u32[]{:S(2)}) collective-permute-start(f32[8,128]{1,0:T(8,128)S(1)} %add_add_fusion.refs_0_), channel_id=1, source_target_pairs={{24,0},{28,4},{0,8},{4,12},{8,16},{12,20},{16,24},{20,28},{25,1},{... | collective-permute-start | bytes 12296 | tf_op jit(solution)/shard_map/ppermute | solution.py:448
  80.3 7.9 %collective-permute-start.20 = (f32[8,128]{1,0:T(8,128)S(1)}, f32[8,128]{1,0:T(8,128)S(1)}, u32[]{:S(2)}, u32[]{:S(2)}) collective-permute-start(f32[8,128]{1,0:T(8,128)S(1)} %add_add_fusion.refs_0_), channel_id=1, source_target_pairs={{20,0},{24,4},{28,8},{0,12},{4,16},{8,20},{12,24},{16,28},{21,1},{... | collective-permute-start | bytes 12296 | tf_op jit(solution)/shard_map/ppermute | solution.py:448
  84.2 4.0 %collective-permute-start.19 = (f32[8,128]{1,0:T(8,128)S(1)}, f32[8,128]{1,0:T(8,128)S(1)}, u32[]{:S(2)}, u32[]{:S(2)}) collective-permute-start(f32[8,128]{1,0:T(8,128)S(1)} %add_add_fusion.refs_0_), channel_id=1, source_target_pairs={{16,0},{20,4},{24,8},{28,12},{0,16},{4,20},{8,24},{12,28},{17,1},{... | collective-permute-start | bytes 12296 | tf_op jit(solution)/shard_map/ppermute | solution.py:448
  84.2 4.0 %collective-permute-start.18 = (f32[8,128]{1,0:T(8,128)S(1)}, f32[8,128]{1,0:T(8,128)S(1)}, u32[]{:S(2)}, u32[]{:S(2)}) collective-permute-start(f32[8,128]{1,0:T(8,128)S(1)} %add_add_fusion.refs_0_), channel_id=1, source_target_pairs={{12,0},{16,4},{20,8},{24,12},{28,16},{0,20},{4,24},{8,28},{13,1},{... | collective-permute-start | bytes 12296 | tf_op jit(solution)/shard_map/ppermute | solution.py:448
  (6 other events, 41.1 us)

commit v9 on v8

--- a/solution.py
+++ b/solution.py
@@ -55,7 +55,7 @@
     return bell, distance / projector_width * bell
 
 
-def tables_kernel(atoms, site_ref, stencil_ref, near_ref, far_ref, zy_ref, xbell_ref, xslope_ref, y_ref):
+def tables_kernel(atoms, site_ref, stencil_ref, yz_ref, zy_ref, xbell_ref, xslope_ref, y_ref):
     width = xbell_ref.shape[0]
     kinds = 2 * atoms
     group = LANES // width
@@ -79,10 +79,9 @@
     shape = (2 * LANES, LANES)
     first = lax.broadcasted_iota(jnp.int32, shape, 0)
     last = lax.broadcasted_iota(jnp.int32, shape, 1)
-    near_ref[:, :LANES] = stencil_ref[:, :LANES]
-    far_ref[...] = stencil_ref[:, LANES:]
+    yz_ref[:, : 3 * LANES] = stencil_ref[...]
     inward = jnp.where(groups_agree(first, last), factor(first % width, last), 0.0)
-    near_ref[:, LANES:] = inward.astype(jnp.bfloat16)
+    yz_ref[:, 3 * LANES :] = inward.astype(jnp.bfloat16)
     outward = jnp.where(groups_agree(last, first), factor(last % width, first), 0.0)
     zy_ref[...] = outward.astype(jnp.bfloat16)
 
@@ -185,8 +184,8 @@
 def propagate_in_kernel(
     count, vector_value, source_ref, field_ref, total_ref, potential_ref, tables, scratch, width, kinds
 ):
-    near_ref, far_ref, zy_ref, xbell_ref, xslope_ref, y_ref = tables
-    split_ref, first_ref, second_ref, partial_ref, spread_ref, diagonal_ref = scratch
+    yz_ref, zy_ref, xbell_ref, xslope_ref, y_ref = tables
+    split_ref, product_ref, partial_ref, spread_ref, diagonal_ref = scratch
     diagonal_ref[...] = (3.0 * SECOND[0] - 0.5 * vector_value * vector_value / KINETIC) - potential_ref[
         ...
     ] * (1.0 / KINETIC)
@@ -223,12 +222,12 @@
         outers = {}
         for orbital in range(count):
             rows = pl.ds(2 * orbital * cell_rows, 2 * cell_rows)
-            first_ref[rows, :] = jnp.dot(split_ref[rows, :], near_ref[...], preferred_element_type=jnp.float32)
+            product_ref[rows, :] = jnp.dot(split_ref[rows, :], yz_ref[...], preferred_element_type=jnp.float32)
             for number in (2 * orbital, 2 * orbital + 1):
                 bells = [jnp.zeros((ROWS, LANES), jnp.float32) for _ in range(2)]
                 inclines = [jnp.zeros((ROWS, LANES), jnp.float32) for _ in range(2)]
                 for plane in range(width):
-                    inner = first_ref[pl.ds(number * cell_rows + plane * ROWS, ROWS), LANES:]
+                    inner = product_ref[pl.ds(number * cell_rows + plane * ROWS, ROWS), 3 * LANES :]
                     turn = plane % 2
                     bells[turn] = bells[turn] + inner * xbell_ref[plane]
                     inclines[turn] = inclines[turn] + inner * xslope_ref[plane]
@@ -239,8 +238,6 @@
                 third = total_of_groups(bell * y_ref[1], kinds)
                 outers[number] = (kinetic * (first * y_ref[2] + third * y_ref[4]), kinetic * (second * y_ref[3]))
         for orbital in range(count):
-            rows = pl.ds(2 * orbital * cell_rows, 2 * cell_rows)
-            second_ref[rows, :] = jnp.dot(split_ref[rows, :], far_ref[...], preferred_element_type=jnp.float32)
             for start in range(0, width, block):
                 near = [
                     {plane: field_ref[number, plane % width] for plane in range(start - 4, start + block + 4)}
@@ -250,9 +247,9 @@
                     images, drifts = [], []
                     for part in range(2):
                         line = pl.ds((2 * orbital + part) * cell_rows + plane * ROWS, ROWS)
-                        total = first_ref[line, :LANES]
-                        total = total + pltpu.roll(second_ref[line, :LANES], ROWS - 1, 0)
-                        total = total + pltpu.roll(second_ref[line, LANES:], 1, 0)
+                        total = product_ref[line, :LANES]
+                        total = total + pltpu.roll(product_ref[line, LANES : 2 * LANES], ROWS - 1, 0)
+                        total = total + pltpu.roll(product_ref[line, 2 * LANES : 3 * LANES], 1, 0)
                         total = total + diagonal_ref[plane] * near[part][plane]
                         moved = None
                         for reach in range(1, 5):
@@ -273,12 +270,12 @@
                     spread = xbell * outers[number][0][None] + xslope * outers[number][1][None]
                     store_split(spread_ref, number, start, spread)
             rows = pl.ds(real * cell_rows, 2 * cell_rows)
-            first_ref[rows, :LANES] = jnp.dot(
+            product_ref[rows, :LANES] = jnp.dot(
                 spread_ref[rows, :], zy_ref[...], preferred_element_type=jnp.float32
             )
             for start in range(0, width, block):
                 spreads = [
-                    first_ref[pl.ds(number * cell_rows + start * ROWS, slab), :LANES].reshape(block, ROWS, LANES)
+                    product_ref[pl.ds(number * cell_rows + start * ROWS, slab), :LANES].reshape(block, ROWS, LANES)
                     for number in (real, imaginary)
                 ]
                 new = (
@@ -316,12 +313,12 @@
 
 def first_kernel(parts, count, kinds, opening, scalar_ref, *refs):
     if opening:
-        piece_ref, *tables, total_ref, out_ref, potential_ref, field_ref = refs[:11]
-        scratch = refs[11:]
+        piece_ref, *tables, total_ref, out_ref, potential_ref, field_ref = refs[:10]
+        scratch = refs[10:]
     else:
         here_ref, pieces, refs = refs[0], refs[1 : 1 + parts], refs[1 + parts :]
-        potential_ref, *tables, sums_ref, total_ref, out_ref, field_ref = refs[:11]
-        scratch = refs[11:]
+        potential_ref, *tables, sums_ref, total_ref, out_ref, field_ref = refs[:10]
+        scratch = refs[10:]
     width = total_ref.shape[1]
     planes = width // parts
     for step in range(parts):
@@ -354,8 +351,8 @@
         first_sums_ref = seen[0]
     else:
         vector_ref, first_sums_ref, sums_ref, *refs = refs
-    psi_ref, potential_ref, *tables = refs[:8]
-    refs = refs[8:]
+    psi_ref, potential_ref, *tables = refs[:7]
+    refs = refs[7:]
     piece_ref, *refs = refs
     if opening and not closing:
         vector_ref, *refs = refs
@@ -491,15 +488,14 @@
     tables = pl.pallas_call(
         functools.partial(tables_kernel, atoms),
         out_shape=[
-            jax.ShapeDtypeStruct((2 * LANES, 2 * LANES), jnp.bfloat16),
-            jax.ShapeDtypeStruct((2 * LANES, 2 * LANES), jnp.bfloat16),
+            jax.ShapeDtypeStruct((2 * LANES, 4 * LANES), jnp.bfloat16),
             jax.ShapeDtypeStruct((2 * LANES, LANES), jnp.bfloat16),
             float_array(width, ROWS, LANES),
             float_array(width, ROWS, LANES),
             float_array(5, ROWS, LANES),
         ],
         in_specs=[smem(), vmem()],
-        out_specs=[vmem()] * 6,
+        out_specs=[vmem()] * 5,
         compiler_params=params,
     )(atom_sites, stencil_weights(width))
 
@@ -538,8 +534,7 @@
             scratch_shapes=[cell] * cells
             + [
                 pltpu.VMEM((rows, 2 * LANES), jnp.bfloat16),
-                pltpu.VMEM((rows, 2 * LANES), jnp.float32),
-                pltpu.VMEM((rows, 2 * LANES), jnp.float32),
+                pltpu.VMEM((rows, 4 * LANES), jnp.float32),
                 cell,
                 pltpu.VMEM((rows, 2 * LANES), jnp.bfloat16),
                 pltpu.VMEM((width, ROWS, LANES), jnp.float32),

time: 93.4 us -> 93.3 us (level)
  no operation moved by 1% of the time
where the time goes in v9:
time: 93.3 us; the launch traced here: 91.9 us
  starting transfers between devices  47.3 us (51%)
  Pallas kernels  32.9 us (35%)
  waiting for transfers between devices  9.94 us (11%)
  between operations  1.46 us (2%)
    ppermute x23, starting transfers between devices, shifted(): lax.ppermute(value, axis_name, [((index + shift) % count, index) for inde...  33.9 us
    pallas_call x4, Pallas kernels, micro_call(): pl.pallas_call(kernel, out_shape=outputs, in_specs=[smem() if number < sc...  24.7 us
    all_to_all x3, starting transfers between devices, exchanged(): return lax.all_to_all(value, axes, split_axis=0, concat_axis=0, tiled=True)  13.4 us
    ppermute x23, waiting for transfers between devices, shifted(): lax.ppermute(value, axis_name, [((index + shift) % count, index) for inde...  9.93 us
    pallas_call x1, Pallas kernels, per_device(): pl.pallas_call(functools.partial(pack_kernel, parts, share, main_count, 0...  2.06 us
    pallas_call x1, Pallas kernels, per_device(): pl.pallas_call(functools.partial(pack_pieces_kernel, parts, share, last_c...  1.93 us
  transfers between devices with their start and end apart: 26, of which 9 were waited for; matrix products, arithmetic and copies ran while one was open for 0% of the time, Pallas kernels for 20%

profile of v9, /device:TPU:0, one launch (start us, length us, event | category | flops | bytes accessed | tf_op | source)
XLA Modules:
  0.0 91.9 jit_solution(2015932582455573312)
XLA Ops:
  0.6 2.1 %shard_map.77 = f32[4,5,64,128]{3,2,1,0:T(8,128)} custom-call(f32[2,16,64,128]{3,2,1,0:T(8,128)} %bitcast.19, f32[64,128]{1,0:T(8,128)} %bitcast.22), custom_call_target="tpu_custom_call" | custom-call | tf_op jit(solution)/shard_map/pallas_call | solution.py:476
  2.7 6.5 %all-to-all-start = ((f32[4,5,64,128]{3,2,1,0:T(8,128)}), f32[4,5,64,128]{3,2,1,0:T(8,128)S(1)}, u32[]{:S(2)}, u32[]{:S(2)}) async-start(f32[4,5,64,128]{3,2,1,0:T(8,128)} %shard_map.77), calls=%async_computation | async-start | bytes 1310720 | tf_op jit(solution)/shard_map/all_to_all | solution.py:441
  9.2 1.5 %collective-permute-start.5 = (f32[2,64]{1,0:T(2,128)S(1)}, f32[2,64]{1,0:T(2,128)S(1)}, u32[]{:S(2)}, u32[]{:S(2)}) collective-permute-start(f32[2,64]{1,0:T(2,128)S(1)} %copy-done.1), channel_id=1, source_target_pairs={{24,0},{28,4},{0,8},{4,12},{8,16},{12,20},{16,24},{20,28},{25,1},{... | collective-permute-start | bytes 1544 | tf_op jit(solution)/shard_map/ppermute | solution.py:445
  10.7 2.4 %collective-permute-start.4 = (f32[2,64]{1,0:T(2,128)S(1)}, f32[2,64]{1,0:T(2,128)S(1)}, u32[]{:S(2)}, u32[]{:S(2)}) collective-permute-start(f32[2,64]{1,0:T(2,128)S(1)} %copy-done.1), channel_id=1, source_target_pairs={{20,0},{24,4},{28,8},{0,12},{4,16},{8,20},{12,24},{16,28},{21,1},{... | collective-permute-start | bytes 1544 | tf_op jit(solution)/shard_map/ppermute | solution.py:445
  13.7 1.4 %collective-permute-start.1 = (f32[2,64]{1,0:T(2,128)S(1)}, f32[2,64]{1,0:T(2,128)S(1)}, u32[]{:S(2)}, u32[]{:S(2)}) collective-permute-start(f32[2,64]{1,0:T(2,128)S(1)} %copy-done.1), channel_id=1, source_target_pairs={{8,0},{12,4},{16,8},{20,12},{24,16},{28,20},{0,24},{4,28},{9,1},{1... | collective-permute-start | bytes 1544 | tf_op jit(solution)/shard_map/ppermute | solution.py:445
  15.2 2.3 %collective-permute-start = (f32[2,64]{1,0:T(2,128)S(1)}, f32[2,64]{1,0:T(2,128)S(1)}, u32[]{:S(2)}, u32[]{:S(2)}) collective-permute-start(f32[2,64]{1,0:T(2,128)S(1)} %copy-done.1), channel_id=1, source_target_pairs={{4,0},{8,4},{12,8},{16,12},{20,16},{24,20},{28,24},{0,28},{5,1},{9... | collective-permute-start | bytes 1544 | tf_op jit(solution)/shard_map/ppermute | solution.py:445
  20.0 1.9 %shard_map.79 = (f32[4,64,128]{2,1,0:T(8,128)}, f32[4,64,128]{2,1,0:T(8,128)}, f32[4,64,128]{2,1,0:T(8,128)}, f32[4,64,128]{2,1,0:T(8,128)}) custom-call(s32[1]{0:T(128)} %bitcast.9.here_ref.refs_0_, f32[2,16,64,128]{3,2,1,0:T(8,128)} %bitcast.20), custom_call_target="tpu_custom_call" | custom-call | tf_op jit(solution)/shard_map/pallas_call | solution.py:512
  21.9 2.1 %collective-permute-start.7 = (f32[4,64,128]{2,1,0:T(8,128)}, f32[4,64,128]{2,1,0:T(8,128)S(1)}, u32[]{:S(2)}, u32[]{:S(2)}) collective-permute-start(f32[4,64,128]{2,1,0:T(8,128)} %get-tuple-element.30), channel_id=1, source_target_pairs={{3,0},{0,1},{1,2},{2,3},{7,4},{4,5},{5,6},{6,7},{11,8},{8,9},{9,10... | collective-permute-start | bytes 393224 | tf_op jit(solution)/shard_map/ppermute | solution.py:445
  24.0 2.4 %collective-permute-start.8 = (f32[4,64,128]{2,1,0:T(8,128)}, f32[4,64,128]{2,1,0:T(8,128)S(1)}, u32[]{:S(2)}, u32[]{:S(2)}) collective-permute-start(f32[4,64,128]{2,1,0:T(8,128)} %get-tuple-element.31), channel_id=1, source_target_pairs={{2,0},{3,1},{0,2},{1,3},{6,4},{7,5},{4,6},{5,7},{10,8},{11,9},{8,1... | collective-permute-start | bytes 393224 | tf_op jit(solution)/shard_map/ppermute | solution.py:445
  26.4 1.5 %collective-permute-start.9 = (f32[4,64,128]{2,1,0:T(8,128)}, f32[4,64,128]{2,1,0:T(8,128)S(1)}, u32[]{:S(2)}, u32[]{:S(2)}) collective-permute-start(f32[4,64,128]{2,1,0:T(8,128)} %get-tuple-element.32), channel_id=1, source_target_pairs={{1,0},{2,1},{3,2},{0,3},{5,4},{6,5},{7,6},{4,7},{9,8},{10,9},{11,1... | collective-permute-start | bytes 393224 | tf_op jit(solution)/shard_map/ppermute | solution.py:445
  27.8 5.7 %shard_map.81 = (f32[4,32,8,128]{3,2,1,0:T(8,128)S(1)}, f32[2,8,128]{2,1,0:T(8,128)S(1)}, f32[32,8,128]{2,1,0:T(8,128)S(1)}) custom-call(f32[3]{0:T(128)S(1)} %shard_map.78.scalar_ref, f32[4,5,64,128]{3,2,1,0:T(8,128)S(1)} %all-to-all-done.refs_0_, bf16[256,512]{1,0:T(8,128)(2,1)S(1)} %get-tuple-element.33.refs_1_.refs_6_.refs_5_, ...), custom_call_target="tpu_custom_call" | custom-call | flops 1610612736 | bytes 4194304 | tf_op jit(solution)/shard_map/pallas_call | solution.py:529
  33.5 2.0 %collective-permute-done.8.refs_3_ = f32[4,64,128]{2,1,0:T(8,128)S(1)} collective-permute-done((f32[4,64,128]{2,1,0:T(8,128)}, f32[4,64,128]{2,1,0:T(8,128)S(1)}, u32[]{:S(2)}, u32[]{:S(2)}) %collective-permute-start.8) | collective-permute-done | bytes 131104 | tf_op jit(solution)/shard_map/ppermute | solution.py:445
  35.5 5.7 %shard_map.82 = (f32[4,32,8,128]{3,2,1,0:T(8,128)S(1)}, f32[2,8,128]{2,1,0:T(8,128)S(1)}) custom-call(f32[3]{0:T(128)S(1)} %shard_map.78.scalar_ref, s32[1]{0:T(128)} %bitcast.9.here_ref.refs_0_, f32[4,64,128]{2,1,0:T(8,128)S(1)} %copy-done.2, f32[4,64,128]{2,1,0:T(8,128)S(1)} %collective-permute-done.7.refs_2_, ...), custom_call_target="tpu_custom_call" | custom-call | flops 1610612736 | bytes 4194304 | tf_op jit(solution)/shard_map/pallas_call | solution.py:529
  41.2 3.4 %collective-permute-start.12 = (f32[2,8,128]{2,1,0:T(8,128)S(1)}, f32[2,8,128]{2,1,0:T(8,128)S(1)}, u32[]{:S(2)}, u32[]{:S(2)}) collective-permute-start(f32[2,8,128]{2,1,0:T(8,128)S(1)} %get-tuple-element.40.refs_0_.refs_1_), channel_id=1, source_target_pairs={{3,0},{0,1},{1,2},{2,3},{7,4},{4,5},{5,6},{6,7},{11,8},{8,9},{9,10... | collective-permute-start | bytes 24584 | tf_op jit(solution)/shard_map/ppermute | solution.py:445
  44.6 2.0 %collective-permute-start.11 = (f32[2,8,128]{2,1,0:T(8,128)S(1)}, f32[2,8,128]{2,1,0:T(8,128)S(1)}, u32[]{:S(2)}, u32[]{:S(2)}) collective-permute-start(f32[2,8,128]{2,1,0:T(8,128)S(1)} %get-tuple-element.40.refs_0_.refs_1_), channel_id=1, source_target_pairs={{2,0},{3,1},{0,2},{1,3},{6,4},{7,5},{4,6},{5,7},{10,8},{11,9},{8,1... | collective-permute-start | bytes 24584 | tf_op jit(solution)/shard_map/ppermute | solution.py:445
  50.3 6.4 %shard_map.83 = (f32[4,4,64,128]{3,2,1,0:T(8,128)}, f32[1]{0:T(128)}, f32[2,8,128]{2,1,0:T(8,128)S(1)}) custom-call(f32[3]{0:T(128)S(1)} %shard_map.78.scalar_ref, f32[2,8,128]{2,1,0:T(8,128)S(1)} %get-tuple-element.40.refs_0_.refs_1_, f32[2,8,128]{2,1,0:T(8,128)S(1)} %collective-permute-done.10.refs_1_, f32[2,8,128]{2,1,0:T(8,128)S(1)} %collective-permute-done.11.refs_2_, ...), custom_call_target="tpu_custom_call" | custom-call | flops 1610612736 | bytes 4194304 | tf_op jit(solution)/shard_map/pallas_call | solution.py:529
  56.6 3.5 %all-to-all-start.2 = ((f32[4,4,64,128]{3,2,1,0:T(8,128)}), f32[4,4,64,128]{3,2,1,0:T(8,128)S(1)}, u32[]{:S(2)}, u32[]{:S(2)}) async-start(f32[4,4,64,128]{3,2,1,0:T(8,128)} %get-tuple-element.48), calls=%async_computation.2 | async-start | bytes 1048576 | tf_op jit(solution)/shard_map/all_to_all | solution.py:441
  60.1 7.0 %shard_map.84 = (f32[4,4,64,128]{3,2,1,0:T(8,128)}, f32[8,128]{1,0:T(8,128)S(1)}) custom-call(f32[3]{0:T(128)S(1)} %shard_map.78.scalar_ref, f32[1]{0:T(128)} %get-tuple-element.42.refs_0_, f32[2,8,128]{2,1,0:T(8,128)S(1)} %get-tuple-element.40.refs_0_.refs_1_, f32[2,8,128]{2,1,0:T(8,128)S(1)} %get-tuple-element.43.refs_2_, ...), custom_call_target="tpu_custom_call" | custom-call | flops 1610612736 | bytes 4194304 | tf_op jit(solution)/shard_map/pallas_call | solution.py:529
  67.1 2.0 %collective-permute-start.15 = (f32[8,128]{1,0:T(8,128)S(1)}, f32[8,128]{1,0:T(8,128)S(1)}, u32[]{:S(2)}, u32[]{:S(2)}) collective-permute-start(f32[8,128]{1,0:T(8,128)S(1)} %get-tuple-element.46), channel_id=1, source_target_pairs={{3,0},{0,1},{1,2},{2,3},{7,4},{4,5},{5,6},{6,7},{11,8},{8,9},{9,10... | collective-permute-start | bytes 12296 | tf_op jit(solution)/shard_map/ppermute | solution.py:445
  69.1 1.8 %collective-permute-start.14 = (f32[8,128]{1,0:T(8,128)S(1)}, f32[8,128]{1,0:T(8,128)S(1)}, u32[]{:S(2)}, u32[]{:S(2)}) collective-permute-start(f32[8,128]{1,0:T(8,128)S(1)} %get-tuple-element.46), channel_id=1, source_target_pairs={{1,0},{2,1},{3,2},{0,3},{5,4},{6,5},{7,6},{4,7},{9,8},{10,9},{11,1... | collective-permute-start | bytes 12296 | tf_op jit(solution)/shard_map/ppermute | solution.py:445
  73.1 2.3 %collective-permute-done.13 = f32[8,128]{1,0:T(8,128)S(1)} collective-permute-done((f32[8,128]{1,0:T(8,128)S(1)}, f32[8,128]{1,0:T(8,128)S(1)}, u32[]{:S(2)}, u32[]{:S(2)}) %collective-permute-start.13) | collective-permute-done | bytes 4128 | tf_op jit(solution)/shard_map/ppermute | solution.py:445
  75.4 3.5 %all-to-all-start.1 = ((f32[4,4,64,128]{3,2,1,0:T(8,128)}), f32[4,4,64,128]{3,2,1,0:T(8,128)S(1)}, u32[]{:S(2)}, u32[]{:S(2)}) async-start(f32[4,4,64,128]{3,2,1,0:T(8,128)} %get-tuple-element.47), calls=%async_computation.1 | async-start | bytes 1048576 | tf_op jit(solution)/shard_map/all_to_all | solution.py:441
  80.2 3.9 %collective-permute-start.20 = (f32[8,128]{1,0:T(8,128)S(1)}, f32[8,128]{1,0:T(8,128)S(1)}, u32[]{:S(2)}, u32[]{:S(2)}) collective-permute-start(f32[8,128]{1,0:T(8,128)S(1)} %add_add_fusion.refs_0_), channel_id=1, source_target_pairs={{20,0},{24,4},{28,8},{0,12},{4,16},{8,20},{12,24},{16,28},{21,1},{... | collective-permute-start | bytes 12296 | tf_op jit(solution)/shard_map/ppermute | solution.py:445
  85.9 2.1 %collective-permute-start.16 = (f32[8,128]{1,0:T(8,128)S(1)}, f32[8,128]{1,0:T(8,128)S(1)}, u32[]{:S(2)}, u32[]{:S(2)}) collective-permute-start(f32[8,128]{1,0:T(8,128)S(1)} %add_add_fusion.refs_0_), channel_id=1, source_target_pairs={{4,0},{8,4},{12,8},{16,12},{20,16},{24,20},{28,24},{0,28},{5,1},{9... | collective-permute-start | bytes 12296 | tf_op jit(solution)/shard_map/ppermute | solution.py:445
  (51 shorter events, 15.2 us)
Async XLA Ops:
  2.7 25.1 %all-to-all-start = ((f32[4,5,64,128]{3,2,1,0:T(8,128)}), f32[4,5,64,128]{3,2,1,0:T(8,128)S(1)}, u32[]{:S(2)}, u32[]{:S(2)}) async-start(f32[4,5,64,128]{3,2,1,0:T(8,128)} %shard_map.77), calls=%async_computation | async-start | bytes 1310720 | tf_op jit(solution)/shard_map/all_to_all | solution.py:441
  9.2 4.5 %collective-permute-start.6 = (f32[2,64]{1,0:T(2,128)S(1)}, f32[2,64]{1,0:T(2,128)S(1)}, u32[]{:S(2)}, u32[]{:S(2)}) collective-permute-start(f32[2,64]{1,0:T(2,128)S(1)} %copy-done.1), channel_id=1, source_target_pairs={{28,0},{0,4},{4,8},{8,12},{12,16},{16,20},{20,24},{24,28},{29,1},{... | collective-permute-start | bytes 1544 | tf_op jit(solution)/shard_map/ppermute | solution.py:445
  9.2 6.0 %collective-permute-start.5 = (f32[2,64]{1,0:T(2,128)S(1)}, f32[2,64]{1,0:T(2,128)S(1)}, u32[]{:S(2)}, u32[]{:S(2)}) collective-permute-start(f32[2,64]{1,0:T(2,128)S(1)} %copy-done.1), channel_id=1, source_target_pairs={{24,0},{28,4},{0,8},{4,12},{8,16},{12,20},{16,24},{20,28},{25,1},{... | collective-permute-start | bytes 1544 | tf_op jit(solution)/shard_map/ppermute | solution.py:445
  10.7 8.5 %collective-permute-start.4 = (f32[2,64]{1,0:T(2,128)S(1)}, f32[2,64]{1,0:T(2,128)S(1)}, u32[]{:S(2)}, u32[]{:S(2)}) collective-permute-start(f32[2,64]{1,0:T(2,128)S(1)} %copy-done.1), channel_id=1, source_target_pairs={{20,0},{24,4},{28,8},{0,12},{4,16},{8,20},{12,24},{16,28},{21,1},{... | collective-permute-start | bytes 1544 | tf_op jit(solution)/shard_map/ppermute | solution.py:445
  13.1 6.1 %collective-permute-start.3 = (f32[2,64]{1,0:T(2,128)S(1)}, f32[2,64]{1,0:T(2,128)S(1)}, u32[]{:S(2)}, u32[]{:S(2)}) collective-permute-start(f32[2,64]{1,0:T(2,128)S(1)} %copy-done.1), channel_id=1, source_target_pairs={{16,0},{20,4},{24,8},{28,12},{0,16},{4,20},{8,24},{12,28},{17,1},{... | collective-permute-start | bytes 1544 | tf_op jit(solution)/shard_map/ppermute | solution.py:445
  13.6 5.6 %collective-permute-start.2 = (f32[2,64]{1,0:T(2,128)S(1)}, f32[2,64]{1,0:T(2,128)S(1)}, u32[]{:S(2)}, u32[]{:S(2)}) collective-permute-start(f32[2,64]{1,0:T(2,128)S(1)} %copy-done.1), channel_id=1, source_target_pairs={{12,0},{16,4},{20,8},{24,12},{28,16},{0,20},{4,24},{8,28},{13,1},{... | collective-permute-start | bytes 1544 | tf_op jit(solution)/shard_map/ppermute | solution.py:445
  13.7 5.5 %collective-permute-start.1 = (f32[2,64]{1,0:T(2,128)S(1)}, f32[2,64]{1,0:T(2,128)S(1)}, u32[]{:S(2)}, u32[]{:S(2)}) collective-permute-start(f32[2,64]{1,0:T(2,128)S(1)} %copy-done.1), channel_id=1, source_target_pairs={{8,0},{12,4},{16,8},{20,12},{24,16},{28,20},{0,24},{4,28},{9,1},{1... | collective-permute-start | bytes 1544 | tf_op jit(solution)/shard_map/ppermute | solution.py:445
  15.2 4.1 %collective-permute-start = (f32[2,64]{1,0:T(2,128)S(1)}, f32[2,64]{1,0:T(2,128)S(1)}, u32[]{:S(2)}, u32[]{:S(2)}) collective-permute-start(f32[2,64]{1,0:T(2,128)S(1)} %copy-done.1), channel_id=1, source_target_pairs={{4,0},{8,4},{12,8},{16,12},{20,16},{24,20},{28,24},{0,28},{5,1},{9... | collective-permute-start | bytes 1544 | tf_op jit(solution)/shard_map/ppermute | solution.py:445
  21.9 11.6 %collective-permute-start.7 = (f32[4,64,128]{2,1,0:T(8,128)}, f32[4,64,128]{2,1,0:T(8,128)S(1)}, u32[]{:S(2)}, u32[]{:S(2)}) collective-permute-start(f32[4,64,128]{2,1,0:T(8,128)} %get-tuple-element.30), channel_id=1, source_target_pairs={{3,0},{0,1},{1,2},{2,3},{7,4},{4,5},{5,6},{6,7},{11,8},{8,9},{9,10... | collective-permute-start | bytes 393224 | tf_op jit(solution)/shard_map/ppermute | solution.py:445
  24.0 11.5 %collective-permute-start.8 = (f32[4,64,128]{2,1,0:T(8,128)}, f32[4,64,128]{2,1,0:T(8,128)S(1)}, u32[]{:S(2)}, u32[]{:S(2)}) collective-permute-start(f32[4,64,128]{2,1,0:T(8,128)} %get-tuple-element.31), channel_id=1, source_target_pairs={{2,0},{3,1},{0,2},{1,3},{6,4},{7,5},{4,6},{5,7},{10,8},{11,9},{8,1... | collective-permute-start | bytes 393224 | tf_op jit(solution)/shard_map/ppermute | solution.py:445
  26.4 9.2 %collective-permute-start.9 = (f32[4,64,128]{2,1,0:T(8,128)}, f32[4,64,128]{2,1,0:T(8,128)S(1)}, u32[]{:S(2)}, u32[]{:S(2)}) collective-permute-start(f32[4,64,128]{2,1,0:T(8,128)} %get-tuple-element.32), channel_id=1, source_target_pairs={{1,0},{2,1},{3,2},{0,3},{5,4},{6,5},{7,6},{4,7},{9,8},{10,9},{11,1... | collective-permute-start | bytes 393224 | tf_op jit(solution)/shard_map/ppermute | solution.py:445
  41.2 6.5 %collective-permute-start.12 = (f32[2,8,128]{2,1,0:T(8,128)S(1)}, f32[2,8,128]{2,1,0:T(8,128)S(1)}, u32[]{:S(2)}, u32[]{:S(2)}) collective-permute-start(f32[2,8,128]{2,1,0:T(8,128)S(1)} %get-tuple-element.40.refs_0_.refs_1_), channel_id=1, source_target_pairs={{3,0},{0,1},{1,2},{2,3},{7,4},{4,5},{5,6},{6,7},{11,8},{8,9},{9,10... | collective-permute-start | bytes 24584 | tf_op jit(solution)/shard_map/ppermute | solution.py:445
  44.6 4.5 %collective-permute-start.11 = (f32[2,8,128]{2,1,0:T(8,128)S(1)}, f32[2,8,128]{2,1,0:T(8,128)S(1)}, u32[]{:S(2)}, u32[]{:S(2)}) collective-permute-start(f32[2,8,128]{2,1,0:T(8,128)S(1)} %get-tuple-element.40.refs_0_.refs_1_), channel_id=1, source_target_pairs={{2,0},{3,1},{0,2},{1,3},{6,4},{7,5},{4,6},{5,7},{10,8},{11,9},{8,1... | collective-permute-start | bytes 24584 | tf_op jit(solution)/shard_map/ppermute | solution.py:445
  46.6 3.7 %collective-permute-start.10 = (f32[2,8,128]{2,1,0:T(8,128)S(1)}, f32[2,8,128]{2,1,0:T(8,128)S(1)}, u32[]{:S(2)}, u32[]{:S(2)}) collective-permute-start(f32[2,8,128]{2,1,0:T(8,128)S(1)} %get-tuple-element.40.refs_0_.refs_1_), channel_id=1, source_target_pairs={{1,0},{2,1},{3,2},{0,3},{5,4},{6,5},{7,6},{4,7},{9,8},{10,9},{11,1... | collective-permute-start | bytes 24584 | tf_op jit(solution)/shard_map/ppermute | solution.py:445
  56.6 18.8 %all-to-all-start.2 = ((f32[4,4,64,128]{3,2,1,0:T(8,128)}), f32[4,4,64,128]{3,2,1,0:T(8,128)S(1)}, u32[]{:S(2)}, u32[]{:S(2)}) async-start(f32[4,4,64,128]{3,2,1,0:T(8,128)} %get-tuple-element.48), calls=%async_computation.2 | async-start | bytes 1048576 | tf_op jit(solution)/shard_map/all_to_all | solution.py:441
  67.1 5.5 %collective-permute-start.15 = (f32[8,128]{1,0:T(8,128)S(1)}, f32[8,128]{1,0:T(8,128)S(1)}, u32[]{:S(2)}, u32[]{:S(2)}) collective-permute-start(f32[8,128]{1,0:T(8,128)S(1)} %get-tuple-element.46), channel_id=1, source_target_pairs={{3,0},{0,1},{1,2},{2,3},{7,4},{4,5},{5,6},{6,7},{11,8},{8,9},{9,10... | collective-permute-start | bytes 12296 | tf_op jit(solution)/shard_map/ppermute | solution.py:445
  69.1 4.0 %collective-permute-start.14 = (f32[8,128]{1,0:T(8,128)S(1)}, f32[8,128]{1,0:T(8,128)S(1)}, u32[]{:S(2)}, u32[]{:S(2)}) collective-permute-start(f32[8,128]{1,0:T(8,128)S(1)} %get-tuple-element.46), channel_id=1, source_target_pairs={{1,0},{2,1},{3,2},{0,3},{5,4},{6,5},{7,6},{4,7},{9,8},{10,9},{11,1... | collective-permute-start | bytes 12296 | tf_op jit(solution)/shard_map/ppermute | solution.py:445
  70.9 4.5 %collective-permute-start.13 = (f32[8,128]{1,0:T(8,128)S(1)}, f32[8,128]{1,0:T(8,128)S(1)}, u32[]{:S(2)}, u32[]{:S(2)}) collective-permute-start(f32[8,128]{1,0:T(8,128)S(1)} %get-tuple-element.46), channel_id=1, source_target_pairs={{2,0},{3,1},{0,2},{1,3},{6,4},{7,5},{4,6},{5,7},{10,8},{11,9},{8,1... | collective-permute-start | bytes 12296 | tf_op jit(solution)/shard_map/ppermute | solution.py:445
  75.4 15.6 %all-to-all-start.1 = ((f32[4,4,64,128]{3,2,1,0:T(8,128)}), f32[4,4,64,128]{3,2,1,0:T(8,128)S(1)}, u32[]{:S(2)}, u32[]{:S(2)}) async-start(f32[4,4,64,128]{3,2,1,0:T(8,128)} %get-tuple-element.47), calls=%async_computation.1 | async-start | bytes 1048576 | tf_op jit(solution)/shard_map/all_to_all | solution.py:441
  78.9 5.8 %collective-permute-start.22 = (f32[8,128]{1,0:T(8,128)S(1)}, f32[8,128]{1,0:T(8,128)S(1)}, u32[]{:S(2)}, u32[]{:S(2)}) collective-permute-start(f32[8,128]{1,0:T(8,128)S(1)} %add_add_fusion.refs_0_), channel_id=1, source_target_pairs={{28,0},{0,4},{4,8},{8,12},{12,16},{16,20},{20,24},{24,28},{29,1},{... | collective-permute-start | bytes 12296 | tf_op jit(solution)/shard_map/ppermute | solution.py:445
  79.0 6.9 %collective-permute-start.21 = (f32[8,128]{1,0:T(8,128)S(1)}, f32[8,128]{1,0:T(8,128)S(1)}, u32[]{:S(2)}, u32[]{:S(2)}) collective-permute-start(f32[8,128]{1,0:T(8,128)S(1)} %add_add_fusion.refs_0_), channel_id=1, source_target_pairs={{24,0},{28,4},{0,8},{4,12},{8,16},{12,20},{16,24},{20,28},{25,1},{... | collective-permute-start | bytes 12296 | tf_op jit(solution)/shard_map/ppermute | solution.py:445
  80.2 7.9 %collective-permute-start.20 = (f32[8,128]{1,0:T(8,128)S(1)}, f32[8,128]{1,0:T(8,128)S(1)}, u32[]{:S(2)}, u32[]{:S(2)}) collective-permute-start(f32[8,128]{1,0:T(8,128)S(1)} %add_add_fusion.refs_0_), channel_id=1, source_target_pairs={{20,0},{24,4},{28,8},{0,12},{4,16},{8,20},{12,24},{16,28},{21,1},{... | collective-permute-start | bytes 12296 | tf_op jit(solution)/shard_map/ppermute | solution.py:445
  84.1 4.0 %collective-permute-start.19 = (f32[8,128]{1,0:T(8,128)S(1)}, f32[8,128]{1,0:T(8,128)S(1)}, u32[]{:S(2)}, u32[]{:S(2)}) collective-permute-start(f32[8,128]{1,0:T(8,128)S(1)} %add_add_fusion.refs_0_), channel_id=1, source_target_pairs={{16,0},{20,4},{24,8},{28,12},{0,16},{4,20},{8,24},{12,28},{17,1},{... | collective-permute-start | bytes 12296 | tf_op jit(solution)/shard_map/ppermute | solution.py:445
  84.1 4.0 %collective-permute-start.18 = (f32[8,128]{1,0:T(8,128)S(1)}, f32[8,128]{1,0:T(8,128)S(1)}, u32[]{:S(2)}, u32[]{:S(2)}) collective-permute-start(f32[8,128]{1,0:T(8,128)S(1)} %add_add_fusion.refs_0_), channel_id=1, source_target_pairs={{12,0},{16,4},{20,8},{24,12},{28,16},{0,20},{4,24},{8,28},{13,1},{... | collective-permute-start | bytes 12296 | tf_op jit(solution)/shard_map/ppermute | solution.py:445
  (6 other events, 41.1 us)

commit v10 on v9

--- a/solution.py
+++ b/solution.py
@@ -213,9 +213,8 @@
                 field_ref[number, start : start + block] = planes
                 total_ref[number, start : start + block] = planes
 
-    def one_order(order, carry):
-        inverse = jnp.where(order == 1, 1.0, jnp.where(order == 2, 0.5, jnp.where(order == 3, 1.0 / 3.0, 0.25)))
-        step_scale = inverse * time_step
+    def one_order(order):
+        step_scale = time_step / order
         kinetic = step_scale * KINETIC
         drift = step_scale * SLOPE * vector_value
         slopes = [drift * weight for weight in FIRST]
@@ -283,12 +282,13 @@
                     partial_ref[imaginary, start : start + block] + spreads[0],
                 )
                 for number, value in zip((real, imaginary), new):
-                    field_ref[number, start : start + block] = value
                     total_ref[number, start : start + block] += value
-                    store_split(split_ref, number, start, value)
-        return carry
-
-    lax.fori_loop(1, ORDER + 1, one_order, 0)
+                    if order < ORDER:
+                        field_ref[number, start : start + block] = value
+                        store_split(split_ref, number, start, value)
+
+    for order in range(1, ORDER + 1):
+        one_order(order)
 
 
 def sums_in_kernel(count, total_ref, width):

time: 93.3 us -> 92.5 us (level)
  waiting for transfers between devices: 9.94 us -> 10.9 us
    pallas_call x4, Pallas kernels: 24.7 us -> 23.7 us  [micro_call(): pl.pallas_call(kernel, out_shape=outputs, in_specs=[smem() if number < sc...]
  transfers between devices with their start and end apart: 26 -> 26, of which waited for: 9 -> 10; matrix products, arithmetic and copies ran while one was open for 0% -> 0% of each run, Pallas kernels for 20% -> 19%
where the time goes in v10:
time: 92.5 us; the launch traced here: 91.5 us
  starting transfers between devices  46.8 us (51%)
  Pallas kernels  32 us (35%)
  waiting for transfers between devices  10.9 us (12%)
  between operations  1.62 us (2%)
    ppermute x23, starting transfers between devices, shifted(): lax.ppermute(value, axis_name, [((index + shift) % count, index) for inde...  33.4 us
    pallas_call x4, Pallas kernels, micro_call(): pl.pallas_call(kernel, out_shape=outputs, in_specs=[smem() if number < sc...  23.7 us
    all_to_all x3, starting transfers between devices, exchanged(): return lax.all_to_all(value, axes, split_axis=0, concat_axis=0, tiled=True)  13.4 us
    ppermute x23, waiting for transfers between devices, shifted(): lax.ppermute(value, axis_name, [((index + shift) % count, index) for inde...  10.4 us
    pallas_call x1, Pallas kernels, per_device(): pl.pallas_call(functools.partial(pack_kernel, parts, share, main_count, 0...  2.06 us
    pallas_call x1, Pallas kernels, per_device(): pl.pallas_call(functools.partial(pack_pieces_kernel, parts, share, last_c...  1.93 us
  transfers between devices with their start and end apart: 26, of which 10 were waited for; matrix products, arithmetic and copies ran while one was open for 0% of the time, Pallas kernels for 19%

profile of v10, /device:TPU:0, one launch (start us, length us, event | category | flops | bytes accessed | tf_op | source)
XLA Modules:
  0.0 91.5 jit_solution(10055099842433362071)
XLA Ops:
  0.6 2.1 %shard_map.77 = f32[4,5,64,128]{3,2,1,0:T(8,128)} custom-call(f32[2,16,64,128]{3,2,1,0:T(8,128)} %bitcast.19, f32[64,128]{1,0:T(8,128)} %bitcast.22), custom_call_target="tpu_custom_call" | custom-call | tf_op jit(solution)/shard_map/pallas_call | solution.py:476
  2.7 6.5 %all-to-all-start = ((f32[4,5,64,128]{3,2,1,0:T(8,128)}), f32[4,5,64,128]{3,2,1,0:T(8,128)S(1)}, u32[]{:S(2)}, u32[]{:S(2)}) async-start(f32[4,5,64,128]{3,2,1,0:T(8,128)} %shard_map.77), calls=%async_computation | async-start | bytes 1310720 | tf_op jit(solution)/shard_map/all_to_all | solution.py:441
  9.2 1.5 %collective-permute-start.5 = (f32[2,64]{1,0:T(2,128)S(1)}, f32[2,64]{1,0:T(2,128)S(1)}, u32[]{:S(2)}, u32[]{:S(2)}) collective-permute-start(f32[2,64]{1,0:T(2,128)S(1)} %copy-done.1), channel_id=1, source_target_pairs={{24,0},{28,4},{0,8},{4,12},{8,16},{12,20},{16,24},{20,28},{25,1},{... | collective-permute-start | bytes 1544 | tf_op jit(solution)/shard_map/ppermute | solution.py:445
  10.7 2.4 %collective-permute-start.4 = (f32[2,64]{1,0:T(2,128)S(1)}, f32[2,64]{1,0:T(2,128)S(1)}, u32[]{:S(2)}, u32[]{:S(2)}) collective-permute-start(f32[2,64]{1,0:T(2,128)S(1)} %copy-done.1), channel_id=1, source_target_pairs={{20,0},{24,4},{28,8},{0,12},{4,16},{8,20},{12,24},{16,28},{21,1},{... | collective-permute-start | bytes 1544 | tf_op jit(solution)/shard_map/ppermute | solution.py:445
  13.7 1.4 %collective-permute-start.1 = (f32[2,64]{1,0:T(2,128)S(1)}, f32[2,64]{1,0:T(2,128)S(1)}, u32[]{:S(2)}, u32[]{:S(2)}) collective-permute-start(f32[2,64]{1,0:T(2,128)S(1)} %copy-done.1), channel_id=1, source_target_pairs={{8,0},{12,4},{16,8},{20,12},{24,16},{28,20},{0,24},{4,28},{9,1},{1... | collective-permute-start | bytes 1544 | tf_op jit(solution)/shard_map/ppermute | solution.py:445
  15.2 2.3 %collective-permute-start = (f32[2,64]{1,0:T(2,128)S(1)}, f32[2,64]{1,0:T(2,128)S(1)}, u32[]{:S(2)}, u32[]{:S(2)}) collective-permute-start(f32[2,64]{1,0:T(2,128)S(1)} %copy-done.1), channel_id=1, source_target_pairs={{4,0},{8,4},{12,8},{16,12},{20,16},{24,20},{28,24},{0,28},{5,1},{9... | collective-permute-start | bytes 1544 | tf_op jit(solution)/shard_map/ppermute | solution.py:445
  20.0 1.9 %shard_map.79 = (f32[4,64,128]{2,1,0:T(8,128)}, f32[4,64,128]{2,1,0:T(8,128)}, f32[4,64,128]{2,1,0:T(8,128)}, f32[4,64,128]{2,1,0:T(8,128)}) custom-call(s32[1]{0:T(128)} %bitcast.9.here_ref.refs_0_, f32[2,16,64,128]{3,2,1,0:T(8,128)} %bitcast.20), custom_call_target="tpu_custom_call" | custom-call | tf_op jit(solution)/shard_map/pallas_call | solution.py:512
  21.9 2.1 %collective-permute-start.7 = (f32[4,64,128]{2,1,0:T(8,128)}, f32[4,64,128]{2,1,0:T(8,128)S(1)}, u32[]{:S(2)}, u32[]{:S(2)}) collective-permute-start(f32[4,64,128]{2,1,0:T(8,128)} %get-tuple-element.30), channel_id=1, source_target_pairs={{3,0},{0,1},{1,2},{2,3},{7,4},{4,5},{5,6},{6,7},{11,8},{8,9},{9,10... | collective-permute-start | bytes 393224 | tf_op jit(solution)/shard_map/ppermute | solution.py:445
  24.0 2.4 %collective-permute-start.8 = (f32[4,64,128]{2,1,0:T(8,128)}, f32[4,64,128]{2,1,0:T(8,128)S(1)}, u32[]{:S(2)}, u32[]{:S(2)}) collective-permute-start(f32[4,64,128]{2,1,0:T(8,128)} %get-tuple-element.31), channel_id=1, source_target_pairs={{2,0},{3,1},{0,2},{1,3},{6,4},{7,5},{4,6},{5,7},{10,8},{11,9},{8,1... | collective-permute-start | bytes 393224 | tf_op jit(solution)/shard_map/ppermute | solution.py:445
  26.4 1.5 %collective-permute-start.9 = (f32[4,64,128]{2,1,0:T(8,128)}, f32[4,64,128]{2,1,0:T(8,128)S(1)}, u32[]{:S(2)}, u32[]{:S(2)}) collective-permute-start(f32[4,64,128]{2,1,0:T(8,128)} %get-tuple-element.32), channel_id=1, source_target_pairs={{1,0},{2,1},{3,2},{0,3},{5,4},{6,5},{7,6},{4,7},{9,8},{10,9},{11,1... | collective-permute-start | bytes 393224 | tf_op jit(solution)/shard_map/ppermute | solution.py:445
  27.8 5.3 %shard_map.81 = (f32[4,32,8,128]{3,2,1,0:T(8,128)S(1)}, f32[2,8,128]{2,1,0:T(8,128)S(1)}, f32[32,8,128]{2,1,0:T(8,128)S(1)}) custom-call(f32[3]{0:T(128)S(1)} %shard_map.78.scalar_ref, f32[4,5,64,128]{3,2,1,0:T(8,128)S(1)} %all-to-all-done.refs_0_, bf16[256,512]{1,0:T(8,128)(2,1)S(1)} %get-tuple-element.33.refs_1_.refs_6_.refs_5_, ...), custom_call_target="tpu_custom_call" | custom-call | flops 1610612736 | bytes 4194304 | tf_op jit(solution)/shard_map/pallas_call | solution.py:529
  33.1 2.4 %collective-permute-done.8.refs_3_ = f32[4,64,128]{2,1,0:T(8,128)S(1)} collective-permute-done((f32[4,64,128]{2,1,0:T(8,128)}, f32[4,64,128]{2,1,0:T(8,128)S(1)}, u32[]{:S(2)}, u32[]{:S(2)}) %collective-permute-start.8) | collective-permute-done | bytes 131104 | tf_op jit(solution)/shard_map/ppermute | solution.py:445
  35.5 5.4 %shard_map.82 = (f32[4,32,8,128]{3,2,1,0:T(8,128)S(1)}, f32[2,8,128]{2,1,0:T(8,128)S(1)}) custom-call(f32[3]{0:T(128)S(1)} %shard_map.78.scalar_ref, s32[1]{0:T(128)} %bitcast.9.here_ref.refs_0_, f32[4,64,128]{2,1,0:T(8,128)S(1)} %copy-done.2, f32[4,64,128]{2,1,0:T(8,128)S(1)} %collective-permute-done.7.refs_2_, ...), custom_call_target="tpu_custom_call" | custom-call | flops 1610612736 | bytes 4194304 | tf_op jit(solution)/shard_map/pallas_call | solution.py:529
  40.9 3.3 %collective-permute-start.12 = (f32[2,8,128]{2,1,0:T(8,128)S(1)}, f32[2,8,128]{2,1,0:T(8,128)S(1)}, u32[]{:S(2)}, u32[]{:S(2)}) collective-permute-start(f32[2,8,128]{2,1,0:T(8,128)S(1)} %get-tuple-element.40.refs_0_.refs_1_), channel_id=1, source_target_pairs={{3,0},{0,1},{1,2},{2,3},{7,4},{4,5},{5,6},{6,7},{11,8},{8,9},{9,10... | collective-permute-start | bytes 24584 | tf_op jit(solution)/shard_map/ppermute | solution.py:445
  44.3 2.0 %collective-permute-start.11 = (f32[2,8,128]{2,1,0:T(8,128)S(1)}, f32[2,8,128]{2,1,0:T(8,128)S(1)}, u32[]{:S(2)}, u32[]{:S(2)}) collective-permute-start(f32[2,8,128]{2,1,0:T(8,128)S(1)} %get-tuple-element.40.refs_0_.refs_1_), channel_id=1, source_target_pairs={{2,0},{3,1},{0,2},{1,3},{6,4},{7,5},{4,6},{5,7},{10,8},{11,9},{8,1... | collective-permute-start | bytes 24584 | tf_op jit(solution)/shard_map/ppermute | solution.py:445
  50.0 6.3 %shard_map.83 = (f32[4,4,64,128]{3,2,1,0:T(8,128)}, f32[1]{0:T(128)}, f32[2,8,128]{2,1,0:T(8,128)S(1)}) custom-call(f32[3]{0:T(128)S(1)} %shard_map.78.scalar_ref, f32[2,8,128]{2,1,0:T(8,128)S(1)} %get-tuple-element.40.refs_0_.refs_1_, f32[2,8,128]{2,1,0:T(8,128)S(1)} %collective-permute-done.10.refs_1_, f32[2,8,128]{2,1,0:T(8,128)S(1)} %collective-permute-done.11.refs_2_, ...), custom_call_target="tpu_custom_call" | custom-call | flops 1610612736 | bytes 4194304 | tf_op jit(solution)/shard_map/pallas_call | solution.py:529
  56.3 3.5 %all-to-all-start.2 = ((f32[4,4,64,128]{3,2,1,0:T(8,128)}), f32[4,4,64,128]{3,2,1,0:T(8,128)S(1)}, u32[]{:S(2)}, u32[]{:S(2)}) async-start(f32[4,4,64,128]{3,2,1,0:T(8,128)} %get-tuple-element.48), calls=%async_computation.2 | async-start | bytes 1048576 | tf_op jit(solution)/shard_map/all_to_all | solution.py:441
  59.8 6.8 %shard_map.84 = (f32[4,4,64,128]{3,2,1,0:T(8,128)}, f32[8,128]{1,0:T(8,128)S(1)}) custom-call(f32[3]{0:T(128)S(1)} %shard_map.78.scalar_ref, f32[1]{0:T(128)} %get-tuple-element.42.refs_0_, f32[2,8,128]{2,1,0:T(8,128)S(1)} %get-tuple-element.40.refs_0_.refs_1_, f32[2,8,128]{2,1,0:T(8,128)S(1)} %get-tuple-element.43.refs_2_, ...), custom_call_target="tpu_custom_call" | custom-call | flops 1610612736 | bytes 4194304 | tf_op jit(solution)/shard_map/pallas_call | solution.py:529
  66.6 2.0 %collective-permute-start.15 = (f32[8,128]{1,0:T(8,128)S(1)}, f32[8,128]{1,0:T(8,128)S(1)}, u32[]{:S(2)}, u32[]{:S(2)}) collective-permute-start(f32[8,128]{1,0:T(8,128)S(1)} %get-tuple-element.46), channel_id=1, source_target_pairs={{3,0},{0,1},{1,2},{2,3},{7,4},{4,5},{5,6},{6,7},{11,8},{8,9},{9,10... | collective-permute-start | bytes 12296 | tf_op jit(solution)/shard_map/ppermute | solution.py:445
  68.6 1.8 %collective-permute-start.14 = (f32[8,128]{1,0:T(8,128)S(1)}, f32[8,128]{1,0:T(8,128)S(1)}, u32[]{:S(2)}, u32[]{:S(2)}) collective-permute-start(f32[8,128]{1,0:T(8,128)S(1)} %get-tuple-element.46), channel_id=1, source_target_pairs={{1,0},{2,1},{3,2},{0,3},{5,4},{6,5},{7,6},{4,7},{9,8},{10,9},{11,1... | collective-permute-start | bytes 12296 | tf_op jit(solution)/shard_map/ppermute | solution.py:445
  72.6 2.3 %collective-permute-done.13 = f32[8,128]{1,0:T(8,128)S(1)} collective-permute-done((f32[8,128]{1,0:T(8,128)S(1)}, f32[8,128]{1,0:T(8,128)S(1)}, u32[]{:S(2)}, u32[]{:S(2)}) %collective-permute-start.13) | collective-permute-done | bytes 4128 | tf_op jit(solution)/shard_map/ppermute | solution.py:445
  74.9 3.5 %all-to-all-start.1 = ((f32[4,4,64,128]{3,2,1,0:T(8,128)}), f32[4,4,64,128]{3,2,1,0:T(8,128)S(1)}, u32[]{:S(2)}, u32[]{:S(2)}) async-start(f32[4,4,64,128]{3,2,1,0:T(8,128)} %get-tuple-element.47), calls=%async_computation.1 | async-start | bytes 1048576 | tf_op jit(solution)/shard_map/all_to_all | solution.py:441
  79.7 3.5 %collective-permute-start.20 = (f32[8,128]{1,0:T(8,128)S(1)}, f32[8,128]{1,0:T(8,128)S(1)}, u32[]{:S(2)}, u32[]{:S(2)}) collective-permute-start(f32[8,128]{1,0:T(8,128)S(1)} %add_add_fusion.refs_0_), channel_id=1, source_target_pairs={{20,0},{24,4},{28,8},{0,12},{4,16},{8,20},{12,24},{16,28},{21,1},{... | collective-permute-start | bytes 12296 | tf_op jit(solution)/shard_map/ppermute | solution.py:445
  84.9 2.1 %collective-permute-start.16 = (f32[8,128]{1,0:T(8,128)S(1)}, f32[8,128]{1,0:T(8,128)S(1)}, u32[]{:S(2)}, u32[]{:S(2)}) collective-permute-start(f32[8,128]{1,0:T(8,128)S(1)} %add_add_fusion.refs_0_), channel_id=1, source_target_pairs={{4,0},{8,4},{12,8},{16,12},{20,16},{24,20},{28,24},{0,28},{5,1},{9... | collective-permute-start | bytes 12296 | tf_op jit(solution)/shard_map/ppermute | solution.py:445
  (51 shorter events, 15.7 us)
Async XLA Ops:
  2.7 25.1 %all-to-all-start = ((f32[4,5,64,128]{3,2,1,0:T(8,128)}), f32[4,5,64,128]{3,2,1,0:T(8,128)S(1)}, u32[]{:S(2)}, u32[]{:S(2)}) async-start(f32[4,5,64,128]{3,2,1,0:T(8,128)} %shard_map.77), calls=%async_computation | async-start | bytes 1310720 | tf_op jit(solution)/shard_map/all_to_all | solution.py:441
  9.2 4.5 %collective-permute-start.6 = (f32[2,64]{1,0:T(2,128)S(1)}, f32[2,64]{1,0:T(2,128)S(1)}, u32[]{:S(2)}, u32[]{:S(2)}) collective-permute-start(f32[2,64]{1,0:T(2,128)S(1)} %copy-done.1), channel_id=1, source_target_pairs={{28,0},{0,4},{4,8},{8,12},{12,16},{16,20},{20,24},{24,28},{29,1},{... | collective-permute-start | bytes 1544 | tf_op jit(solution)/shard_map/ppermute | solution.py:445
  9.2 6.0 %collective-permute-start.5 = (f32[2,64]{1,0:T(2,128)S(1)}, f32[2,64]{1,0:T(2,128)S(1)}, u32[]{:S(2)}, u32[]{:S(2)}) collective-permute-start(f32[2,64]{1,0:T(2,128)S(1)} %copy-done.1), channel_id=1, source_target_pairs={{24,0},{28,4},{0,8},{4,12},{8,16},{12,20},{16,24},{20,28},{25,1},{... | collective-permute-start | bytes 1544 | tf_op jit(solution)/shard_map/ppermute | solution.py:445
  10.7 8.5 %collective-permute-start.4 = (f32[2,64]{1,0:T(2,128)S(1)}, f32[2,64]{1,0:T(2,128)S(1)}, u32[]{:S(2)}, u32[]{:S(2)}) collective-permute-start(f32[2,64]{1,0:T(2,128)S(1)} %copy-done.1), channel_id=1, source_target_pairs={{20,0},{24,4},{28,8},{0,12},{4,16},{8,20},{12,24},{16,28},{21,1},{... | collective-permute-start | bytes 1544 | tf_op jit(solution)/shard_map/ppermute | solution.py:445
  13.1 6.1 %collective-permute-start.3 = (f32[2,64]{1,0:T(2,128)S(1)}, f32[2,64]{1,0:T(2,128)S(1)}, u32[]{:S(2)}, u32[]{:S(2)}) collective-permute-start(f32[2,64]{1,0:T(2,128)S(1)} %copy-done.1), channel_id=1, source_target_pairs={{16,0},{20,4},{24,8},{28,12},{0,16},{4,20},{8,24},{12,28},{17,1},{... | collective-permute-start | bytes 1544 | tf_op jit(solution)/shard_map/ppermute | solution.py:445
  13.6 5.6 %collective-permute-start.2 = (f32[2,64]{1,0:T(2,128)S(1)}, f32[2,64]{1,0:T(2,128)S(1)}, u32[]{:S(2)}, u32[]{:S(2)}) collective-permute-start(f32[2,64]{1,0:T(2,128)S(1)} %copy-done.1), channel_id=1, source_target_pairs={{12,0},{16,4},{20,8},{24,12},{28,16},{0,20},{4,24},{8,28},{13,1},{... | collective-permute-start | bytes 1544 | tf_op jit(solution)/shard_map/ppermute | solution.py:445
  13.7 5.5 %collective-permute-start.1 = (f32[2,64]{1,0:T(2,128)S(1)}, f32[2,64]{1,0:T(2,128)S(1)}, u32[]{:S(2)}, u32[]{:S(2)}) collective-permute-start(f32[2,64]{1,0:T(2,128)S(1)} %copy-done.1), channel_id=1, source_target_pairs={{8,0},{12,4},{16,8},{20,12},{24,16},{28,20},{0,24},{4,28},{9,1},{1... | collective-permute-start | bytes 1544 | tf_op jit(solution)/shard_map/ppermute | solution.py:445
  15.2 4.1 %collective-permute-start = (f32[2,64]{1,0:T(2,128)S(1)}, f32[2,64]{1,0:T(2,128)S(1)}, u32[]{:S(2)}, u32[]{:S(2)}) collective-permute-start(f32[2,64]{1,0:T(2,128)S(1)} %copy-done.1), channel_id=1, source_target_pairs={{4,0},{8,4},{12,8},{16,12},{20,16},{24,20},{28,24},{0,28},{5,1},{9... | collective-permute-start | bytes 1544 | tf_op jit(solution)/shard_map/ppermute | solution.py:445
  21.9 11.2 %collective-permute-start.7 = (f32[4,64,128]{2,1,0:T(8,128)}, f32[4,64,128]{2,1,0:T(8,128)S(1)}, u32[]{:S(2)}, u32[]{:S(2)}) collective-permute-start(f32[4,64,128]{2,1,0:T(8,128)} %get-tuple-element.30), channel_id=1, source_target_pairs={{3,0},{0,1},{1,2},{2,3},{7,4},{4,5},{5,6},{6,7},{11,8},{8,9},{9,10... | collective-permute-start | bytes 393224 | tf_op jit(solution)/shard_map/ppermute | solution.py:445
  24.0 11.5 %collective-permute-start.8 = (f32[4,64,128]{2,1,0:T(8,128)}, f32[4,64,128]{2,1,0:T(8,128)S(1)}, u32[]{:S(2)}, u32[]{:S(2)}) collective-permute-start(f32[4,64,128]{2,1,0:T(8,128)} %get-tuple-element.31), channel_id=1, source_target_pairs={{2,0},{3,1},{0,2},{1,3},{6,4},{7,5},{4,6},{5,7},{10,8},{11,9},{8,1... | collective-permute-start | bytes 393224 | tf_op jit(solution)/shard_map/ppermute | solution.py:445
  26.4 9.2 %collective-permute-start.9 = (f32[4,64,128]{2,1,0:T(8,128)}, f32[4,64,128]{2,1,0:T(8,128)S(1)}, u32[]{:S(2)}, u32[]{:S(2)}) collective-permute-start(f32[4,64,128]{2,1,0:T(8,128)} %get-tuple-element.32), channel_id=1, source_target_pairs={{1,0},{2,1},{3,2},{0,3},{5,4},{6,5},{7,6},{4,7},{9,8},{10,9},{11,1... | collective-permute-start | bytes 393224 | tf_op jit(solution)/shard_map/ppermute | solution.py:445
  40.9 6.5 %collective-permute-start.12 = (f32[2,8,128]{2,1,0:T(8,128)S(1)}, f32[2,8,128]{2,1,0:T(8,128)S(1)}, u32[]{:S(2)}, u32[]{:S(2)}) collective-permute-start(f32[2,8,128]{2,1,0:T(8,128)S(1)} %get-tuple-element.40.refs_0_.refs_1_), channel_id=1, source_target_pairs={{3,0},{0,1},{1,2},{2,3},{7,4},{4,5},{5,6},{6,7},{11,8},{8,9},{9,10... | collective-permute-start | bytes 24584 | tf_op jit(solution)/shard_map/ppermute | solution.py:445
  44.3 4.5 %collective-permute-start.11 = (f32[2,8,128]{2,1,0:T(8,128)S(1)}, f32[2,8,128]{2,1,0:T(8,128)S(1)}, u32[]{:S(2)}, u32[]{:S(2)}) collective-permute-start(f32[2,8,128]{2,1,0:T(8,128)S(1)} %get-tuple-element.40.refs_0_.refs_1_), channel_id=1, source_target_pairs={{2,0},{3,1},{0,2},{1,3},{6,4},{7,5},{4,6},{5,7},{10,8},{11,9},{8,1... | collective-permute-start | bytes 24584 | tf_op jit(solution)/shard_map/ppermute | solution.py:445
  46.3 3.7 %collective-permute-start.10 = (f32[2,8,128]{2,1,0:T(8,128)S(1)}, f32[2,8,128]{2,1,0:T(8,128)S(1)}, u32[]{:S(2)}, u32[]{:S(2)}) collective-permute-start(f32[2,8,128]{2,1,0:T(8,128)S(1)} %get-tuple-element.40.refs_0_.refs_1_), channel_id=1, source_target_pairs={{1,0},{2,1},{3,2},{0,3},{5,4},{6,5},{7,6},{4,7},{9,8},{10,9},{11,1... | collective-permute-start | bytes 24584 | tf_op jit(solution)/shard_map/ppermute | solution.py:445
  56.3 18.6 %all-to-all-start.2 = ((f32[4,4,64,128]{3,2,1,0:T(8,128)}), f32[4,4,64,128]{3,2,1,0:T(8,128)S(1)}, u32[]{:S(2)}, u32[]{:S(2)}) async-start(f32[4,4,64,128]{3,2,1,0:T(8,128)} %get-tuple-element.48), calls=%async_computation.2 | async-start | bytes 1048576 | tf_op jit(solution)/shard_map/all_to_all | solution.py:441
  66.6 5.5 %collective-permute-start.15 = (f32[8,128]{1,0:T(8,128)S(1)}, f32[8,128]{1,0:T(8,128)S(1)}, u32[]{:S(2)}, u32[]{:S(2)}) collective-permute-start(f32[8,128]{1,0:T(8,128)S(1)} %get-tuple-element.46), channel_id=1, source_target_pairs={{3,0},{0,1},{1,2},{2,3},{7,4},{4,5},{5,6},{6,7},{11,8},{8,9},{9,10... | collective-permute-start | bytes 12296 | tf_op jit(solution)/shard_map/ppermute | solution.py:445
  68.6 4.0 %collective-permute-start.14 = (f32[8,128]{1,0:T(8,128)S(1)}, f32[8,128]{1,0:T(8,128)S(1)}, u32[]{:S(2)}, u32[]{:S(2)}) collective-permute-start(f32[8,128]{1,0:T(8,128)S(1)} %get-tuple-element.46), channel_id=1, source_target_pairs={{1,0},{2,1},{3,2},{0,3},{5,4},{6,5},{7,6},{4,7},{9,8},{10,9},{11,1... | collective-permute-start | bytes 12296 | tf_op jit(solution)/shard_map/ppermute | solution.py:445
  70.4 4.5 %collective-permute-start.13 = (f32[8,128]{1,0:T(8,128)S(1)}, f32[8,128]{1,0:T(8,128)S(1)}, u32[]{:S(2)}, u32[]{:S(2)}) collective-permute-start(f32[8,128]{1,0:T(8,128)S(1)} %get-tuple-element.46), channel_id=1, source_target_pairs={{2,0},{3,1},{0,2},{1,3},{6,4},{7,5},{4,6},{5,7},{10,8},{11,9},{8,1... | collective-permute-start | bytes 12296 | tf_op jit(solution)/shard_map/ppermute | solution.py:445
  74.9 15.6 %all-to-all-start.1 = ((f32[4,4,64,128]{3,2,1,0:T(8,128)}), f32[4,4,64,128]{3,2,1,0:T(8,128)S(1)}, u32[]{:S(2)}, u32[]{:S(2)}) async-start(f32[4,4,64,128]{3,2,1,0:T(8,128)} %get-tuple-element.47), calls=%async_computation.1 | async-start | bytes 1048576 | tf_op jit(solution)/shard_map/all_to_all | solution.py:441
  78.4 5.4 %collective-permute-start.22 = (f32[8,128]{1,0:T(8,128)S(1)}, f32[8,128]{1,0:T(8,128)S(1)}, u32[]{:S(2)}, u32[]{:S(2)}) collective-permute-start(f32[8,128]{1,0:T(8,128)S(1)} %add_add_fusion.refs_0_), channel_id=1, source_target_pairs={{28,0},{0,4},{4,8},{8,12},{12,16},{16,20},{20,24},{24,28},{29,1},{... | collective-permute-start | bytes 12296 | tf_op jit(solution)/shard_map/ppermute | solution.py:445
  78.5 6.5 %collective-permute-start.21 = (f32[8,128]{1,0:T(8,128)S(1)}, f32[8,128]{1,0:T(8,128)S(1)}, u32[]{:S(2)}, u32[]{:S(2)}) collective-permute-start(f32[8,128]{1,0:T(8,128)S(1)} %add_add_fusion.refs_0_), channel_id=1, source_target_pairs={{24,0},{28,4},{0,8},{4,12},{8,16},{12,20},{16,24},{20,28},{25,1},{... | collective-permute-start | bytes 12296 | tf_op jit(solution)/shard_map/ppermute | solution.py:445
  79.7 7.4 %collective-permute-start.20 = (f32[8,128]{1,0:T(8,128)S(1)}, f32[8,128]{1,0:T(8,128)S(1)}, u32[]{:S(2)}, u32[]{:S(2)}) collective-permute-start(f32[8,128]{1,0:T(8,128)S(1)} %add_add_fusion.refs_0_), channel_id=1, source_target_pairs={{20,0},{24,4},{28,8},{0,12},{4,16},{8,20},{12,24},{16,28},{21,1},{... | collective-permute-start | bytes 12296 | tf_op jit(solution)/shard_map/ppermute | solution.py:445
  83.2 4.0 %collective-permute-start.19 = (f32[8,128]{1,0:T(8,128)S(1)}, f32[8,128]{1,0:T(8,128)S(1)}, u32[]{:S(2)}, u32[]{:S(2)}) collective-permute-start(f32[8,128]{1,0:T(8,128)S(1)} %add_add_fusion.refs_0_), channel_id=1, source_target_pairs={{16,0},{20,4},{24,8},{28,12},{0,16},{4,20},{8,24},{12,28},{17,1},{... | collective-permute-start | bytes 12296 | tf_op jit(solution)/shard_map/ppermute | solution.py:445
  83.2 4.0 %collective-permute-start.18 = (f32[8,128]{1,0:T(8,128)S(1)}, f32[8,128]{1,0:T(8,128)S(1)}, u32[]{:S(2)}, u32[]{:S(2)}) collective-permute-start(f32[8,128]{1,0:T(8,128)S(1)} %add_add_fusion.refs_0_), channel_id=1, source_target_pairs={{12,0},{16,4},{20,8},{24,12},{28,16},{0,20},{4,24},{8,28},{13,1},{... | collective-permute-start | bytes 12296 | tf_op jit(solution)/shard_map/ppermute | solution.py:445
  (6 other events, 41.1 us)
